TPU v7x, 32 devices: a whole 2x2x4 slice. The times are simulated.
32 devices in a mesh: groups: 2 (over y), dp: 4 (over z), layer: 4 (over x, core).
Axes of the slice: x: 2, y: 2, z: 4, core: 2. Of those that a mesh axis runs over, the one named last changes fastest.
Arguments:
- acts_in: bfloat16 [8, 2, 64, 4, 4096], P(('groups', 'dp'), None, None, 'layer'), parts along dimension 0, may hold values from -6 to 6
- grads_out: bfloat16 [8, 2, 64, 4, 4096], P(('groups', 'dp'), None, None, 'layer'), parts along dimension 0, may hold values from -6 to 6
- proj_in: bfloat16 [4, 4096, 64], P('layer'), may hold values from -0.09375 to 0.09375
- proj_out: bfloat16 [4, 4096, 64], P('layer'), may hold values from -0.09375 to 0.09375
- query_grads: bfloat16 [256, 4, 4096], P('dp', 'layer'), may hold values from -6 to 6
- margin: float32 [8], P(('groups', 'dp')), parts along dimension 0, may hold values from -8 to 8
- labels: int32 [8], P(('groups', 'dp')), parts along dimension 0, may hold values from 0 to 1
- lengths: int32 [8, 2], P(('groups', 'dp')), parts along dimension 0, may hold values from 16 to 64
Outputs:
- scores: float32 [8, 256], P(('groups', 'dp'), 'layer'), parts along dimension 0
There are 2 independent parts, one for each index of `groups`. A program takes and returns all parts, laid end to end along the dimension named above; an argument that names none is the same for every part. Nothing has to cross between parts.
All inputs are finite; a program needn't handle non-finite values.
Results may differ from a plain program's by a relative error of at most 0.011.
Values may be sent and summed in bfloat16 or wider, within the bound.
No kernel may reach another device: no remote copies, remote signals or barrier semaphores. Data moves between devices by JAX's collectives and lax.ppermute only.
A program may use at most 64 MiB of HBM per device.

v0:
```python
import math

import jax
import jax.numpy as jnp
from jax import lax
from jax.sharding import PartitionSpec as P


def local(acts_in, grads_out, proj_in, proj_out, query_grads, margin, labels, lengths):
    pair_count, side_count, seq_len, layer_count, model_width = acts_in.shape
    rank = proj_in.shape[2]
    layers_all = layer_count * lax.axis_size("layer")
    in_coords = jnp.einsum("pstld,ldr->pstlr", acts_in, proj_in, preferred_element_type=jnp.float32)
    out_coords = jnp.einsum(
        "pstld,ldr->pstlr", grads_out, proj_out, preferred_element_type=jnp.float32
    )
    position = jnp.arange(seq_len, dtype=jnp.int32)
    live = (position[None, None, :] < lengths[:, :, None]).astype(jnp.float32)
    side = jnp.arange(side_count, dtype=jnp.int32)
    signs = jnp.where(side[None, :] == labels[:, None], 1.0, -1.0).astype(jnp.float32)
    pair_weight = jax.nn.sigmoid(-margin)
    tok_weight = live * signs[:, :, None] * pair_weight[:, None, None] / math.sqrt(seq_len)
    kron_grads = jnp.einsum("pst,pstlr,pstlk->plrk", tok_weight, out_coords, in_coords)
    grad_rows = kron_grads.reshape(pair_count, layer_count * rank * rank).astype(jnp.bfloat16)
    piece = lax.all_gather(query_grads, "dp", axis=0, tiled=True)
    block = piece.reshape(piece.shape[0], -1)
    part_scores = jnp.einsum("pk,qk->pq", grad_rows, block, preferred_element_type=jnp.float32)
    summed = lax.psum_scatter(part_scores, "layer", scatter_dimension=1, tiled=True)
    return summed / (rank * math.sqrt(layers_all))


def solution(mesh):
    placed = (
        P(("groups", "dp"), None, None, "layer", None),
        P(("groups", "dp"), None, None, "layer", None),
        P("layer", None, None),
        P("layer", None, None),
        P("dp", "layer", None),
        P(("groups", "dp")),
        P(("groups", "dp")),
        P(("groups", "dp"), None),
    )
    return jax.shard_map(
        local, mesh=mesh, in_specs=placed, out_specs=P(("groups", "dp"), "layer"), check_vma=False
    )
```

profile of v0, /device:TPU:0, one launch (start us, length us, event | category | flops | bytes accessed | tf_op | source)
XLA Modules:
  0.0 87.2 jit_solution(16900507008182692994)
XLA Ops:
  6.5 0.0 copy-start
  6.5 0.0 copy-start.2
  6.5 0.0 copy-start.1
  6.5 0.0 all-gather.2.cloned.1.call-start
  6.5 0.7 all-gather.2.cloned.1.call-update
  7.3 0.0 reduce-scatter.4.cloned.1.call-start
  8.7 0.7 fusion.17
  9.5 0.0 copy-done
  9.5 1.7 %convolution_bitcast_fusion = bf16[2,64,64]{1,2,0:T(8,128)(2,1)S(1)} fusion(bf16[1,2,64,1,4096]{4,2,3,1,0:T(8,128)(2,1)S(1)} %copy-done, bf16[1,4096,64]{1,2,0:T(8,128)(2,1)} %param.10), kind=kOutput, calls=%fused_computation.3 | convolution fusion | flops 67108864 | bytes 1589248 | tf_op jit(solution)/shard_map/pstld,ldr->pstlr/dot_general | solution.py:13
  11.1 0.0 copy-done.2
  11.1 0.0 copy-done.1
  11.1 0.7 fusion.8
  11.9 0.1 reshape.89
  12.0 45.6 %all-gather.2.cloned.1.call-done = bf16[256,1,4096]{2,0,1:T(8,128)(2,1)} async-done(((bf16[64,1,4096]{2,0,1:T(8,128)(2,1)}), bf16[256,1,4096]{2,0,1:T(8,128)(2,1)}) %all-gather.2.cloned.1.call-update) | async-done | bytes 2097168 | tf_op jit(solution)/shard_map/all_gather | solution.py:25
  57.6 2.9 %fusion.2 = f32[256,1]{1,0:T(8,128)} fusion(bf16[4096,1]{0,1:T(2,128)(2,1)S(1)} %reshape.89, bf16[256,1,4096]{2,0,1:T(8,128)(2,1)} %all-gather.2.cloned.1.call-done), kind=kOutput, calls=%fused_computation.2 | convolution fusion | flops 2097152 | bytes 2106368
  60.5 0.0 reduce-scatter.4.cloned.1.call-update
  60.5 18.4 %reduce-scatter.4.cloned.1.call-done = f32[64,1]{1,0:T(8,128)} async-done(((f32[256,1]{1,0:T(8,128)}), f32[64,1]{1,0:T(8,128)}) %reduce-scatter.4.cloned.1.call-update) | async-done | bytes 272
  79.0 0.8 copy.13
  79.8 0.5 broadcast_multiply_fusion
  (1 shorter events, 0.0 us)
Async XLA Ops:
  6.5 2.9 %copy-start = (bf16[1,2,64,1,4096]{4,2,3,1,0:T(8,128)(2,1)S(1)}, bf16[1,2,64,1,4096]{4,2,3,1,0:T(8,128)(2,1)}, u32[]{:S(2)}) copy-start(bf16[1,2,64,1,4096]{4,2,3,1,0:T(8,128)(2,1)} %param.8) | copy-start | bytes 3145732
  6.5 4.6 %copy-start.2 = (bf16[1,4096,64]{1,2,0:T(8,128)(2,1)S(1)}, bf16[1,4096,64]{1,2,0:T(8,128)(2,1)}, u32[]{:S(2)}) copy-start(bf16[1,4096,64]{1,2,0:T(8,128)(2,1)} %param.11) | copy-start | bytes 1572868
  6.5 4.6 %copy-start.1 = (bf16[1,2,64,1,4096]{4,2,3,1,0:T(8,128)(2,1)S(1)}, bf16[1,2,64,1,4096]{4,2,3,1,0:T(8,128)(2,1)}, u32[]{:S(2)}) copy-start(bf16[1,2,64,1,4096]{4,2,3,1,0:T(8,128)(2,1)} %param.9) | copy-start | bytes 3145732
  6.5 51.1 %all-gather.2.cloned.1.call-start = ((), (), s32[]{:S(2)}) async-start(), calls=%async_computation.1 | async-start | bytes 2621440 | tf_op jit(solution)/shard_map/all_gather | solution.py:25
  7.3 71.7 %reduce-scatter.4.cloned.1.call-start = ((), (), s32[]{:S(2)}) async-start(), calls=%async_computation.2 | async-start | bytes 163840
Sparse Core Ops, SparseCore 0:
  8.9 48.6 all-gather.1
  60.7 18.2 reduce-scatter.3
where the time goes:
time: 87.5 us; the launch traced here: 87.2 us
  waiting for transfers between devices  64.8 us (74%)
  between operations  14.8 us (17%)
  matrix products  5.33 us (6%)
  other arithmetic  1.26 us (1%)
  local copies, waits for them, and re-layouts  0.93 us (1%)
    all_gather x1, waiting for transfers between devices, local(): piece = lax.all_gather(query_grads, 'dp', axis=0, tiled=True)  45.6 us
    unnamed x3, waiting for transfers between devices  19.2 us
    unnamed x1, matrix products  2.92 us
  transfers between devices with their start and end apart: 2, of which 2 were waited for; matrix products, arithmetic and copies ran while one was open for 4% of the time, Pallas kernels for 0%

commit v1 on v0

--- a/solution.py
+++ b/solution.py
@@ -5,11 +5,38 @@
 from jax import lax
 from jax.sharding import PartitionSpec as P
 
+FEW = 8
+
+
+def gather_pairs(rows, count):
+    got = [rows]
+    for step in range(1, count):
+        pairs = [(i, (i + step) % count) for i in range(count)]
+        got.append(lax.ppermute(rows, "dp", pairs))
+    return got
+
+
+def send_home(scores, dp_count, layer_count):
+    share = dp_count // layer_count
+    mine, layer = lax.axis_index("dp"), lax.axis_index("layer")
+    total = []
+    lane = (mine % share) * layer_count + layer
+    for turn in range(dp_count):
+        pair = (lane + turn) % dp_count
+        row = lax.dynamic_index_in_dim(scores, (mine - pair) % dp_count, 0, keepdims=False)
+        moves = []
+        for d in range(dp_count):
+            for l in range(layer_count):
+                target = ((d % share) * layer_count + l + turn) % dp_count
+                moves.append((d * layer_count + l, target * layer_count + d // share))
+        total.append(lax.ppermute(row, ("dp", "layer"), moves))
+    return total
+
 
 def local(acts_in, grads_out, proj_in, proj_out, query_grads, margin, labels, lengths):
     pair_count, side_count, seq_len, layer_count, model_width = acts_in.shape
     rank = proj_in.shape[2]
-    layers_all = layer_count * lax.axis_size("layer")
+    dp_size, layer_size = lax.axis_size("dp"), lax.axis_size("layer")
     in_coords = jnp.einsum("pstld,ldr->pstlr", acts_in, proj_in, preferred_element_type=jnp.float32)
     out_coords = jnp.einsum(
         "pstld,ldr->pstlr", grads_out, proj_out, preferred_element_type=jnp.float32
@@ -22,11 +49,18 @@
     tok_weight = live * signs[:, :, None] * pair_weight[:, None, None] / math.sqrt(seq_len)
     kron_grads = jnp.einsum("pst,pstlr,pstlk->plrk", tok_weight, out_coords, in_coords)
     grad_rows = kron_grads.reshape(pair_count, layer_count * rank * rank).astype(jnp.bfloat16)
-    piece = lax.all_gather(query_grads, "dp", axis=0, tiled=True)
-    block = piece.reshape(piece.shape[0], -1)
-    part_scores = jnp.einsum("pk,qk->pq", grad_rows, block, preferred_element_type=jnp.float32)
-    summed = lax.psum_scatter(part_scores, "layer", scatter_dimension=1, tiled=True)
-    return summed / (rank * math.sqrt(layers_all))
+    block = query_grads.reshape(query_grads.shape[0], -1)
+    scale = rank * math.sqrt(layer_count * layer_size)
+    if dp_size <= FEW and pair_count == 1 and dp_size % layer_size == 0:
+        rows = jnp.concatenate(gather_pairs(grad_rows, dp_size), axis=0)
+        scores = jnp.einsum("pk,qk->pq", rows, block, preferred_element_type=jnp.float32)
+        parts = send_home(scores, dp_size, layer_size)
+        return sum(parts[1:], parts[0])[None] / scale
+    rows = lax.all_gather(grad_rows, "dp", axis=0, tiled=True)
+    scores = jnp.einsum("pk,qk->pq", rows, block, preferred_element_type=jnp.float32)
+    scores = lax.all_to_all(scores, "dp", split_axis=0, concat_axis=1, tiled=True)
+    summed = lax.psum_scatter(scores, "layer", scatter_dimension=1, tiled=True)
+    return summed / scale
 
 
 def solution(mesh):

time: 87.5 us -> 25.6 us (0.29)
  the two profiles are of different devices: /device:TPU:0 before, /device:TPU:1 now
where the time goes in v1:
time: 25.6 us; the launch traced here: 25.4 us
  starting transfers between devices  13.3 us (52%)
  waiting for transfers between devices  6.41 us (25%)
  matrix products  2.71 us (11%)
  between operations  1.59 us (6%)
  local copies, waits for them, and re-layouts  0.78 us (3%)
  other arithmetic  0.59 us (2%)
    ppermute x4, starting transfers between devices, send_home(): total.append(lax.ppermute(row, ('dp', 'layer'), moves))  8.68 us
    ppermute x3, starting transfers between devices, gather_pairs(): got.append(lax.ppermute(rows, 'dp', pairs))  4.61 us
    ppermute x3, waiting for transfers between devices, gather_pairs(): got.append(lax.ppermute(rows, 'dp', pairs))  3.94 us
    ppermute x4, waiting for transfers between devices, send_home(): total.append(lax.ppermute(row, ('dp', 'layer'), moves))  2.48 us
    dot_general x1, matrix products, local(): jnp.einsum('pstld,ldr->pstlr', acts_in, proj_in, preferred_element_type=j...  1.72 us
    dot_general x1, matrix products, local(): jnp.einsum('pst,pstlr,pstlk->plrk', tok_weight, out_coords, in_coords)  0.74 us
    unnamed x10, local copies, waits for them, and re-layouts  0.67 us
    div x1, other arithmetic, local(): return sum(parts[1:], parts[0])[None] / scale  0.52 us
  transfers between devices with their start and end apart: 7, of which 5 were waited for; matrix products, arithmetic and copies ran while one was open for 0% of the time, Pallas kernels for 0%

profile of v1, /device:TPU:1, one launch (start us, length us, event | category | flops | bytes accessed | tf_op | source)
XLA Modules:
  0.0 25.4 jit_solution(17712247677811821029)
XLA Ops:
  0.0 0.0 copy-start
  0.0 0.0 copy-start.1
  1.5 0.0 copy-done
  1.6 0.0 copy-start.3
  1.6 1.7 %convolution_bitcast_fusion = bf16[2,64,64]{1,2,0:T(8,128)(2,1)S(1)} fusion(bf16[1,2,64,1,4096]{4,2,3,1,0:T(8,128)(2,1)S(1)} %copy-done, bf16[1,4096,64]{1,2,0:T(8,128)(2,1)} %param.10), kind=kOutput, calls=%fused_computation | convolution fusion | flops 67108864 | bytes 1589248 | tf_op jit(solution)/shard_map/pstld,ldr->pstlr/dot_general | solution.py:40
  3.3 0.0 copy-start.4
  3.3 0.6 %copy-done.4 = s32[1,2]{1,0:T(1,128)S(1)} copy-done((s32[1,2]{1,0:T(1,128)S(1)}, s32[1,2]{1,0:T(1,128)}, u32[]{:S(2)}) %copy-start.4) | copy-done | bytes 32
  4.0 0.1 fusion.21
  4.0 0.0 copy-done.1
  4.0 0.0 copy-done.3
  4.0 0.0 copy-start.2
  4.0 0.7 %fusion.3 = bf16[64,64]{1,0:T(8,128)(2,1)S(1)} fusion(bf16[2,64,64]{1,2,0:T(8,128)(2,1)S(1)} %convolution_bitcast_fusion, bf16[1,2,64,1,4096]{4,2,3,1,0:T(8,128)(2,1)S(1)} %copy-done.1, bf16[1,4096,64]{1,2,0:T(8,128)(2,1)S(1)} %copy-done.3, f32[2,64]{1,0:T(2,128)S(1)} %fusion.21), kind=kOutput, calls=%fused_computation.5 | convolution fusion | flops 68165632 | bytes 1597952 | tf_op jit(solution)/shard_map/pst,pstlr,pstlk->plrk/dot_general | solution.py:50
  4.8 0.1 convert_element_type.16
  4.9 4.2 %collective-permute-start.2 = (bf16[1,4096]{1,0:T(2,128)(2,1)S(1)}, bf16[1,4096]{1,0:T(2,128)(2,1)S(1)}, u32[]{:S(2)}, u32[]{:S(2)}) collective-permute-start(bf16[1,4096]{1,0:T(2,128)(2,1)S(1)} %convert_element_type.16), channel_id=1, source_target_pairs={{0,12},{4,0},{8,4},{12,8},{1,13},{5,1},{9,5},{13,9},{2,14},{6,2},{... | collective-permute-start | bytes 24584 | tf_op jit(solution)/shard_map/ppermute | solution.py:15
  9.0 0.0 collective-permute-start.1
  9.0 0.4 %collective-permute-start = (bf16[1,4096]{1,0:T(2,128)(2,1)S(1)}, bf16[1,4096]{1,0:T(2,128)(2,1)S(1)}, u32[]{:S(2)}, u32[]{:S(2)}) collective-permute-start(bf16[1,4096]{1,0:T(2,128)(2,1)S(1)} %convert_element_type.16), channel_id=1, source_target_pairs={{0,4},{4,8},{8,12},{12,0},{1,5},{5,9},{9,13},{13,1},{2,6},{6,10},{... | collective-permute-start | bytes 24584 | tf_op jit(solution)/shard_map/ppermute | solution.py:15
  9.5 0.4 %collective-permute-done.2 = bf16[1,4096]{1,0:T(2,128)(2,1)S(1)} collective-permute-done((bf16[1,4096]{1,0:T(2,128)(2,1)S(1)}, bf16[1,4096]{1,0:T(2,128)(2,1)S(1)}, u32[]{:S(2)}, u32[]{:S(2)}) %collective-permute-start.2) | collective-permute-done | bytes 8224 | tf_op jit(solution)/shard_map/ppermute | solution.py:15
  9.9 2.6 %collective-permute-done.1 = bf16[1,4096]{1,0:T(2,128)(2,1)S(1)} collective-permute-done((bf16[1,4096]{1,0:T(2,128)(2,1)S(1)}, bf16[1,4096]{1,0:T(2,128)(2,1)S(1)}, u32[]{:S(2)}, u32[]{:S(2)}) %collective-permute-start.1) | collective-permute-done | bytes 8224 | tf_op jit(solution)/shard_map/ppermute | solution.py:15
  12.5 0.9 %collective-permute-done = bf16[1,4096]{1,0:T(2,128)(2,1)S(1)} collective-permute-done((bf16[1,4096]{1,0:T(2,128)(2,1)S(1)}, bf16[1,4096]{1,0:T(2,128)(2,1)S(1)}, u32[]{:S(2)}, u32[]{:S(2)}) %collective-permute-start) | collective-permute-done | bytes 8224 | tf_op jit(solution)/shard_map/ppermute | solution.py:15
  13.4 0.0 copy-done.2
  13.4 0.2 fusion.7
  13.7 2.2 %collective-permute-start.6 = (f32[64]{0:T(128)S(1)}, f32[64]{0:T(128)S(1)}, u32[]{:S(2)}, u32[]{:S(2)}) collective-permute-start(f32[64]{0:T(128)S(1)} %get-tuple-element.6), channel_id=1, source_target_pairs={{0,12},{1,0},{2,4},{3,8},{4,13},{5,1},{6,5},{7,9},{8,14},{9,2},{10... | collective-permute-start | bytes 776 | tf_op jit(solution)/shard_map/ppermute | solution.py:32
  15.9 0.2 collective-permute-start.5
  16.1 5.4 %collective-permute-start.3 = (f32[64]{0:T(128)S(1)}, f32[64]{0:T(128)S(1)}, u32[]{:S(2)}, u32[]{:S(2)}) collective-permute-start(f32[64]{0:T(128)S(1)} %get-tuple-element.8), channel_id=1, source_target_pairs={{0,0},{1,4},{2,8},{3,12},{4,1},{5,5},{6,9},{7,13},{8,2},{9,6},{10,... | collective-permute-start | bytes 776 | tf_op jit(solution)/shard_map/ppermute | solution.py:32
  21.5 0.9 %collective-permute-start.4 = (f32[64]{0:T(128)S(1)}, f32[64]{0:T(128)S(1)}, u32[]{:S(2)}, u32[]{:S(2)}) collective-permute-start(f32[64]{0:T(128)S(1)} %get-tuple-element.5), channel_id=1, source_target_pairs={{0,4},{1,8},{2,12},{3,0},{4,5},{5,9},{6,13},{7,1},{8,6},{9,10},{10... | collective-permute-start | bytes 776 | tf_op jit(solution)/shard_map/ppermute | solution.py:32
  22.4 0.0 collective-permute-done.6
  22.4 0.0 collective-permute-done.5
  22.4 0.3 %collective-permute-done.3 = f32[64]{0:T(128)S(1)} collective-permute-done((f32[64]{0:T(128)S(1)}, f32[64]{0:T(128)S(1)}, u32[]{:S(2)}, u32[]{:S(2)}) %collective-permute-start.3) | collective-permute-done | bytes 288 | tf_op jit(solution)/shard_map/ppermute | solution.py:32
  22.7 2.1 %collective-permute-done.4 = f32[64]{0:T(128)S(1)} collective-permute-done((f32[64]{0:T(128)S(1)}, f32[64]{0:T(128)S(1)}, u32[]{:S(2)}, u32[]{:S(2)}) %collective-permute-start.4) | collective-permute-done | bytes 288 | tf_op jit(solution)/shard_map/ppermute | solution.py:32
  24.9 0.5 %multiply_bitcast_fusion = f32[1,64]{1,0:T(1,128)} fusion(f32[64]{0:T(128)S(1)} %collective-permute-done.6, f32[64]{0:T(128)S(1)} %collective-permute-done.5, f32[64]{0:T(128)S(1)} %collective-permute-done.3, f32[64]{0:T(128)S(1)} %collective-permute-done.4), kind=kLoop, calls=%fused_computation.32 | loop fusion | flops 256 | bytes 1280 | tf_op jit(solution)/shard_map/div | solution.py:58
  (2 shorter events, 0.0 us)
Async XLA Ops:
  0.0 1.5 %copy-start = (bf16[1,2,64,1,4096]{4,2,3,1,0:T(8,128)(2,1)S(1)}, bf16[1,2,64,1,4096]{4,2,3,1,0:T(8,128)(2,1)}, u32[]{:S(2)}) copy-start(bf16[1,2,64,1,4096]{4,2,3,1,0:T(8,128)(2,1)} %param.8) | copy-start | bytes 3145732
  0.0 4.0 %copy-start.1 = (bf16[1,2,64,1,4096]{4,2,3,1,0:T(8,128)(2,1)S(1)}, bf16[1,2,64,1,4096]{4,2,3,1,0:T(8,128)(2,1)}, u32[]{:S(2)}) copy-start(bf16[1,2,64,1,4096]{4,2,3,1,0:T(8,128)(2,1)} %param.9) | copy-start | bytes 3145732
  1.6 2.5 %copy-start.3 = (bf16[1,4096,64]{1,2,0:T(8,128)(2,1)S(1)}, bf16[1,4096,64]{1,2,0:T(8,128)(2,1)}, u32[]{:S(2)}) copy-start(bf16[1,4096,64]{1,2,0:T(8,128)(2,1)} %param.11) | copy-start | bytes 1572868
  3.3 0.7 %copy-start.4 = (s32[1,2]{1,0:T(1,128)S(1)}, s32[1,2]{1,0:T(1,128)}, u32[]{:S(2)}) copy-start(s32[1,2]{1,0:T(1,128)} %param.15) | copy-start | bytes 28
  4.0 9.4 %copy-start.2 = (bf16[64,1,4096]{2,0,1:T(8,128)(2,1)S(1)}, bf16[64,1,4096]{2,0,1:T(8,128)(2,1)}, u32[]{:S(2)}) copy-start(bf16[64,1,4096]{2,0,1:T(8,128)(2,1)} %param.12) | copy-start | bytes 1572868
  4.9 5.0 %collective-permute-start.2 = (bf16[1,4096]{1,0:T(2,128)(2,1)S(1)}, bf16[1,4096]{1,0:T(2,128)(2,1)S(1)}, u32[]{:S(2)}, u32[]{:S(2)}) collective-permute-start(bf16[1,4096]{1,0:T(2,128)(2,1)S(1)} %convert_element_type.16), channel_id=1, source_target_pairs={{0,12},{4,0},{8,4},{12,8},{1,13},{5,1},{9,5},{13,9},{2,14},{6,2},{... | collective-permute-start | bytes 24584 | tf_op jit(solution)/shard_map/ppermute | solution.py:15
  9.0 3.5 %collective-permute-start.1 = (bf16[1,4096]{1,0:T(2,128)(2,1)S(1)}, bf16[1,4096]{1,0:T(2,128)(2,1)S(1)}, u32[]{:S(2)}, u32[]{:S(2)}) collective-permute-start(bf16[1,4096]{1,0:T(2,128)(2,1)S(1)} %convert_element_type.16), channel_id=1, source_target_pairs={{0,8},{4,12},{8,0},{12,4},{1,9},{5,13},{9,1},{13,5},{2,10},{6,14},... | collective-permute-start | bytes 24584 | tf_op jit(solution)/shard_map/ppermute | solution.py:15
  9.0 4.4 %collective-permute-start = (bf16[1,4096]{1,0:T(2,128)(2,1)S(1)}, bf16[1,4096]{1,0:T(2,128)(2,1)S(1)}, u32[]{:S(2)}, u32[]{:S(2)}) collective-permute-start(bf16[1,4096]{1,0:T(2,128)(2,1)S(1)} %convert_element_type.16), channel_id=1, source_target_pairs={{0,4},{4,8},{8,12},{12,0},{1,5},{5,9},{9,13},{13,1},{2,6},{6,10},{... | collective-permute-start | bytes 24584 | tf_op jit(solution)/shard_map/ppermute | solution.py:15
  13.7 8.7 %collective-permute-start.6 = (f32[64]{0:T(128)S(1)}, f32[64]{0:T(128)S(1)}, u32[]{:S(2)}, u32[]{:S(2)}) collective-permute-start(f32[64]{0:T(128)S(1)} %get-tuple-element.6), channel_id=1, source_target_pairs={{0,12},{1,0},{2,4},{3,8},{4,13},{5,1},{6,5},{7,9},{8,14},{9,2},{10... | collective-permute-start | bytes 776 | tf_op jit(solution)/shard_map/ppermute | solution.py:32
  15.9 6.5 %collective-permute-start.5 = (f32[64]{0:T(128)S(1)}, f32[64]{0:T(128)S(1)}, u32[]{:S(2)}, u32[]{:S(2)}) collective-permute-start(f32[64]{0:T(128)S(1)} %get-tuple-element.7), channel_id=1, source_target_pairs={{0,8},{1,12},{2,0},{3,4},{4,9},{5,13},{6,1},{7,5},{8,10},{9,14},{1... | collective-permute-start | bytes 776 | tf_op jit(solution)/shard_map/ppermute | solution.py:32
  16.1 6.6 %collective-permute-start.3 = (f32[64]{0:T(128)S(1)}, f32[64]{0:T(128)S(1)}, u32[]{:S(2)}, u32[]{:S(2)}) collective-permute-start(f32[64]{0:T(128)S(1)} %get-tuple-element.8), channel_id=1, source_target_pairs={{0,0},{1,4},{2,8},{3,12},{4,1},{5,5},{6,9},{7,13},{8,2},{9,6},{10,... | collective-permute-start | bytes 776 | tf_op jit(solution)/shard_map/ppermute | solution.py:32
  21.5 3.4 %collective-permute-start.4 = (f32[64]{0:T(128)S(1)}, f32[64]{0:T(128)S(1)}, u32[]{:S(2)}, u32[]{:S(2)}) collective-permute-start(f32[64]{0:T(128)S(1)} %get-tuple-element.5), channel_id=1, source_target_pairs={{0,4},{1,8},{2,12},{3,0},{4,5},{5,9},{6,13},{7,1},{8,6},{9,10},{10... | collective-permute-start | bytes 776 | tf_op jit(solution)/shard_map/ppermute | solution.py:32

commit v2 on v0

--- a/solution.py
+++ b/solution.py
@@ -5,11 +5,27 @@
 from jax import lax
 from jax.sharding import PartitionSpec as P
 
+FEW = 8
+
+
+def gather_pairs(rows, count):
+    return lax.all_to_all(jnp.broadcast_to(rows, (count, rows.shape[1])), "dp", 0, 0, tiled=True)
+
+
+def send_home(scores, dp_count, layer_count):
+    share = dp_count // layer_count
+    mine = lax.axis_index("dp")
+    here = jnp.arange(layer_count)[None, :, None] == mine // share
+    out = jnp.where(here, scores[:, None, :], 0.0).reshape(dp_count * layer_count, -1)
+    got = lax.all_to_all(out, ("dp", "layer"), 0, 0, tiled=True)
+    got = got.reshape(layer_count, share, layer_count, -1)
+    return got.sum(axis=(0, 2)).reshape(1, -1)
+
 
 def local(acts_in, grads_out, proj_in, proj_out, query_grads, margin, labels, lengths):
     pair_count, side_count, seq_len, layer_count, model_width = acts_in.shape
     rank = proj_in.shape[2]
-    layers_all = layer_count * lax.axis_size("layer")
+    dp_size, layer_size = lax.axis_size("dp"), lax.axis_size("layer")
     in_coords = jnp.einsum("pstld,ldr->pstlr", acts_in, proj_in, preferred_element_type=jnp.float32)
     out_coords = jnp.einsum(
         "pstld,ldr->pstlr", grads_out, proj_out, preferred_element_type=jnp.float32
@@ -22,11 +38,17 @@
     tok_weight = live * signs[:, :, None] * pair_weight[:, None, None] / math.sqrt(seq_len)
     kron_grads = jnp.einsum("pst,pstlr,pstlk->plrk", tok_weight, out_coords, in_coords)
     grad_rows = kron_grads.reshape(pair_count, layer_count * rank * rank).astype(jnp.bfloat16)
-    piece = lax.all_gather(query_grads, "dp", axis=0, tiled=True)
-    block = piece.reshape(piece.shape[0], -1)
-    part_scores = jnp.einsum("pk,qk->pq", grad_rows, block, preferred_element_type=jnp.float32)
-    summed = lax.psum_scatter(part_scores, "layer", scatter_dimension=1, tiled=True)
-    return summed / (rank * math.sqrt(layers_all))
+    block = query_grads.reshape(query_grads.shape[0], -1)
+    scale = rank * math.sqrt(layer_count * layer_size)
+    if dp_size <= FEW and pair_count == 1 and dp_size % layer_size == 0:
+        rows = gather_pairs(grad_rows, dp_size)
+        scores = jnp.einsum("pk,qk->pq", rows, block, preferred_element_type=jnp.float32)
+        return send_home(scores, dp_size, layer_size) / scale
+    rows = lax.all_gather(grad_rows, "dp", axis=0, tiled=True)
+    scores = jnp.einsum("pk,qk->pq", rows, block, preferred_element_type=jnp.float32)
+    scores = lax.all_to_all(scores, "dp", split_axis=0, concat_axis=1, tiled=True)
+    summed = lax.psum_scatter(scores, "layer", scatter_dimension=1, tiled=True)
+    return summed / scale
 
 
 def solution(mesh):

time: 87.5 us -> 29.4 us (0.34)
  waiting for transfers between devices: 64.8 us -> 5.55 us
  between operations: 14.8 us -> 1.61 us
  blocking collectives: 0 us -> 9.26 us
  starting transfers between devices: 0.04 us -> 6.32 us
  matrix products: 5.33 us -> 2.71 us
  local copies, waits for them, and re-layouts: 0.93 us -> 2.1 us
    all_gather x1 -> x0, waiting for transfers between devices: 45.6 us -> none  [local(): piece = lax.all_gather(query_grads, 'dp', axis=0, tiled=True)]
    unnamed x3 -> x0, waiting for transfers between devices: 19.2 us -> none
    all_to_all x0 -> x1, blocking collectives: none -> 9.26 us  [send_home(): got = lax.all_to_all(out, ('dp', 'layer'), 0, 0, tiled=True)]
    all_to_all x0 -> x1, starting transfers between devices: none -> 6.32 us  [gather_pairs(): lax.all_to_all(jnp.broadcast_to(rows, (count, rows.shape[1])), 'dp', 0, 0...]
    all_to_all x0 -> x1, waiting for transfers between devices: none -> 5.55 us  [gather_pairs(): lax.all_to_all(jnp.broadcast_to(rows, (count, rows.shape[1])), 'dp', 0, 0...]
    unnamed x1 -> x0, matrix products: 2.92 us -> none
  transfers between devices with their start and end apart: 2 -> 1, of which waited for: 2 -> 1; matrix products, arithmetic and copies ran while one was open for 4% -> 0% of each run, Pallas kernels for 0% -> 0%
where the time goes in v2:
time: 29.4 us; the launch traced here: 29.1 us
  blocking collectives  9.26 us (31%)
  starting transfers between devices  6.32 us (21%)
  waiting for transfers between devices  5.55 us (19%)
  matrix products  2.71 us (9%)
  local copies, waits for them, and re-layouts  2.1 us (7%)
  between operations  1.61 us (5%)
  other arithmetic  1.54 us (5%)
    all_to_all x1, blocking collectives, send_home(): got = lax.all_to_all(out, ('dp', 'layer'), 0, 0, tiled=True)  9.26 us
    all_to_all x1, starting transfers between devices, gather_pairs(): lax.all_to_all(jnp.broadcast_to(rows, (count, rows.shape[1])), 'dp', 0, 0...  6.32 us
    all_to_all x1, waiting for transfers between devices, gather_pairs(): lax.all_to_all(jnp.broadcast_to(rows, (count, rows.shape[1])), 'dp', 0, 0...  5.55 us
    dot_general x1, matrix products, local(): jnp.einsum('pstld,ldr->pstlr', acts_in, proj_in, preferred_element_type=j...  1.72 us
    unnamed x12, local copies, waits for them, and re-layouts  1.35 us
    broadcast_in_dim x1, other arithmetic, gather_pairs(): jnp.broadcast_to(rows, (count, rows.shape[1]))  0.83 us
    dot_general x1, matrix products, local(): jnp.einsum('pst,pstlr,pstlk->plrk', tok_weight, out_coords, in_coords)  0.74 us
  transfers between devices with their start and end apart: 1, of which 1 were waited for; matrix products, arithmetic and copies ran while one was open for 0% of the time, Pallas kernels for 0%

profile of v2, /device:TPU:0, one launch (start us, length us, event | category | flops | bytes accessed | tf_op | source)
XLA Modules:
  0.0 29.1 jit_solution(542955798109275424)
XLA Ops:
  0.0 0.0 copy-start
  0.0 0.0 copy-start.1
  1.5 0.0 copy-done
  1.6 0.0 copy-start.3
  1.6 1.7 %convolution_bitcast_fusion = bf16[2,64,64]{1,2,0:T(8,128)(2,1)S(1)} fusion(bf16[1,2,64,1,4096]{4,2,3,1,0:T(8,128)(2,1)S(1)} %copy-done, bf16[1,4096,64]{1,2,0:T(8,128)(2,1)} %param.10), kind=kOutput, calls=%fused_computation | convolution fusion | flops 67108864 | bytes 1589248 | tf_op jit(solution)/shard_map/pstld,ldr->pstlr/dot_general | solution.py:29
  3.3 0.0 copy-start.4
  3.3 0.7 %copy-done.4 = s32[1,2]{1,0:T(1,128)S(1)} copy-done((s32[1,2]{1,0:T(1,128)S(1)}, s32[1,2]{1,0:T(1,128)}, u32[]{:S(2)}) %copy-start.4) | copy-done | bytes 32
  4.0 0.1 fusion.16
  4.0 0.0 copy-done.1
  4.0 0.0 copy-done.3
  4.0 0.0 copy-start.2
  4.0 0.7 %fusion.3 = bf16[64,64]{1,0:T(8,128)(2,1)S(1)} fusion(bf16[2,64,64]{1,2,0:T(8,128)(2,1)S(1)} %convolution_bitcast_fusion, bf16[1,2,64,1,4096]{4,2,3,1,0:T(8,128)(2,1)S(1)} %copy-done.1, bf16[1,4096,64]{1,2,0:T(8,128)(2,1)S(1)} %copy-done.3, f32[2,64]{1,0:T(2,128)S(1)} %fusion.16), kind=kOutput, calls=%fused_computation.5 | convolution fusion | flops 68165632 | bytes 1597952 | tf_op jit(solution)/shard_map/pst,pstlr,pstlk->plrk/dot_general | solution.py:39
  4.8 0.1 convert_element_type.13
  4.9 0.5 %broadcast.98 = bf16[]{:T(256)} broadcast(bf16[]{:T(256)} %constant.46), dimensions={} | broadcast | bytes 4 | tf_op jit(solution)/shard_map/broadcast_in_dim | solution.py:12
  5.4 0.8 %reduce.3 = bf16[4,4096]{1,0:T(4,128)(2,1)S(1)} reduce(bf16[4,1,4096]{2,1,0:T(2,128)(2,1)S(1)} %broadcast_in_dim.52, bf16[]{:T(256)} %broadcast.98), dimensions={1}, to_apply=%broadcast_in_dim.52.reduce_sub_computation | reduce | bytes 65538 | tf_op jit(solution)/shard_map/broadcast_in_dim | solution.py:12
  6.3 0.6 %reshape.157 = bf16[4,2,2048]{2,1,0:T(2,128)(2,1)} reshape(bf16[4,4096]{1,0:T(4,128)(2,1)S(1)} %reduce.3) | data formatting | bytes 65536
  6.9 6.3 %all-to-all-start = ((bf16[4,2,2048]{2,1,0:T(2,128)(2,1)}), bf16[4,2,2048]{2,1,0:T(2,128)(2,1)S(1)}, u32[]{:S(2)}, u32[]{:S(2)}) async-start(bf16[4,2,2048]{2,1,0:T(2,128)(2,1)} %reshape.157), calls=%async_computation | async-start | bytes 65536 | tf_op jit(solution)/shard_map/all_to_all | solution.py:12
  13.2 0.1 broadcast_in_dim.48
  13.3 5.6 %all-to-all-done = bf16[4,2,2048]{2,1,0:T(2,128)(2,1)S(1)} async-done(((bf16[4,2,2048]{2,1,0:T(2,128)(2,1)}), bf16[4,2,2048]{2,1,0:T(2,128)(2,1)S(1)}, u32[]{:S(2)}, u32[]{:S(2)}) %all-to-all-start) | async-done | bytes 32800 | tf_op jit(solution)/shard_map/all_to_all | solution.py:12
  18.9 0.0 copy-done.2
  18.9 0.2 fusion.7
  19.2 0.1 broadcast_select_fusion
  19.3 9.3 %all_to_all.15 = f32[16,1,64]{2,1,0:T(1,128)S(1)} all-to-all(f32[16,1,64]{2,1,0:T(1,128)S(1)} %broadcast_select_fusion), channel_id=1, replica_groups=mesh['groups'=2,'dp'=4,'layer'=4] {'dp','layer'}, dimensions={0} | all-to-all | bytes 8192 | tf_op jit(solution)/shard_map/all_to_all | solution.py:20
  28.6 0.5 %multiply_bitcast_fusion = f32[1,64]{1,0:T(1,128)} fusion(f32[64]{0:T(128)S(1)} %reduce_sum.9), kind=kLoop, calls=%fused_computation.20 | loop fusion | flops 64 | bytes 512 | tf_op jit(solution)/shard_map/div | solution.py:46
  (7 shorter events, 0.1 us)
Async XLA Ops:
  0.0 1.5 %copy-start = (bf16[1,2,64,1,4096]{4,2,3,1,0:T(8,128)(2,1)S(1)}, bf16[1,2,64,1,4096]{4,2,3,1,0:T(8,128)(2,1)}, u32[]{:S(2)}) copy-start(bf16[1,2,64,1,4096]{4,2,3,1,0:T(8,128)(2,1)} %param.8) | copy-start | bytes 3145732
  0.0 4.0 %copy-start.1 = (bf16[1,2,64,1,4096]{4,2,3,1,0:T(8,128)(2,1)S(1)}, bf16[1,2,64,1,4096]{4,2,3,1,0:T(8,128)(2,1)}, u32[]{:S(2)}) copy-start(bf16[1,2,64,1,4096]{4,2,3,1,0:T(8,128)(2,1)} %param.9) | copy-start | bytes 3145732
  1.6 2.5 %copy-start.3 = (bf16[1,4096,64]{1,2,0:T(8,128)(2,1)S(1)}, bf16[1,4096,64]{1,2,0:T(8,128)(2,1)}, u32[]{:S(2)}) copy-start(bf16[1,4096,64]{1,2,0:T(8,128)(2,1)} %param.11) | copy-start | bytes 1572868
  3.3 0.7 %copy-start.4 = (s32[1,2]{1,0:T(1,128)S(1)}, s32[1,2]{1,0:T(1,128)}, u32[]{:S(2)}) copy-start(s32[1,2]{1,0:T(1,128)} %param.15) | copy-start | bytes 28
  4.0 14.9 %copy-start.2 = (bf16[64,1,4096]{2,0,1:T(8,128)(2,1)S(1)}, bf16[64,1,4096]{2,0,1:T(8,128)(2,1)}, u32[]{:S(2)}) copy-start(bf16[64,1,4096]{2,0,1:T(8,128)(2,1)} %param.12) | copy-start | bytes 1572868
  6.9 12.0 %all-to-all-start = ((bf16[4,2,2048]{2,1,0:T(2,128)(2,1)}), bf16[4,2,2048]{2,1,0:T(2,128)(2,1)S(1)}, u32[]{:S(2)}, u32[]{:S(2)}) async-start(bf16[4,2,2048]{2,1,0:T(2,128)(2,1)} %reshape.157), calls=%async_computation | async-start | bytes 65536 | tf_op jit(solution)/shard_map/all_to_all | solution.py:12

commit v3 on v0

--- a/solution.py
+++ b/solution.py
@@ -5,11 +5,43 @@
 from jax import lax
 from jax.sharding import PartitionSpec as P
 
+FIRST = (3, 2, 1, 0)
+SECOND = (0, 1, 2, 3)
+
+
+def swap(x):
+    return lax.ppermute(x, "layer", [(i, i ^ 1) for i in range(lax.axis_size("layer"))])
+
+
+def along_dp(x, steps):
+    count = len(steps)
+    moves = [(d * count + i, (d ^ steps[i]) * count + i) for d in range(count) for i in range(count)]
+    return lax.ppermute(x, ("dp", "layer"), moves)
+
+
+def to_owner(x, steps):
+    count = len(steps)
+    moves = [(d * count + i, (d ^ steps[i]) * count + d) for d in range(count) for i in range(count)]
+    return lax.ppermute(x, ("dp", "layer"), moves)
+
+
+def shared_scores(own_row, own_block):
+    other_block = swap(own_block)
+    rows = jnp.concatenate([own_row, swap(own_row)], axis=0)
+    first, second = along_dp(rows, FIRST), along_dp(rows, SECOND)
+
+    def score(got):
+        one = jnp.einsum("k,qk->q", got[0], own_block, preferred_element_type=jnp.float32)
+        two = jnp.einsum("k,qk->q", got[1], other_block, preferred_element_type=jnp.float32)
+        return one + two
+
+    return (to_owner(score(first), FIRST) + to_owner(score(second), SECOND))[None]
+
 
 def local(acts_in, grads_out, proj_in, proj_out, query_grads, margin, labels, lengths):
     pair_count, side_count, seq_len, layer_count, model_width = acts_in.shape
     rank = proj_in.shape[2]
-    layers_all = layer_count * lax.axis_size("layer")
+    dp_size, layer_size = lax.axis_size("dp"), lax.axis_size("layer")
     in_coords = jnp.einsum("pstld,ldr->pstlr", acts_in, proj_in, preferred_element_type=jnp.float32)
     out_coords = jnp.einsum(
         "pstld,ldr->pstlr", grads_out, proj_out, preferred_element_type=jnp.float32
@@ -22,11 +54,15 @@
     tok_weight = live * signs[:, :, None] * pair_weight[:, None, None] / math.sqrt(seq_len)
     kron_grads = jnp.einsum("pst,pstlr,pstlk->plrk", tok_weight, out_coords, in_coords)
     grad_rows = kron_grads.reshape(pair_count, layer_count * rank * rank).astype(jnp.bfloat16)
-    piece = lax.all_gather(query_grads, "dp", axis=0, tiled=True)
-    block = piece.reshape(piece.shape[0], -1)
-    part_scores = jnp.einsum("pk,qk->pq", grad_rows, block, preferred_element_type=jnp.float32)
-    summed = lax.psum_scatter(part_scores, "layer", scatter_dimension=1, tiled=True)
-    return summed / (rank * math.sqrt(layers_all))
+    block = query_grads.reshape(query_grads.shape[0], -1)
+    scale = rank * math.sqrt(layer_count * layer_size)
+    if pair_count == layer_count == 1 and dp_size == layer_size == len(FIRST):
+        return shared_scores(grad_rows, block) / scale
+    rows = lax.all_gather(grad_rows, "dp", axis=0, tiled=True)
+    scores = jnp.einsum("pk,qk->pq", rows, block, preferred_element_type=jnp.float32)
+    scores = lax.all_to_all(scores, "dp", split_axis=0, concat_axis=1, tiled=True)
+    summed = lax.psum_scatter(scores, "layer", scatter_dimension=1, tiled=True)
+    return summed / scale
 
 
 def solution(mesh):

time: 87.5 us -> 25.8 us (0.29)
  waiting for transfers between devices: 64.8 us -> 2.94 us
  starting transfers between devices: 0.04 us -> 16.1 us
  between operations: 14.8 us -> 1.66 us
  matrix products: 5.33 us -> 3.46 us
    all_gather x1 -> x0, waiting for transfers between devices: 45.6 us -> none  [local(): piece = lax.all_gather(query_grads, 'dp', axis=0, tiled=True)]
    unnamed x3 -> x0, waiting for transfers between devices: 19.2 us -> none
    ppermute x0 -> x6, starting transfers between devices: none -> 16.1 us  [the longest x2 8.44 us: to_owner(): return lax.ppermute(x, ('dp', 'layer'), moves)]
    ppermute x0 -> x6, waiting for transfers between devices: none -> 2.94 us  [the longest x2 1.27 us: to_owner(): return lax.ppermute(x, ('dp', 'layer'), moves)]
    unnamed x1 -> x0, matrix products: 2.92 us -> none
    dot_general x0 -> x4, matrix products: none -> 0.98 us  [the longest x2 0.51 us: score(): jnp.einsum('k,qk->q', got[0], own_block, preferred_element_type=jnp.float32)]
  transfers between devices with their start and end apart: 2 -> 6, of which waited for: 2 -> 3; matrix products, arithmetic and copies ran while one was open for 4% -> 14% of each run, Pallas kernels for 0% -> 0%
where the time goes in v3:
time: 25.8 us; the launch traced here: 25.5 us
  starting transfers between devices  16.1 us (62%)
  matrix products  3.46 us (13%)
  waiting for transfers between devices  2.94 us (11%)
  between operations  1.66 us (6%)
  local copies, waits for them, and re-layouts  0.76 us (3%)
  other arithmetic  0.63 us (2%)
    ppermute x2, starting transfers between devices, to_owner(): return lax.ppermute(x, ('dp', 'layer'), moves)  8.44 us
    ppermute x2, starting transfers between devices, along_dp(): return lax.ppermute(x, ('dp', 'layer'), moves)  7.16 us
    dot_general x1, matrix products, local(): jnp.einsum('pstld,ldr->pstlr', acts_in, proj_in, preferred_element_type=j...  1.73 us
    ppermute x2, waiting for transfers between devices, to_owner(): return lax.ppermute(x, ('dp', 'layer'), moves)  1.27 us
    ppermute x2, waiting for transfers between devices, swap(): lax.ppermute(x, 'layer', [(i, i ^ 1) for i in range(lax.axis_size('layer'...  1.16 us
    dot_general x1, matrix products, local(): jnp.einsum('pst,pstlr,pstlk->plrk', tok_weight, out_coords, in_coords)  0.74 us
    unnamed x10, local copies, waits for them, and re-layouts  0.67 us
  transfers between devices with their start and end apart: 6, of which 3 were waited for; matrix products, arithmetic and copies ran while one was open for 14% of the time, Pallas kernels for 0%

profile of v3, /device:TPU:0, one launch (start us, length us, event | category | flops | bytes accessed | tf_op | source)
XLA Modules:
  0.0 25.5 jit_solution(14253031399723971889)
XLA Ops:
  0.0 0.0 copy-start
  0.0 0.0 copy-start.1
  0.0 0.5 %collective-permute-start.2 = (bf16[64,4096]{1,0:T(8,128)(2,1)}, bf16[64,4096]{1,0:T(8,128)(2,1)S(1)}, u32[]{:S(2)}, u32[]{:S(2)}) collective-permute-start(bf16[64,4096]{1,0:T(8,128)(2,1)} %bitcast.79), channel_id=1, source_target_pairs={{0,1},{1,0},{2,3},{3,2},{4,5},{5,4},{6,7},{7,6},{8,9},{9,8},{10,11... | collective-permute-start | bytes 1572872 | tf_op jit(solution)/shard_map/ppermute | solution.py:13
  2.0 0.0 copy-done
  2.0 0.0 copy-start.2
  2.0 1.7 %convolution_bitcast_fusion = bf16[2,64,64]{1,2,0:T(8,128)(2,1)S(1)} fusion(bf16[1,2,64,1,4096]{4,2,3,1,0:T(8,128)(2,1)S(1)} %copy-done, bf16[1,4096,64]{1,2,0:T(8,128)(2,1)} %param.10), kind=kOutput, calls=%fused_computation | convolution fusion | flops 67108864 | bytes 1589248 | tf_op jit(solution)/shard_map/pstld,ldr->pstlr/dot_general | solution.py:45
  3.8 0.0 copy-start.3
  3.8 0.7 %copy-done.3 = s32[1,2]{1,0:T(1,128)S(1)} copy-done((s32[1,2]{1,0:T(1,128)S(1)}, s32[1,2]{1,0:T(1,128)}, u32[]{:S(2)}) %copy-start.3) | copy-done | bytes 32
  4.4 0.1 fusion.14
  4.5 0.0 copy-done.1
  4.5 0.0 copy-done.2
  4.5 0.7 %fusion.3 = bf16[64,64]{1,0:T(8,128)(2,1)S(1)} fusion(bf16[2,64,64]{1,2,0:T(8,128)(2,1)S(1)} %convolution_bitcast_fusion, bf16[1,2,64,1,4096]{4,2,3,1,0:T(8,128)(2,1)S(1)} %copy-done.1, bf16[1,4096,64]{1,2,0:T(8,128)(2,1)S(1)} %copy-done.2, f32[2,64]{1,0:T(2,128)S(1)} %fusion.14), kind=kOutput, calls=%fused_computation.5 | convolution fusion | flops 68165632 | bytes 1597952 | tf_op jit(solution)/shard_map/pst,pstlr,pstlk->plrk/dot_general | solution.py:55
  5.3 0.0 copy-start.4
  5.3 0.1 convert_element_type.16
  5.3 0.0 collective-permute-start
  5.4 1.2 %collective-permute-done = bf16[1,4096]{1,0:T(2,128)(2,1)S(1)} collective-permute-done((bf16[1,4096]{1,0:T(2,128)(2,1)S(1)}, bf16[1,4096]{1,0:T(2,128)(2,1)S(1)}, u32[]{:S(2)}, u32[]{:S(2)}) %collective-permute-start) | collective-permute-done | bytes 8224 | tf_op jit(solution)/shard_map/ppermute | solution.py:13
  6.6 0.7 %collective-permute-start.4 = (bf16[2,4096]{1,0:T(2,128)(2,1)S(1)}, bf16[2,4096]{1,0:T(2,128)(2,1)S(1)}, u32[]{:S(2)}, u32[]{:S(2)}) collective-permute-start(bf16[2,4096]{1,0:T(2,128)(2,1)S(1)} %pad_maximum_fusion), channel_id=1, source_target_pairs={{0,0},{1,5},{2,10},{3,15},{4,4},{5,1},{6,14},{7,11},{8,8},{9,13},{... | collective-permute-start | bytes 49160 | tf_op jit(solution)/shard_map/ppermute | solution.py:19
  7.3 6.5 %collective-permute-start.1 = (bf16[2,4096]{1,0:T(2,128)(2,1)S(1)}, bf16[2,4096]{1,0:T(2,128)(2,1)S(1)}, u32[]{:S(2)}, u32[]{:S(2)}) collective-permute-start(bf16[2,4096]{1,0:T(2,128)(2,1)S(1)} %pad_maximum_fusion), channel_id=1, source_target_pairs={{0,12},{1,9},{2,6},{3,3},{4,8},{5,13},{6,2},{7,7},{8,4},{9,1},{10,... | collective-permute-start | bytes 49160 | tf_op jit(solution)/shard_map/ppermute | solution.py:19
  13.8 0.0 collective-permute-done.4
  13.8 0.0 collective-permute-done.2
  13.8 0.2 convolution_bitcast_fusion.2
  14.0 0.0 copy-done.4
  14.0 0.3 fusion.4
  14.3 0.7 %collective-permute-start.5 = (f32[64]{0:T(128)S(1)}, f32[64]{0:T(128)S(1)}, u32[]{:S(2)}, u32[]{:S(2)}) collective-permute-start(f32[64]{0:T(128)S(1)} %fusion.4), channel_id=1, source_target_pairs={{0,0},{1,4},{2,8},{3,12},{4,5},{5,1},{6,13},{7,9},{8,10},{9,14},{1... | collective-permute-start | bytes 776 | tf_op jit(solution)/shard_map/ppermute | solution.py:25
  15.0 0.5 %collective-permute-done.1 = bf16[2,4096]{1,0:T(2,128)(2,1)S(1)} collective-permute-done((bf16[2,4096]{1,0:T(2,128)(2,1)S(1)}, bf16[2,4096]{1,0:T(2,128)(2,1)S(1)}, u32[]{:S(2)}, u32[]{:S(2)}) %collective-permute-start.1) | collective-permute-done | bytes 16416 | tf_op jit(solution)/shard_map/ppermute | solution.py:19
  15.5 0.2 convolution_bitcast_fusion.4
  15.7 0.3 fusion.5
  16.0 7.8 %collective-permute-start.3 = (f32[64]{0:T(128)S(1)}, f32[64]{0:T(128)S(1)}, u32[]{:S(2)}, u32[]{:S(2)}) collective-permute-start(f32[64]{0:T(128)S(1)} %fusion.5), channel_id=1, source_target_pairs={{0,12},{1,8},{2,4},{3,0},{4,9},{5,13},{6,1},{7,5},{8,6},{9,2},{10,... | collective-permute-start | bytes 776 | tf_op jit(solution)/shard_map/ppermute | solution.py:25
  23.7 0.0 collective-permute-done.5
  23.8 1.3 %collective-permute-done.3 = f32[64]{0:T(128)S(1)} collective-permute-done((f32[64]{0:T(128)S(1)}, f32[64]{0:T(128)S(1)}, u32[]{:S(2)}, u32[]{:S(2)}) %collective-permute-start.3) | collective-permute-done | bytes 288 | tf_op jit(solution)/shard_map/ppermute | solution.py:25
  25.0 0.5 %multiply_bitcast_fusion = f32[1,64]{1,0:T(1,128)} fusion(f32[64]{0:T(128)S(1)} %collective-permute-done.3, f32[64]{0:T(128)S(1)} %collective-permute-done.5), kind=kLoop, calls=%fused_computation.26 | loop fusion | flops 128 | bytes 768 | tf_op jit(solution)/shard_map/div | solution.py:60
  (2 shorter events, 0.0 us)
Async XLA Ops:
  0.0 2.0 %copy-start = (bf16[1,2,64,1,4096]{4,2,3,1,0:T(8,128)(2,1)S(1)}, bf16[1,2,64,1,4096]{4,2,3,1,0:T(8,128)(2,1)}, u32[]{:S(2)}) copy-start(bf16[1,2,64,1,4096]{4,2,3,1,0:T(8,128)(2,1)} %param.8) | copy-start | bytes 3145732
  0.0 4.5 %copy-start.1 = (bf16[1,2,64,1,4096]{4,2,3,1,0:T(8,128)(2,1)S(1)}, bf16[1,2,64,1,4096]{4,2,3,1,0:T(8,128)(2,1)}, u32[]{:S(2)}) copy-start(bf16[1,2,64,1,4096]{4,2,3,1,0:T(8,128)(2,1)} %param.9) | copy-start | bytes 3145732
  0.0 13.8 %collective-permute-start.2 = (bf16[64,4096]{1,0:T(8,128)(2,1)}, bf16[64,4096]{1,0:T(8,128)(2,1)S(1)}, u32[]{:S(2)}, u32[]{:S(2)}) collective-permute-start(bf16[64,4096]{1,0:T(8,128)(2,1)} %bitcast.79), channel_id=1, source_target_pairs={{0,1},{1,0},{2,3},{3,2},{4,5},{5,4},{6,7},{7,6},{8,9},{9,8},{10,11... | collective-permute-start | bytes 1572872 | tf_op jit(solution)/shard_map/ppermute | solution.py:13
  2.0 2.5 %copy-start.2 = (bf16[1,4096,64]{1,2,0:T(8,128)(2,1)S(1)}, bf16[1,4096,64]{1,2,0:T(8,128)(2,1)}, u32[]{:S(2)}) copy-start(bf16[1,4096,64]{1,2,0:T(8,128)(2,1)} %param.11) | copy-start | bytes 1572868
  3.8 0.7 %copy-start.3 = (s32[1,2]{1,0:T(1,128)S(1)}, s32[1,2]{1,0:T(1,128)}, u32[]{:S(2)}) copy-start(s32[1,2]{1,0:T(1,128)} %param.15) | copy-start | bytes 28
  5.3 8.8 %copy-start.4 = (bf16[64,1,4096]{2,0,1:T(8,128)(2,1)S(1)}, bf16[64,1,4096]{2,0,1:T(8,128)(2,1)}, u32[]{:S(2)}) copy-start(bf16[64,1,4096]{2,0,1:T(8,128)(2,1)} %param.12) | copy-start | bytes 1572868
  5.3 1.2 %collective-permute-start = (bf16[1,4096]{1,0:T(2,128)(2,1)S(1)}, bf16[1,4096]{1,0:T(2,128)(2,1)S(1)}, u32[]{:S(2)}, u32[]{:S(2)}) collective-permute-start(bf16[1,4096]{1,0:T(2,128)(2,1)S(1)} %convert_element_type.16), channel_id=1, source_target_pairs={{0,1},{1,0},{2,3},{3,2},{4,5},{5,4},{6,7},{7,6},{8,9},{9,8},{10,11... | collective-permute-start | bytes 24584 | tf_op jit(solution)/shard_map/ppermute | solution.py:13
  6.6 7.2 %collective-permute-start.4 = (bf16[2,4096]{1,0:T(2,128)(2,1)S(1)}, bf16[2,4096]{1,0:T(2,128)(2,1)S(1)}, u32[]{:S(2)}, u32[]{:S(2)}) collective-permute-start(bf16[2,4096]{1,0:T(2,128)(2,1)S(1)} %pad_maximum_fusion), channel_id=1, source_target_pairs={{0,0},{1,5},{2,10},{3,15},{4,4},{5,1},{6,14},{7,11},{8,8},{9,13},{... | collective-permute-start | bytes 49160 | tf_op jit(solution)/shard_map/ppermute | solution.py:19
  7.3 8.2 %collective-permute-start.1 = (bf16[2,4096]{1,0:T(2,128)(2,1)S(1)}, bf16[2,4096]{1,0:T(2,128)(2,1)S(1)}, u32[]{:S(2)}, u32[]{:S(2)}) collective-permute-start(bf16[2,4096]{1,0:T(2,128)(2,1)S(1)} %pad_maximum_fusion), channel_id=1, source_target_pairs={{0,12},{1,9},{2,6},{3,3},{4,8},{5,13},{6,2},{7,7},{8,4},{9,1},{10,... | collective-permute-start | bytes 49160 | tf_op jit(solution)/shard_map/ppermute | solution.py:19
  14.3 9.5 %collective-permute-start.5 = (f32[64]{0:T(128)S(1)}, f32[64]{0:T(128)S(1)}, u32[]{:S(2)}, u32[]{:S(2)}) collective-permute-start(f32[64]{0:T(128)S(1)} %fusion.4), channel_id=1, source_target_pairs={{0,0},{1,4},{2,8},{3,12},{4,5},{5,1},{6,13},{7,9},{8,10},{9,14},{1... | collective-permute-start | bytes 776 | tf_op jit(solution)/shard_map/ppermute | solution.py:25
  16.0 9.1 %collective-permute-start.3 = (f32[64]{0:T(128)S(1)}, f32[64]{0:T(128)S(1)}, u32[]{:S(2)}, u32[]{:S(2)}) collective-permute-start(f32[64]{0:T(128)S(1)} %fusion.5), channel_id=1, source_target_pairs={{0,12},{1,8},{2,4},{3,0},{4,9},{5,13},{6,1},{7,5},{8,6},{9,2},{10,... | collective-permute-start | bytes 776 | tf_op jit(solution)/shard_map/ppermute | solution.py:25

commit v4 on v3

--- a/solution.py
+++ b/solution.py
@@ -1,3 +1,4 @@
+import functools
 import math
 
 import jax
@@ -5,37 +6,48 @@
 from jax import lax
 from jax.sharding import PartitionSpec as P
 
-FIRST = (3, 2, 1, 0)
-SECOND = (0, 1, 2, 3)
+FIRST = ((1, 3, 2, 0), (0, 2, 1, 3), (3, 1, 0, 2), (2, 0, 3, 1))
+SECOND = ((2, 0, 3, 1), (1, 3, 2, 0), (0, 2, 1, 3), (3, 1, 0, 2))
 
 
 def swap(x):
     return lax.ppermute(x, "layer", [(i, i ^ 1) for i in range(lax.axis_size("layer"))])
 
 
-def along_dp(x, steps):
-    count = len(steps)
-    moves = [(d * count + i, (d ^ steps[i]) * count + i) for d in range(count) for i in range(count)]
-    return lax.ppermute(x, ("dp", "layer"), moves)
+def fetch_pair(x, slot):
+    count = len(slot)
+    moves, own = [], []
+    for d in range(count):
+        for i in range(count):
+            if slot[d][i] == d:
+                own.append(d * count + i)
+            else:
+                moves.append((slot[d][i] * count + i, d * count + i))
+    fill = zip(own, own[1::-1] + own[:1:-1])
+    here = lax.axis_index("dp") * count + lax.axis_index("layer")
+    is_own = functools.reduce(jnp.logical_or, [here == i for i in own])
+    return lax.ppermute(x, ("dp", "layer"), moves + list(fill)), is_own
 
 
-def to_owner(x, steps):
-    count = len(steps)
-    moves = [(d * count + i, (d ^ steps[i]) * count + d) for d in range(count) for i in range(count)]
+def to_owner(x, slot):
+    count = len(slot)
+    moves = [(d * count + i, slot[d][i] * count + d) for d in range(count) for i in range(count)]
     return lax.ppermute(x, ("dp", "layer"), moves)
 
 
 def shared_scores(own_row, own_block):
     other_block = swap(own_block)
     rows = jnp.concatenate([own_row, swap(own_row)], axis=0)
-    first, second = along_dp(rows, FIRST), along_dp(rows, SECOND)
+    (first, first_own), (second, second_own) = fetch_pair(rows, FIRST), fetch_pair(rows, SECOND)
 
     def score(got):
         one = jnp.einsum("k,qk->q", got[0], own_block, preferred_element_type=jnp.float32)
         two = jnp.einsum("k,qk->q", got[1], other_block, preferred_element_type=jnp.float32)
         return one + two
 
-    return (to_owner(score(first), FIRST) + to_owner(score(second), SECOND))[None]
+    own = score(rows)
+    first, second = jnp.where(first_own, own, score(first)), jnp.where(second_own, own, score(second))
+    return (to_owner(first, FIRST) + to_owner(second, SECOND))[None]
 
 
 def local(acts_in, grads_out, proj_in, proj_out, query_grads, margin, labels, lengths):

time: 25.8 us -> 22.2 us (0.86)
  starting transfers between devices: 16.1 us -> 9.5 us
  matrix products: 3.46 us -> 7.07 us
  waiting for transfers between devices: 2.94 us -> 2.07 us
    ppermute x2, starting transfers between devices: 8.44 us -> 3.79 us  [to_owner(): return lax.ppermute(x, ('dp', 'layer'), moves)]
    dot_general x2 -> x3, matrix products: 0.47 us -> 3.85 us  [score(): jnp.einsum('k,qk->q', got[1], other_block, preferred_element_type=jnp.flo...]
    ppermute x2, starting transfers between devices: 7.16 us -> 5.22 us  [fetch_pair(): return (lax.ppermute(x, ('dp', 'layer'), moves + list(fill)), is_own)]
    ppermute x2, waiting for transfers between devices: 0.51 us -> 0.01 us  [fetch_pair(): return (lax.ppermute(x, ('dp', 'layer'), moves + list(fill)), is_own)]
    ppermute x2, waiting for transfers between devices: 1.16 us -> 0.77 us  [swap(): lax.ppermute(x, 'layer', [(i, i ^ 1) for i in range(lax.axis_size('layer'...]
    dot_general x2 -> x3, matrix products: 0.51 us -> 0.76 us  [score(): jnp.einsum('k,qk->q', got[0], own_block, preferred_element_type=jnp.float32)]
  transfers between devices with their start and end apart: 6 -> 6, of which waited for: 3 -> 2; matrix products, arithmetic and copies ran while one was open for 14% -> 34% of each run, Pallas kernels for 0% -> 0%
where the time goes in v4:
time: 22.2 us; the launch traced here: 21.8 us
  starting transfers between devices  9.5 us (43%)
  matrix products  7.07 us (32%)
  waiting for transfers between devices  2.07 us (9%)
  between operations  1.61 us (7%)
  local copies, waits for them, and re-layouts  0.92 us (4%)
  other arithmetic  0.63 us (3%)
    ppermute x2, starting transfers between devices, fetch_pair(): return (lax.ppermute(x, ('dp', 'layer'), moves + list(fill)), is_own)  5.22 us
    dot_general x3, matrix products, score(): jnp.einsum('k,qk->q', got[1], other_block, preferred_element_type=jnp.flo...  3.85 us
    ppermute x2, starting transfers between devices, to_owner(): return lax.ppermute(x, ('dp', 'layer'), moves)  3.79 us
    dot_general x1, matrix products, local(): jnp.einsum('pstld,ldr->pstlr', acts_in, proj_in, preferred_element_type=j...  1.73 us
    ppermute x2, waiting for transfers between devices, to_owner(): return lax.ppermute(x, ('dp', 'layer'), moves)  1.29 us
    ppermute x2, waiting for transfers between devices, swap(): lax.ppermute(x, 'layer', [(i, i ^ 1) for i in range(lax.axis_size('layer'...  0.77 us
    dot_general x3, matrix products, score(): jnp.einsum('k,qk->q', got[0], own_block, preferred_element_type=jnp.float32)  0.76 us
    dot_general x1, matrix products, local(): jnp.einsum('pst,pstlr,pstlk->plrk', tok_weight, out_coords, in_coords)  0.74 us
  transfers between devices with their start and end apart: 6, of which 2 were waited for; matrix products, arithmetic and copies ran while one was open for 34% of the time, Pallas kernels for 0%

profile of v4, /device:TPU:0, one launch (start us, length us, event | category | flops | bytes accessed | tf_op | source)
XLA Modules:
  0.0 21.8 jit_solution(11940523167630460416)
XLA Ops:
  0.0 0.0 copy-start
  0.0 0.0 copy-start.1
  0.0 0.5 %collective-permute-start.1 = (bf16[64,4096]{1,0:T(8,128)(2,1)}, bf16[64,4096]{1,0:T(8,128)(2,1)}, u32[]{:S(2)}, u32[]{:S(2)}) collective-permute-start(bf16[64,4096]{1,0:T(8,128)(2,1)} %bitcast.96), channel_id=1, source_target_pairs={{0,1},{1,0},{2,3},{3,2},{4,5},{5,4},{6,7},{7,6},{8,9},{9,8},{10,11... | collective-permute-start | bytes 1572872 | tf_op jit(solution)/shard_map/ppermute | solution.py:14
  2.0 0.0 copy-done
  2.0 0.0 copy-start.2
  2.0 1.7 %convolution_bitcast_fusion = bf16[2,64,64]{1,2,0:T(8,128)(2,1)S(1)} fusion(bf16[1,2,64,1,4096]{4,2,3,1,0:T(8,128)(2,1)S(1)} %copy-done, bf16[1,4096,64]{1,2,0:T(8,128)(2,1)} %param.10), kind=kOutput, calls=%fused_computation | convolution fusion | flops 67108864 | bytes 1589248 | tf_op jit(solution)/shard_map/pstld,ldr->pstlr/dot_general | solution.py:57
  3.8 0.7 %copy-done.3 = s32[1,2]{1,0:T(1,128)S(1)} copy-done((s32[1,2]{1,0:T(1,128)S(1)}, s32[1,2]{1,0:T(1,128)}, u32[]{:S(2)}) %copy-start.3) | copy-done | bytes 32
  4.4 0.1 fusion.18
  4.5 0.0 copy-done.1
  4.5 0.0 copy-done.2
  4.5 0.7 %fusion.3 = bf16[64,64]{1,0:T(8,128)(2,1)S(1)} fusion(bf16[2,64,64]{1,2,0:T(8,128)(2,1)S(1)} %convolution_bitcast_fusion, bf16[1,2,64,1,4096]{4,2,3,1,0:T(8,128)(2,1)S(1)} %copy-done.1, bf16[1,4096,64]{1,2,0:T(8,128)(2,1)S(1)} %copy-done.2, f32[2,64]{1,0:T(2,128)S(1)} %fusion.18), kind=kOutput, calls=%fused_computation.5 | convolution fusion | flops 68165632 | bytes 1597952 | tf_op jit(solution)/shard_map/pst,pstlr,pstlk->plrk/dot_general | solution.py:67
  5.3 0.1 convert_element_type.21
  5.4 0.0 collective-permute-start
  5.4 0.1 reshape.98
  5.5 0.1 copy-done.4
  5.6 0.2 %convolution_bitcast_fusion.7 = f32[64]{0:T(128)S(1)} fusion(bf16[4096,1]{0,1:T(2,128)(2,1)S(1)} %reshape.98, bf16[64,1,4096]{2,0,1:T(8,128)(2,1)S(1)} %copy-done.4), kind=kOutput, calls=%fused_computation.16 | convolution fusion | flops 524288 | bytes 532736 | tf_op jit(solution)/shard_map/k,qk->q/dot_general | solution.py:44
  5.8 0.8 %collective-permute-done = bf16[1,4096]{1,0:T(2,128)(2,1)S(1)} collective-permute-done((bf16[1,4096]{1,0:T(2,128)(2,1)S(1)}, bf16[1,4096]{1,0:T(2,128)(2,1)S(1)}, u32[]{:S(2)}, u32[]{:S(2)}) %collective-permute-start) | collective-permute-done | bytes 8224 | tf_op jit(solution)/shard_map/ppermute | solution.py:14
  6.6 2.6 %collective-permute-start.2 = (bf16[2,4096]{1,0:T(2,128)(2,1)S(1)}, bf16[2,4096]{1,0:T(2,128)(2,1)S(1)}, u32[]{:S(2)}, u32[]{:S(2)}) collective-permute-start(bf16[2,4096]{1,0:T(2,128)(2,1)S(1)} %pad_maximum_fusion), channel_id=1, source_target_pairs={{4,0},{13,1},{10,2},{0,4},{9,5},{15,7},{12,8},{5,9},{2,10},{8,12},... | collective-permute-start | bytes 49160 | tf_op jit(solution)/shard_map/ppermute | solution.py:29
  9.2 2.6 %collective-permute-start.4 = (bf16[2,4096]{1,0:T(2,128)(2,1)S(1)}, bf16[2,4096]{1,0:T(2,128)(2,1)S(1)}, u32[]{:S(2)}, u32[]{:S(2)}) collective-permute-start(bf16[2,4096]{1,0:T(2,128)(2,1)S(1)} %pad_maximum_fusion), channel_id=1, source_target_pairs={{8,0},{14,2},{7,3},{13,5},{10,6},{3,7},{0,8},{6,10},{15,11},{5,13}... | collective-permute-start | bytes 49160 | tf_op jit(solution)/shard_map/ppermute | solution.py:29
  11.8 0.0 collective-permute-done.1
  11.8 1.3 %fusion.8 = f32[64]{0:T(128)S(1)} fusion(f32[64]{0:T(128)S(1)} %convolution_bitcast_fusion.7, bf16[64,4096]{1,0:T(8,128)(2,1)} %collective-permute-done.1, bf16[1,4096]{1,0:T(2,128)(2,1)S(1)} %collective-permute-done), kind=kOutput, calls=%fused_computation.15 | convolution fusion | flops 524352 | bytes 532992 | tf_op jit(solution)/shard_map/k,qk->q/dot_general | solution.py:45
  13.1 0.0 collective-permute-done.2
  13.1 1.3 %convolution_bitcast_fusion.4 = f32[64]{0:T(128)S(1)} fusion(bf16[64,4096]{1,0:T(8,128)(2,1)} %collective-permute-done.1, bf16[2,4096]{1,0:T(2,128)(2,1)S(1)} %collective-permute-done.2), kind=kOutput, calls=%fused_computation.10 | convolution fusion | flops 524288 | bytes 540928 | tf_op jit(solution)/shard_map/k,qk->q/dot_general | solution.py:45
  14.4 0.3 %fusion.7 = f32[64]{0:T(128)S(1)} fusion(f32[64]{0:T(128)S(1)} %fusion.8, f32[64]{0:T(128)S(1)} %convolution_bitcast_fusion.4, bf16[2,4096]{1,0:T(2,128)(2,1)S(1)} %collective-permute-done.2, pred[]{:T(512)S(6)} %or.20, bf16[64,1,4096]{2,0,1:T(8,128)(2,1)S(1)} %copy-done.4), kind=kOutput, calls=%fused_computation.13 | convolution fusion | flops 524416 | bytes 541441 | tf_op jit(solution)/shard_map/k,qk->q/dot_general | solution.py:44
  14.7 1.2 %collective-permute-start.3 = (f32[64]{0:T(128)S(1)}, f32[64]{0:T(128)S(1)}, u32[]{:S(2)}, u32[]{:S(2)}) collective-permute-start(f32[64]{0:T(128)S(1)} %fusion.7), channel_id=1, source_target_pairs={{0,4},{1,12},{2,8},{3,0},{4,1},{5,9},{6,5},{7,13},{8,14},{9,6},{10... | collective-permute-start | bytes 776 | tf_op jit(solution)/shard_map/ppermute | solution.py:35
  15.8 0.0 collective-permute-done.4
  15.8 1.3 %convolution_bitcast_fusion.2 = f32[64]{0:T(128)S(1)} fusion(bf16[64,4096]{1,0:T(8,128)(2,1)} %collective-permute-done.1, bf16[2,4096]{1,0:T(2,128)(2,1)S(1)} %collective-permute-done.4), kind=kOutput, calls=%fused_computation.6 | convolution fusion | flops 524288 | bytes 540928 | tf_op jit(solution)/shard_map/k,qk->q/dot_general | solution.py:45
  17.1 0.3 %fusion.5 = f32[64]{0:T(128)S(1)} fusion(f32[64]{0:T(128)S(1)} %fusion.8, f32[64]{0:T(128)S(1)} %convolution_bitcast_fusion.2, bf16[2,4096]{1,0:T(2,128)(2,1)S(1)} %collective-permute-done.4, pred[]{:T(512)S(6)} %or.23, bf16[64,1,4096]{2,0,1:T(8,128)(2,1)S(1)} %copy-done.4), kind=kOutput, calls=%fused_computation.9 | convolution fusion | flops 524416 | bytes 541441 | tf_op jit(solution)/shard_map/k,qk->q/dot_general | solution.py:44
  17.4 2.6 %collective-permute-start.5 = (f32[64]{0:T(128)S(1)}, f32[64]{0:T(128)S(1)}, u32[]{:S(2)}, u32[]{:S(2)}) collective-permute-start(f32[64]{0:T(128)S(1)} %fusion.5), channel_id=1, source_target_pairs={{0,8},{1,0},{2,12},{3,4},{4,5},{5,13},{6,9},{7,1},{8,2},{9,10},{10... | collective-permute-start | bytes 776 | tf_op jit(solution)/shard_map/ppermute | solution.py:35
  20.0 0.0 collective-permute-done.3
  20.0 1.3 %collective-permute-done.5 = f32[64]{0:T(128)S(1)} collective-permute-done((f32[64]{0:T(128)S(1)}, f32[64]{0:T(128)S(1)}, u32[]{:S(2)}, u32[]{:S(2)}) %collective-permute-start.5) | collective-permute-done | bytes 288 | tf_op jit(solution)/shard_map/ppermute | solution.py:35
  21.3 0.5 %multiply_bitcast_fusion = f32[1,64]{1,0:T(1,128)} fusion(f32[64]{0:T(128)S(1)} %collective-permute-done.3, f32[64]{0:T(128)S(1)} %collective-permute-done.5), kind=kLoop, calls=%fused_computation.32 | loop fusion | flops 128 | bytes 768 | tf_op jit(solution)/shard_map/div | solution.py:72
  (4 shorter events, 0.0 us)
Async XLA Ops:
  0.0 2.0 %copy-start = (bf16[1,2,64,1,4096]{4,2,3,1,0:T(8,128)(2,1)S(1)}, bf16[1,2,64,1,4096]{4,2,3,1,0:T(8,128)(2,1)}, u32[]{:S(2)}) copy-start(bf16[1,2,64,1,4096]{4,2,3,1,0:T(8,128)(2,1)} %param.8) | copy-start | bytes 3145732
  0.0 4.5 %copy-start.1 = (bf16[1,2,64,1,4096]{4,2,3,1,0:T(8,128)(2,1)S(1)}, bf16[1,2,64,1,4096]{4,2,3,1,0:T(8,128)(2,1)}, u32[]{:S(2)}) copy-start(bf16[1,2,64,1,4096]{4,2,3,1,0:T(8,128)(2,1)} %param.9) | copy-start | bytes 3145732
  0.0 11.8 %collective-permute-start.1 = (bf16[64,4096]{1,0:T(8,128)(2,1)}, bf16[64,4096]{1,0:T(8,128)(2,1)}, u32[]{:S(2)}, u32[]{:S(2)}) collective-permute-start(bf16[64,4096]{1,0:T(8,128)(2,1)} %bitcast.96), channel_id=1, source_target_pairs={{0,1},{1,0},{2,3},{3,2},{4,5},{5,4},{6,7},{7,6},{8,9},{9,8},{10,11... | collective-permute-start | bytes 1572872 | tf_op jit(solution)/shard_map/ppermute | solution.py:14
  2.0 2.5 %copy-start.2 = (bf16[1,4096,64]{1,2,0:T(8,128)(2,1)S(1)}, bf16[1,4096,64]{1,2,0:T(8,128)(2,1)}, u32[]{:S(2)}) copy-start(bf16[1,4096,64]{1,2,0:T(8,128)(2,1)} %param.11) | copy-start | bytes 1572868
  3.8 0.7 %copy-start.3 = (s32[1,2]{1,0:T(1,128)S(1)}, s32[1,2]{1,0:T(1,128)}, u32[]{:S(2)}) copy-start(s32[1,2]{1,0:T(1,128)} %param.15) | copy-start | bytes 28
  4.5 1.0 %copy-start.4 = (bf16[64,1,4096]{2,0,1:T(8,128)(2,1)S(1)}, bf16[64,1,4096]{2,0,1:T(8,128)(2,1)}, u32[]{:S(2)}) copy-start(bf16[64,1,4096]{2,0,1:T(8,128)(2,1)} %param.12) | copy-start | bytes 1572868
  5.4 1.2 %collective-permute-start = (bf16[1,4096]{1,0:T(2,128)(2,1)S(1)}, bf16[1,4096]{1,0:T(2,128)(2,1)S(1)}, u32[]{:S(2)}, u32[]{:S(2)}) collective-permute-start(bf16[1,4096]{1,0:T(2,128)(2,1)S(1)} %convert_element_type.21), channel_id=1, source_target_pairs={{0,1},{1,0},{2,3},{3,2},{4,5},{5,4},{6,7},{7,6},{8,9},{9,8},{10,11... | collective-permute-start | bytes 24584 | tf_op jit(solution)/shard_map/ppermute | solution.py:14
  6.6 6.5 %collective-permute-start.2 = (bf16[2,4096]{1,0:T(2,128)(2,1)S(1)}, bf16[2,4096]{1,0:T(2,128)(2,1)S(1)}, u32[]{:S(2)}, u32[]{:S(2)}) collective-permute-start(bf16[2,4096]{1,0:T(2,128)(2,1)S(1)} %pad_maximum_fusion), channel_id=1, source_target_pairs={{4,0},{13,1},{10,2},{0,4},{9,5},{15,7},{12,8},{5,9},{2,10},{8,12},... | collective-permute-start | bytes 49160 | tf_op jit(solution)/shard_map/ppermute | solution.py:29
  9.2 6.6 %collective-permute-start.4 = (bf16[2,4096]{1,0:T(2,128)(2,1)S(1)}, bf16[2,4096]{1,0:T(2,128)(2,1)S(1)}, u32[]{:S(2)}, u32[]{:S(2)}) collective-permute-start(bf16[2,4096]{1,0:T(2,128)(2,1)S(1)} %pad_maximum_fusion), channel_id=1, source_target_pairs={{8,0},{14,2},{7,3},{13,5},{10,6},{3,7},{0,8},{6,10},{15,11},{5,13}... | collective-permute-start | bytes 49160 | tf_op jit(solution)/shard_map/ppermute | solution.py:29
  14.7 5.3 %collective-permute-start.3 = (f32[64]{0:T(128)S(1)}, f32[64]{0:T(128)S(1)}, u32[]{:S(2)}, u32[]{:S(2)}) collective-permute-start(f32[64]{0:T(128)S(1)} %fusion.7), channel_id=1, source_target_pairs={{0,4},{1,12},{2,8},{3,0},{4,1},{5,9},{6,5},{7,13},{8,14},{9,6},{10... | collective-permute-start | bytes 776 | tf_op jit(solution)/shard_map/ppermute | solution.py:35
  17.4 3.9 %collective-permute-start.5 = (f32[64]{0:T(128)S(1)}, f32[64]{0:T(128)S(1)}, u32[]{:S(2)}, u32[]{:S(2)}) collective-permute-start(f32[64]{0:T(128)S(1)} %fusion.5), channel_id=1, source_target_pairs={{0,8},{1,0},{2,12},{3,4},{4,5},{5,13},{6,9},{7,1},{8,2},{9,10},{10... | collective-permute-start | bytes 776 | tf_op jit(solution)/shard_map/ppermute | solution.py:35

commit v5 on v4

--- a/solution.py
+++ b/solution.py
@@ -4,10 +4,98 @@
 import jax
 import jax.numpy as jnp
 from jax import lax
+from jax.experimental import pallas as pl
+from jax.experimental.pallas import tpu as pltpu
 from jax.sharding import PartitionSpec as P
 
-FIRST = ((1, 3, 2, 0), (0, 2, 1, 3), (3, 1, 0, 2), (2, 0, 3, 1))
-SECOND = ((2, 0, 3, 1), (1, 3, 2, 0), (0, 2, 1, 3), (3, 1, 0, 2))
+FIRST = ((2, 0, 3, 1), (1, 3, 2, 0), (0, 2, 1, 3), (3, 1, 0, 2))
+SECOND = ((1, 3, 2, 0), (0, 2, 1, 3), (3, 1, 0, 2), (2, 0, 3, 1))
+
+
+CHUNKS = 2
+
+
+def pair_kernel(seq_len, acts, proj_in, grads, proj_out, lengths, out, *scratch):
+    acts_v, pin_v, grads_v, pout_v, kron_v, lengths_s, sems = scratch
+    width = acts.shape[1] // CHUNKS
+    limits = pltpu.make_async_copy(lengths, lengths_s, sems.at[4 * CHUNKS])
+    loads = []
+    for pair in (((acts, acts_v), (proj_in, pin_v)), ((grads, grads_v), (proj_out, pout_v))):
+        for c in range(CHUNKS):
+            part = pl.ds(c * width, width)
+            loads.append([
+                pltpu.make_async_copy(src.at[:, part], dst.at[:, part], sems.at[2 * len(loads) + i])
+                for i, (src, dst) in enumerate(pair)
+            ])
+    for copies in loads:
+        for copy in copies:
+            copy.start()
+    limits.start()
+
+    def project(left, right, steps):
+        total = None
+        for c, copies in enumerate(steps):
+            for copy in copies:
+                copy.wait()
+            part = pl.ds(c * width, width)
+            term = lax.dot_general(
+                left[:, part], right[:, part], (((1,), (1,)), ((), ())), preferred_element_type=jnp.float32
+            )
+            total = term if total is None else total + term
+        return total
+
+    in_coords = project(acts_v, pin_v, loads[:CHUNKS])
+    limits.wait()
+    token = lax.broadcasted_iota(jnp.int32, in_coords.shape, 0)
+    side = token // seq_len
+    live = token - side * seq_len < jnp.where(side == 0, lengths_s[0, 0], lengths_s[0, 1])
+    weight = jnp.where(live, jnp.where(side == 0, 1.0, -1.0), 0.0)
+    in_coords = (in_coords * weight).astype(jnp.bfloat16)
+    out_coords = project(pout_v, grads_v, loads[CHUNKS:]).astype(jnp.bfloat16)
+    kron_v[...] = jnp.dot(out_coords, in_coords, preferred_element_type=jnp.float32)
+    half = kron_v.shape[0] // 2
+    rows = jnp.concatenate([kron_v[pl.ds(i, half, stride=2), :] for i in range(2)], axis=1)
+    for i in range(half):
+        out[:, pl.ds(i * rows.shape[1], rows.shape[1])] = rows[i : i + 1].astype(out.dtype)
+
+
+def pair_gradient(acts_in, grads_out, proj_in, proj_out, lengths):
+    _, sides, seq_len, _, model_width = acts_in.shape
+    rank = proj_in.shape[2]
+    tokens = sides * seq_len
+    anywhere = pl.BlockSpec(memory_space=pl.ANY)
+    return pl.pallas_call(
+        functools.partial(pair_kernel, seq_len),
+        out_shape=jax.ShapeDtypeStruct((1, rank * rank), jnp.bfloat16),
+        in_specs=[anywhere] * 5,
+        out_specs=pl.BlockSpec(memory_space=pltpu.VMEM),
+        scratch_shapes=[
+            pltpu.VMEM((tokens, model_width), jnp.bfloat16),
+            pltpu.VMEM((rank, model_width), jnp.bfloat16),
+            pltpu.VMEM((tokens, model_width), jnp.bfloat16),
+            pltpu.VMEM((rank, model_width), jnp.bfloat16),
+            pltpu.VMEM((rank, rank), jnp.float32),
+            pltpu.SMEM((1, 2), jnp.int32),
+            pltpu.SemaphoreType.DMA((4 * CHUNKS + 1,)),
+        ],
+        compiler_params=pltpu.CompilerParams(vmem_limit_bytes=32 * 1024 * 1024),
+        cost_estimate=pl.CostEstimate(
+            flops=4 * tokens * model_width * rank,
+            bytes_accessed=4 * (tokens + rank) * model_width,
+            transcendentals=0,
+        ),
+    )(
+        *(
+            pltpu.with_memory_space_constraint(x, pltpu.HBM)
+            for x in (
+                acts_in.reshape(tokens, model_width),
+                jnp.swapaxes(proj_in, 1, 2).reshape(rank, model_width),
+                grads_out.reshape(tokens, model_width),
+                jnp.swapaxes(proj_out, 1, 2).reshape(rank, model_width),
+                lengths,
+            )
+        )
+    )
 
 
 def swap(x):
@@ -50,31 +138,37 @@
     return (to_owner(first, FIRST) + to_owner(second, SECOND))[None]
 
 
-def local(acts_in, grads_out, proj_in, proj_out, query_grads, margin, labels, lengths):
-    pair_count, side_count, seq_len, layer_count, model_width = acts_in.shape
-    rank = proj_in.shape[2]
-    dp_size, layer_size = lax.axis_size("dp"), lax.axis_size("layer")
+def pair_gradients(acts_in, grads_out, proj_in, proj_out, lengths):
+    pair_count, side_count, seq_len, layer_count, _ = acts_in.shape
     in_coords = jnp.einsum("pstld,ldr->pstlr", acts_in, proj_in, preferred_element_type=jnp.float32)
     out_coords = jnp.einsum(
         "pstld,ldr->pstlr", grads_out, proj_out, preferred_element_type=jnp.float32
     )
     position = jnp.arange(seq_len, dtype=jnp.int32)
     live = (position[None, None, :] < lengths[:, :, None]).astype(jnp.float32)
-    side = jnp.arange(side_count, dtype=jnp.int32)
-    signs = jnp.where(side[None, :] == labels[:, None], 1.0, -1.0).astype(jnp.float32)
-    pair_weight = jax.nn.sigmoid(-margin)
-    tok_weight = live * signs[:, :, None] * pair_weight[:, None, None] / math.sqrt(seq_len)
-    kron_grads = jnp.einsum("pst,pstlr,pstlk->plrk", tok_weight, out_coords, in_coords)
-    grad_rows = kron_grads.reshape(pair_count, layer_count * rank * rank).astype(jnp.bfloat16)
+    signs = 1.0 - 2.0 * jnp.arange(side_count, dtype=jnp.float32)
+    kron_grads = jnp.einsum("pst,pstlr,pstlk->plrk", live * signs[:, None], out_coords, in_coords)
+    return kron_grads.reshape(pair_count, -1).astype(jnp.bfloat16)
+
+
+def local(acts_in, grads_out, proj_in, proj_out, query_grads, margin, labels, lengths):
+    pair_count, side_count, _, layer_count, _ = acts_in.shape
+    rank = proj_in.shape[2]
+    dp_size, layer_size = lax.axis_size("dp"), lax.axis_size("layer")
     block = query_grads.reshape(query_grads.shape[0], -1)
-    scale = rank * math.sqrt(layer_count * layer_size)
-    if pair_count == layer_count == 1 and dp_size == layer_size == len(FIRST):
-        return shared_scores(grad_rows, block) / scale
+    one_each = pair_count == layer_count == 1 and side_count == 2
+    form = pair_gradient if one_each else pair_gradients
+    grad_rows = form(acts_in, grads_out, proj_in, proj_out, lengths)
+    margin, labels, grad_rows = lax.optimization_barrier((margin, labels, grad_rows))
+    scale = rank * math.sqrt(layer_count * layer_size) * math.sqrt(acts_in.shape[2])
+    factor = jax.nn.sigmoid(-margin) * jnp.where(labels == 0, 1.0, -1.0) / scale
+    if one_each and dp_size == layer_size == len(FIRST):
+        return shared_scores(grad_rows, block) * factor[:, None]
     rows = lax.all_gather(grad_rows, "dp", axis=0, tiled=True)
     scores = jnp.einsum("pk,qk->pq", rows, block, preferred_element_type=jnp.float32)
     scores = lax.all_to_all(scores, "dp", split_axis=0, concat_axis=1, tiled=True)
     summed = lax.psum_scatter(scores, "layer", scatter_dimension=1, tiled=True)
-    return summed / scale
+    return summed * factor[:, None]
 
 
 def solution(mesh):

time: 22.2 us -> 19.4 us (0.87)
  the two profiles are of different devices: /device:TPU:0 before, /device:TPU:2 now
where the time goes in v5:
time: 19.4 us; the launch traced here: 19.2 us
  starting transfers between devices  7.16 us (37%)
  waiting for transfers between devices  5.46 us (28%)
  Pallas kernels  3.1 us (16%)
  matrix products  1.47 us (8%)
  between operations  1.46 us (8%)
  other arithmetic  0.56 us (3%)
    ppermute x2, starting transfers between devices, fetch_pair(): return (lax.ppermute(x, ('dp', 'layer'), moves + list(fill)), is_own)  3.67 us
    pallas_call x1, Pallas kernels, pair_gradient(): pl.pallas_call(functools.partial(pair_kernel, seq_len), out_shape=jax.Sha...  3.1 us
    ppermute x2, starting transfers between devices, to_owner(): return lax.ppermute(x, ('dp', 'layer'), moves)  2.91 us
    ppermute x2, waiting for transfers between devices, to_owner(): return lax.ppermute(x, ('dp', 'layer'), moves)  2.79 us
    ppermute x2, waiting for transfers between devices, fetch_pair(): return (lax.ppermute(x, ('dp', 'layer'), moves + list(fill)), is_own)  2.66 us
    dot_general x3, matrix products, score(): jnp.einsum('k,qk->q', got[0], own_block, preferred_element_type=jnp.float32)  0.76 us
    dot_general x3, matrix products, score(): jnp.einsum('k,qk->q', got[1], other_block, preferred_element_type=jnp.flo...  0.72 us
    ppermute x2, starting transfers between devices, swap(): lax.ppermute(x, 'layer', [(i, i ^ 1) for i in range(lax.axis_size('layer'...  0.58 us
  transfers between devices with their start and end apart: 6, of which 4 were waited for; matrix products, arithmetic and copies ran while one was open for 8% of the time, Pallas kernels for 16%

profile of v5, /device:TPU:2, one launch (start us, length us, event | category | flops | bytes accessed | tf_op | source)
XLA Modules:
  0.0 19.2 jit_solution(5742870677976637156)
XLA Ops:
  0.0 0.0 collective-permute-start.1
  0.0 0.0 copy-start
  0.0 3.1 %shard_map.82 = bf16[1,4096]{1,0:T(2,128)(2,1)S(1)} custom-call(bf16[128,4096]{1,0:T(8,128)(2,1)} %bitcast.61, bf16[64,4096]{1,0:T(8,128)(2,1)} %bitcast.63, bf16[128,4096]{1,0:T(8,128)(2,1)} %bitcast.62, bf16[64,4096]{1,0:T(8,128)(2,1)} %bitcast.64, s32[1,2]{1,0:T(1,128)} %lengths.1), custom_call_target="tpu_custom_call" | custom-call | flops 134217728 | bytes 3145728 | tf_op jit(solution)/shard_map/pallas_call | solution.py:67
  3.1 0.6 %collective-permute-start = (bf16[1,4096]{1,0:T(2,128)(2,1)S(1)}, bf16[1,4096]{1,0:T(2,128)(2,1)S(1)}, u32[]{:S(2)}, u32[]{:S(2)}) collective-permute-start(bf16[1,4096]{1,0:T(2,128)(2,1)S(1)} %shard_map.82), channel_id=1, source_target_pairs={{0,1},{1,0},{2,3},{3,2},{4,5},{5,4},{6,7},{7,6},{8,9},{9,8},{10,11... | collective-permute-start | bytes 24584 | tf_op jit(solution)/shard_map/ppermute | solution.py:102
  3.7 0.0 copy-done
  3.7 0.2 %convolution_bitcast_fusion.5 = f32[64]{0:T(128)S(1)} fusion(bf16[1,4096]{1,0:T(2,128)(2,1)S(1)} %shard_map.82, bf16[64,1,4096]{2,0,1:T(8,128)(2,1)S(1)} %copy-done), kind=kOutput, calls=%fused_computation.10 | convolution fusion | flops 524288 | bytes 532736 | tf_op jit(solution)/shard_map/k,qk->q/dot_general | solution.py:132
  5.4 0.0 collective-permute-done
  5.4 3.7 %collective-permute-start.2 = (bf16[2,4096]{1,0:T(2,128)(2,1)S(1)}, bf16[2,4096]{1,0:T(2,128)(2,1)S(1)}, u32[]{:S(2)}, u32[]{:S(2)}) collective-permute-start(bf16[2,4096]{1,0:T(2,128)(2,1)S(1)} %pad_maximum_fusion), channel_id=1, source_target_pairs={{8,0},{14,2},{7,3},{13,5},{10,6},{3,7},{0,8},{6,10},{15,11},{5,13}... | collective-permute-start | bytes 49160 | tf_op jit(solution)/shard_map/ppermute | solution.py:117
  9.1 0.0 collective-permute-start.4
  9.1 0.0 collective-permute-done.1
  9.1 0.2 %fusion.4 = f32[64]{0:T(128)S(1)} fusion(f32[64]{0:T(128)S(1)} %convolution_bitcast_fusion.5, bf16[64,4096]{1,0:T(8,128)(2,1)S(1)} %collective-permute-done.1, bf16[1,4096]{1,0:T(2,128)(2,1)S(1)} %collective-permute-done), kind=kOutput, calls=%fused_computation.9 | convolution fusion | flops 524352 | bytes 532992 | tf_op jit(solution)/shard_map/k,qk->q/dot_general | solution.py:133
  9.3 1.7 %collective-permute-done.2 = bf16[2,4096]{1,0:T(2,128)(2,1)S(1)} collective-permute-done((bf16[2,4096]{1,0:T(2,128)(2,1)S(1)}, bf16[2,4096]{1,0:T(2,128)(2,1)S(1)}, u32[]{:S(2)}, u32[]{:S(2)}) %collective-permute-start.2) | collective-permute-done | bytes 16416 | tf_op jit(solution)/shard_map/ppermute | solution.py:117
  11.0 0.2 %convolution_bitcast_fusion.2 = f32[64]{0:T(128)S(1)} fusion(bf16[64,4096]{1,0:T(8,128)(2,1)S(1)} %collective-permute-done.1, bf16[2,4096]{1,0:T(2,128)(2,1)S(1)} %collective-permute-done.2), kind=kOutput, calls=%fused_computation.4 | convolution fusion | flops 524288 | bytes 540928 | tf_op jit(solution)/shard_map/k,qk->q/dot_general | solution.py:133
  11.3 0.3 %fusion.3 = f32[64]{0:T(128)S(1)} fusion(f32[64]{0:T(128)S(1)} %fusion.4, f32[64]{0:T(128)S(1)} %convolution_bitcast_fusion.2, bf16[2,4096]{1,0:T(2,128)(2,1)S(1)} %collective-permute-done.2, pred[]{:T(512)S(6)} %or.20, bf16[64,1,4096]{2,0,1:T(8,128)(2,1)S(1)} %copy-done), kind=kOutput, calls=%fused_computation.7 | convolution fusion | flops 524416 | bytes 541441 | tf_op jit(solution)/shard_map/k,qk->q/dot_general | solution.py:132
  11.5 1.2 %collective-permute-start.3 = (f32[64]{0:T(128)S(1)}, f32[64]{0:T(128)S(1)}, u32[]{:S(2)}, u32[]{:S(2)}) collective-permute-start(f32[64]{0:T(128)S(1)} %fusion.3), channel_id=1, source_target_pairs={{0,8},{1,0},{2,12},{3,4},{4,5},{5,13},{6,9},{7,1},{8,2},{9,10},{10... | collective-permute-start | bytes 776 | tf_op jit(solution)/shard_map/ppermute | solution.py:123
  12.7 1.0 %collective-permute-done.4 = bf16[2,4096]{1,0:T(2,128)(2,1)S(1)} collective-permute-done((bf16[2,4096]{1,0:T(2,128)(2,1)S(1)}, bf16[2,4096]{1,0:T(2,128)(2,1)S(1)}, u32[]{:S(2)}, u32[]{:S(2)}) %collective-permute-start.4) | collective-permute-done | bytes 16416 | tf_op jit(solution)/shard_map/ppermute | solution.py:117
  13.7 0.2 %convolution_bitcast_fusion = f32[64]{0:T(128)S(1)} fusion(bf16[64,4096]{1,0:T(8,128)(2,1)S(1)} %collective-permute-done.1, bf16[2,4096]{1,0:T(2,128)(2,1)S(1)} %collective-permute-done.4), kind=kOutput, calls=%fused_computation | convolution fusion | flops 524288 | bytes 540928 | tf_op jit(solution)/shard_map/k,qk->q/dot_general | solution.py:133
  14.0 0.3 %fusion.1 = f32[64]{0:T(128)S(1)} fusion(f32[64]{0:T(128)S(1)} %fusion.4, f32[64]{0:T(128)S(1)} %convolution_bitcast_fusion, bf16[2,4096]{1,0:T(2,128)(2,1)S(1)} %collective-permute-done.4, pred[]{:T(512)S(6)} %or.23, bf16[64,1,4096]{2,0,1:T(8,128)(2,1)S(1)} %copy-done), kind=kOutput, calls=%fused_computation.3 | convolution fusion | flops 524416 | bytes 541441 | tf_op jit(solution)/shard_map/k,qk->q/dot_general | solution.py:132
  14.2 1.7 %collective-permute-start.5 = (f32[64]{0:T(128)S(1)}, f32[64]{0:T(128)S(1)}, u32[]{:S(2)}, u32[]{:S(2)}) collective-permute-start(f32[64]{0:T(128)S(1)} %fusion.1), channel_id=1, source_target_pairs={{0,4},{1,12},{2,8},{3,0},{4,1},{5,9},{6,5},{7,13},{8,14},{9,6},{10... | collective-permute-start | bytes 776 | tf_op jit(solution)/shard_map/ppermute | solution.py:123
  15.9 1.0 %collective-permute-done.3 = f32[64]{0:T(128)S(1)} collective-permute-done((f32[64]{0:T(128)S(1)}, f32[64]{0:T(128)S(1)}, u32[]{:S(2)}, u32[]{:S(2)}) %collective-permute-start.3) | collective-permute-done | bytes 288 | tf_op jit(solution)/shard_map/ppermute | solution.py:123
  16.9 1.8 %collective-permute-done.5 = f32[64]{0:T(128)S(1)} collective-permute-done((f32[64]{0:T(128)S(1)}, f32[64]{0:T(128)S(1)}, u32[]{:S(2)}, u32[]{:S(2)}) %collective-permute-start.5) | collective-permute-done | bytes 288 | tf_op jit(solution)/shard_map/ppermute | solution.py:123
  18.7 0.5 %multiply_bitcast_fusion = f32[1,64]{1,0:T(1,128)} fusion(f32[64]{0:T(128)S(1)} %collective-permute-done.3, f32[64]{0:T(128)S(1)} %collective-permute-done.5, f32[]{:T(128)} %bitcast.13), kind=kLoop, calls=%fused_computation.18 | loop fusion | flops 128 | bytes 772 | tf_op jit(solution)/shard_map/mul | solution.py:166
  (1 shorter events, 0.0 us)
Async XLA Ops:
  0.0 9.1 %collective-permute-start.1 = (bf16[64,4096]{1,0:T(8,128)(2,1)}, bf16[64,4096]{1,0:T(8,128)(2,1)S(1)}, u32[]{:S(2)}, u32[]{:S(2)}) collective-permute-start(bf16[64,4096]{1,0:T(8,128)(2,1)} %bitcast.65), channel_id=1, source_target_pairs={{0,1},{1,0},{2,3},{3,2},{4,5},{5,4},{6,7},{7,6},{8,9},{9,8},{10,11... | collective-permute-start | bytes 1572872 | tf_op jit(solution)/shard_map/ppermute | solution.py:102
  0.0 3.7 %copy-start = (bf16[64,1,4096]{2,0,1:T(8,128)(2,1)S(1)}, bf16[64,1,4096]{2,0,1:T(8,128)(2,1)}, u32[]{:S(2)}) copy-start(bf16[64,1,4096]{2,0,1:T(8,128)(2,1)} %param.12) | copy-start | bytes 1572868
  3.1 2.2 %collective-permute-start = (bf16[1,4096]{1,0:T(2,128)(2,1)S(1)}, bf16[1,4096]{1,0:T(2,128)(2,1)S(1)}, u32[]{:S(2)}, u32[]{:S(2)}) collective-permute-start(bf16[1,4096]{1,0:T(2,128)(2,1)S(1)} %shard_map.82), channel_id=1, source_target_pairs={{0,1},{1,0},{2,3},{3,2},{4,5},{5,4},{6,7},{7,6},{8,9},{9,8},{10,11... | collective-permute-start | bytes 24584 | tf_op jit(solution)/shard_map/ppermute | solution.py:102
  5.4 5.6 %collective-permute-start.2 = (bf16[2,4096]{1,0:T(2,128)(2,1)S(1)}, bf16[2,4096]{1,0:T(2,128)(2,1)S(1)}, u32[]{:S(2)}, u32[]{:S(2)}) collective-permute-start(bf16[2,4096]{1,0:T(2,128)(2,1)S(1)} %pad_maximum_fusion), channel_id=1, source_target_pairs={{8,0},{14,2},{7,3},{13,5},{10,6},{3,7},{0,8},{6,10},{15,11},{5,13}... | collective-permute-start | bytes 49160 | tf_op jit(solution)/shard_map/ppermute | solution.py:117
  9.1 4.6 %collective-permute-start.4 = (bf16[2,4096]{1,0:T(2,128)(2,1)S(1)}, bf16[2,4096]{1,0:T(2,128)(2,1)S(1)}, u32[]{:S(2)}, u32[]{:S(2)}) collective-permute-start(bf16[2,4096]{1,0:T(2,128)(2,1)S(1)} %pad_maximum_fusion), channel_id=1, source_target_pairs={{4,0},{13,1},{10,2},{0,4},{9,5},{15,7},{12,8},{5,9},{2,10},{8,12},... | collective-permute-start | bytes 49160 | tf_op jit(solution)/shard_map/ppermute | solution.py:117
  11.5 5.4 %collective-permute-start.3 = (f32[64]{0:T(128)S(1)}, f32[64]{0:T(128)S(1)}, u32[]{:S(2)}, u32[]{:S(2)}) collective-permute-start(f32[64]{0:T(128)S(1)} %fusion.3), channel_id=1, source_target_pairs={{0,8},{1,0},{2,12},{3,4},{4,5},{5,13},{6,9},{7,1},{8,2},{9,10},{10... | collective-permute-start | bytes 776 | tf_op jit(solution)/shard_map/ppermute | solution.py:123
  14.2 4.5 %collective-permute-start.5 = (f32[64]{0:T(128)S(1)}, f32[64]{0:T(128)S(1)}, u32[]{:S(2)}, u32[]{:S(2)}) collective-permute-start(f32[64]{0:T(128)S(1)} %fusion.1), channel_id=1, source_target_pairs={{0,4},{1,12},{2,8},{3,0},{4,1},{5,9},{6,5},{7,13},{8,14},{9,6},{10... | collective-permute-start | bytes 776 | tf_op jit(solution)/shard_map/ppermute | solution.py:123

commit v6 on v5

--- a/solution.py
+++ b/solution.py
@@ -8,10 +8,8 @@
 from jax.experimental.pallas import tpu as pltpu
 from jax.sharding import PartitionSpec as P
 
-FIRST = ((2, 0, 3, 1), (1, 3, 2, 0), (0, 2, 1, 3), (3, 1, 0, 2))
-SECOND = ((1, 3, 2, 0), (0, 2, 1, 3), (3, 1, 0, 2), (2, 0, 3, 1))
-
-
+FIRST = ((3, 1, 2, 0), (1, 2, 0, 3), (0, 3, 1, 2), (2, 0, 3, 1))
+SECOND = ((2, 0, 1, 3), (0, 3, 2, 1), (1, 2, 3, 0), (3, 1, 0, 2))
 CHUNKS = 2
 
 
@@ -102,19 +100,18 @@
     return lax.ppermute(x, "layer", [(i, i ^ 1) for i in range(lax.axis_size("layer"))])
 
 
+def own_places(slot):
+    return [(d, i) for d, row in enumerate(slot) for i, pair in enumerate(row) if pair == d]
+
+
 def fetch_pair(x, slot):
     count = len(slot)
-    moves, own = [], []
-    for d in range(count):
-        for i in range(count):
-            if slot[d][i] == d:
-                own.append(d * count + i)
-            else:
-                moves.append((slot[d][i] * count + i, d * count + i))
+    moves = [
+        (slot[d][i] * count + i, d * count + i) for d in range(count) for i in range(count) if slot[d][i] != d
+    ]
+    own = [d * count + i for d, i in own_places(slot)]
     fill = zip(own, own[1::-1] + own[:1:-1])
-    here = lax.axis_index("dp") * count + lax.axis_index("layer")
-    is_own = functools.reduce(jnp.logical_or, [here == i for i in own])
-    return lax.ppermute(x, ("dp", "layer"), moves + list(fill)), is_own
+    return lax.ppermute(x, ("dp", "layer"), moves + list(fill))
 
 
 def to_owner(x, slot):
@@ -123,19 +120,52 @@
     return lax.ppermute(x, ("dp", "layer"), moves)
 
 
-def shared_scores(own_row, own_block):
-    other_block = swap(own_block)
+def row_scores(rows, own_block, other_block):
+    one, two = (
+        lax.dot_general(rows, block[...], (((1,), (1,)), ((), ())), preferred_element_type=jnp.float32)
+        for block in (own_block, other_block)
+    )
+    return one[:1] + two[1:]
+
+
+def own_kernel(scale, margin, label, rows, own_block, other_block, out, factor):
+    out[...] = row_scores(rows[...], own_block, other_block)
+    sign = jnp.where(label[0] == 0, 1.0, -1.0)
+    factor[...] = sign / ((1.0 + jnp.exp(jnp.full(factor.shape, margin[0], jnp.float32))) * scale)
+
+
+def slot_kernel(slot, rows, own, own_block, other_block, out):
+    here = lax.axis_index("dp") * len(slot) + lax.axis_index("layer")
+    is_own = functools.reduce(jnp.logical_or, [here == d * len(slot) + i for d, i in own_places(slot)])
+    out[...] = jnp.where(is_own, own[...], row_scores(rows[...], own_block, other_block))
+
+
+def shared_scores(own_row, own_block, margin, labels, scale):
+    blocks = [pltpu.with_memory_space_constraint(x, pltpu.VMEM) for x in (own_block, swap(own_block))]
     rows = jnp.concatenate([own_row, swap(own_row)], axis=0)
-    (first, first_own), (second, second_own) = fetch_pair(rows, FIRST), fetch_pair(rows, SECOND)
-
-    def score(got):
-        one = jnp.einsum("k,qk->q", got[0], own_block, preferred_element_type=jnp.float32)
-        two = jnp.einsum("k,qk->q", got[1], other_block, preferred_element_type=jnp.float32)
-        return one + two
-
-    own = score(rows)
-    first, second = jnp.where(first_own, own, score(first)), jnp.where(second_own, own, score(second))
-    return (to_owner(first, FIRST) + to_owner(second, SECOND))[None]
+    first, second = fetch_pair(rows, FIRST), fetch_pair(rows, SECOND)
+    scalar, vector = pl.BlockSpec(memory_space=pltpu.SMEM), pl.BlockSpec(memory_space=pltpu.VMEM)
+    line = jax.ShapeDtypeStruct((1, own_block.shape[0]), jnp.float32)
+    cost = pl.CostEstimate(flops=8 * own_block.size, bytes_accessed=4 * own_block.size, transcendentals=0)
+    own, factor = pl.pallas_call(
+        functools.partial(own_kernel, scale),
+        out_shape=(line, line),
+        in_specs=[scalar] * 2 + [vector] * 3,
+        out_specs=(vector, vector),
+        cost_estimate=cost,
+    )(margin, labels, rows, *blocks)
+
+    def score(got, slot):
+        return pl.pallas_call(
+            functools.partial(slot_kernel, slot),
+            out_shape=line,
+            in_specs=[vector] * 4,
+            out_specs=vector,
+            cost_estimate=cost,
+        )(got, own, *blocks)
+
+    first, second = to_owner(score(first, FIRST), FIRST), to_owner(score(second, SECOND), SECOND)
+    return (first + second) * factor
 
 
 def pair_gradients(acts_in, grads_out, proj_in, proj_out, lengths):
@@ -159,11 +189,10 @@
     one_each = pair_count == layer_count == 1 and side_count == 2
     form = pair_gradient if one_each else pair_gradients
     grad_rows = form(acts_in, grads_out, proj_in, proj_out, lengths)
-    margin, labels, grad_rows = lax.optimization_barrier((margin, labels, grad_rows))
     scale = rank * math.sqrt(layer_count * layer_size) * math.sqrt(acts_in.shape[2])
+    if one_each and dp_size == layer_size == len(FIRST):
+        return shared_scores(grad_rows, block, margin, labels, scale)
     factor = jax.nn.sigmoid(-margin) * jnp.where(labels == 0, 1.0, -1.0) / scale
-    if one_each and dp_size == layer_size == len(FIRST):
-        return shared_scores(grad_rows, block) * factor[:, None]
     rows = lax.all_gather(grad_rows, "dp", axis=0, tiled=True)
     scores = jnp.einsum("pk,qk->pq", rows, block, preferred_element_type=jnp.float32)
     scores = lax.all_to_all(scores, "dp", split_axis=0, concat_axis=1, tiled=True)

time: 19.4 us -> 23.7 us (1.22)
  the two profiles are of different devices: /device:TPU:2 before, /device:TPU:0 now
where the time goes in v6:
time: 23.7 us; the launch traced here: 23.3 us
  starting transfers between devices  9.64 us (41%)
  Pallas kernels  8.01 us (34%)
  waiting for transfers between devices  2.49 us (11%)
  between operations  1.35 us (6%)
  local copies, waits for them, and re-layouts  1.21 us (5%)
  other arithmetic  0.56 us (2%)
    ppermute x2, starting transfers between devices, to_owner(): return lax.ppermute(x, ('dp', 'layer'), moves)  4.95 us
    ppermute x2, starting transfers between devices, fetch_pair(): return lax.ppermute(x, ('dp', 'layer'), moves + list(fill))  4.11 us
    pallas_call x2, Pallas kernels, score(): pl.pallas_call(functools.partial(slot_kernel, slot), out_shape=line, in_s...  3.28 us
    pallas_call x1, Pallas kernels, pair_gradient(): pl.pallas_call(functools.partial(pair_kernel, seq_len), out_shape=jax.Sha...  3.11 us
    pallas_call x1, Pallas kernels, shared_scores(): pl.pallas_call(functools.partial(own_kernel, scale), out_shape=(line, lin...  1.62 us
    ppermute x2, waiting for transfers between devices, to_owner(): return lax.ppermute(x, ('dp', 'layer'), moves)  1.35 us
    unnamed x10, local copies, waits for them, and re-layouts  1.21 us
    ppermute x2, waiting for transfers between devices, swap(): lax.ppermute(x, 'layer', [(i, i ^ 1) for i in range(lax.axis_size('layer'...  1.13 us
  transfers between devices with their start and end apart: 6, of which 2 were waited for; matrix products, arithmetic and copies ran while one was open for 0% of the time, Pallas kernels for 34%

profile of v6, /device:TPU:0, one launch (start us, length us, event | category | flops | bytes accessed | tf_op | source)
XLA Modules:
  0.0 23.3 jit_solution(11266600149034933601)
XLA Ops:
  0.0 0.5 %collective-permute-start.2 = (bf16[64,4096]{1,0:T(8,128)(2,1)}, bf16[64,4096]{1,0:T(8,128)(2,1)S(1)}, u32[]{:S(2)}, u32[]{:S(2)}) collective-permute-start(bf16[64,4096]{1,0:T(8,128)(2,1)} %bitcast.9), channel_id=1, source_target_pairs={{0,1},{1,0},{2,3},{3,2},{4,5},{5,4},{6,7},{7,6},{8,9},{9,8},{10,11... | collective-permute-start | bytes 1572872 | tf_op jit(solution)/shard_map/ppermute | solution.py:100
  0.5 0.0 copy-start
  0.5 3.1 %shard_map.82 = bf16[1,4096]{1,0:T(2,128)(2,1)S(1)} custom-call(bf16[128,4096]{1,0:T(8,128)(2,1)} %bitcast.13, bf16[64,4096]{1,0:T(8,128)(2,1)} %bitcast.15, bf16[128,4096]{1,0:T(8,128)(2,1)} %bitcast.14, bf16[64,4096]{1,0:T(8,128)(2,1)} %bitcast.16, s32[1,2]{1,0:T(1,128)} %lengths.1), custom_call_target="tpu_custom_call" | custom-call | flops 134217728 | bytes 3145728 | tf_op jit(solution)/shard_map/pallas_call | solution.py:65
  3.6 0.1 collective-permute-start
  3.7 1.1 %collective-permute-done = bf16[1,4096]{1,0:T(2,128)(2,1)S(1)} collective-permute-done((bf16[1,4096]{1,0:T(2,128)(2,1)S(1)}, bf16[1,4096]{1,0:T(2,128)(2,1)S(1)}, u32[]{:S(2)}, u32[]{:S(2)}) %collective-permute-start) | collective-permute-done | bytes 8224 | tf_op jit(solution)/shard_map/ppermute | solution.py:100
  4.9 0.0 copy-start.1
  4.9 3.8 %collective-permute-start.1 = (bf16[2,4096]{1,0:T(2,128)(2,1)S(1)}, bf16[2,4096]{1,0:T(2,128)(2,1)S(1)}, u32[]{:S(2)}, u32[]{:S(2)}) collective-permute-start(bf16[2,4096]{1,0:T(2,128)(2,1)S(1)} %pad_maximum_fusion.rows), channel_id=1, source_target_pairs={{12,0},{5,1},{10,2},{9,5},{2,6},{15,7},{0,8},{13,9},{6,10},{8,12},... | collective-permute-start | bytes 49160 | tf_op jit(solution)/shard_map/ppermute | solution.py:114
  8.7 0.3 %collective-permute-start.4 = (bf16[2,4096]{1,0:T(2,128)(2,1)S(1)}, bf16[2,4096]{1,0:T(2,128)(2,1)S(1)}, u32[]{:S(2)}, u32[]{:S(2)}) collective-permute-start(bf16[2,4096]{1,0:T(2,128)(2,1)S(1)} %pad_maximum_fusion.rows), channel_id=1, source_target_pairs={{8,0},{6,2},{15,3},{0,4},{13,5},{10,6},{4,8},{14,10},{3,11},{5,13}... | collective-permute-start | bytes 49160 | tf_op jit(solution)/shard_map/ppermute | solution.py:114
  10.3 0.0 collective-permute-done.2.other_block
  10.3 0.0 copy-done.1
  10.3 0.0 copy-done
  10.3 1.6 %shard_map.83 = (f32[1,64]{1,0:T(1,128)}, f32[1,64]{1,0:T(1,128)}) custom-call(f32[1]{0:T(128)S(6)} %copy.9.margin, s32[1]{0:T(128)S(6)} %copy.10.label, bf16[2,4096]{1,0:T(2,128)(2,1)} %copy-done.1, bf16[64,4096]{1,0:T(8,128)(2,1)S(1)} %bitcast.10, bf16[64,4096]{1,0:T(8,128)(2,1)S(1)} %collective-permute-done.2.other_block), custom_call_target="tpu_custom_call" | custom-call | flops 2097152 | bytes 1048576 | tf_op jit(solution)/shard_map/pallas_call | solution.py:150
  11.9 0.0 collective-permute-done.1.rows
  11.9 0.0 copy-start.3
  11.9 0.6 %copy-done.3 = bf16[2,4096]{1,0:T(2,128)(2,1)} copy-done((bf16[2,4096]{1,0:T(2,128)(2,1)}, bf16[2,4096]{1,0:T(2,128)(2,1)S(1)}, u32[]{:S(2)}) %copy-start.3) | copy-done | bytes 16408
  12.5 1.6 %shard_map.84 = f32[1,64]{1,0:T(1,128)} custom-call(bf16[2,4096]{1,0:T(2,128)(2,1)} %copy-done.3, f32[1,64]{1,0:T(1,128)} %get-tuple-element.7.own, bf16[64,4096]{1,0:T(8,128)(2,1)S(1)} %bitcast.11, bf16[64,4096]{1,0:T(8,128)(2,1)S(1)} %collective-permute-done.2.other_block), custom_call_target="tpu_custom_call" | custom-call | flops 2097152 | bytes 1048576 | tf_op jit(solution)/shard_map/pallas_call | solution.py:159
  14.2 1.5 %collective-permute-start.3 = (f32[1,64]{1,0:T(1,128)}, f32[1,64]{1,0:T(1,128)S(1)}, u32[]{:S(2)}, u32[]{:S(2)}) collective-permute-start(f32[1,64]{1,0:T(1,128)} %shard_map.84), channel_id=1, source_target_pairs={{0,12},{1,4},{2,8},{3,0},{4,5},{5,9},{6,1},{7,13},{8,2},{9,14},{10... | collective-permute-start | bytes 776 | tf_op jit(solution)/shard_map/ppermute | solution.py:120
  15.6 0.0 collective-permute-done.4.rows
  15.7 0.0 copy-start.2
  15.7 0.6 %copy-done.2 = bf16[2,4096]{1,0:T(2,128)(2,1)} copy-done((bf16[2,4096]{1,0:T(2,128)(2,1)}, bf16[2,4096]{1,0:T(2,128)(2,1)S(1)}, u32[]{:S(2)}) %copy-start.2) | copy-done | bytes 16408
  16.3 1.7 %shard_map.85 = f32[1,64]{1,0:T(1,128)} custom-call(bf16[2,4096]{1,0:T(2,128)(2,1)} %copy-done.2, f32[1,64]{1,0:T(1,128)} %get-tuple-element.7.own, bf16[64,4096]{1,0:T(8,128)(2,1)S(1)} %bitcast.12, bf16[64,4096]{1,0:T(8,128)(2,1)S(1)} %collective-permute-done.2.other_block), custom_call_target="tpu_custom_call" | custom-call | flops 2097152 | bytes 1048576 | tf_op jit(solution)/shard_map/pallas_call | solution.py:159
  17.9 0.0 copy-start.4
  17.9 3.5 %collective-permute-start.5 = (f32[1,64]{1,0:T(1,128)}, f32[1,64]{1,0:T(1,128)S(1)}, u32[]{:S(2)}, u32[]{:S(2)}) collective-permute-start(f32[1,64]{1,0:T(1,128)} %shard_map.85), channel_id=1, source_target_pairs={{0,8},{1,0},{2,4},{3,12},{4,1},{5,13},{6,9},{7,5},{8,6},{9,10},{10... | collective-permute-start | bytes 776 | tf_op jit(solution)/shard_map/ppermute | solution.py:120
  21.4 0.0 collective-permute-done.3
  21.4 1.4 %collective-permute-done.5 = f32[1,64]{1,0:T(1,128)S(1)} collective-permute-done((f32[1,64]{1,0:T(1,128)}, f32[1,64]{1,0:T(1,128)S(1)}, u32[]{:S(2)}, u32[]{:S(2)}) %collective-permute-start.5) | collective-permute-done | bytes 288 | tf_op jit(solution)/shard_map/ppermute | solution.py:120
  22.7 0.0 copy-done.4
  22.7 0.5 %add_multiply_fusion = f32[1,64]{1,0:T(1,128)} fusion(f32[1,64]{1,0:T(1,128)S(1)} %copy-done.4, f32[1,64]{1,0:T(1,128)S(1)} %collective-permute-done.3, f32[1,64]{1,0:T(1,128)S(1)} %collective-permute-done.5), kind=kLoop, calls=%fused_computation.1 | loop fusion | flops 128 | bytes 1024 | tf_op jit(solution)/shard_map/mul | solution.py:168
  (1 shorter events, 0.0 us)
Async XLA Ops:
  0.0 10.3 %collective-permute-start.2 = (bf16[64,4096]{1,0:T(8,128)(2,1)}, bf16[64,4096]{1,0:T(8,128)(2,1)S(1)}, u32[]{:S(2)}, u32[]{:S(2)}) collective-permute-start(bf16[64,4096]{1,0:T(8,128)(2,1)} %bitcast.9), channel_id=1, source_target_pairs={{0,1},{1,0},{2,3},{3,2},{4,5},{5,4},{6,7},{7,6},{8,9},{9,8},{10,11... | collective-permute-start | bytes 1572872 | tf_op jit(solution)/shard_map/ppermute | solution.py:100
  0.5 9.9 %copy-start = (bf16[64,1,4096]{2,0,1:T(8,128)(2,1)S(1)}, bf16[64,1,4096]{2,0,1:T(8,128)(2,1)}, u32[]{:S(2)}) copy-start(bf16[64,1,4096]{2,0,1:T(8,128)(2,1)} %param.12) | copy-start | bytes 1572868
  3.6 1.2 %collective-permute-start = (bf16[1,4096]{1,0:T(2,128)(2,1)S(1)}, bf16[1,4096]{1,0:T(2,128)(2,1)S(1)}, u32[]{:S(2)}, u32[]{:S(2)}) collective-permute-start(bf16[1,4096]{1,0:T(2,128)(2,1)S(1)} %shard_map.82), channel_id=1, source_target_pairs={{0,1},{1,0},{2,3},{3,2},{4,5},{5,4},{6,7},{7,6},{8,9},{9,8},{10,11... | collective-permute-start | bytes 24584 | tf_op jit(solution)/shard_map/ppermute | solution.py:100
  4.9 5.4 %copy-start.1 = (bf16[2,4096]{1,0:T(2,128)(2,1)}, bf16[2,4096]{1,0:T(2,128)(2,1)S(1)}, u32[]{:S(2)}) copy-start(bf16[2,4096]{1,0:T(2,128)(2,1)S(1)} %pad_maximum_fusion.rows) | copy-start | bytes 49156
  4.9 7.1 %collective-permute-start.1 = (bf16[2,4096]{1,0:T(2,128)(2,1)S(1)}, bf16[2,4096]{1,0:T(2,128)(2,1)S(1)}, u32[]{:S(2)}, u32[]{:S(2)}) collective-permute-start(bf16[2,4096]{1,0:T(2,128)(2,1)S(1)} %pad_maximum_fusion.rows), channel_id=1, source_target_pairs={{12,0},{5,1},{10,2},{9,5},{2,6},{15,7},{0,8},{13,9},{6,10},{8,12},... | collective-permute-start | bytes 49160 | tf_op jit(solution)/shard_map/ppermute | solution.py:114
  8.7 7.0 %collective-permute-start.4 = (bf16[2,4096]{1,0:T(2,128)(2,1)S(1)}, bf16[2,4096]{1,0:T(2,128)(2,1)S(1)}, u32[]{:S(2)}, u32[]{:S(2)}) collective-permute-start(bf16[2,4096]{1,0:T(2,128)(2,1)S(1)} %pad_maximum_fusion.rows), channel_id=1, source_target_pairs={{8,0},{6,2},{15,3},{0,4},{13,5},{10,6},{4,8},{14,10},{3,11},{5,13}... | collective-permute-start | bytes 49160 | tf_op jit(solution)/shard_map/ppermute | solution.py:114
  11.9 0.6 %copy-start.3 = (bf16[2,4096]{1,0:T(2,128)(2,1)}, bf16[2,4096]{1,0:T(2,128)(2,1)S(1)}, u32[]{:S(2)}) copy-start(bf16[2,4096]{1,0:T(2,128)(2,1)S(1)} %collective-permute-done.1.rows) | copy-start | bytes 49156
  14.2 7.2 %collective-permute-start.3 = (f32[1,64]{1,0:T(1,128)}, f32[1,64]{1,0:T(1,128)S(1)}, u32[]{:S(2)}, u32[]{:S(2)}) collective-permute-start(f32[1,64]{1,0:T(1,128)} %shard_map.84), channel_id=1, source_target_pairs={{0,12},{1,4},{2,8},{3,0},{4,5},{5,9},{6,1},{7,13},{8,2},{9,14},{10... | collective-permute-start | bytes 776 | tf_op jit(solution)/shard_map/ppermute | solution.py:120
  15.7 0.6 %copy-start.2 = (bf16[2,4096]{1,0:T(2,128)(2,1)}, bf16[2,4096]{1,0:T(2,128)(2,1)S(1)}, u32[]{:S(2)}) copy-start(bf16[2,4096]{1,0:T(2,128)(2,1)S(1)} %collective-permute-done.4.rows) | copy-start | bytes 49156
  17.9 4.8 %copy-start.4 = (f32[1,64]{1,0:T(1,128)S(1)}, f32[1,64]{1,0:T(1,128)}, u32[]{:S(2)}) copy-start(f32[1,64]{1,0:T(1,128)} %get-tuple-element.8) | copy-start | bytes 772
  17.9 4.8 %collective-permute-start.5 = (f32[1,64]{1,0:T(1,128)}, f32[1,64]{1,0:T(1,128)S(1)}, u32[]{:S(2)}, u32[]{:S(2)}) collective-permute-start(f32[1,64]{1,0:T(1,128)} %shard_map.85), channel_id=1, source_target_pairs={{0,8},{1,0},{2,4},{3,12},{4,1},{5,13},{6,9},{7,5},{8,6},{9,10},{10... | collective-permute-start | bytes 776 | tf_op jit(solution)/shard_map/ppermute | solution.py:120

commit v7 on v6

--- a/solution.py
+++ b/solution.py
@@ -8,8 +8,8 @@
 from jax.experimental.pallas import tpu as pltpu
 from jax.sharding import PartitionSpec as P
 
-FIRST = ((3, 1, 2, 0), (1, 2, 0, 3), (0, 3, 1, 2), (2, 0, 3, 1))
-SECOND = ((2, 0, 1, 3), (0, 3, 2, 1), (1, 2, 3, 0), (3, 1, 0, 2))
+FIRST = ((2, 0, 1, 3), (0, 3, 2, 1), (1, 2, 3, 0), (3, 1, 0, 2))
+SECOND = ((3, 1, 2, 0), (1, 2, 0, 3), (0, 3, 1, 2), (2, 0, 3, 1))
 CHUNKS = 2
 
 
@@ -120,52 +120,33 @@
     return lax.ppermute(x, ("dp", "layer"), moves)
 
 
-def row_scores(rows, own_block, other_block):
-    one, two = (
-        lax.dot_general(rows, block[...], (((1,), (1,)), ((), ())), preferred_element_type=jnp.float32)
-        for block in (own_block, other_block)
-    )
-    return one[:1] + two[1:]
-
-
-def own_kernel(scale, margin, label, rows, own_block, other_block, out, factor):
-    out[...] = row_scores(rows[...], own_block, other_block)
+def factor_kernel(scale, margin, label, rows, factor):
     sign = jnp.where(label[0] == 0, 1.0, -1.0)
     factor[...] = sign / ((1.0 + jnp.exp(jnp.full(factor.shape, margin[0], jnp.float32))) * scale)
 
 
-def slot_kernel(slot, rows, own, own_block, other_block, out):
-    here = lax.axis_index("dp") * len(slot) + lax.axis_index("layer")
-    is_own = functools.reduce(jnp.logical_or, [here == d * len(slot) + i for d, i in own_places(slot)])
-    out[...] = jnp.where(is_own, own[...], row_scores(rows[...], own_block, other_block))
-
-
 def shared_scores(own_row, own_block, margin, labels, scale):
-    blocks = [pltpu.with_memory_space_constraint(x, pltpu.VMEM) for x in (own_block, swap(own_block))]
+    blocks = own_block, swap(own_block)
     rows = jnp.concatenate([own_row, swap(own_row)], axis=0)
     first, second = fetch_pair(rows, FIRST), fetch_pair(rows, SECOND)
-    scalar, vector = pl.BlockSpec(memory_space=pltpu.SMEM), pl.BlockSpec(memory_space=pltpu.VMEM)
-    line = jax.ShapeDtypeStruct((1, own_block.shape[0]), jnp.float32)
-    cost = pl.CostEstimate(flops=8 * own_block.size, bytes_accessed=4 * own_block.size, transcendentals=0)
-    own, factor = pl.pallas_call(
-        functools.partial(own_kernel, scale),
-        out_shape=(line, line),
-        in_specs=[scalar] * 2 + [vector] * 3,
-        out_specs=(vector, vector),
-        cost_estimate=cost,
-    )(margin, labels, rows, *blocks)
+    factor = pl.pallas_call(
+        functools.partial(factor_kernel, scale),
+        out_shape=jax.ShapeDtypeStruct(own_block.shape[:1], jnp.float32),
+        in_specs=[pl.BlockSpec(memory_space=pltpu.SMEM)] * 2 + [pl.BlockSpec(memory_space=pl.ANY)],
+        out_specs=pl.BlockSpec(memory_space=pltpu.VMEM),
+        cost_estimate=pl.CostEstimate(flops=0, bytes_accessed=4 * own_block.shape[0], transcendentals=0),
+    )(margin, labels, rows)
+    here = lax.axis_index("dp") * len(FIRST) + lax.axis_index("layer")
 
     def score(got, slot):
-        return pl.pallas_call(
-            functools.partial(slot_kernel, slot),
-            out_shape=line,
-            in_specs=[vector] * 4,
-            out_specs=vector,
-            cost_estimate=cost,
-        )(got, own, *blocks)
+        is_own = functools.reduce(jnp.logical_or, [here == d * len(slot) + i for d, i in own_places(slot)])
+        return sum(
+            jnp.einsum("k,qk->q", jnp.where(is_own, mine, row), block, preferred_element_type=jnp.float32)
+            for mine, row, block in zip(rows, got, blocks)
+        )
 
     first, second = to_owner(score(first, FIRST), FIRST), to_owner(score(second, SECOND), SECOND)
-    return (first + second) * factor
+    return ((first + second) * factor)[None]
 
 
 def pair_gradients(acts_in, grads_out, proj_in, proj_out, lengths):

time: 23.7 us -> 18.8 us (0.79); the launches traced: 23.3 us -> 18.7 us
  Pallas kernels: 8.01 us -> 3.64 us
  starting transfers between devices: 9.64 us -> 7.92 us
  local copies, waits for them, and re-layouts: 1.21 us -> 0.01 us
  waiting for transfers between devices: 2.49 us -> 3.54 us
  matrix products: 0 us -> 0.99 us
  other arithmetic: 0.56 us -> 1.22 us
    pallas_call x3 -> x1, Pallas kernels: 4.9 us -> 0.6 us  [shared_scores(): pl.pallas_call(functools.partial(factor_kernel, scale), out_shape=jax.Sha...]
    ppermute x2, waiting for transfers between devices: 0.01 us -> 2.41 us  [fetch_pair(): return lax.ppermute(x, ('dp', 'layer'), moves + list(fill))]
    ppermute x2, starting transfers between devices: 4.95 us -> 3.22 us  [to_owner(): return lax.ppermute(x, ('dp', 'layer'), moves)]
    ppermute x2, waiting for transfers between devices: 1.35 us -> 0.01 us  [to_owner(): return lax.ppermute(x, ('dp', 'layer'), moves)]
    unnamed x10 -> x4, local copies, waits for them, and re-layouts: 1.21 us -> 0.01 us
    broadcast_in_dim x0 -> x1, other arithmetic: none -> 1.18 us  [shared_scores(): return ((first + second) * factor)[None]]
    dot_general x0 -> x4, matrix products: none -> 0.99 us  [score(): jnp.einsum('k,qk->q', jnp.where(is_own, mine, row), block, preferred_elem...]
    mul x1 -> x0, other arithmetic: 0.51 us -> none  [shared_scores(): return (first + second) * factor]
  transfers between devices with their start and end apart: 6 -> 6, of which waited for: 2 -> 2; matrix products, arithmetic and copies ran while one was open for 0% -> 6% of each run, Pallas kernels for 34% -> 19%
where the time goes in v7:
time: 18.8 us; the launch traced here: 18.7 us
  starting transfers between devices  7.92 us (42%)
  Pallas kernels  3.64 us (19%)
  waiting for transfers between devices  3.54 us (19%)
  between operations  1.34 us (7%)
  other arithmetic  1.22 us (6%)
  matrix products  0.99 us (5%)
    ppermute x2, starting transfers between devices, fetch_pair(): return lax.ppermute(x, ('dp', 'layer'), moves + list(fill))  4.12 us
    ppermute x2, starting transfers between devices, to_owner(): return lax.ppermute(x, ('dp', 'layer'), moves)  3.22 us
    pallas_call x1, Pallas kernels, pair_gradient(): pl.pallas_call(functools.partial(pair_kernel, seq_len), out_shape=jax.Sha...  3.04 us
    ppermute x2, waiting for transfers between devices, fetch_pair(): return lax.ppermute(x, ('dp', 'layer'), moves + list(fill))  2.41 us
    broadcast_in_dim x1, other arithmetic, shared_scores(): return ((first + second) * factor)[None]  1.18 us
    ppermute x2, waiting for transfers between devices, swap(): lax.ppermute(x, 'layer', [(i, i ^ 1) for i in range(lax.axis_size('layer'...  1.12 us
    dot_general x4, matrix products, score(): jnp.einsum('k,qk->q', jnp.where(is_own, mine, row), block, preferred_elem...  0.99 us
    pallas_call x1, Pallas kernels, shared_scores(): pl.pallas_call(functools.partial(factor_kernel, scale), out_shape=jax.Sha...  0.6 us
  transfers between devices with their start and end apart: 6, of which 2 were waited for; matrix products, arithmetic and copies ran while one was open for 6% of the time, Pallas kernels for 19%

profile of v7, /device:TPU:0, one launch (start us, length us, event | category | flops | bytes accessed | tf_op | source)
XLA Modules:
  0.0 18.7 jit_solution(11092375365252650768)
XLA Ops:
  0.0 0.5 %collective-permute-start.2 = (bf16[64,4096]{1,0:T(8,128)(2,1)}, bf16[64,4096]{1,0:T(8,128)(2,1)S(1)}, u32[]{:S(2)}, u32[]{:S(2)}) collective-permute-start(bf16[64,4096]{1,0:T(8,128)(2,1)} %bitcast.45), channel_id=1, source_target_pairs={{0,1},{1,0},{2,3},{3,2},{4,5},{5,4},{6,7},{7,6},{8,9},{9,8},{10,11... | collective-permute-start | bytes 1572872 | tf_op jit(solution)/shard_map/ppermute | solution.py:100
  0.5 3.0 %shard_map.82 = bf16[1,4096]{1,0:T(2,128)(2,1)S(1)} custom-call(bf16[128,4096]{1,0:T(8,128)(2,1)} %bitcast.41, bf16[64,4096]{1,0:T(8,128)(2,1)} %bitcast.43, bf16[128,4096]{1,0:T(8,128)(2,1)} %bitcast.42, bf16[64,4096]{1,0:T(8,128)(2,1)} %bitcast.44, s32[1,2]{1,0:T(1,128)} %lengths.1), custom_call_target="tpu_custom_call" | custom-call | flops 134217728 | bytes 3145728 | tf_op jit(solution)/shard_map/pallas_call | solution.py:65
  3.5 0.0 copy-start.1
  3.5 0.1 collective-permute-start
  3.6 1.1 %collective-permute-done = bf16[1,4096]{1,0:T(2,128)(2,1)S(1)} collective-permute-done((bf16[1,4096]{1,0:T(2,128)(2,1)S(1)}, bf16[1,4096]{1,0:T(2,128)(2,1)S(1)}, u32[]{:S(2)}, u32[]{:S(2)}) %collective-permute-start) | collective-permute-done | bytes 8224 | tf_op jit(solution)/shard_map/ppermute | solution.py:100
  4.8 0.0 copy-start
  4.8 3.8 %collective-permute-start.4 = (bf16[2,4096]{1,0:T(2,128)(2,1)S(1)}, bf16[2,4096]{1,0:T(2,128)(2,1)S(1)}, u32[]{:S(2)}, u32[]{:S(2)}) collective-permute-start(bf16[2,4096]{1,0:T(2,128)(2,1)S(1)} %pad_maximum_fusion.rows), channel_id=1, source_target_pairs={{12,0},{5,1},{10,2},{9,5},{2,6},{15,7},{0,8},{13,9},{6,10},{8,12},... | collective-permute-start | bytes 49160 | tf_op jit(solution)/shard_map/ppermute | solution.py:114
  8.6 0.0 copy-done
  8.6 0.3 %collective-permute-start.1 = (bf16[2,4096]{1,0:T(2,128)(2,1)S(1)}, bf16[2,4096]{1,0:T(2,128)(2,1)S(1)}, u32[]{:S(2)}, u32[]{:S(2)}) collective-permute-start(bf16[2,4096]{1,0:T(2,128)(2,1)S(1)} %pad_maximum_fusion.rows), channel_id=1, source_target_pairs={{8,0},{6,2},{15,3},{0,4},{13,5},{10,6},{4,8},{14,10},{3,11},{5,13}... | collective-permute-start | bytes 49160 | tf_op jit(solution)/shard_map/ppermute | solution.py:114
  8.9 2.4 %collective-permute-done.4 = bf16[2,4096]{1,0:T(2,128)(2,1)S(1)} collective-permute-done((bf16[2,4096]{1,0:T(2,128)(2,1)S(1)}, bf16[2,4096]{1,0:T(2,128)(2,1)S(1)}, u32[]{:S(2)}, u32[]{:S(2)}) %collective-permute-start.4) | collective-permute-done | bytes 16416 | tf_op jit(solution)/shard_map/ppermute | solution.py:114
  11.4 0.0 collective-permute-done.2
  11.4 0.2 %convolution_bitcast_fusion = f32[64]{0:T(128)S(1)} fusion(bf16[64,4096]{1,0:T(8,128)(2,1)S(1)} %collective-permute-done.2, bf16[1,4096]{1,0:T(2,128)(2,1)S(1)} %collective-permute-done, pred[]{:T(512)S(6)} %or.23, bf16[2,4096]{1,0:T(2,128)(2,1)S(1)} %collective-permute-done.4), kind=kOutput, calls=%fused_computation | convolution fusion | flops 528384 | bytes 549121 | tf_op jit(solution)/shard_map/k,qk->q/dot_general | solution.py:144
  11.6 0.0 copy-done.1
  11.6 0.3 %fusion = f32[64]{0:T(128)S(1)} fusion(f32[64]{0:T(128)S(1)} %convolution_bitcast_fusion, bf16[1,4096]{1,0:T(2,128)(2,1)S(1)} %shard_map.82, pred[]{:T(512)S(6)} %or.23, bf16[2,4096]{1,0:T(2,128)(2,1)S(1)} %collective-permute-done.4, bf16[64,1,4096]{2,0,1:T(8,128)(2,1)S(1)} %copy-done.1), kind=kOutput, calls=%fused_computation.2 | convolution fusion | flops 528448 | bytes 549377 | tf_op jit(solution)/shard_map/k,qk->q/dot_general | solution.py:144
  11.9 2.2 %collective-permute-start.5 = (f32[64]{0:T(128)S(1)}, f32[64]{0:T(128)S(1)}, u32[]{:S(2)}, u32[]{:S(2)}) collective-permute-start(f32[64]{0:T(128)S(1)} %fusion), channel_id=1, source_target_pairs={{0,12},{1,4},{2,8},{3,0},{4,5},{5,9},{6,1},{7,13},{8,2},{9,14},{10... | collective-permute-start | bytes 776 | tf_op jit(solution)/shard_map/ppermute | solution.py:120
  14.0 0.0 collective-permute-done.1
  14.0 0.2 %convolution_bitcast_fusion.2 = f32[64]{0:T(128)S(1)} fusion(bf16[64,4096]{1,0:T(8,128)(2,1)S(1)} %collective-permute-done.2, bf16[1,4096]{1,0:T(2,128)(2,1)S(1)} %collective-permute-done, pred[]{:T(512)S(6)} %or.20, bf16[2,4096]{1,0:T(2,128)(2,1)S(1)} %collective-permute-done.1), kind=kOutput, calls=%fused_computation.3 | convolution fusion | flops 528384 | bytes 549121 | tf_op jit(solution)/shard_map/k,qk->q/dot_general | solution.py:144
  14.3 0.3 %fusion.1 = f32[64]{0:T(128)S(1)} fusion(f32[64]{0:T(128)S(1)} %convolution_bitcast_fusion.2, bf16[1,4096]{1,0:T(2,128)(2,1)S(1)} %shard_map.82, pred[]{:T(512)S(6)} %or.20, bf16[2,4096]{1,0:T(2,128)(2,1)S(1)} %collective-permute-done.1, bf16[64,1,4096]{2,0,1:T(8,128)(2,1)S(1)} %copy-done.1), kind=kOutput, calls=%fused_computation.5 | convolution fusion | flops 528448 | bytes 549377 | tf_op jit(solution)/shard_map/k,qk->q/dot_general | solution.py:144
  14.5 1.0 %collective-permute-start.3 = (f32[64]{0:T(128)S(1)}, f32[64]{0:T(128)S(1)}, u32[]{:S(2)}, u32[]{:S(2)}) collective-permute-start(f32[64]{0:T(128)S(1)} %fusion.1), channel_id=1, source_target_pairs={{0,8},{1,0},{2,4},{3,12},{4,1},{5,13},{6,9},{7,5},{8,6},{9,10},{10... | collective-permute-start | bytes 776 | tf_op jit(solution)/shard_map/ppermute | solution.py:120
  16.9 0.6 %shard_map.83 = f32[64]{0:T(128)} custom-call(f32[1]{0:T(128)S(6)} %copy.9.margin, s32[1]{0:T(128)S(6)} %copy.10.label, bf16[2,4096]{1,0:T(2,128)(2,1)} %copy-done), custom_call_target="tpu_custom_call" | custom-call | bytes 256 | tf_op jit(solution)/shard_map/pallas_call | solution.py:132
  17.5 0.0 collective-permute-done.5
  17.5 0.0 collective-permute-done.3
  17.5 1.2 %multiply_bitcast_fusion = f32[1,64]{1,0:T(1,128)} fusion(f32[64]{0:T(128)} %shard_map.83, f32[64]{0:T(128)S(1)} %collective-permute-done.3, f32[64]{0:T(128)S(1)} %collective-permute-done.5), kind=kLoop, calls=%fused_computation.19 | loop fusion | flops 128 | bytes 1024 | tf_op jit(solution)/shard_map/broadcast_in_dim | solution.py:149
  (1 shorter events, 0.0 us)
Async XLA Ops:
  0.0 11.4 %collective-permute-start.2 = (bf16[64,4096]{1,0:T(8,128)(2,1)}, bf16[64,4096]{1,0:T(8,128)(2,1)S(1)}, u32[]{:S(2)}, u32[]{:S(2)}) collective-permute-start(bf16[64,4096]{1,0:T(8,128)(2,1)} %bitcast.45), channel_id=1, source_target_pairs={{0,1},{1,0},{2,3},{3,2},{4,5},{5,4},{6,7},{7,6},{8,9},{9,8},{10,11... | collective-permute-start | bytes 1572872 | tf_op jit(solution)/shard_map/ppermute | solution.py:100
  3.5 8.1 %copy-start.1 = (bf16[64,1,4096]{2,0,1:T(8,128)(2,1)S(1)}, bf16[64,1,4096]{2,0,1:T(8,128)(2,1)}, u32[]{:S(2)}) copy-start(bf16[64,1,4096]{2,0,1:T(8,128)(2,1)} %param.12) | copy-start | bytes 1572868
  3.5 1.2 %collective-permute-start = (bf16[1,4096]{1,0:T(2,128)(2,1)S(1)}, bf16[1,4096]{1,0:T(2,128)(2,1)S(1)}, u32[]{:S(2)}, u32[]{:S(2)}) collective-permute-start(bf16[1,4096]{1,0:T(2,128)(2,1)S(1)} %shard_map.82), channel_id=1, source_target_pairs={{0,1},{1,0},{2,3},{3,2},{4,5},{5,4},{6,7},{7,6},{8,9},{9,8},{10,11... | collective-permute-start | bytes 24584 | tf_op jit(solution)/shard_map/ppermute | solution.py:100
  4.8 3.8 %copy-start = (bf16[2,4096]{1,0:T(2,128)(2,1)}, bf16[2,4096]{1,0:T(2,128)(2,1)S(1)}, u32[]{:S(2)}) copy-start(bf16[2,4096]{1,0:T(2,128)(2,1)S(1)} %pad_maximum_fusion.rows) | copy-start | bytes 49156
  4.8 6.5 %collective-permute-start.4 = (bf16[2,4096]{1,0:T(2,128)(2,1)S(1)}, bf16[2,4096]{1,0:T(2,128)(2,1)S(1)}, u32[]{:S(2)}, u32[]{:S(2)}) collective-permute-start(bf16[2,4096]{1,0:T(2,128)(2,1)S(1)} %pad_maximum_fusion.rows), channel_id=1, source_target_pairs={{12,0},{5,1},{10,2},{9,5},{2,6},{15,7},{0,8},{13,9},{6,10},{8,12},... | collective-permute-start | bytes 49160 | tf_op jit(solution)/shard_map/ppermute | solution.py:114
  8.6 5.4 %collective-permute-start.1 = (bf16[2,4096]{1,0:T(2,128)(2,1)S(1)}, bf16[2,4096]{1,0:T(2,128)(2,1)S(1)}, u32[]{:S(2)}, u32[]{:S(2)}) collective-permute-start(bf16[2,4096]{1,0:T(2,128)(2,1)S(1)} %pad_maximum_fusion.rows), channel_id=1, source_target_pairs={{8,0},{6,2},{15,3},{0,4},{13,5},{10,6},{4,8},{14,10},{3,11},{5,13}... | collective-permute-start | bytes 49160 | tf_op jit(solution)/shard_map/ppermute | solution.py:114
  11.9 5.6 %collective-permute-start.5 = (f32[64]{0:T(128)S(1)}, f32[64]{0:T(128)S(1)}, u32[]{:S(2)}, u32[]{:S(2)}) collective-permute-start(f32[64]{0:T(128)S(1)} %fusion), channel_id=1, source_target_pairs={{0,12},{1,4},{2,8},{3,0},{4,5},{5,9},{6,1},{7,13},{8,2},{9,14},{10... | collective-permute-start | bytes 776 | tf_op jit(solution)/shard_map/ppermute | solution.py:120
  14.5 2.9 %collective-permute-start.3 = (f32[64]{0:T(128)S(1)}, f32[64]{0:T(128)S(1)}, u32[]{:S(2)}, u32[]{:S(2)}) collective-permute-start(f32[64]{0:T(128)S(1)} %fusion.1), channel_id=1, source_target_pairs={{0,8},{1,0},{2,4},{3,12},{4,1},{5,13},{6,9},{7,5},{8,6},{9,10},{10... | collective-permute-start | bytes 776 | tf_op jit(solution)/shard_map/ppermute | solution.py:120

commit v8 on v7

--- a/solution.py
+++ b/solution.py
@@ -134,6 +134,7 @@
         out_shape=jax.ShapeDtypeStruct(own_block.shape[:1], jnp.float32),
         in_specs=[pl.BlockSpec(memory_space=pltpu.SMEM)] * 2 + [pl.BlockSpec(memory_space=pl.ANY)],
         out_specs=pl.BlockSpec(memory_space=pltpu.VMEM),
+        compiler_params=pltpu.CompilerParams(vmem_limit_bytes=1024 * 1024),
         cost_estimate=pl.CostEstimate(flops=0, bytes_accessed=4 * own_block.shape[0], transcendentals=0),
     )(margin, labels, rows)
     here = lax.axis_index("dp") * len(FIRST) + lax.axis_index("layer")

time: 18.8 us -> 17.8 us (0.947)
  the two profiles are of different devices: /device:TPU:0 before, /device:TPU:11 now
where the time goes in v8:
time: 17.8 us; the launch traced here: 17.6 us
  starting transfers between devices  7.6 us (43%)
  waiting for transfers between devices  4.06 us (23%)
  Pallas kernels  3.06 us (17%)
  between operations  1.35 us (8%)
  matrix products  0.99 us (6%)
  other arithmetic  0.56 us (3%)
    ppermute x2, starting transfers between devices, fetch_pair(): return lax.ppermute(x, ('dp', 'layer'), moves + list(fill))  3.51 us
    ppermute x2, starting transfers between devices, to_owner(): return lax.ppermute(x, ('dp', 'layer'), moves)  3.34 us
    pallas_call x1, Pallas kernels, pair_gradient(): pl.pallas_call(functools.partial(pair_kernel, seq_len), out_shape=jax.Sha...  3.05 us
    ppermute x2, waiting for transfers between devices, to_owner(): return lax.ppermute(x, ('dp', 'layer'), moves)  2.86 us
    ppermute x2, waiting for transfers between devices, swap(): lax.ppermute(x, 'layer', [(i, i ^ 1) for i in range(lax.axis_size('layer'...  1.17 us
    dot_general x4, matrix products, score(): jnp.einsum('k,qk->q', jnp.where(is_own, mine, row), block, preferred_elem...  0.99 us
    ppermute x2, starting transfers between devices, swap(): lax.ppermute(x, 'layer', [(i, i ^ 1) for i in range(lax.axis_size('layer'...  0.75 us
    broadcast_in_dim x1, other arithmetic, shared_scores(): return ((first + second) * factor)[None]  0.51 us
  transfers between devices with their start and end apart: 6, of which 2 were waited for; matrix products, arithmetic and copies ran while one was open for 6% of the time, Pallas kernels for 17%

profile of v8, /device:TPU:11, one launch (start us, length us, event | category | flops | bytes accessed | tf_op | source)
XLA Modules:
  0.0 17.6 jit_solution(15803820113096007552)
XLA Ops:
  0.0 0.7 %collective-permute-start.2 = (bf16[64,4096]{1,0:T(8,128)(2,1)}, bf16[64,4096]{1,0:T(8,128)(2,1)S(1)}, u32[]{:S(2)}, u32[]{:S(2)}) collective-permute-start(bf16[64,4096]{1,0:T(8,128)(2,1)} %bitcast.45), channel_id=1, source_target_pairs={{0,1},{1,0},{2,3},{3,2},{4,5},{5,4},{6,7},{7,6},{8,9},{9,8},{10,11... | collective-permute-start | bytes 1572872 | tf_op jit(solution)/shard_map/ppermute | solution.py:100
  0.7 3.0 %shard_map.82 = bf16[1,4096]{1,0:T(2,128)(2,1)S(1)} custom-call(bf16[128,4096]{1,0:T(8,128)(2,1)} %bitcast.41, bf16[64,4096]{1,0:T(8,128)(2,1)} %bitcast.43, bf16[128,4096]{1,0:T(8,128)(2,1)} %bitcast.42, bf16[64,4096]{1,0:T(8,128)(2,1)} %bitcast.44, s32[1,2]{1,0:T(1,128)} %lengths.1), custom_call_target="tpu_custom_call" | custom-call | flops 134217728 | bytes 3145728 | tf_op jit(solution)/shard_map/pallas_call | solution.py:65
  3.7 0.0 copy-start
  3.7 0.1 collective-permute-start
  3.8 1.2 %collective-permute-done = bf16[1,4096]{1,0:T(2,128)(2,1)S(1)} collective-permute-done((bf16[1,4096]{1,0:T(2,128)(2,1)S(1)}, bf16[1,4096]{1,0:T(2,128)(2,1)S(1)}, u32[]{:S(2)}, u32[]{:S(2)}) %collective-permute-start) | collective-permute-done | bytes 8224 | tf_op jit(solution)/shard_map/ppermute | solution.py:100
  5.0 2.4 %collective-permute-start.4 = (bf16[2,4096]{1,0:T(2,128)(2,1)S(1)}, bf16[2,4096]{1,0:T(2,128)(2,1)S(1)}, u32[]{:S(2)}, u32[]{:S(2)}) collective-permute-start(bf16[2,4096]{1,0:T(2,128)(2,1)S(1)} %pad_maximum_fusion.rows), channel_id=1, source_target_pairs={{12,0},{5,1},{10,2},{9,5},{2,6},{15,7},{0,8},{13,9},{6,10},{8,12},... | collective-permute-start | bytes 49160 | tf_op jit(solution)/shard_map/ppermute | solution.py:114
  7.4 1.2 %collective-permute-start.1 = (bf16[2,4096]{1,0:T(2,128)(2,1)S(1)}, bf16[2,4096]{1,0:T(2,128)(2,1)S(1)}, u32[]{:S(2)}, u32[]{:S(2)}) collective-permute-start(bf16[2,4096]{1,0:T(2,128)(2,1)S(1)} %pad_maximum_fusion.rows), channel_id=1, source_target_pairs={{8,0},{6,2},{15,3},{0,4},{13,5},{10,6},{4,8},{14,10},{3,11},{5,13}... | collective-permute-start | bytes 49160 | tf_op jit(solution)/shard_map/ppermute | solution.py:114
  8.6 0.0 collective-permute-done.4
  8.6 0.0 collective-permute-done.2
  8.6 0.2 %convolution_bitcast_fusion = f32[64]{0:T(128)S(1)} fusion(bf16[64,4096]{1,0:T(8,128)(2,1)S(1)} %collective-permute-done.2, bf16[1,4096]{1,0:T(2,128)(2,1)S(1)} %collective-permute-done, pred[]{:T(512)S(6)} %or.23, bf16[2,4096]{1,0:T(2,128)(2,1)S(1)} %collective-permute-done.4), kind=kOutput, calls=%fused_computation | convolution fusion | flops 528384 | bytes 549121 | tf_op jit(solution)/shard_map/k,qk->q/dot_general | solution.py:145
  8.8 0.0 copy-done
  8.8 0.3 %fusion = f32[64]{0:T(128)S(1)} fusion(f32[64]{0:T(128)S(1)} %convolution_bitcast_fusion, bf16[1,4096]{1,0:T(2,128)(2,1)S(1)} %shard_map.82, pred[]{:T(512)S(6)} %or.23, bf16[2,4096]{1,0:T(2,128)(2,1)S(1)} %collective-permute-done.4, bf16[64,1,4096]{2,0,1:T(8,128)(2,1)S(1)} %copy-done), kind=kOutput, calls=%fused_computation.2 | convolution fusion | flops 528448 | bytes 549377 | tf_op jit(solution)/shard_map/k,qk->q/dot_general | solution.py:145
  9.1 3.3 %collective-permute-start.5 = (f32[64]{0:T(128)S(1)}, f32[64]{0:T(128)S(1)}, u32[]{:S(2)}, u32[]{:S(2)}) collective-permute-start(f32[64]{0:T(128)S(1)} %fusion), channel_id=1, source_target_pairs={{0,12},{1,4},{2,8},{3,0},{4,5},{5,9},{6,1},{7,13},{8,2},{9,14},{10... | collective-permute-start | bytes 776 | tf_op jit(solution)/shard_map/ppermute | solution.py:120
  12.4 0.0 collective-permute-done.1
  12.4 0.2 %convolution_bitcast_fusion.2 = f32[64]{0:T(128)S(1)} fusion(bf16[64,4096]{1,0:T(8,128)(2,1)S(1)} %collective-permute-done.2, bf16[1,4096]{1,0:T(2,128)(2,1)S(1)} %collective-permute-done, pred[]{:T(512)S(6)} %or.20, bf16[2,4096]{1,0:T(2,128)(2,1)S(1)} %collective-permute-done.1), kind=kOutput, calls=%fused_computation.3 | convolution fusion | flops 528384 | bytes 549121 | tf_op jit(solution)/shard_map/k,qk->q/dot_general | solution.py:145
  12.6 0.3 %fusion.1 = f32[64]{0:T(128)S(1)} fusion(f32[64]{0:T(128)S(1)} %convolution_bitcast_fusion.2, bf16[1,4096]{1,0:T(2,128)(2,1)S(1)} %shard_map.82, pred[]{:T(512)S(6)} %or.20, bf16[2,4096]{1,0:T(2,128)(2,1)S(1)} %collective-permute-done.1, bf16[64,1,4096]{2,0,1:T(8,128)(2,1)S(1)} %copy-done), kind=kOutput, calls=%fused_computation.5 | convolution fusion | flops 528448 | bytes 549377 | tf_op jit(solution)/shard_map/k,qk->q/dot_general | solution.py:145
  12.9 0.0 collective-permute-start.3
  14.2 0.0 collective-permute-done.5
  14.2 2.9 %collective-permute-done.3 = f32[64]{0:T(128)S(1)} collective-permute-done((f32[64]{0:T(128)S(1)}, f32[64]{0:T(128)S(1)}, u32[]{:S(2)}, u32[]{:S(2)}) %collective-permute-start.3) | collective-permute-done | bytes 288 | tf_op jit(solution)/shard_map/ppermute | solution.py:120
  17.1 0.5 %multiply_bitcast_fusion = f32[1,64]{1,0:T(1,128)} fusion(f32[64]{0:T(128)S(1)} %shard_map.83, f32[64]{0:T(128)S(1)} %collective-permute-done.3, f32[64]{0:T(128)S(1)} %collective-permute-done.5), kind=kLoop, calls=%fused_computation.19 | loop fusion | flops 128 | bytes 1024 | tf_op jit(solution)/shard_map/broadcast_in_dim | solution.py:150
  (2 shorter events, 0.1 us)
Async XLA Ops:
  0.0 8.6 %collective-permute-start.2 = (bf16[64,4096]{1,0:T(8,128)(2,1)}, bf16[64,4096]{1,0:T(8,128)(2,1)S(1)}, u32[]{:S(2)}, u32[]{:S(2)}) collective-permute-start(bf16[64,4096]{1,0:T(8,128)(2,1)} %bitcast.45), channel_id=1, source_target_pairs={{0,1},{1,0},{2,3},{3,2},{4,5},{5,4},{6,7},{7,6},{8,9},{9,8},{10,11... | collective-permute-start | bytes 1572872 | tf_op jit(solution)/shard_map/ppermute | solution.py:100
  3.7 5.1 %copy-start = (bf16[64,1,4096]{2,0,1:T(8,128)(2,1)S(1)}, bf16[64,1,4096]{2,0,1:T(8,128)(2,1)}, u32[]{:S(2)}) copy-start(bf16[64,1,4096]{2,0,1:T(8,128)(2,1)} %param.12) | copy-start | bytes 1572868
  3.7 1.2 %collective-permute-start = (bf16[1,4096]{1,0:T(2,128)(2,1)S(1)}, bf16[1,4096]{1,0:T(2,128)(2,1)S(1)}, u32[]{:S(2)}, u32[]{:S(2)}) collective-permute-start(bf16[1,4096]{1,0:T(2,128)(2,1)S(1)} %shard_map.82), channel_id=1, source_target_pairs={{0,1},{1,0},{2,3},{3,2},{4,5},{5,4},{6,7},{7,6},{8,9},{9,8},{10,11... | collective-permute-start | bytes 24584 | tf_op jit(solution)/shard_map/ppermute | solution.py:100
  5.0 3.5 %collective-permute-start.4 = (bf16[2,4096]{1,0:T(2,128)(2,1)S(1)}, bf16[2,4096]{1,0:T(2,128)(2,1)S(1)}, u32[]{:S(2)}, u32[]{:S(2)}) collective-permute-start(bf16[2,4096]{1,0:T(2,128)(2,1)S(1)} %pad_maximum_fusion.rows), channel_id=1, source_target_pairs={{12,0},{5,1},{10,2},{9,5},{2,6},{15,7},{0,8},{13,9},{6,10},{8,12},... | collective-permute-start | bytes 49160 | tf_op jit(solution)/shard_map/ppermute | solution.py:114
  7.4 5.0 %collective-permute-start.1 = (bf16[2,4096]{1,0:T(2,128)(2,1)S(1)}, bf16[2,4096]{1,0:T(2,128)(2,1)S(1)}, u32[]{:S(2)}, u32[]{:S(2)}) collective-permute-start(bf16[2,4096]{1,0:T(2,128)(2,1)S(1)} %pad_maximum_fusion.rows), channel_id=1, source_target_pairs={{8,0},{6,2},{15,3},{0,4},{13,5},{10,6},{4,8},{14,10},{3,11},{5,13}... | collective-permute-start | bytes 49160 | tf_op jit(solution)/shard_map/ppermute | solution.py:114
  9.1 5.2 %collective-permute-start.5 = (f32[64]{0:T(128)S(1)}, f32[64]{0:T(128)S(1)}, u32[]{:S(2)}, u32[]{:S(2)}) collective-permute-start(f32[64]{0:T(128)S(1)} %fusion), channel_id=1, source_target_pairs={{0,12},{1,4},{2,8},{3,0},{4,5},{5,9},{6,1},{7,13},{8,2},{9,14},{10... | collective-permute-start | bytes 776 | tf_op jit(solution)/shard_map/ppermute | solution.py:120
  12.9 4.2 %collective-permute-start.3 = (f32[64]{0:T(128)S(1)}, f32[64]{0:T(128)S(1)}, u32[]{:S(2)}, u32[]{:S(2)}) collective-permute-start(f32[64]{0:T(128)S(1)} %fusion.1), channel_id=1, source_target_pairs={{0,8},{1,0},{2,4},{3,12},{4,1},{5,13},{6,9},{7,5},{8,6},{9,10},{10... | collective-permute-start | bytes 776 | tf_op jit(solution)/shard_map/ppermute | solution.py:120

commit v9 on v8

--- a/solution.py
+++ b/solution.py
@@ -10,48 +10,51 @@
 
 FIRST = ((2, 0, 1, 3), (0, 3, 2, 1), (1, 2, 3, 0), (3, 1, 0, 2))
 SECOND = ((3, 1, 2, 0), (1, 2, 0, 3), (0, 3, 1, 2), (2, 0, 3, 1))
-CHUNKS = 2
+CHUNKS = 4
 
 
-def pair_kernel(seq_len, acts, proj_in, grads, proj_out, lengths, out, *scratch):
-    acts_v, pin_v, grads_v, pout_v, kron_v, lengths_s, sems = scratch
-    width = acts.shape[1] // CHUNKS
-    limits = pltpu.make_async_copy(lengths, lengths_s, sems.at[4 * CHUNKS])
-    loads = []
-    for pair in (((acts, acts_v), (proj_in, pin_v)), ((grads, grads_v), (proj_out, pout_v))):
-        for c in range(CHUNKS):
-            part = pl.ds(c * width, width)
-            loads.append([
-                pltpu.make_async_copy(src.at[:, part], dst.at[:, part], sems.at[2 * len(loads) + i])
-                for i, (src, dst) in enumerate(pair)
-            ])
+def pair_kernel(seq_len, acts, grads, proj_in, proj_out, lengths, out, *scratch):
+    tokens_v, proj_v, kron_v, lengths_s, sems, lengths_sem = scratch
+    tokens, model_width = acts.shape
+    rank = proj_in.shape[0]
+    width = model_width // CHUNKS
+    limits = pltpu.make_async_copy(lengths, lengths_s, lengths_sem)
+    loads = [
+        [
+            pltpu.make_async_copy(
+                src.at[:, pl.ds(c * width, width)],
+                dst.at[pl.ds(half * src.shape[0], src.shape[0]), pl.ds(c * width, width)],
+                sems.at[c, 2 * half + i],
+            )
+            for half, pair in enumerate(((acts, proj_in), (grads, proj_out)))
+            for i, (src, dst) in enumerate(zip(pair, (tokens_v, proj_v)))
+        ]
+        for c in range(CHUNKS)
+    ]
     for copies in loads:
         for copy in copies:
             copy.start()
     limits.start()
-
-    def project(left, right, steps):
-        total = None
-        for c, copies in enumerate(steps):
-            for copy in copies:
-                copy.wait()
-            part = pl.ds(c * width, width)
-            term = lax.dot_general(
-                left[:, part], right[:, part], (((1,), (1,)), ((), ())), preferred_element_type=jnp.float32
-            )
-            total = term if total is None else total + term
-        return total
-
-    in_coords = project(acts_v, pin_v, loads[:CHUNKS])
+    coords = None
+    for c, copies in enumerate(loads):
+        for copy in copies:
+            copy.wait()
+        part = pl.ds(c * width, width)
+        term = lax.dot_general(
+            proj_v[:, part], tokens_v[:, part], (((1,), (1,)), ((), ())), preferred_element_type=jnp.float32
+        )
+        coords = term if coords is None else coords + term
     limits.wait()
-    token = lax.broadcasted_iota(jnp.int32, in_coords.shape, 0)
+    token = lax.broadcasted_iota(jnp.int32, (1, tokens), 1)
     side = token // seq_len
     live = token - side * seq_len < jnp.where(side == 0, lengths_s[0, 0], lengths_s[0, 1])
     weight = jnp.where(live, jnp.where(side == 0, 1.0, -1.0), 0.0)
-    in_coords = (in_coords * weight).astype(jnp.bfloat16)
-    out_coords = project(pout_v, grads_v, loads[CHUNKS:]).astype(jnp.bfloat16)
-    kron_v[...] = jnp.dot(out_coords, in_coords, preferred_element_type=jnp.float32)
-    half = kron_v.shape[0] // 2
+    in_coords = (coords[:rank, :tokens] * weight).astype(jnp.bfloat16)
+    out_coords = coords[rank:, tokens:].astype(jnp.bfloat16)
+    kron_v[...] = lax.dot_general(
+        out_coords, in_coords, (((1,), (1,)), ((), ())), preferred_element_type=jnp.float32
+    )
+    half = rank // 2
     rows = jnp.concatenate([kron_v[pl.ds(i, half, stride=2), :] for i in range(2)], axis=1)
     for i in range(half):
         out[:, pl.ds(i * rows.shape[1], rows.shape[1])] = rows[i : i + 1].astype(out.dtype)
@@ -61,20 +64,18 @@
     _, sides, seq_len, _, model_width = acts_in.shape
     rank = proj_in.shape[2]
     tokens = sides * seq_len
-    anywhere = pl.BlockSpec(memory_space=pl.ANY)
     return pl.pallas_call(
         functools.partial(pair_kernel, seq_len),
         out_shape=jax.ShapeDtypeStruct((1, rank * rank), jnp.bfloat16),
-        in_specs=[anywhere] * 5,
+        in_specs=[pl.BlockSpec(memory_space=pl.ANY)] * 5,
         out_specs=pl.BlockSpec(memory_space=pltpu.VMEM),
         scratch_shapes=[
-            pltpu.VMEM((tokens, model_width), jnp.bfloat16),
-            pltpu.VMEM((rank, model_width), jnp.bfloat16),
-            pltpu.VMEM((tokens, model_width), jnp.bfloat16),
-            pltpu.VMEM((rank, model_width), jnp.bfloat16),
+            pltpu.VMEM((2 * tokens, model_width), jnp.bfloat16),
+            pltpu.VMEM((2 * rank, model_width), jnp.bfloat16),
             pltpu.VMEM((rank, rank), jnp.float32),
             pltpu.SMEM((1, 2), jnp.int32),
-            pltpu.SemaphoreType.DMA((4 * CHUNKS + 1,)),
+            pltpu.SemaphoreType.DMA((CHUNKS, 4)),
+            pltpu.SemaphoreType.DMA,
         ],
         compiler_params=pltpu.CompilerParams(vmem_limit_bytes=32 * 1024 * 1024),
         cost_estimate=pl.CostEstimate(
@@ -87,8 +88,8 @@
             pltpu.with_memory_space_constraint(x, pltpu.HBM)
             for x in (
                 acts_in.reshape(tokens, model_width),
+                grads_out.reshape(tokens, model_width),
                 jnp.swapaxes(proj_in, 1, 2).reshape(rank, model_width),
-                grads_out.reshape(tokens, model_width),
                 jnp.swapaxes(proj_out, 1, 2).reshape(rank, model_width),
                 lengths,
             )

time: 17.8 us -> 17.9 us (level)
  transfers between devices with their start and end apart: 6 -> 6, of which waited for: 2 -> 2; matrix products, arithmetic and copies ran while one was open for 6% -> 6% of each run, Pallas kernels for 17% -> 18%
where the time goes in v9:
time: 17.9 us; the launch traced here: 17.8 us
  starting transfers between devices  7.6 us (42%)
  waiting for transfers between devices  4.06 us (23%)
  Pallas kernels  3.22 us (18%)
  between operations  1.35 us (8%)
  matrix products  0.99 us (6%)
  other arithmetic  0.56 us (3%)
    ppermute x2, starting transfers between devices, fetch_pair(): return lax.ppermute(x, ('dp', 'layer'), moves + list(fill))  3.51 us
    ppermute x2, starting transfers between devices, to_owner(): return lax.ppermute(x, ('dp', 'layer'), moves)  3.34 us
    pallas_call x1, Pallas kernels, pair_gradient(): pl.pallas_call(functools.partial(pair_kernel, seq_len), out_shape=jax.Sha...  3.21 us
    ppermute x2, waiting for transfers between devices, to_owner(): return lax.ppermute(x, ('dp', 'layer'), moves)  2.86 us
    ppermute x2, waiting for transfers between devices, swap(): lax.ppermute(x, 'layer', [(i, i ^ 1) for i in range(lax.axis_size('layer'...  1.17 us
    dot_general x4, matrix products, score(): jnp.einsum('k,qk->q', jnp.where(is_own, mine, row), block, preferred_elem...  0.99 us
    ppermute x2, starting transfers between devices, swap(): lax.ppermute(x, 'layer', [(i, i ^ 1) for i in range(lax.axis_size('layer'...  0.75 us
    broadcast_in_dim x1, other arithmetic, shared_scores(): return ((first + second) * factor)[None]  0.51 us
  transfers between devices with their start and end apart: 6, of which 2 were waited for; matrix products, arithmetic and copies ran while one was open for 6% of the time, Pallas kernels for 18%

profile of v9, /device:TPU:11, one launch (start us, length us, event | category | flops | bytes accessed | tf_op | source)
XLA Modules:
  0.0 17.8 jit_solution(2947925230846431948)
XLA Ops:
  0.0 0.7 %collective-permute-start.2 = (bf16[64,4096]{1,0:T(8,128)(2,1)}, bf16[64,4096]{1,0:T(8,128)(2,1)S(1)}, u32[]{:S(2)}, u32[]{:S(2)}) collective-permute-start(bf16[64,4096]{1,0:T(8,128)(2,1)} %bitcast.45), channel_id=1, source_target_pairs={{0,1},{1,0},{2,3},{3,2},{4,5},{5,4},{6,7},{7,6},{8,9},{9,8},{10,11... | collective-permute-start | bytes 1572872 | tf_op jit(solution)/shard_map/ppermute | solution.py:101
  0.7 3.2 %shard_map.82 = bf16[1,4096]{1,0:T(2,128)(2,1)S(1)} custom-call(bf16[128,4096]{1,0:T(8,128)(2,1)} %bitcast.41, bf16[128,4096]{1,0:T(8,128)(2,1)} %bitcast.42, bf16[64,4096]{1,0:T(8,128)(2,1)} %bitcast.43, bf16[64,4096]{1,0:T(8,128)(2,1)} %bitcast.44, s32[1,2]{1,0:T(1,128)} %lengths.1), custom_call_target="tpu_custom_call" | custom-call | flops 134217728 | bytes 3145728 | tf_op jit(solution)/shard_map/pallas_call | solution.py:67
  3.9 0.0 copy-start
  3.9 0.1 collective-permute-start
  4.0 1.2 %collective-permute-done = bf16[1,4096]{1,0:T(2,128)(2,1)S(1)} collective-permute-done((bf16[1,4096]{1,0:T(2,128)(2,1)S(1)}, bf16[1,4096]{1,0:T(2,128)(2,1)S(1)}, u32[]{:S(2)}, u32[]{:S(2)}) %collective-permute-start) | collective-permute-done | bytes 8224 | tf_op jit(solution)/shard_map/ppermute | solution.py:101
  5.2 2.4 %collective-permute-start.4 = (bf16[2,4096]{1,0:T(2,128)(2,1)S(1)}, bf16[2,4096]{1,0:T(2,128)(2,1)S(1)}, u32[]{:S(2)}, u32[]{:S(2)}) collective-permute-start(bf16[2,4096]{1,0:T(2,128)(2,1)S(1)} %pad_maximum_fusion.rows), channel_id=1, source_target_pairs={{12,0},{5,1},{10,2},{9,5},{2,6},{15,7},{0,8},{13,9},{6,10},{8,12},... | collective-permute-start | bytes 49160 | tf_op jit(solution)/shard_map/ppermute | solution.py:115
  7.6 1.2 %collective-permute-start.1 = (bf16[2,4096]{1,0:T(2,128)(2,1)S(1)}, bf16[2,4096]{1,0:T(2,128)(2,1)S(1)}, u32[]{:S(2)}, u32[]{:S(2)}) collective-permute-start(bf16[2,4096]{1,0:T(2,128)(2,1)S(1)} %pad_maximum_fusion.rows), channel_id=1, source_target_pairs={{8,0},{6,2},{15,3},{0,4},{13,5},{10,6},{4,8},{14,10},{3,11},{5,13}... | collective-permute-start | bytes 49160 | tf_op jit(solution)/shard_map/ppermute | solution.py:115
  8.7 0.0 collective-permute-done.4
  8.7 0.0 collective-permute-done.2
  8.7 0.2 %convolution_bitcast_fusion = f32[64]{0:T(128)S(1)} fusion(bf16[64,4096]{1,0:T(8,128)(2,1)S(1)} %collective-permute-done.2, bf16[1,4096]{1,0:T(2,128)(2,1)S(1)} %collective-permute-done, pred[]{:T(512)S(6)} %or.23, bf16[2,4096]{1,0:T(2,128)(2,1)S(1)} %collective-permute-done.4), kind=kOutput, calls=%fused_computation | convolution fusion | flops 528384 | bytes 549121 | tf_op jit(solution)/shard_map/k,qk->q/dot_general | solution.py:146
  9.0 0.0 copy-done
  9.0 0.3 %fusion = f32[64]{0:T(128)S(1)} fusion(f32[64]{0:T(128)S(1)} %convolution_bitcast_fusion, bf16[1,4096]{1,0:T(2,128)(2,1)S(1)} %shard_map.82, pred[]{:T(512)S(6)} %or.23, bf16[2,4096]{1,0:T(2,128)(2,1)S(1)} %collective-permute-done.4, bf16[64,1,4096]{2,0,1:T(8,128)(2,1)S(1)} %copy-done), kind=kOutput, calls=%fused_computation.2 | convolution fusion | flops 528448 | bytes 549377 | tf_op jit(solution)/shard_map/k,qk->q/dot_general | solution.py:146
  9.2 3.3 %collective-permute-start.5 = (f32[64]{0:T(128)S(1)}, f32[64]{0:T(128)S(1)}, u32[]{:S(2)}, u32[]{:S(2)}) collective-permute-start(f32[64]{0:T(128)S(1)} %fusion), channel_id=1, source_target_pairs={{0,12},{1,4},{2,8},{3,0},{4,5},{5,9},{6,1},{7,13},{8,2},{9,14},{10... | collective-permute-start | bytes 776 | tf_op jit(solution)/shard_map/ppermute | solution.py:121
  12.5 0.0 collective-permute-done.1
  12.6 0.2 %convolution_bitcast_fusion.2 = f32[64]{0:T(128)S(1)} fusion(bf16[64,4096]{1,0:T(8,128)(2,1)S(1)} %collective-permute-done.2, bf16[1,4096]{1,0:T(2,128)(2,1)S(1)} %collective-permute-done, pred[]{:T(512)S(6)} %or.20, bf16[2,4096]{1,0:T(2,128)(2,1)S(1)} %collective-permute-done.1), kind=kOutput, calls=%fused_computation.3 | convolution fusion | flops 528384 | bytes 549121 | tf_op jit(solution)/shard_map/k,qk->q/dot_general | solution.py:146
  12.8 0.3 %fusion.1 = f32[64]{0:T(128)S(1)} fusion(f32[64]{0:T(128)S(1)} %convolution_bitcast_fusion.2, bf16[1,4096]{1,0:T(2,128)(2,1)S(1)} %shard_map.82, pred[]{:T(512)S(6)} %or.20, bf16[2,4096]{1,0:T(2,128)(2,1)S(1)} %collective-permute-done.1, bf16[64,1,4096]{2,0,1:T(8,128)(2,1)S(1)} %copy-done), kind=kOutput, calls=%fused_computation.5 | convolution fusion | flops 528448 | bytes 549377 | tf_op jit(solution)/shard_map/k,qk->q/dot_general | solution.py:146
  13.0 0.0 collective-permute-start.3
  14.4 0.0 collective-permute-done.5
  14.4 2.9 %collective-permute-done.3 = f32[64]{0:T(128)S(1)} collective-permute-done((f32[64]{0:T(128)S(1)}, f32[64]{0:T(128)S(1)}, u32[]{:S(2)}, u32[]{:S(2)}) %collective-permute-start.3) | collective-permute-done | bytes 288 | tf_op jit(solution)/shard_map/ppermute | solution.py:121
  17.3 0.5 %multiply_bitcast_fusion = f32[1,64]{1,0:T(1,128)} fusion(f32[64]{0:T(128)S(1)} %shard_map.83, f32[64]{0:T(128)S(1)} %collective-permute-done.3, f32[64]{0:T(128)S(1)} %collective-permute-done.5), kind=kLoop, calls=%fused_computation.19 | loop fusion | flops 128 | bytes 1024 | tf_op jit(solution)/shard_map/broadcast_in_dim | solution.py:151
  (2 shorter events, 0.1 us)
Async XLA Ops:
  0.0 8.7 %collective-permute-start.2 = (bf16[64,4096]{1,0:T(8,128)(2,1)}, bf16[64,4096]{1,0:T(8,128)(2,1)S(1)}, u32[]{:S(2)}, u32[]{:S(2)}) collective-permute-start(bf16[64,4096]{1,0:T(8,128)(2,1)} %bitcast.45), channel_id=1, source_target_pairs={{0,1},{1,0},{2,3},{3,2},{4,5},{5,4},{6,7},{7,6},{8,9},{9,8},{10,11... | collective-permute-start | bytes 1572872 | tf_op jit(solution)/shard_map/ppermute | solution.py:101
  3.9 5.1 %copy-start = (bf16[64,1,4096]{2,0,1:T(8,128)(2,1)S(1)}, bf16[64,1,4096]{2,0,1:T(8,128)(2,1)}, u32[]{:S(2)}) copy-start(bf16[64,1,4096]{2,0,1:T(8,128)(2,1)} %param.12) | copy-start | bytes 1572868
  3.9 1.2 %collective-permute-start = (bf16[1,4096]{1,0:T(2,128)(2,1)S(1)}, bf16[1,4096]{1,0:T(2,128)(2,1)S(1)}, u32[]{:S(2)}, u32[]{:S(2)}) collective-permute-start(bf16[1,4096]{1,0:T(2,128)(2,1)S(1)} %shard_map.82), channel_id=1, source_target_pairs={{0,1},{1,0},{2,3},{3,2},{4,5},{5,4},{6,7},{7,6},{8,9},{9,8},{10,11... | collective-permute-start | bytes 24584 | tf_op jit(solution)/shard_map/ppermute | solution.py:101
  5.2 3.5 %collective-permute-start.4 = (bf16[2,4096]{1,0:T(2,128)(2,1)S(1)}, bf16[2,4096]{1,0:T(2,128)(2,1)S(1)}, u32[]{:S(2)}, u32[]{:S(2)}) collective-permute-start(bf16[2,4096]{1,0:T(2,128)(2,1)S(1)} %pad_maximum_fusion.rows), channel_id=1, source_target_pairs={{12,0},{5,1},{10,2},{9,5},{2,6},{15,7},{0,8},{13,9},{6,10},{8,12},... | collective-permute-start | bytes 49160 | tf_op jit(solution)/shard_map/ppermute | solution.py:115
  7.6 5.0 %collective-permute-start.1 = (bf16[2,4096]{1,0:T(2,128)(2,1)S(1)}, bf16[2,4096]{1,0:T(2,128)(2,1)S(1)}, u32[]{:S(2)}, u32[]{:S(2)}) collective-permute-start(bf16[2,4096]{1,0:T(2,128)(2,1)S(1)} %pad_maximum_fusion.rows), channel_id=1, source_target_pairs={{8,0},{6,2},{15,3},{0,4},{13,5},{10,6},{4,8},{14,10},{3,11},{5,13}... | collective-permute-start | bytes 49160 | tf_op jit(solution)/shard_map/ppermute | solution.py:115
  9.2 5.2 %collective-permute-start.5 = (f32[64]{0:T(128)S(1)}, f32[64]{0:T(128)S(1)}, u32[]{:S(2)}, u32[]{:S(2)}) collective-permute-start(f32[64]{0:T(128)S(1)} %fusion), channel_id=1, source_target_pairs={{0,12},{1,4},{2,8},{3,0},{4,5},{5,9},{6,1},{7,13},{8,2},{9,14},{10... | collective-permute-start | bytes 776 | tf_op jit(solution)/shard_map/ppermute | solution.py:121
  13.0 4.2 %collective-permute-start.3 = (f32[64]{0:T(128)S(1)}, f32[64]{0:T(128)S(1)}, u32[]{:S(2)}, u32[]{:S(2)}) collective-permute-start(f32[64]{0:T(128)S(1)} %fusion.1), channel_id=1, source_target_pairs={{0,8},{1,0},{2,4},{3,12},{4,1},{5,13},{6,9},{7,5},{8,6},{9,10},{10... | collective-permute-start | bytes 776 | tf_op jit(solution)/shard_map/ppermute | solution.py:121

commit v10 on v9

--- a/solution.py
+++ b/solution.py
@@ -10,7 +10,7 @@
 
 FIRST = ((2, 0, 1, 3), (0, 3, 2, 1), (1, 2, 3, 0), (3, 1, 0, 2))
 SECOND = ((3, 1, 2, 0), (1, 2, 0, 3), (0, 3, 1, 2), (2, 0, 3, 1))
-CHUNKS = 4
+CHUNKS = 2
 
 
 def pair_kernel(seq_len, acts, grads, proj_in, proj_out, lengths, out, *scratch):
@@ -41,18 +41,18 @@
             copy.wait()
         part = pl.ds(c * width, width)
         term = lax.dot_general(
-            proj_v[:, part], tokens_v[:, part], (((1,), (1,)), ((), ())), preferred_element_type=jnp.float32
+            tokens_v[:, part], proj_v[:, part], (((1,), (1,)), ((), ())), preferred_element_type=jnp.float32
         )
         coords = term if coords is None else coords + term
     limits.wait()
-    token = lax.broadcasted_iota(jnp.int32, (1, tokens), 1)
+    token = lax.broadcasted_iota(jnp.int32, (tokens, 1), 0)
     side = token // seq_len
     live = token - side * seq_len < jnp.where(side == 0, lengths_s[0, 0], lengths_s[0, 1])
     weight = jnp.where(live, jnp.where(side == 0, 1.0, -1.0), 0.0)
-    in_coords = (coords[:rank, :tokens] * weight).astype(jnp.bfloat16)
-    out_coords = coords[rank:, tokens:].astype(jnp.bfloat16)
+    in_coords = (coords[:tokens, :rank] * weight).astype(jnp.bfloat16)
+    out_coords = coords[tokens:, rank:].astype(jnp.bfloat16)
     kron_v[...] = lax.dot_general(
-        out_coords, in_coords, (((1,), (1,)), ((), ())), preferred_element_type=jnp.float32
+        out_coords, in_coords, (((0,), (0,)), ((), ())), preferred_element_type=jnp.float32
     )
     half = rank // 2
     rows = jnp.concatenate([kron_v[pl.ds(i, half, stride=2), :] for i in range(2)], axis=1)

time: 17.9 us -> 17.7 us (0.989)
  Pallas kernels: 3.22 us -> 2.96 us
    pallas_call x1, Pallas kernels: 3.21 us -> 2.95 us  [pair_gradient(): pl.pallas_call(functools.partial(pair_kernel, seq_len), out_shape=jax.Sha...]
  transfers between devices with their start and end apart: 6 -> 6, of which waited for: 2 -> 2; matrix products, arithmetic and copies ran while one was open for 6% -> 6% of each run, Pallas kernels for 18% -> 17%
where the time goes in v10:
time: 17.7 us; the launch traced here: 17.5 us
  starting transfers between devices  7.6 us (43%)
  waiting for transfers between devices  4.06 us (23%)
  Pallas kernels  2.96 us (17%)
  between operations  1.35 us (8%)
  matrix products  0.99 us (6%)
  other arithmetic  0.56 us (3%)
    ppermute x2, starting transfers between devices, fetch_pair(): return lax.ppermute(x, ('dp', 'layer'), moves + list(fill))  3.51 us
    ppermute x2, starting transfers between devices, to_owner(): return lax.ppermute(x, ('dp', 'layer'), moves)  3.34 us
    pallas_call x1, Pallas kernels, pair_gradient(): pl.pallas_call(functools.partial(pair_kernel, seq_len), out_shape=jax.Sha...  2.95 us
    ppermute x2, waiting for transfers between devices, to_owner(): return lax.ppermute(x, ('dp', 'layer'), moves)  2.86 us
    ppermute x2, waiting for transfers between devices, swap(): lax.ppermute(x, 'layer', [(i, i ^ 1) for i in range(lax.axis_size('layer'...  1.17 us
    dot_general x4, matrix products, score(): jnp.einsum('k,qk->q', jnp.where(is_own, mine, row), block, preferred_elem...  0.99 us
    ppermute x2, starting transfers between devices, swap(): lax.ppermute(x, 'layer', [(i, i ^ 1) for i in range(lax.axis_size('layer'...  0.75 us
    broadcast_in_dim x1, other arithmetic, shared_scores(): return ((first + second) * factor)[None]  0.51 us
  transfers between devices with their start and end apart: 6, of which 2 were waited for; matrix products, arithmetic and copies ran while one was open for 6% of the time, Pallas kernels for 17%

profile of v10, /device:TPU:11, one launch (start us, length us, event | category | flops | bytes accessed | tf_op | source)
XLA Modules:
  0.0 17.5 jit_solution(2528860745228388991)
XLA Ops:
  0.0 0.7 %collective-permute-start.2 = (bf16[64,4096]{1,0:T(8,128)(2,1)}, bf16[64,4096]{1,0:T(8,128)(2,1)S(1)}, u32[]{:S(2)}, u32[]{:S(2)}) collective-permute-start(bf16[64,4096]{1,0:T(8,128)(2,1)} %bitcast.45), channel_id=1, source_target_pairs={{0,1},{1,0},{2,3},{3,2},{4,5},{5,4},{6,7},{7,6},{8,9},{9,8},{10,11... | collective-permute-start | bytes 1572872 | tf_op jit(solution)/shard_map/ppermute | solution.py:101
  0.7 2.9 %shard_map.82 = bf16[1,4096]{1,0:T(2,128)(2,1)S(1)} custom-call(bf16[128,4096]{1,0:T(8,128)(2,1)} %bitcast.41, bf16[128,4096]{1,0:T(8,128)(2,1)} %bitcast.42, bf16[64,4096]{1,0:T(8,128)(2,1)} %bitcast.43, bf16[64,4096]{1,0:T(8,128)(2,1)} %bitcast.44, s32[1,2]{1,0:T(1,128)} %lengths.1), custom_call_target="tpu_custom_call" | custom-call | flops 134217728 | bytes 3145728 | tf_op jit(solution)/shard_map/pallas_call | solution.py:67
  3.6 0.0 copy-start
  3.6 0.1 collective-permute-start
  3.7 1.2 %collective-permute-done = bf16[1,4096]{1,0:T(2,128)(2,1)S(1)} collective-permute-done((bf16[1,4096]{1,0:T(2,128)(2,1)S(1)}, bf16[1,4096]{1,0:T(2,128)(2,1)S(1)}, u32[]{:S(2)}, u32[]{:S(2)}) %collective-permute-start) | collective-permute-done | bytes 8224 | tf_op jit(solution)/shard_map/ppermute | solution.py:101
  4.9 2.4 %collective-permute-start.4 = (bf16[2,4096]{1,0:T(2,128)(2,1)S(1)}, bf16[2,4096]{1,0:T(2,128)(2,1)S(1)}, u32[]{:S(2)}, u32[]{:S(2)}) collective-permute-start(bf16[2,4096]{1,0:T(2,128)(2,1)S(1)} %pad_maximum_fusion.rows), channel_id=1, source_target_pairs={{12,0},{5,1},{10,2},{9,5},{2,6},{15,7},{0,8},{13,9},{6,10},{8,12},... | collective-permute-start | bytes 49160 | tf_op jit(solution)/shard_map/ppermute | solution.py:115
  7.3 1.2 %collective-permute-start.1 = (bf16[2,4096]{1,0:T(2,128)(2,1)S(1)}, bf16[2,4096]{1,0:T(2,128)(2,1)S(1)}, u32[]{:S(2)}, u32[]{:S(2)}) collective-permute-start(bf16[2,4096]{1,0:T(2,128)(2,1)S(1)} %pad_maximum_fusion.rows), channel_id=1, source_target_pairs={{8,0},{6,2},{15,3},{0,4},{13,5},{10,6},{4,8},{14,10},{3,11},{5,13}... | collective-permute-start | bytes 49160 | tf_op jit(solution)/shard_map/ppermute | solution.py:115
  8.4 0.0 collective-permute-done.4
  8.5 0.0 collective-permute-done.2
  8.5 0.2 %convolution_bitcast_fusion = f32[64]{0:T(128)S(1)} fusion(bf16[64,4096]{1,0:T(8,128)(2,1)S(1)} %collective-permute-done.2, bf16[1,4096]{1,0:T(2,128)(2,1)S(1)} %collective-permute-done, pred[]{:T(512)S(6)} %or.23, bf16[2,4096]{1,0:T(2,128)(2,1)S(1)} %collective-permute-done.4), kind=kOutput, calls=%fused_computation | convolution fusion | flops 528384 | bytes 549121 | tf_op jit(solution)/shard_map/k,qk->q/dot_general | solution.py:146
  8.7 0.0 copy-done
  8.7 0.3 %fusion = f32[64]{0:T(128)S(1)} fusion(f32[64]{0:T(128)S(1)} %convolution_bitcast_fusion, bf16[1,4096]{1,0:T(2,128)(2,1)S(1)} %shard_map.82, pred[]{:T(512)S(6)} %or.23, bf16[2,4096]{1,0:T(2,128)(2,1)S(1)} %collective-permute-done.4, bf16[64,1,4096]{2,0,1:T(8,128)(2,1)S(1)} %copy-done), kind=kOutput, calls=%fused_computation.2 | convolution fusion | flops 528448 | bytes 549377 | tf_op jit(solution)/shard_map/k,qk->q/dot_general | solution.py:146
  9.0 3.3 %collective-permute-start.5 = (f32[64]{0:T(128)S(1)}, f32[64]{0:T(128)S(1)}, u32[]{:S(2)}, u32[]{:S(2)}) collective-permute-start(f32[64]{0:T(128)S(1)} %fusion), channel_id=1, source_target_pairs={{0,12},{1,4},{2,8},{3,0},{4,5},{5,9},{6,1},{7,13},{8,2},{9,14},{10... | collective-permute-start | bytes 776 | tf_op jit(solution)/shard_map/ppermute | solution.py:121
  12.3 0.0 collective-permute-done.1
  12.3 0.2 %convolution_bitcast_fusion.2 = f32[64]{0:T(128)S(1)} fusion(bf16[64,4096]{1,0:T(8,128)(2,1)S(1)} %collective-permute-done.2, bf16[1,4096]{1,0:T(2,128)(2,1)S(1)} %collective-permute-done, pred[]{:T(512)S(6)} %or.20, bf16[2,4096]{1,0:T(2,128)(2,1)S(1)} %collective-permute-done.1), kind=kOutput, calls=%fused_computation.3 | convolution fusion | flops 528384 | bytes 549121 | tf_op jit(solution)/shard_map/k,qk->q/dot_general | solution.py:146
  12.5 0.3 %fusion.1 = f32[64]{0:T(128)S(1)} fusion(f32[64]{0:T(128)S(1)} %convolution_bitcast_fusion.2, bf16[1,4096]{1,0:T(2,128)(2,1)S(1)} %shard_map.82, pred[]{:T(512)S(6)} %or.20, bf16[2,4096]{1,0:T(2,128)(2,1)S(1)} %collective-permute-done.1, bf16[64,1,4096]{2,0,1:T(8,128)(2,1)S(1)} %copy-done), kind=kOutput, calls=%fused_computation.5 | convolution fusion | flops 528448 | bytes 549377 | tf_op jit(solution)/shard_map/k,qk->q/dot_general | solution.py:146
  12.8 0.0 collective-permute-start.3
  14.1 0.0 collective-permute-done.5
  14.1 2.9 %collective-permute-done.3 = f32[64]{0:T(128)S(1)} collective-permute-done((f32[64]{0:T(128)S(1)}, f32[64]{0:T(128)S(1)}, u32[]{:S(2)}, u32[]{:S(2)}) %collective-permute-start.3) | collective-permute-done | bytes 288 | tf_op jit(solution)/shard_map/ppermute | solution.py:121
  17.0 0.5 %multiply_bitcast_fusion = f32[1,64]{1,0:T(1,128)} fusion(f32[64]{0:T(128)S(1)} %shard_map.83, f32[64]{0:T(128)S(1)} %collective-permute-done.3, f32[64]{0:T(128)S(1)} %collective-permute-done.5), kind=kLoop, calls=%fused_computation.19 | loop fusion | flops 128 | bytes 1024 | tf_op jit(solution)/shard_map/broadcast_in_dim | solution.py:151
  (2 shorter events, 0.1 us)
Async XLA Ops:
  0.0 8.5 %collective-permute-start.2 = (bf16[64,4096]{1,0:T(8,128)(2,1)}, bf16[64,4096]{1,0:T(8,128)(2,1)S(1)}, u32[]{:S(2)}, u32[]{:S(2)}) collective-permute-start(bf16[64,4096]{1,0:T(8,128)(2,1)} %bitcast.45), channel_id=1, source_target_pairs={{0,1},{1,0},{2,3},{3,2},{4,5},{5,4},{6,7},{7,6},{8,9},{9,8},{10,11... | collective-permute-start | bytes 1572872 | tf_op jit(solution)/shard_map/ppermute | solution.py:101
  3.6 5.1 %copy-start = (bf16[64,1,4096]{2,0,1:T(8,128)(2,1)S(1)}, bf16[64,1,4096]{2,0,1:T(8,128)(2,1)}, u32[]{:S(2)}) copy-start(bf16[64,1,4096]{2,0,1:T(8,128)(2,1)} %param.12) | copy-start | bytes 1572868
  3.6 1.2 %collective-permute-start = (bf16[1,4096]{1,0:T(2,128)(2,1)S(1)}, bf16[1,4096]{1,0:T(2,128)(2,1)S(1)}, u32[]{:S(2)}, u32[]{:S(2)}) collective-permute-start(bf16[1,4096]{1,0:T(2,128)(2,1)S(1)} %shard_map.82), channel_id=1, source_target_pairs={{0,1},{1,0},{2,3},{3,2},{4,5},{5,4},{6,7},{7,6},{8,9},{9,8},{10,11... | collective-permute-start | bytes 24584 | tf_op jit(solution)/shard_map/ppermute | solution.py:101
  4.9 3.5 %collective-permute-start.4 = (bf16[2,4096]{1,0:T(2,128)(2,1)S(1)}, bf16[2,4096]{1,0:T(2,128)(2,1)S(1)}, u32[]{:S(2)}, u32[]{:S(2)}) collective-permute-start(bf16[2,4096]{1,0:T(2,128)(2,1)S(1)} %pad_maximum_fusion.rows), channel_id=1, source_target_pairs={{12,0},{5,1},{10,2},{9,5},{2,6},{15,7},{0,8},{13,9},{6,10},{8,12},... | collective-permute-start | bytes 49160 | tf_op jit(solution)/shard_map/ppermute | solution.py:115
  7.3 5.0 %collective-permute-start.1 = (bf16[2,4096]{1,0:T(2,128)(2,1)S(1)}, bf16[2,4096]{1,0:T(2,128)(2,1)S(1)}, u32[]{:S(2)}, u32[]{:S(2)}) collective-permute-start(bf16[2,4096]{1,0:T(2,128)(2,1)S(1)} %pad_maximum_fusion.rows), channel_id=1, source_target_pairs={{8,0},{6,2},{15,3},{0,4},{13,5},{10,6},{4,8},{14,10},{3,11},{5,13}... | collective-permute-start | bytes 49160 | tf_op jit(solution)/shard_map/ppermute | solution.py:115
  9.0 5.2 %collective-permute-start.5 = (f32[64]{0:T(128)S(1)}, f32[64]{0:T(128)S(1)}, u32[]{:S(2)}, u32[]{:S(2)}) collective-permute-start(f32[64]{0:T(128)S(1)} %fusion), channel_id=1, source_target_pairs={{0,12},{1,4},{2,8},{3,0},{4,5},{5,9},{6,1},{7,13},{8,2},{9,14},{10... | collective-permute-start | bytes 776 | tf_op jit(solution)/shard_map/ppermute | solution.py:121
  12.8 4.2 %collective-permute-start.3 = (f32[64]{0:T(128)S(1)}, f32[64]{0:T(128)S(1)}, u32[]{:S(2)}, u32[]{:S(2)}) collective-permute-start(f32[64]{0:T(128)S(1)} %fusion.1), channel_id=1, source_target_pairs={{0,8},{1,0},{2,4},{3,12},{4,1},{5,13},{6,9},{7,5},{8,6},{9,10},{10... | collective-permute-start | bytes 776 | tf_op jit(solution)/shard_map/ppermute | solution.py:121

commit v11 on v10

--- a/solution.py
+++ b/solution.py
@@ -8,8 +8,8 @@
 from jax.experimental.pallas import tpu as pltpu
 from jax.sharding import PartitionSpec as P
 
-FIRST = ((2, 0, 1, 3), (0, 3, 2, 1), (1, 2, 3, 0), (3, 1, 0, 2))
-SECOND = ((3, 1, 2, 0), (1, 2, 0, 3), (0, 3, 1, 2), (2, 0, 3, 1))
+FIRST = ((3, 0, 2, 1), (1, 2, 0, 3), (0, 3, 1, 2), (2, 1, 3, 0))
+SECOND = ((2, 1, 0, 3), (0, 3, 2, 1), (1, 2, 3, 0), (3, 0, 1, 2))
 CHUNKS = 2
 
 
@@ -110,9 +110,7 @@
     moves = [
         (slot[d][i] * count + i, d * count + i) for d in range(count) for i in range(count) if slot[d][i] != d
     ]
-    own = [d * count + i for d, i in own_places(slot)]
-    fill = zip(own, own[1::-1] + own[:1:-1])
-    return lax.ppermute(x, ("dp", "layer"), moves + list(fill))
+    return lax.ppermute(x, ("dp", "layer"), moves)
 
 
 def to_owner(x, slot):

time: 17.7 us -> 20.7 us (1.17)
  the two profiles are of different devices: /device:TPU:11 before, /device:TPU:1 now
where the time goes in v11:
time: 20.7 us; the launch traced here: 20.5 us
  starting transfers between devices  12.4 us (60%)
  Pallas kernels  2.96 us (14%)
  waiting for transfers between devices  2.22 us (11%)
  between operations  1.38 us (7%)
  matrix products  0.99 us (5%)
  other arithmetic  0.56 us (3%)
    ppermute x2, starting transfers between devices, fetch_pair(): return lax.ppermute(x, ('dp', 'layer'), moves)  7.23 us
    ppermute x2, starting transfers between devices, to_owner(): return lax.ppermute(x, ('dp', 'layer'), moves)  4.56 us
    pallas_call x1, Pallas kernels, pair_gradient(): pl.pallas_call(functools.partial(pair_kernel, seq_len), out_shape=jax.Sha...  2.95 us
    ppermute x2, waiting for transfers between devices, to_owner(): return lax.ppermute(x, ('dp', 'layer'), moves)  1.23 us
    dot_general x4, matrix products, score(): jnp.einsum('k,qk->q', jnp.where(is_own, mine, row), block, preferred_elem...  0.99 us
    ppermute x2, waiting for transfers between devices, swap(): lax.ppermute(x, 'layer', [(i, i ^ 1) for i in range(lax.axis_size('layer'...  0.84 us
    ppermute x2, starting transfers between devices, swap(): lax.ppermute(x, 'layer', [(i, i ^ 1) for i in range(lax.axis_size('layer'...  0.57 us
    broadcast_in_dim x1, other arithmetic, shared_scores(): return ((first + second) * factor)[None]  0.51 us
  transfers between devices with their start and end apart: 6, of which 3 were waited for; matrix products, arithmetic and copies ran while one was open for 5% of the time, Pallas kernels for 14%

profile of v11, /device:TPU:1, one launch (start us, length us, event | category | flops | bytes accessed | tf_op | source)
XLA Modules:
  0.0 20.5 jit_solution(9616746110717489327)
XLA Ops:
  0.0 0.1 collective-permute-start.2
  0.1 2.9 %shard_map.82 = bf16[1,4096]{1,0:T(2,128)(2,1)S(1)} custom-call(bf16[128,4096]{1,0:T(8,128)(2,1)} %bitcast.41, bf16[128,4096]{1,0:T(8,128)(2,1)} %bitcast.42, bf16[64,4096]{1,0:T(8,128)(2,1)} %bitcast.43, bf16[64,4096]{1,0:T(8,128)(2,1)} %bitcast.44, s32[1,2]{1,0:T(1,128)} %lengths.1), custom_call_target="tpu_custom_call" | custom-call | flops 134217728 | bytes 3145728 | tf_op jit(solution)/shard_map/pallas_call | solution.py:67
  3.0 0.0 copy-start
  3.0 0.5 %collective-permute-start = (bf16[1,4096]{1,0:T(2,128)(2,1)S(1)}, bf16[1,4096]{1,0:T(2,128)(2,1)S(1)}, u32[]{:S(2)}, u32[]{:S(2)}) collective-permute-start(bf16[1,4096]{1,0:T(2,128)(2,1)S(1)} %shard_map.82), channel_id=1, source_target_pairs={{0,1},{1,0},{2,3},{3,2},{4,5},{5,4},{6,7},{7,6},{8,9},{9,8},{10,11... | collective-permute-start | bytes 24584 | tf_op jit(solution)/shard_map/ppermute | solution.py:101
  3.5 0.8 %collective-permute-done = bf16[1,4096]{1,0:T(2,128)(2,1)S(1)} collective-permute-done((bf16[1,4096]{1,0:T(2,128)(2,1)S(1)}, bf16[1,4096]{1,0:T(2,128)(2,1)S(1)}, u32[]{:S(2)}, u32[]{:S(2)}) %collective-permute-start) | collective-permute-done | bytes 8224 | tf_op jit(solution)/shard_map/ppermute | solution.py:101
  4.4 6.6 %collective-permute-start.4 = (bf16[2,4096]{1,0:T(2,128)(2,1)S(1)}, bf16[2,4096]{1,0:T(2,128)(2,1)S(1)}, u32[]{:S(2)}, u32[]{:S(2)}) collective-permute-start(bf16[2,4096]{1,0:T(2,128)(2,1)S(1)} %pad_maximum_fusion.rows), channel_id=1, source_target_pairs={{8,0},{5,1},{15,3},{0,4},{13,5},{10,6},{4,8},{14,10},{3,11},{1,13}... | collective-permute-start | bytes 49160 | tf_op jit(solution)/shard_map/ppermute | solution.py:113
  11.0 0.7 %collective-permute-start.1 = (bf16[2,4096]{1,0:T(2,128)(2,1)S(1)}, bf16[2,4096]{1,0:T(2,128)(2,1)S(1)}, u32[]{:S(2)}, u32[]{:S(2)}) collective-permute-start(bf16[2,4096]{1,0:T(2,128)(2,1)S(1)} %pad_maximum_fusion.rows), channel_id=1, source_target_pairs={{12,0},{10,2},{7,3},{9,5},{2,6},{15,7},{0,8},{13,9},{6,10},{8,12},... | collective-permute-start | bytes 49160 | tf_op jit(solution)/shard_map/ppermute | solution.py:113
  11.7 0.1 collective-permute-done.4
  11.9 0.0 collective-permute-done.2
  11.9 0.2 %convolution_bitcast_fusion = f32[64]{0:T(128)S(1)} fusion(bf16[64,4096]{1,0:T(8,128)(2,1)S(1)} %collective-permute-done.2, bf16[1,4096]{1,0:T(2,128)(2,1)S(1)} %collective-permute-done, pred[]{:T(512)S(6)} %or.23, bf16[2,4096]{1,0:T(2,128)(2,1)S(1)} %collective-permute-done.4), kind=kOutput, calls=%fused_computation | convolution fusion | flops 528384 | bytes 549121 | tf_op jit(solution)/shard_map/k,qk->q/dot_general | solution.py:144
  12.1 0.0 copy-done
  12.1 0.3 %fusion = f32[64]{0:T(128)S(1)} fusion(f32[64]{0:T(128)S(1)} %convolution_bitcast_fusion, bf16[1,4096]{1,0:T(2,128)(2,1)S(1)} %shard_map.82, pred[]{:T(512)S(6)} %or.23, bf16[2,4096]{1,0:T(2,128)(2,1)S(1)} %collective-permute-done.4, bf16[64,1,4096]{2,0,1:T(8,128)(2,1)S(1)} %copy-done), kind=kOutput, calls=%fused_computation.2 | convolution fusion | flops 528448 | bytes 549377 | tf_op jit(solution)/shard_map/k,qk->q/dot_general | solution.py:144
  12.3 0.9 %collective-permute-start.5 = (f32[64]{0:T(128)S(1)}, f32[64]{0:T(128)S(1)}, u32[]{:S(2)}, u32[]{:S(2)}) collective-permute-start(f32[64]{0:T(128)S(1)} %fusion), channel_id=1, source_target_pairs={{0,8},{1,4},{2,0},{3,12},{4,1},{5,13},{6,9},{7,5},{8,6},{9,10},{10... | collective-permute-start | bytes 776 | tf_op jit(solution)/shard_map/ppermute | solution.py:119
  13.3 0.0 collective-permute-done.1
  13.3 0.2 %convolution_bitcast_fusion.2 = f32[64]{0:T(128)S(1)} fusion(bf16[64,4096]{1,0:T(8,128)(2,1)S(1)} %collective-permute-done.2, bf16[1,4096]{1,0:T(2,128)(2,1)S(1)} %collective-permute-done, pred[]{:T(512)S(6)} %or.20, bf16[2,4096]{1,0:T(2,128)(2,1)S(1)} %collective-permute-done.1), kind=kOutput, calls=%fused_computation.3 | convolution fusion | flops 528384 | bytes 549121 | tf_op jit(solution)/shard_map/k,qk->q/dot_general | solution.py:144
  13.5 0.3 %fusion.1 = f32[64]{0:T(128)S(1)} fusion(f32[64]{0:T(128)S(1)} %convolution_bitcast_fusion.2, bf16[1,4096]{1,0:T(2,128)(2,1)S(1)} %shard_map.82, pred[]{:T(512)S(6)} %or.20, bf16[2,4096]{1,0:T(2,128)(2,1)S(1)} %collective-permute-done.1, bf16[64,1,4096]{2,0,1:T(8,128)(2,1)S(1)} %copy-done), kind=kOutput, calls=%fused_computation.5 | convolution fusion | flops 528448 | bytes 549377 | tf_op jit(solution)/shard_map/k,qk->q/dot_general | solution.py:144
  13.8 3.6 %collective-permute-start.3 = (f32[64]{0:T(128)S(1)}, f32[64]{0:T(128)S(1)}, u32[]{:S(2)}, u32[]{:S(2)}) collective-permute-start(f32[64]{0:T(128)S(1)} %fusion.1), channel_id=1, source_target_pairs={{0,12},{1,0},{2,8},{3,4},{4,5},{5,9},{6,1},{7,13},{8,2},{9,14},{10... | collective-permute-start | bytes 776 | tf_op jit(solution)/shard_map/ppermute | solution.py:119
  18.7 0.0 collective-permute-done.5
  18.7 1.2 %collective-permute-done.3 = f32[64]{0:T(128)S(1)} collective-permute-done((f32[64]{0:T(128)S(1)}, f32[64]{0:T(128)S(1)}, u32[]{:S(2)}, u32[]{:S(2)}) %collective-permute-start.3) | collective-permute-done | bytes 288 | tf_op jit(solution)/shard_map/ppermute | solution.py:119
  20.0 0.5 %multiply_bitcast_fusion = f32[1,64]{1,0:T(1,128)} fusion(f32[64]{0:T(128)S(1)} %shard_map.83, f32[64]{0:T(128)S(1)} %collective-permute-done.3, f32[64]{0:T(128)S(1)} %collective-permute-done.5), kind=kLoop, calls=%fused_computation.19 | loop fusion | flops 128 | bytes 1024 | tf_op jit(solution)/shard_map/broadcast_in_dim | solution.py:149
  (2 shorter events, 0.1 us)
Async XLA Ops:
  0.0 11.9 %collective-permute-start.2 = (bf16[64,4096]{1,0:T(8,128)(2,1)}, bf16[64,4096]{1,0:T(8,128)(2,1)S(1)}, u32[]{:S(2)}, u32[]{:S(2)}) collective-permute-start(bf16[64,4096]{1,0:T(8,128)(2,1)} %bitcast.45), channel_id=1, source_target_pairs={{0,1},{1,0},{2,3},{3,2},{4,5},{5,4},{6,7},{7,6},{8,9},{9,8},{10,11... | collective-permute-start | bytes 1572872 | tf_op jit(solution)/shard_map/ppermute | solution.py:101
  3.0 9.1 %copy-start = (bf16[64,1,4096]{2,0,1:T(8,128)(2,1)S(1)}, bf16[64,1,4096]{2,0,1:T(8,128)(2,1)}, u32[]{:S(2)}) copy-start(bf16[64,1,4096]{2,0,1:T(8,128)(2,1)} %param.12) | copy-start | bytes 1572868
  3.0 1.4 %collective-permute-start = (bf16[1,4096]{1,0:T(2,128)(2,1)S(1)}, bf16[1,4096]{1,0:T(2,128)(2,1)S(1)}, u32[]{:S(2)}, u32[]{:S(2)}) collective-permute-start(bf16[1,4096]{1,0:T(2,128)(2,1)S(1)} %shard_map.82), channel_id=1, source_target_pairs={{0,1},{1,0},{2,3},{3,2},{4,5},{5,4},{6,7},{7,6},{8,9},{9,8},{10,11... | collective-permute-start | bytes 24584 | tf_op jit(solution)/shard_map/ppermute | solution.py:101
  4.4 7.4 %collective-permute-start.4 = (bf16[2,4096]{1,0:T(2,128)(2,1)S(1)}, bf16[2,4096]{1,0:T(2,128)(2,1)S(1)}, u32[]{:S(2)}, u32[]{:S(2)}) collective-permute-start(bf16[2,4096]{1,0:T(2,128)(2,1)S(1)} %pad_maximum_fusion.rows), channel_id=1, source_target_pairs={{8,0},{5,1},{15,3},{0,4},{13,5},{10,6},{4,8},{14,10},{3,11},{1,13}... | collective-permute-start | bytes 49160 | tf_op jit(solution)/shard_map/ppermute | solution.py:113
  11.0 2.2 %collective-permute-start.1 = (bf16[2,4096]{1,0:T(2,128)(2,1)S(1)}, bf16[2,4096]{1,0:T(2,128)(2,1)S(1)}, u32[]{:S(2)}, u32[]{:S(2)}) collective-permute-start(bf16[2,4096]{1,0:T(2,128)(2,1)S(1)} %pad_maximum_fusion.rows), channel_id=1, source_target_pairs={{12,0},{10,2},{7,3},{9,5},{2,6},{15,7},{0,8},{13,9},{6,10},{8,12},... | collective-permute-start | bytes 49160 | tf_op jit(solution)/shard_map/ppermute | solution.py:113
  12.3 6.4 %collective-permute-start.5 = (f32[64]{0:T(128)S(1)}, f32[64]{0:T(128)S(1)}, u32[]{:S(2)}, u32[]{:S(2)}) collective-permute-start(f32[64]{0:T(128)S(1)} %fusion), channel_id=1, source_target_pairs={{0,8},{1,4},{2,0},{3,12},{4,1},{5,13},{6,9},{7,5},{8,6},{9,10},{10... | collective-permute-start | bytes 776 | tf_op jit(solution)/shard_map/ppermute | solution.py:119
  13.8 6.2 %collective-permute-start.3 = (f32[64]{0:T(128)S(1)}, f32[64]{0:T(128)S(1)}, u32[]{:S(2)}, u32[]{:S(2)}) collective-permute-start(f32[64]{0:T(128)S(1)} %fusion.1), channel_id=1, source_target_pairs={{0,12},{1,0},{2,8},{3,4},{4,5},{5,9},{6,1},{7,13},{8,2},{9,14},{10... | collective-permute-start | bytes 776 | tf_op jit(solution)/shard_map/ppermute | solution.py:119

commit v12 on v10

--- a/solution.py
+++ b/solution.py
@@ -10,7 +10,7 @@
 
 FIRST = ((2, 0, 1, 3), (0, 3, 2, 1), (1, 2, 3, 0), (3, 1, 0, 2))
 SECOND = ((3, 1, 2, 0), (1, 2, 0, 3), (0, 3, 1, 2), (2, 0, 3, 1))
-CHUNKS = 2
+CHUNKS = 4
 
 
 def pair_kernel(seq_len, acts, grads, proj_in, proj_out, lengths, out, *scratch):
@@ -31,10 +31,15 @@
         ]
         for c in range(CHUNKS)
     ]
+    limits.start()
     for copies in loads:
         for copy in copies:
             copy.start()
-    limits.start()
+    limits.wait()
+    token = lax.broadcasted_iota(jnp.int32, (tokens, 1), 0)
+    side = token // seq_len
+    live = token - side * seq_len < jnp.where(side == 0, lengths_s[0, 0], lengths_s[0, 1])
+    weight = jnp.where(live, jnp.where(side == 0, 1.0, -1.0), 0.0)
     coords = None
     for c, copies in enumerate(loads):
         for copy in copies:
@@ -44,11 +49,6 @@
             tokens_v[:, part], proj_v[:, part], (((1,), (1,)), ((), ())), preferred_element_type=jnp.float32
         )
         coords = term if coords is None else coords + term
-    limits.wait()
-    token = lax.broadcasted_iota(jnp.int32, (tokens, 1), 0)
-    side = token // seq_len
-    live = token - side * seq_len < jnp.where(side == 0, lengths_s[0, 0], lengths_s[0, 1])
-    weight = jnp.where(live, jnp.where(side == 0, 1.0, -1.0), 0.0)
     in_coords = (coords[:tokens, :rank] * weight).astype(jnp.bfloat16)
     out_coords = coords[tokens:, rank:].astype(jnp.bfloat16)
     kron_v[...] = lax.dot_general(

time: 17.7 us -> 17.9 us (1.011)
  Pallas kernels: 2.96 us -> 3.14 us
    pallas_call x1, Pallas kernels: 2.95 us -> 3.13 us  [pair_gradient(): pl.pallas_call(functools.partial(pair_kernel, seq_len), out_shape=jax.Sha...]
  transfers between devices with their start and end apart: 6 -> 6, of which waited for: 2 -> 2; matrix products, arithmetic and copies ran while one was open for 6% -> 6% of each run, Pallas kernels for 17% -> 18%
where the time goes in v12:
time: 17.9 us; the launch traced here: 17.7 us
  starting transfers between devices  7.6 us (42%)
  waiting for transfers between devices  4.06 us (23%)
  Pallas kernels  3.14 us (18%)
  between operations  1.35 us (8%)
  matrix products  0.99 us (6%)
  other arithmetic  0.56 us (3%)
    ppermute x2, starting transfers between devices, fetch_pair(): return lax.ppermute(x, ('dp', 'layer'), moves + list(fill))  3.51 us
    ppermute x2, starting transfers between devices, to_owner(): return lax.ppermute(x, ('dp', 'layer'), moves)  3.34 us
    pallas_call x1, Pallas kernels, pair_gradient(): pl.pallas_call(functools.partial(pair_kernel, seq_len), out_shape=jax.Sha...  3.13 us
    ppermute x2, waiting for transfers between devices, to_owner(): return lax.ppermute(x, ('dp', 'layer'), moves)  2.86 us
    ppermute x2, waiting for transfers between devices, swap(): lax.ppermute(x, 'layer', [(i, i ^ 1) for i in range(lax.axis_size('layer'...  1.17 us
    dot_general x4, matrix products, score(): jnp.einsum('k,qk->q', jnp.where(is_own, mine, row), block, preferred_elem...  0.99 us
    ppermute x2, starting transfers between devices, swap(): lax.ppermute(x, 'layer', [(i, i ^ 1) for i in range(lax.axis_size('layer'...  0.75 us
    broadcast_in_dim x1, other arithmetic, shared_scores(): return ((first + second) * factor)[None]  0.51 us
  transfers between devices with their start and end apart: 6, of which 2 were waited for; matrix products, arithmetic and copies ran while one was open for 6% of the time, Pallas kernels for 18%

profile of v12, /device:TPU:11, one launch (start us, length us, event | category | flops | bytes accessed | tf_op | source)
XLA Modules:
  0.0 17.7 jit_solution(1341231318267434374)
XLA Ops:
  0.0 0.7 %collective-permute-start.2 = (bf16[64,4096]{1,0:T(8,128)(2,1)}, bf16[64,4096]{1,0:T(8,128)(2,1)S(1)}, u32[]{:S(2)}, u32[]{:S(2)}) collective-permute-start(bf16[64,4096]{1,0:T(8,128)(2,1)} %bitcast.45), channel_id=1, source_target_pairs={{0,1},{1,0},{2,3},{3,2},{4,5},{5,4},{6,7},{7,6},{8,9},{9,8},{10,11... | collective-permute-start | bytes 1572872 | tf_op jit(solution)/shard_map/ppermute | solution.py:101
  0.7 3.1 %shard_map.82 = bf16[1,4096]{1,0:T(2,128)(2,1)S(1)} custom-call(bf16[128,4096]{1,0:T(8,128)(2,1)} %bitcast.41, bf16[128,4096]{1,0:T(8,128)(2,1)} %bitcast.42, bf16[64,4096]{1,0:T(8,128)(2,1)} %bitcast.43, bf16[64,4096]{1,0:T(8,128)(2,1)} %bitcast.44, s32[1,2]{1,0:T(1,128)} %lengths.1), custom_call_target="tpu_custom_call" | custom-call | flops 134217728 | bytes 3145728 | tf_op jit(solution)/shard_map/pallas_call | solution.py:67
  3.8 0.0 copy-start
  3.8 0.1 collective-permute-start
  3.9 1.2 %collective-permute-done = bf16[1,4096]{1,0:T(2,128)(2,1)S(1)} collective-permute-done((bf16[1,4096]{1,0:T(2,128)(2,1)S(1)}, bf16[1,4096]{1,0:T(2,128)(2,1)S(1)}, u32[]{:S(2)}, u32[]{:S(2)}) %collective-permute-start) | collective-permute-done | bytes 8224 | tf_op jit(solution)/shard_map/ppermute | solution.py:101
  5.1 2.4 %collective-permute-start.4 = (bf16[2,4096]{1,0:T(2,128)(2,1)S(1)}, bf16[2,4096]{1,0:T(2,128)(2,1)S(1)}, u32[]{:S(2)}, u32[]{:S(2)}) collective-permute-start(bf16[2,4096]{1,0:T(2,128)(2,1)S(1)} %pad_maximum_fusion.rows), channel_id=1, source_target_pairs={{12,0},{5,1},{10,2},{9,5},{2,6},{15,7},{0,8},{13,9},{6,10},{8,12},... | collective-permute-start | bytes 49160 | tf_op jit(solution)/shard_map/ppermute | solution.py:115
  7.5 1.2 %collective-permute-start.1 = (bf16[2,4096]{1,0:T(2,128)(2,1)S(1)}, bf16[2,4096]{1,0:T(2,128)(2,1)S(1)}, u32[]{:S(2)}, u32[]{:S(2)}) collective-permute-start(bf16[2,4096]{1,0:T(2,128)(2,1)S(1)} %pad_maximum_fusion.rows), channel_id=1, source_target_pairs={{8,0},{6,2},{15,3},{0,4},{13,5},{10,6},{4,8},{14,10},{3,11},{5,13}... | collective-permute-start | bytes 49160 | tf_op jit(solution)/shard_map/ppermute | solution.py:115
  8.6 0.0 collective-permute-done.4
  8.7 0.0 collective-permute-done.2
  8.7 0.2 %convolution_bitcast_fusion = f32[64]{0:T(128)S(1)} fusion(bf16[64,4096]{1,0:T(8,128)(2,1)S(1)} %collective-permute-done.2, bf16[1,4096]{1,0:T(2,128)(2,1)S(1)} %collective-permute-done, pred[]{:T(512)S(6)} %or.23, bf16[2,4096]{1,0:T(2,128)(2,1)S(1)} %collective-permute-done.4), kind=kOutput, calls=%fused_computation | convolution fusion | flops 528384 | bytes 549121 | tf_op jit(solution)/shard_map/k,qk->q/dot_general | solution.py:146
  8.9 0.0 copy-done
  8.9 0.3 %fusion = f32[64]{0:T(128)S(1)} fusion(f32[64]{0:T(128)S(1)} %convolution_bitcast_fusion, bf16[1,4096]{1,0:T(2,128)(2,1)S(1)} %shard_map.82, pred[]{:T(512)S(6)} %or.23, bf16[2,4096]{1,0:T(2,128)(2,1)S(1)} %collective-permute-done.4, bf16[64,1,4096]{2,0,1:T(8,128)(2,1)S(1)} %copy-done), kind=kOutput, calls=%fused_computation.2 | convolution fusion | flops 528448 | bytes 549377 | tf_op jit(solution)/shard_map/k,qk->q/dot_general | solution.py:146
  9.2 3.3 %collective-permute-start.5 = (f32[64]{0:T(128)S(1)}, f32[64]{0:T(128)S(1)}, u32[]{:S(2)}, u32[]{:S(2)}) collective-permute-start(f32[64]{0:T(128)S(1)} %fusion), channel_id=1, source_target_pairs={{0,12},{1,4},{2,8},{3,0},{4,5},{5,9},{6,1},{7,13},{8,2},{9,14},{10... | collective-permute-start | bytes 776 | tf_op jit(solution)/shard_map/ppermute | solution.py:121
  12.5 0.0 collective-permute-done.1
  12.5 0.2 %convolution_bitcast_fusion.2 = f32[64]{0:T(128)S(1)} fusion(bf16[64,4096]{1,0:T(8,128)(2,1)S(1)} %collective-permute-done.2, bf16[1,4096]{1,0:T(2,128)(2,1)S(1)} %collective-permute-done, pred[]{:T(512)S(6)} %or.20, bf16[2,4096]{1,0:T(2,128)(2,1)S(1)} %collective-permute-done.1), kind=kOutput, calls=%fused_computation.3 | convolution fusion | flops 528384 | bytes 549121 | tf_op jit(solution)/shard_map/k,qk->q/dot_general | solution.py:146
  12.7 0.3 %fusion.1 = f32[64]{0:T(128)S(1)} fusion(f32[64]{0:T(128)S(1)} %convolution_bitcast_fusion.2, bf16[1,4096]{1,0:T(2,128)(2,1)S(1)} %shard_map.82, pred[]{:T(512)S(6)} %or.20, bf16[2,4096]{1,0:T(2,128)(2,1)S(1)} %collective-permute-done.1, bf16[64,1,4096]{2,0,1:T(8,128)(2,1)S(1)} %copy-done), kind=kOutput, calls=%fused_computation.5 | convolution fusion | flops 528448 | bytes 549377 | tf_op jit(solution)/shard_map/k,qk->q/dot_general | solution.py:146
  13.0 0.0 collective-permute-start.3
  14.3 0.0 collective-permute-done.5
  14.3 2.9 %collective-permute-done.3 = f32[64]{0:T(128)S(1)} collective-permute-done((f32[64]{0:T(128)S(1)}, f32[64]{0:T(128)S(1)}, u32[]{:S(2)}, u32[]{:S(2)}) %collective-permute-start.3) | collective-permute-done | bytes 288 | tf_op jit(solution)/shard_map/ppermute | solution.py:121
  17.2 0.5 %multiply_bitcast_fusion = f32[1,64]{1,0:T(1,128)} fusion(f32[64]{0:T(128)S(1)} %shard_map.83, f32[64]{0:T(128)S(1)} %collective-permute-done.3, f32[64]{0:T(128)S(1)} %collective-permute-done.5), kind=kLoop, calls=%fused_computation.19 | loop fusion | flops 128 | bytes 1024 | tf_op jit(solution)/shard_map/broadcast_in_dim | solution.py:151
  (2 shorter events, 0.1 us)
Async XLA Ops:
  0.0 8.7 %collective-permute-start.2 = (bf16[64,4096]{1,0:T(8,128)(2,1)}, bf16[64,4096]{1,0:T(8,128)(2,1)S(1)}, u32[]{:S(2)}, u32[]{:S(2)}) collective-permute-start(bf16[64,4096]{1,0:T(8,128)(2,1)} %bitcast.45), channel_id=1, source_target_pairs={{0,1},{1,0},{2,3},{3,2},{4,5},{5,4},{6,7},{7,6},{8,9},{9,8},{10,11... | collective-permute-start | bytes 1572872 | tf_op jit(solution)/shard_map/ppermute | solution.py:101
  3.8 5.1 %copy-start = (bf16[64,1,4096]{2,0,1:T(8,128)(2,1)S(1)}, bf16[64,1,4096]{2,0,1:T(8,128)(2,1)}, u32[]{:S(2)}) copy-start(bf16[64,1,4096]{2,0,1:T(8,128)(2,1)} %param.12) | copy-start | bytes 1572868
  3.8 1.2 %collective-permute-start = (bf16[1,4096]{1,0:T(2,128)(2,1)S(1)}, bf16[1,4096]{1,0:T(2,128)(2,1)S(1)}, u32[]{:S(2)}, u32[]{:S(2)}) collective-permute-start(bf16[1,4096]{1,0:T(2,128)(2,1)S(1)} %shard_map.82), channel_id=1, source_target_pairs={{0,1},{1,0},{2,3},{3,2},{4,5},{5,4},{6,7},{7,6},{8,9},{9,8},{10,11... | collective-permute-start | bytes 24584 | tf_op jit(solution)/shard_map/ppermute | solution.py:101
  5.1 3.5 %collective-permute-start.4 = (bf16[2,4096]{1,0:T(2,128)(2,1)S(1)}, bf16[2,4096]{1,0:T(2,128)(2,1)S(1)}, u32[]{:S(2)}, u32[]{:S(2)}) collective-permute-start(bf16[2,4096]{1,0:T(2,128)(2,1)S(1)} %pad_maximum_fusion.rows), channel_id=1, source_target_pairs={{12,0},{5,1},{10,2},{9,5},{2,6},{15,7},{0,8},{13,9},{6,10},{8,12},... | collective-permute-start | bytes 49160 | tf_op jit(solution)/shard_map/ppermute | solution.py:115
  7.5 5.0 %collective-permute-start.1 = (bf16[2,4096]{1,0:T(2,128)(2,1)S(1)}, bf16[2,4096]{1,0:T(2,128)(2,1)S(1)}, u32[]{:S(2)}, u32[]{:S(2)}) collective-permute-start(bf16[2,4096]{1,0:T(2,128)(2,1)S(1)} %pad_maximum_fusion.rows), channel_id=1, source_target_pairs={{8,0},{6,2},{15,3},{0,4},{13,5},{10,6},{4,8},{14,10},{3,11},{5,13}... | collective-permute-start | bytes 49160 | tf_op jit(solution)/shard_map/ppermute | solution.py:115
  9.2 5.2 %collective-permute-start.5 = (f32[64]{0:T(128)S(1)}, f32[64]{0:T(128)S(1)}, u32[]{:S(2)}, u32[]{:S(2)}) collective-permute-start(f32[64]{0:T(128)S(1)} %fusion), channel_id=1, source_target_pairs={{0,12},{1,4},{2,8},{3,0},{4,5},{5,9},{6,1},{7,13},{8,2},{9,14},{10... | collective-permute-start | bytes 776 | tf_op jit(solution)/shard_map/ppermute | solution.py:121
  13.0 4.2 %collective-permute-start.3 = (f32[64]{0:T(128)S(1)}, f32[64]{0:T(128)S(1)}, u32[]{:S(2)}, u32[]{:S(2)}) collective-permute-start(f32[64]{0:T(128)S(1)} %fusion.1), channel_id=1, source_target_pairs={{0,8},{1,0},{2,4},{3,12},{4,1},{5,13},{6,9},{7,5},{8,6},{9,10},{10... | collective-permute-start | bytes 776 | tf_op jit(solution)/shard_map/ppermute | solution.py:121

commit v13 on v10

--- a/solution.py
+++ b/solution.py
@@ -31,10 +31,10 @@
         ]
         for c in range(CHUNKS)
     ]
+    limits.start()
     for copies in loads:
-        for copy in copies:
-            copy.start()
-    limits.start()
+        for i, copy in enumerate(copies):
+            copy.start(priority=i // 2)
     coords = None
     for c, copies in enumerate(loads):
         for copy in copies:

time: 17.7 us -> 17.7 us (level)
  no operation moved by 1% of the time
where the time goes in v13:
time: 17.7 us; the launch traced here: 17.5 us
  starting transfers between devices  7.6 us (43%)
  waiting for transfers between devices  4.06 us (23%)
  Pallas kernels  2.96 us (17%)
  between operations  1.35 us (8%)
  matrix products  0.99 us (6%)
  other arithmetic  0.56 us (3%)
    ppermute x2, starting transfers between devices, fetch_pair(): return lax.ppermute(x, ('dp', 'layer'), moves + list(fill))  3.51 us
    ppermute x2, starting transfers between devices, to_owner(): return lax.ppermute(x, ('dp', 'layer'), moves)  3.34 us
    pallas_call x1, Pallas kernels, pair_gradient(): pl.pallas_call(functools.partial(pair_kernel, seq_len), out_shape=jax.Sha...  2.95 us
    ppermute x2, waiting for transfers between devices, to_owner(): return lax.ppermute(x, ('dp', 'layer'), moves)  2.86 us
    ppermute x2, waiting for transfers between devices, swap(): lax.ppermute(x, 'layer', [(i, i ^ 1) for i in range(lax.axis_size('layer'...  1.17 us
    dot_general x4, matrix products, score(): jnp.einsum('k,qk->q', jnp.where(is_own, mine, row), block, preferred_elem...  0.99 us
    ppermute x2, starting transfers between devices, swap(): lax.ppermute(x, 'layer', [(i, i ^ 1) for i in range(lax.axis_size('layer'...  0.75 us
    broadcast_in_dim x1, other arithmetic, shared_scores(): return ((first + second) * factor)[None]  0.51 us
  transfers between devices with their start and end apart: 6, of which 2 were waited for; matrix products, arithmetic and copies ran while one was open for 6% of the time, Pallas kernels for 17%

profile of v13, /device:TPU:11, one launch (start us, length us, event | category | flops | bytes accessed | tf_op | source)
XLA Modules:
  0.0 17.5 jit_solution(11918701759556513492)
XLA Ops:
  0.0 0.7 %collective-permute-start.2 = (bf16[64,4096]{1,0:T(8,128)(2,1)}, bf16[64,4096]{1,0:T(8,128)(2,1)S(1)}, u32[]{:S(2)}, u32[]{:S(2)}) collective-permute-start(bf16[64,4096]{1,0:T(8,128)(2,1)} %bitcast.45), channel_id=1, source_target_pairs={{0,1},{1,0},{2,3},{3,2},{4,5},{5,4},{6,7},{7,6},{8,9},{9,8},{10,11... | collective-permute-start | bytes 1572872 | tf_op jit(solution)/shard_map/ppermute | solution.py:101
  0.7 2.9 %shard_map.82 = bf16[1,4096]{1,0:T(2,128)(2,1)S(1)} custom-call(bf16[128,4096]{1,0:T(8,128)(2,1)} %bitcast.41, bf16[128,4096]{1,0:T(8,128)(2,1)} %bitcast.42, bf16[64,4096]{1,0:T(8,128)(2,1)} %bitcast.43, bf16[64,4096]{1,0:T(8,128)(2,1)} %bitcast.44, s32[1,2]{1,0:T(1,128)} %lengths.1), custom_call_target="tpu_custom_call" | custom-call | flops 134217728 | bytes 3145728 | tf_op jit(solution)/shard_map/pallas_call | solution.py:67
  3.6 0.0 copy-start
  3.6 0.1 collective-permute-start
  3.7 1.2 %collective-permute-done = bf16[1,4096]{1,0:T(2,128)(2,1)S(1)} collective-permute-done((bf16[1,4096]{1,0:T(2,128)(2,1)S(1)}, bf16[1,4096]{1,0:T(2,128)(2,1)S(1)}, u32[]{:S(2)}, u32[]{:S(2)}) %collective-permute-start) | collective-permute-done | bytes 8224 | tf_op jit(solution)/shard_map/ppermute | solution.py:101
  4.9 2.4 %collective-permute-start.4 = (bf16[2,4096]{1,0:T(2,128)(2,1)S(1)}, bf16[2,4096]{1,0:T(2,128)(2,1)S(1)}, u32[]{:S(2)}, u32[]{:S(2)}) collective-permute-start(bf16[2,4096]{1,0:T(2,128)(2,1)S(1)} %pad_maximum_fusion.rows), channel_id=1, source_target_pairs={{12,0},{5,1},{10,2},{9,5},{2,6},{15,7},{0,8},{13,9},{6,10},{8,12},... | collective-permute-start | bytes 49160 | tf_op jit(solution)/shard_map/ppermute | solution.py:115
  7.3 1.2 %collective-permute-start.1 = (bf16[2,4096]{1,0:T(2,128)(2,1)S(1)}, bf16[2,4096]{1,0:T(2,128)(2,1)S(1)}, u32[]{:S(2)}, u32[]{:S(2)}) collective-permute-start(bf16[2,4096]{1,0:T(2,128)(2,1)S(1)} %pad_maximum_fusion.rows), channel_id=1, source_target_pairs={{8,0},{6,2},{15,3},{0,4},{13,5},{10,6},{4,8},{14,10},{3,11},{5,13}... | collective-permute-start | bytes 49160 | tf_op jit(solution)/shard_map/ppermute | solution.py:115
  8.4 0.0 collective-permute-done.4
  8.5 0.0 collective-permute-done.2
  8.5 0.2 %convolution_bitcast_fusion = f32[64]{0:T(128)S(1)} fusion(bf16[64,4096]{1,0:T(8,128)(2,1)S(1)} %collective-permute-done.2, bf16[1,4096]{1,0:T(2,128)(2,1)S(1)} %collective-permute-done, pred[]{:T(512)S(6)} %or.23, bf16[2,4096]{1,0:T(2,128)(2,1)S(1)} %collective-permute-done.4), kind=kOutput, calls=%fused_computation | convolution fusion | flops 528384 | bytes 549121 | tf_op jit(solution)/shard_map/k,qk->q/dot_general | solution.py:146
  8.7 0.0 copy-done
  8.7 0.3 %fusion = f32[64]{0:T(128)S(1)} fusion(f32[64]{0:T(128)S(1)} %convolution_bitcast_fusion, bf16[1,4096]{1,0:T(2,128)(2,1)S(1)} %shard_map.82, pred[]{:T(512)S(6)} %or.23, bf16[2,4096]{1,0:T(2,128)(2,1)S(1)} %collective-permute-done.4, bf16[64,1,4096]{2,0,1:T(8,128)(2,1)S(1)} %copy-done), kind=kOutput, calls=%fused_computation.2 | convolution fusion | flops 528448 | bytes 549377 | tf_op jit(solution)/shard_map/k,qk->q/dot_general | solution.py:146
  9.0 3.3 %collective-permute-start.5 = (f32[64]{0:T(128)S(1)}, f32[64]{0:T(128)S(1)}, u32[]{:S(2)}, u32[]{:S(2)}) collective-permute-start(f32[64]{0:T(128)S(1)} %fusion), channel_id=1, source_target_pairs={{0,12},{1,4},{2,8},{3,0},{4,5},{5,9},{6,1},{7,13},{8,2},{9,14},{10... | collective-permute-start | bytes 776 | tf_op jit(solution)/shard_map/ppermute | solution.py:121
  12.3 0.0 collective-permute-done.1
  12.3 0.2 %convolution_bitcast_fusion.2 = f32[64]{0:T(128)S(1)} fusion(bf16[64,4096]{1,0:T(8,128)(2,1)S(1)} %collective-permute-done.2, bf16[1,4096]{1,0:T(2,128)(2,1)S(1)} %collective-permute-done, pred[]{:T(512)S(6)} %or.20, bf16[2,4096]{1,0:T(2,128)(2,1)S(1)} %collective-permute-done.1), kind=kOutput, calls=%fused_computation.3 | convolution fusion | flops 528384 | bytes 549121 | tf_op jit(solution)/shard_map/k,qk->q/dot_general | solution.py:146
  12.5 0.3 %fusion.1 = f32[64]{0:T(128)S(1)} fusion(f32[64]{0:T(128)S(1)} %convolution_bitcast_fusion.2, bf16[1,4096]{1,0:T(2,128)(2,1)S(1)} %shard_map.82, pred[]{:T(512)S(6)} %or.20, bf16[2,4096]{1,0:T(2,128)(2,1)S(1)} %collective-permute-done.1, bf16[64,1,4096]{2,0,1:T(8,128)(2,1)S(1)} %copy-done), kind=kOutput, calls=%fused_computation.5 | convolution fusion | flops 528448 | bytes 549377 | tf_op jit(solution)/shard_map/k,qk->q/dot_general | solution.py:146
  12.8 0.0 collective-permute-start.3
  14.1 0.0 collective-permute-done.5
  14.1 2.9 %collective-permute-done.3 = f32[64]{0:T(128)S(1)} collective-permute-done((f32[64]{0:T(128)S(1)}, f32[64]{0:T(128)S(1)}, u32[]{:S(2)}, u32[]{:S(2)}) %collective-permute-start.3) | collective-permute-done | bytes 288 | tf_op jit(solution)/shard_map/ppermute | solution.py:121
  17.0 0.5 %multiply_bitcast_fusion = f32[1,64]{1,0:T(1,128)} fusion(f32[64]{0:T(128)S(1)} %shard_map.83, f32[64]{0:T(128)S(1)} %collective-permute-done.3, f32[64]{0:T(128)S(1)} %collective-permute-done.5), kind=kLoop, calls=%fused_computation.19 | loop fusion | flops 128 | bytes 1024 | tf_op jit(solution)/shard_map/broadcast_in_dim | solution.py:151
  (2 shorter events, 0.1 us)
Async XLA Ops:
  0.0 8.5 %collective-permute-start.2 = (bf16[64,4096]{1,0:T(8,128)(2,1)}, bf16[64,4096]{1,0:T(8,128)(2,1)S(1)}, u32[]{:S(2)}, u32[]{:S(2)}) collective-permute-start(bf16[64,4096]{1,0:T(8,128)(2,1)} %bitcast.45), channel_id=1, source_target_pairs={{0,1},{1,0},{2,3},{3,2},{4,5},{5,4},{6,7},{7,6},{8,9},{9,8},{10,11... | collective-permute-start | bytes 1572872 | tf_op jit(solution)/shard_map/ppermute | solution.py:101
  3.6 5.1 %copy-start = (bf16[64,1,4096]{2,0,1:T(8,128)(2,1)S(1)}, bf16[64,1,4096]{2,0,1:T(8,128)(2,1)}, u32[]{:S(2)}) copy-start(bf16[64,1,4096]{2,0,1:T(8,128)(2,1)} %param.12) | copy-start | bytes 1572868
  3.6 1.2 %collective-permute-start = (bf16[1,4096]{1,0:T(2,128)(2,1)S(1)}, bf16[1,4096]{1,0:T(2,128)(2,1)S(1)}, u32[]{:S(2)}, u32[]{:S(2)}) collective-permute-start(bf16[1,4096]{1,0:T(2,128)(2,1)S(1)} %shard_map.82), channel_id=1, source_target_pairs={{0,1},{1,0},{2,3},{3,2},{4,5},{5,4},{6,7},{7,6},{8,9},{9,8},{10,11... | collective-permute-start | bytes 24584 | tf_op jit(solution)/shard_map/ppermute | solution.py:101
  4.9 3.5 %collective-permute-start.4 = (bf16[2,4096]{1,0:T(2,128)(2,1)S(1)}, bf16[2,4096]{1,0:T(2,128)(2,1)S(1)}, u32[]{:S(2)}, u32[]{:S(2)}) collective-permute-start(bf16[2,4096]{1,0:T(2,128)(2,1)S(1)} %pad_maximum_fusion.rows), channel_id=1, source_target_pairs={{12,0},{5,1},{10,2},{9,5},{2,6},{15,7},{0,8},{13,9},{6,10},{8,12},... | collective-permute-start | bytes 49160 | tf_op jit(solution)/shard_map/ppermute | solution.py:115
  7.3 5.0 %collective-permute-start.1 = (bf16[2,4096]{1,0:T(2,128)(2,1)S(1)}, bf16[2,4096]{1,0:T(2,128)(2,1)S(1)}, u32[]{:S(2)}, u32[]{:S(2)}) collective-permute-start(bf16[2,4096]{1,0:T(2,128)(2,1)S(1)} %pad_maximum_fusion.rows), channel_id=1, source_target_pairs={{8,0},{6,2},{15,3},{0,4},{13,5},{10,6},{4,8},{14,10},{3,11},{5,13}... | collective-permute-start | bytes 49160 | tf_op jit(solution)/shard_map/ppermute | solution.py:115
  9.0 5.2 %collective-permute-start.5 = (f32[64]{0:T(128)S(1)}, f32[64]{0:T(128)S(1)}, u32[]{:S(2)}, u32[]{:S(2)}) collective-permute-start(f32[64]{0:T(128)S(1)} %fusion), channel_id=1, source_target_pairs={{0,12},{1,4},{2,8},{3,0},{4,5},{5,9},{6,1},{7,13},{8,2},{9,14},{10... | collective-permute-start | bytes 776 | tf_op jit(solution)/shard_map/ppermute | solution.py:121
  12.8 4.2 %collective-permute-start.3 = (f32[64]{0:T(128)S(1)}, f32[64]{0:T(128)S(1)}, u32[]{:S(2)}, u32[]{:S(2)}) collective-permute-start(f32[64]{0:T(128)S(1)} %fusion.1), channel_id=1, source_target_pairs={{0,8},{1,0},{2,4},{3,12},{4,1},{5,13},{6,9},{7,5},{8,6},{9,10},{10... | collective-permute-start | bytes 776 | tf_op jit(solution)/shard_map/ppermute | solution.py:121

commit v14 on v13

--- a/solution.py
+++ b/solution.py
@@ -10,51 +10,37 @@
 
 FIRST = ((2, 0, 1, 3), (0, 3, 2, 1), (1, 2, 3, 0), (3, 1, 0, 2))
 SECOND = ((3, 1, 2, 0), (1, 2, 0, 3), (0, 3, 1, 2), (2, 0, 3, 1))
-CHUNKS = 2
-
-
 def pair_kernel(seq_len, acts, grads, proj_in, proj_out, lengths, out, *scratch):
-    tokens_v, proj_v, kron_v, lengths_s, sems, lengths_sem = scratch
-    tokens, model_width = acts.shape
-    rank = proj_in.shape[0]
-    width = model_width // CHUNKS
-    limits = pltpu.make_async_copy(lengths, lengths_s, lengths_sem)
+    *held, kron_v, lengths_s, sems = scratch
+    limits = pltpu.make_async_copy(lengths, lengths_s, sems.at[len(held)])
     loads = [
-        [
-            pltpu.make_async_copy(
-                src.at[:, pl.ds(c * width, width)],
-                dst.at[pl.ds(half * src.shape[0], src.shape[0]), pl.ds(c * width, width)],
-                sems.at[c, 2 * half + i],
-            )
-            for half, pair in enumerate(((acts, proj_in), (grads, proj_out)))
-            for i, (src, dst) in enumerate(zip(pair, (tokens_v, proj_v)))
-        ]
-        for c in range(CHUNKS)
+        pltpu.make_async_copy(src, dst, sems.at[i])
+        for i, (src, dst) in enumerate(zip((acts, proj_in, grads, proj_out), held))
     ]
     limits.start()
-    for copies in loads:
-        for i, copy in enumerate(copies):
-            copy.start(priority=i // 2)
-    coords = None
-    for c, copies in enumerate(loads):
-        for copy in copies:
+    for i, copy in enumerate(loads):
+        copy.start(priority=i % 2)
+
+    def project(first):
+        for copy in loads[first : first + 2]:
             copy.wait()
-        part = pl.ds(c * width, width)
-        term = lax.dot_general(
-            tokens_v[:, part], proj_v[:, part], (((1,), (1,)), ((), ())), preferred_element_type=jnp.float32
+        tokens, proj = held[first : first + 2]
+        return lax.dot_general(
+            tokens[...], proj[...], (((1,), (1,)), ((), ())), preferred_element_type=jnp.float32
         )
-        coords = term if coords is None else coords + term
+
+    coords = project(0)
     limits.wait()
-    token = lax.broadcasted_iota(jnp.int32, (tokens, 1), 0)
+    token = lax.broadcasted_iota(jnp.int32, (coords.shape[0], 1), 0)
     side = token // seq_len
     live = token - side * seq_len < jnp.where(side == 0, lengths_s[0, 0], lengths_s[0, 1])
     weight = jnp.where(live, jnp.where(side == 0, 1.0, -1.0), 0.0)
-    in_coords = (coords[:tokens, :rank] * weight).astype(jnp.bfloat16)
-    out_coords = coords[tokens:, rank:].astype(jnp.bfloat16)
+    in_coords = (coords * weight).astype(jnp.bfloat16)
+    out_coords = project(2).astype(jnp.bfloat16)
     kron_v[...] = lax.dot_general(
         out_coords, in_coords, (((0,), (0,)), ((), ())), preferred_element_type=jnp.float32
     )
-    half = rank // 2
+    half = kron_v.shape[0] // 2
     rows = jnp.concatenate([kron_v[pl.ds(i, half, stride=2), :] for i in range(2)], axis=1)
     for i in range(half):
         out[:, pl.ds(i * rows.shape[1], rows.shape[1])] = rows[i : i + 1].astype(out.dtype)
@@ -70,12 +56,10 @@
         in_specs=[pl.BlockSpec(memory_space=pl.ANY)] * 5,
         out_specs=pl.BlockSpec(memory_space=pltpu.VMEM),
         scratch_shapes=[
-            pltpu.VMEM((2 * tokens, model_width), jnp.bfloat16),
-            pltpu.VMEM((2 * rank, model_width), jnp.bfloat16),
+            *(pltpu.VMEM((rows, model_width), jnp.bfloat16) for rows in (tokens, rank, tokens, rank)),
             pltpu.VMEM((rank, rank), jnp.float32),
             pltpu.SMEM((1, 2), jnp.int32),
-            pltpu.SemaphoreType.DMA((CHUNKS, 4)),
-            pltpu.SemaphoreType.DMA,
+            pltpu.SemaphoreType.DMA((5,)),
         ],
         compiler_params=pltpu.CompilerParams(vmem_limit_bytes=32 * 1024 * 1024),
         cost_estimate=pl.CostEstimate(

time: 17.7 us -> 18.1 us (1.023)
  the two profiles are of different devices: /device:TPU:11 before, /device:TPU:0 now
where the time goes in v14:
time: 18.1 us; the launch traced here: 17.7 us
  starting transfers between devices  7.74 us (43%)
  waiting for transfers between devices  3.72 us (21%)
  Pallas kernels  3.34 us (18%)
  between operations  1.35 us (7%)
  matrix products  0.99 us (5%)
  other arithmetic  0.56 us (3%)
    ppermute x2, starting transfers between devices, fetch_pair(): return lax.ppermute(x, ('dp', 'layer'), moves + list(fill))  4.12 us
    pallas_call x1, Pallas kernels, pair_gradient(): pl.pallas_call(functools.partial(pair_kernel, seq_len), out_shape=jax.Sha...  3.33 us
    ppermute x2, starting transfers between devices, to_owner(): return lax.ppermute(x, ('dp', 'layer'), moves)  3.05 us
    ppermute x2, waiting for transfers between devices, fetch_pair(): return lax.ppermute(x, ('dp', 'layer'), moves + list(fill))  2.59 us
    ppermute x2, waiting for transfers between devices, swap(): lax.ppermute(x, 'layer', [(i, i ^ 1) for i in range(lax.axis_size('layer'...  1.13 us
    dot_general x4, matrix products, score(): jnp.einsum('k,qk->q', jnp.where(is_own, mine, row), block, preferred_elem...  0.99 us
    ppermute x2, starting transfers between devices, swap(): lax.ppermute(x, 'layer', [(i, i ^ 1) for i in range(lax.axis_size('layer'...  0.57 us
    broadcast_in_dim x1, other arithmetic, shared_scores(): return ((first + second) * factor)[None]  0.52 us
  transfers between devices with their start and end apart: 6, of which 2 were waited for; matrix products, arithmetic and copies ran while one was open for 6% of the time, Pallas kernels for 19%

profile of v14, /device:TPU:0, one launch (start us, length us, event | category | flops | bytes accessed | tf_op | source)
XLA Modules:
  0.0 17.7 jit_solution(4195824221623396707)
XLA Ops:
  0.0 0.5 %collective-permute-start.2 = (bf16[64,4096]{1,0:T(8,128)(2,1)}, bf16[64,4096]{1,0:T(8,128)(2,1)S(1)}, u32[]{:S(2)}, u32[]{:S(2)}) collective-permute-start(bf16[64,4096]{1,0:T(8,128)(2,1)} %bitcast.45), channel_id=1, source_target_pairs={{0,1},{1,0},{2,3},{3,2},{4,5},{5,4},{6,7},{7,6},{8,9},{9,8},{10,11... | collective-permute-start | bytes 1572872 | tf_op jit(solution)/shard_map/ppermute | solution.py:85
  0.5 3.3 %shard_map.82 = bf16[1,4096]{1,0:T(2,128)(2,1)S(1)} custom-call(bf16[128,4096]{1,0:T(8,128)(2,1)} %bitcast.41, bf16[128,4096]{1,0:T(8,128)(2,1)} %bitcast.42, bf16[64,4096]{1,0:T(8,128)(2,1)} %bitcast.43, bf16[64,4096]{1,0:T(8,128)(2,1)} %bitcast.44, s32[1,2]{1,0:T(1,128)} %lengths.1), custom_call_target="tpu_custom_call" | custom-call | flops 134217728 | bytes 3145728 | tf_op jit(solution)/shard_map/pallas_call | solution.py:53
  3.8 0.0 copy-start
  3.8 0.1 collective-permute-start
  3.9 1.1 %collective-permute-done = bf16[1,4096]{1,0:T(2,128)(2,1)S(1)} collective-permute-done((bf16[1,4096]{1,0:T(2,128)(2,1)S(1)}, bf16[1,4096]{1,0:T(2,128)(2,1)S(1)}, u32[]{:S(2)}, u32[]{:S(2)}) %collective-permute-start) | collective-permute-done | bytes 8224 | tf_op jit(solution)/shard_map/ppermute | solution.py:85
  5.1 3.8 %collective-permute-start.4 = (bf16[2,4096]{1,0:T(2,128)(2,1)S(1)}, bf16[2,4096]{1,0:T(2,128)(2,1)S(1)}, u32[]{:S(2)}, u32[]{:S(2)}) collective-permute-start(bf16[2,4096]{1,0:T(2,128)(2,1)S(1)} %pad_maximum_fusion.rows), channel_id=1, source_target_pairs={{12,0},{5,1},{10,2},{9,5},{2,6},{15,7},{0,8},{13,9},{6,10},{8,12},... | collective-permute-start | bytes 49160 | tf_op jit(solution)/shard_map/ppermute | solution.py:99
  8.9 0.3 %collective-permute-start.1 = (bf16[2,4096]{1,0:T(2,128)(2,1)S(1)}, bf16[2,4096]{1,0:T(2,128)(2,1)S(1)}, u32[]{:S(2)}, u32[]{:S(2)}) collective-permute-start(bf16[2,4096]{1,0:T(2,128)(2,1)S(1)} %pad_maximum_fusion.rows), channel_id=1, source_target_pairs={{8,0},{6,2},{15,3},{0,4},{13,5},{10,6},{4,8},{14,10},{3,11},{5,13}... | collective-permute-start | bytes 49160 | tf_op jit(solution)/shard_map/ppermute | solution.py:99
  9.2 2.6 %collective-permute-done.4 = bf16[2,4096]{1,0:T(2,128)(2,1)S(1)} collective-permute-done((bf16[2,4096]{1,0:T(2,128)(2,1)S(1)}, bf16[2,4096]{1,0:T(2,128)(2,1)S(1)}, u32[]{:S(2)}, u32[]{:S(2)}) %collective-permute-start.4) | collective-permute-done | bytes 16416 | tf_op jit(solution)/shard_map/ppermute | solution.py:99
  11.8 0.0 collective-permute-done.2
  11.8 0.2 %convolution_bitcast_fusion = f32[64]{0:T(128)S(1)} fusion(bf16[64,4096]{1,0:T(8,128)(2,1)S(1)} %collective-permute-done.2, bf16[1,4096]{1,0:T(2,128)(2,1)S(1)} %collective-permute-done, pred[]{:T(512)S(6)} %or.23, bf16[2,4096]{1,0:T(2,128)(2,1)S(1)} %collective-permute-done.4), kind=kOutput, calls=%fused_computation | convolution fusion | flops 528384 | bytes 549121 | tf_op jit(solution)/shard_map/k,qk->q/dot_general | solution.py:130
  12.0 0.0 copy-done
  12.1 0.3 %fusion = f32[64]{0:T(128)S(1)} fusion(f32[64]{0:T(128)S(1)} %convolution_bitcast_fusion, bf16[1,4096]{1,0:T(2,128)(2,1)S(1)} %shard_map.82, pred[]{:T(512)S(6)} %or.23, bf16[2,4096]{1,0:T(2,128)(2,1)S(1)} %collective-permute-done.4, bf16[64,1,4096]{2,0,1:T(8,128)(2,1)S(1)} %copy-done), kind=kOutput, calls=%fused_computation.2 | convolution fusion | flops 528448 | bytes 549377 | tf_op jit(solution)/shard_map/k,qk->q/dot_general | solution.py:130
  12.3 1.9 %collective-permute-start.5 = (f32[64]{0:T(128)S(1)}, f32[64]{0:T(128)S(1)}, u32[]{:S(2)}, u32[]{:S(2)}) collective-permute-start(f32[64]{0:T(128)S(1)} %fusion), channel_id=1, source_target_pairs={{0,12},{1,4},{2,8},{3,0},{4,5},{5,9},{6,1},{7,13},{8,2},{9,14},{10... | collective-permute-start | bytes 776 | tf_op jit(solution)/shard_map/ppermute | solution.py:105
  14.2 0.0 collective-permute-done.1
  14.2 0.2 %convolution_bitcast_fusion.2 = f32[64]{0:T(128)S(1)} fusion(bf16[64,4096]{1,0:T(8,128)(2,1)S(1)} %collective-permute-done.2, bf16[1,4096]{1,0:T(2,128)(2,1)S(1)} %collective-permute-done, pred[]{:T(512)S(6)} %or.20, bf16[2,4096]{1,0:T(2,128)(2,1)S(1)} %collective-permute-done.1), kind=kOutput, calls=%fused_computation.3 | convolution fusion | flops 528384 | bytes 549121 | tf_op jit(solution)/shard_map/k,qk->q/dot_general | solution.py:130
  14.4 0.3 %fusion.1 = f32[64]{0:T(128)S(1)} fusion(f32[64]{0:T(128)S(1)} %convolution_bitcast_fusion.2, bf16[1,4096]{1,0:T(2,128)(2,1)S(1)} %shard_map.82, pred[]{:T(512)S(6)} %or.20, bf16[2,4096]{1,0:T(2,128)(2,1)S(1)} %collective-permute-done.1, bf16[64,1,4096]{2,0,1:T(8,128)(2,1)S(1)} %copy-done), kind=kOutput, calls=%fused_computation.5 | convolution fusion | flops 528448 | bytes 549377 | tf_op jit(solution)/shard_map/k,qk->q/dot_general | solution.py:130
  14.7 1.2 %collective-permute-start.3 = (f32[64]{0:T(128)S(1)}, f32[64]{0:T(128)S(1)}, u32[]{:S(2)}, u32[]{:S(2)}) collective-permute-start(f32[64]{0:T(128)S(1)} %fusion.1), channel_id=1, source_target_pairs={{0,8},{1,0},{2,4},{3,12},{4,1},{5,13},{6,9},{7,5},{8,6},{9,10},{10... | collective-permute-start | bytes 776 | tf_op jit(solution)/shard_map/ppermute | solution.py:105
  17.2 0.0 collective-permute-done.5
  17.2 0.0 collective-permute-done.3
  17.2 0.5 %multiply_bitcast_fusion = f32[1,64]{1,0:T(1,128)} fusion(f32[64]{0:T(128)S(1)} %shard_map.83, f32[64]{0:T(128)S(1)} %collective-permute-done.3, f32[64]{0:T(128)S(1)} %collective-permute-done.5), kind=kLoop, calls=%fused_computation.19 | loop fusion | flops 128 | bytes 1024 | tf_op jit(solution)/shard_map/broadcast_in_dim | solution.py:135
  (2 shorter events, 0.1 us)
Async XLA Ops:
  0.0 11.8 %collective-permute-start.2 = (bf16[64,4096]{1,0:T(8,128)(2,1)}, bf16[64,4096]{1,0:T(8,128)(2,1)S(1)}, u32[]{:S(2)}, u32[]{:S(2)}) collective-permute-start(bf16[64,4096]{1,0:T(8,128)(2,1)} %bitcast.45), channel_id=1, source_target_pairs={{0,1},{1,0},{2,3},{3,2},{4,5},{5,4},{6,7},{7,6},{8,9},{9,8},{10,11... | collective-permute-start | bytes 1572872 | tf_op jit(solution)/shard_map/ppermute | solution.py:85
  3.8 8.3 %copy-start = (bf16[64,1,4096]{2,0,1:T(8,128)(2,1)S(1)}, bf16[64,1,4096]{2,0,1:T(8,128)(2,1)}, u32[]{:S(2)}) copy-start(bf16[64,1,4096]{2,0,1:T(8,128)(2,1)} %param.12) | copy-start | bytes 1572868
  3.8 1.2 %collective-permute-start = (bf16[1,4096]{1,0:T(2,128)(2,1)S(1)}, bf16[1,4096]{1,0:T(2,128)(2,1)S(1)}, u32[]{:S(2)}, u32[]{:S(2)}) collective-permute-start(bf16[1,4096]{1,0:T(2,128)(2,1)S(1)} %shard_map.82), channel_id=1, source_target_pairs={{0,1},{1,0},{2,3},{3,2},{4,5},{5,4},{6,7},{7,6},{8,9},{9,8},{10,11... | collective-permute-start | bytes 24584 | tf_op jit(solution)/shard_map/ppermute | solution.py:85
  5.1 6.7 %collective-permute-start.4 = (bf16[2,4096]{1,0:T(2,128)(2,1)S(1)}, bf16[2,4096]{1,0:T(2,128)(2,1)S(1)}, u32[]{:S(2)}, u32[]{:S(2)}) collective-permute-start(bf16[2,4096]{1,0:T(2,128)(2,1)S(1)} %pad_maximum_fusion.rows), channel_id=1, source_target_pairs={{12,0},{5,1},{10,2},{9,5},{2,6},{15,7},{0,8},{13,9},{6,10},{8,12},... | collective-permute-start | bytes 49160 | tf_op jit(solution)/shard_map/ppermute | solution.py:99
  8.9 5.3 %collective-permute-start.1 = (bf16[2,4096]{1,0:T(2,128)(2,1)S(1)}, bf16[2,4096]{1,0:T(2,128)(2,1)S(1)}, u32[]{:S(2)}, u32[]{:S(2)}) collective-permute-start(bf16[2,4096]{1,0:T(2,128)(2,1)S(1)} %pad_maximum_fusion.rows), channel_id=1, source_target_pairs={{8,0},{6,2},{15,3},{0,4},{13,5},{10,6},{4,8},{14,10},{3,11},{5,13}... | collective-permute-start | bytes 49160 | tf_op jit(solution)/shard_map/ppermute | solution.py:99
  12.3 4.9 %collective-permute-start.5 = (f32[64]{0:T(128)S(1)}, f32[64]{0:T(128)S(1)}, u32[]{:S(2)}, u32[]{:S(2)}) collective-permute-start(f32[64]{0:T(128)S(1)} %fusion), channel_id=1, source_target_pairs={{0,12},{1,4},{2,8},{3,0},{4,5},{5,9},{6,1},{7,13},{8,2},{9,14},{10... | collective-permute-start | bytes 776 | tf_op jit(solution)/shard_map/ppermute | solution.py:105
  14.7 2.5 %collective-permute-start.3 = (f32[64]{0:T(128)S(1)}, f32[64]{0:T(128)S(1)}, u32[]{:S(2)}, u32[]{:S(2)}) collective-permute-start(f32[64]{0:T(128)S(1)} %fusion.1), channel_id=1, source_target_pairs={{0,8},{1,0},{2,4},{3,12},{4,1},{5,13},{6,9},{7,5},{8,6},{9,10},{10... | collective-permute-start | bytes 776 | tf_op jit(solution)/shard_map/ppermute | solution.py:105

commit v15 on v13

--- a/solution.py
+++ b/solution.py
@@ -10,7 +10,7 @@
 
 FIRST = ((2, 0, 1, 3), (0, 3, 2, 1), (1, 2, 3, 0), (3, 1, 0, 2))
 SECOND = ((3, 1, 2, 0), (1, 2, 0, 3), (0, 3, 1, 2), (2, 0, 3, 1))
-CHUNKS = 2
+CHUNKS = 1
 
 
 def pair_kernel(seq_len, acts, grads, proj_in, proj_out, lengths, out, *scratch):

time: 17.7 us -> 17.7 us (level)
  the two profiles are of different devices: /device:TPU:11 before, /device:TPU:15 now
where the time goes in v15:
time: 17.7 us; the launch traced here: 17.5 us
  starting transfers between devices  7.6 us (43%)
  waiting for transfers between devices  4.06 us (23%)
  Pallas kernels  2.93 us (17%)
  between operations  1.35 us (8%)
  matrix products  0.99 us (6%)
  other arithmetic  0.56 us (3%)
    ppermute x2, starting transfers between devices, fetch_pair(): return lax.ppermute(x, ('dp', 'layer'), moves + list(fill))  3.51 us
    ppermute x2, starting transfers between devices, to_owner(): return lax.ppermute(x, ('dp', 'layer'), moves)  3.34 us
    pallas_call x1, Pallas kernels, pair_gradient(): pl.pallas_call(functools.partial(pair_kernel, seq_len), out_shape=jax.Sha...  2.92 us
    ppermute x2, waiting for transfers between devices, to_owner(): return lax.ppermute(x, ('dp', 'layer'), moves)  2.86 us
    ppermute x2, waiting for transfers between devices, swap(): lax.ppermute(x, 'layer', [(i, i ^ 1) for i in range(lax.axis_size('layer'...  1.17 us
    dot_general x4, matrix products, score(): jnp.einsum('k,qk->q', jnp.where(is_own, mine, row), block, preferred_elem...  0.99 us
    ppermute x2, starting transfers between devices, swap(): lax.ppermute(x, 'layer', [(i, i ^ 1) for i in range(lax.axis_size('layer'...  0.75 us
    broadcast_in_dim x1, other arithmetic, shared_scores(): return ((first + second) * factor)[None]  0.51 us
  transfers between devices with their start and end apart: 6, of which 2 were waited for; matrix products, arithmetic and copies ran while one was open for 6% of the time, Pallas kernels for 17%

profile of v15, /device:TPU:15, one launch (start us, length us, event | category | flops | bytes accessed | tf_op | source)
XLA Modules:
  0.0 17.5 jit_solution(5297837611329420327)
XLA Ops:
  0.0 0.7 %collective-permute-start.2 = (bf16[64,4096]{1,0:T(8,128)(2,1)}, bf16[64,4096]{1,0:T(8,128)(2,1)S(1)}, u32[]{:S(2)}, u32[]{:S(2)}) collective-permute-start(bf16[64,4096]{1,0:T(8,128)(2,1)} %bitcast.45), channel_id=1, source_target_pairs={{0,1},{1,0},{2,3},{3,2},{4,5},{5,4},{6,7},{7,6},{8,9},{9,8},{10,11... | collective-permute-start | bytes 1572872 | tf_op jit(solution)/shard_map/ppermute | solution.py:101
  0.7 2.9 %shard_map.82 = bf16[1,4096]{1,0:T(2,128)(2,1)S(1)} custom-call(bf16[128,4096]{1,0:T(8,128)(2,1)} %bitcast.41, bf16[128,4096]{1,0:T(8,128)(2,1)} %bitcast.42, bf16[64,4096]{1,0:T(8,128)(2,1)} %bitcast.43, bf16[64,4096]{1,0:T(8,128)(2,1)} %bitcast.44, s32[1,2]{1,0:T(1,128)} %lengths.1), custom_call_target="tpu_custom_call" | custom-call | flops 134217728 | bytes 3145728 | tf_op jit(solution)/shard_map/pallas_call | solution.py:67
  3.6 0.0 copy-start
  3.6 0.1 collective-permute-start
  3.7 1.2 %collective-permute-done = bf16[1,4096]{1,0:T(2,128)(2,1)S(1)} collective-permute-done((bf16[1,4096]{1,0:T(2,128)(2,1)S(1)}, bf16[1,4096]{1,0:T(2,128)(2,1)S(1)}, u32[]{:S(2)}, u32[]{:S(2)}) %collective-permute-start) | collective-permute-done | bytes 8224 | tf_op jit(solution)/shard_map/ppermute | solution.py:101
  4.9 2.4 %collective-permute-start.4 = (bf16[2,4096]{1,0:T(2,128)(2,1)S(1)}, bf16[2,4096]{1,0:T(2,128)(2,1)S(1)}, u32[]{:S(2)}, u32[]{:S(2)}) collective-permute-start(bf16[2,4096]{1,0:T(2,128)(2,1)S(1)} %pad_maximum_fusion.rows), channel_id=1, source_target_pairs={{12,0},{5,1},{10,2},{9,5},{2,6},{15,7},{0,8},{13,9},{6,10},{8,12},... | collective-permute-start | bytes 49160 | tf_op jit(solution)/shard_map/ppermute | solution.py:115
  7.3 1.2 %collective-permute-start.1 = (bf16[2,4096]{1,0:T(2,128)(2,1)S(1)}, bf16[2,4096]{1,0:T(2,128)(2,1)S(1)}, u32[]{:S(2)}, u32[]{:S(2)}) collective-permute-start(bf16[2,4096]{1,0:T(2,128)(2,1)S(1)} %pad_maximum_fusion.rows), channel_id=1, source_target_pairs={{8,0},{6,2},{15,3},{0,4},{13,5},{10,6},{4,8},{14,10},{3,11},{5,13}... | collective-permute-start | bytes 49160 | tf_op jit(solution)/shard_map/ppermute | solution.py:115
  8.4 0.0 collective-permute-done.4
  8.5 0.0 collective-permute-done.2
  8.5 0.2 %convolution_bitcast_fusion = f32[64]{0:T(128)S(1)} fusion(bf16[64,4096]{1,0:T(8,128)(2,1)S(1)} %collective-permute-done.2, bf16[1,4096]{1,0:T(2,128)(2,1)S(1)} %collective-permute-done, pred[]{:T(512)S(6)} %or.23, bf16[2,4096]{1,0:T(2,128)(2,1)S(1)} %collective-permute-done.4), kind=kOutput, calls=%fused_computation | convolution fusion | flops 528384 | bytes 549121 | tf_op jit(solution)/shard_map/k,qk->q/dot_general | solution.py:146
  8.7 0.0 copy-done
  8.7 0.3 %fusion = f32[64]{0:T(128)S(1)} fusion(f32[64]{0:T(128)S(1)} %convolution_bitcast_fusion, bf16[1,4096]{1,0:T(2,128)(2,1)S(1)} %shard_map.82, pred[]{:T(512)S(6)} %or.23, bf16[2,4096]{1,0:T(2,128)(2,1)S(1)} %collective-permute-done.4, bf16[64,1,4096]{2,0,1:T(8,128)(2,1)S(1)} %copy-done), kind=kOutput, calls=%fused_computation.2 | convolution fusion | flops 528448 | bytes 549377 | tf_op jit(solution)/shard_map/k,qk->q/dot_general | solution.py:146
  9.0 3.3 %collective-permute-start.5 = (f32[64]{0:T(128)S(1)}, f32[64]{0:T(128)S(1)}, u32[]{:S(2)}, u32[]{:S(2)}) collective-permute-start(f32[64]{0:T(128)S(1)} %fusion), channel_id=1, source_target_pairs={{0,12},{1,4},{2,8},{3,0},{4,5},{5,9},{6,1},{7,13},{8,2},{9,14},{10... | collective-permute-start | bytes 776 | tf_op jit(solution)/shard_map/ppermute | solution.py:121
  12.3 0.0 collective-permute-done.1
  12.3 0.2 %convolution_bitcast_fusion.2 = f32[64]{0:T(128)S(1)} fusion(bf16[64,4096]{1,0:T(8,128)(2,1)S(1)} %collective-permute-done.2, bf16[1,4096]{1,0:T(2,128)(2,1)S(1)} %collective-permute-done, pred[]{:T(512)S(6)} %or.20, bf16[2,4096]{1,0:T(2,128)(2,1)S(1)} %collective-permute-done.1), kind=kOutput, calls=%fused_computation.3 | convolution fusion | flops 528384 | bytes 549121 | tf_op jit(solution)/shard_map/k,qk->q/dot_general | solution.py:146
  12.5 0.3 %fusion.1 = f32[64]{0:T(128)S(1)} fusion(f32[64]{0:T(128)S(1)} %convolution_bitcast_fusion.2, bf16[1,4096]{1,0:T(2,128)(2,1)S(1)} %shard_map.82, pred[]{:T(512)S(6)} %or.20, bf16[2,4096]{1,0:T(2,128)(2,1)S(1)} %collective-permute-done.1, bf16[64,1,4096]{2,0,1:T(8,128)(2,1)S(1)} %copy-done), kind=kOutput, calls=%fused_computation.5 | convolution fusion | flops 528448 | bytes 549377 | tf_op jit(solution)/shard_map/k,qk->q/dot_general | solution.py:146
  12.8 0.0 collective-permute-start.3
  14.1 0.0 collective-permute-done.5
  14.1 2.9 %collective-permute-done.3 = f32[64]{0:T(128)S(1)} collective-permute-done((f32[64]{0:T(128)S(1)}, f32[64]{0:T(128)S(1)}, u32[]{:S(2)}, u32[]{:S(2)}) %collective-permute-start.3) | collective-permute-done | bytes 288 | tf_op jit(solution)/shard_map/ppermute | solution.py:121
  17.0 0.5 %multiply_bitcast_fusion = f32[1,64]{1,0:T(1,128)} fusion(f32[64]{0:T(128)S(1)} %shard_map.83, f32[64]{0:T(128)S(1)} %collective-permute-done.3, f32[64]{0:T(128)S(1)} %collective-permute-done.5), kind=kLoop, calls=%fused_computation.19 | loop fusion | flops 128 | bytes 1024 | tf_op jit(solution)/shard_map/broadcast_in_dim | solution.py:151
  (2 shorter events, 0.1 us)
Async XLA Ops:
  0.0 8.5 %collective-permute-start.2 = (bf16[64,4096]{1,0:T(8,128)(2,1)}, bf16[64,4096]{1,0:T(8,128)(2,1)S(1)}, u32[]{:S(2)}, u32[]{:S(2)}) collective-permute-start(bf16[64,4096]{1,0:T(8,128)(2,1)} %bitcast.45), channel_id=1, source_target_pairs={{0,1},{1,0},{2,3},{3,2},{4,5},{5,4},{6,7},{7,6},{8,9},{9,8},{10,11... | collective-permute-start | bytes 1572872 | tf_op jit(solution)/shard_map/ppermute | solution.py:101
  3.6 5.1 %copy-start = (bf16[64,1,4096]{2,0,1:T(8,128)(2,1)S(1)}, bf16[64,1,4096]{2,0,1:T(8,128)(2,1)}, u32[]{:S(2)}) copy-start(bf16[64,1,4096]{2,0,1:T(8,128)(2,1)} %param.12) | copy-start | bytes 1572868
  3.6 1.2 %collective-permute-start = (bf16[1,4096]{1,0:T(2,128)(2,1)S(1)}, bf16[1,4096]{1,0:T(2,128)(2,1)S(1)}, u32[]{:S(2)}, u32[]{:S(2)}) collective-permute-start(bf16[1,4096]{1,0:T(2,128)(2,1)S(1)} %shard_map.82), channel_id=1, source_target_pairs={{0,1},{1,0},{2,3},{3,2},{4,5},{5,4},{6,7},{7,6},{8,9},{9,8},{10,11... | collective-permute-start | bytes 24584 | tf_op jit(solution)/shard_map/ppermute | solution.py:101
  4.9 3.5 %collective-permute-start.4 = (bf16[2,4096]{1,0:T(2,128)(2,1)S(1)}, bf16[2,4096]{1,0:T(2,128)(2,1)S(1)}, u32[]{:S(2)}, u32[]{:S(2)}) collective-permute-start(bf16[2,4096]{1,0:T(2,128)(2,1)S(1)} %pad_maximum_fusion.rows), channel_id=1, source_target_pairs={{12,0},{5,1},{10,2},{9,5},{2,6},{15,7},{0,8},{13,9},{6,10},{8,12},... | collective-permute-start | bytes 49160 | tf_op jit(solution)/shard_map/ppermute | solution.py:115
  7.3 5.0 %collective-permute-start.1 = (bf16[2,4096]{1,0:T(2,128)(2,1)S(1)}, bf16[2,4096]{1,0:T(2,128)(2,1)S(1)}, u32[]{:S(2)}, u32[]{:S(2)}) collective-permute-start(bf16[2,4096]{1,0:T(2,128)(2,1)S(1)} %pad_maximum_fusion.rows), channel_id=1, source_target_pairs={{8,0},{6,2},{15,3},{0,4},{13,5},{10,6},{4,8},{14,10},{3,11},{5,13}... | collective-permute-start | bytes 49160 | tf_op jit(solution)/shard_map/ppermute | solution.py:115
  9.0 5.2 %collective-permute-start.5 = (f32[64]{0:T(128)S(1)}, f32[64]{0:T(128)S(1)}, u32[]{:S(2)}, u32[]{:S(2)}) collective-permute-start(f32[64]{0:T(128)S(1)} %fusion), channel_id=1, source_target_pairs={{0,12},{1,4},{2,8},{3,0},{4,5},{5,9},{6,1},{7,13},{8,2},{9,14},{10... | collective-permute-start | bytes 776 | tf_op jit(solution)/shard_map/ppermute | solution.py:121
  12.8 4.2 %collective-permute-start.3 = (f32[64]{0:T(128)S(1)}, f32[64]{0:T(128)S(1)}, u32[]{:S(2)}, u32[]{:S(2)}) collective-permute-start(f32[64]{0:T(128)S(1)} %fusion.1), channel_id=1, source_target_pairs={{0,8},{1,0},{2,4},{3,12},{4,1},{5,13},{6,9},{7,5},{8,6},{9,10},{10... | collective-permute-start | bytes 776 | tf_op jit(solution)/shard_map/ppermute | solution.py:121

commit v16 on v14

--- a/solution.py
+++ b/solution.py
@@ -10,37 +10,41 @@
 
 FIRST = ((2, 0, 1, 3), (0, 3, 2, 1), (1, 2, 3, 0), (3, 1, 0, 2))
 SECOND = ((3, 1, 2, 0), (1, 2, 0, 3), (0, 3, 1, 2), (2, 0, 3, 1))
+PARTS = 4
+
+
 def pair_kernel(seq_len, acts, grads, proj_in, proj_out, lengths, out, *scratch):
-    *held, kron_v, lengths_s, sems = scratch
-    limits = pltpu.make_async_copy(lengths, lengths_s, sems.at[len(held)])
+    tokens_v, proj_v, turned_v, kron_v, lengths_s, sems = scratch
+    tokens = acts.shape[0]
+    rank, model_width = proj_in.shape
+    limits = pltpu.make_async_copy(lengths, lengths_s, sems.at[4])
     loads = [
-        pltpu.make_async_copy(src, dst, sems.at[i])
-        for i, (src, dst) in enumerate(zip((acts, proj_in, grads, proj_out), held))
+        pltpu.make_async_copy(src, dst.at[pl.ds(half * src.shape[0], src.shape[0])], sems.at[2 * i + half])
+        for i, (pair, dst) in enumerate((((proj_in, proj_out), proj_v), ((acts, grads), tokens_v)))
+        for half, src in enumerate(pair)
     ]
     limits.start()
     for i, copy in enumerate(loads):
         copy.start(priority=i % 2)
-
-    def project(first):
-        for copy in loads[first : first + 2]:
-            copy.wait()
-        tokens, proj = held[first : first + 2]
-        return lax.dot_general(
-            tokens[...], proj[...], (((1,), (1,)), ((), ())), preferred_element_type=jnp.float32
-        )
-
-    coords = project(0)
     limits.wait()
-    token = lax.broadcasted_iota(jnp.int32, (coords.shape[0], 1), 0)
+    token = lax.broadcasted_iota(jnp.int32, (tokens, 1), 0)
     side = token // seq_len
     live = token - side * seq_len < jnp.where(side == 0, lengths_s[0, 0], lengths_s[0, 1])
     weight = jnp.where(live, jnp.where(side == 0, 1.0, -1.0), 0.0)
-    in_coords = (coords * weight).astype(jnp.bfloat16)
-    out_coords = project(2).astype(jnp.bfloat16)
+    for copy in loads[:2]:
+        copy.wait()
+    width = model_width // PARTS
+    for c in range(PARTS):
+        turned_v[pl.ds(c * width, width), :] = proj_v[:, pl.ds(c * width, width)].T
+    for copy in loads[2:]:
+        copy.wait()
+    coords = jnp.dot(tokens_v[...], turned_v[...], preferred_element_type=jnp.float32)
+    in_coords = (coords[:tokens, :rank] * weight).astype(jnp.bfloat16)
+    out_coords = coords[tokens:, rank:].astype(jnp.bfloat16)
     kron_v[...] = lax.dot_general(
         out_coords, in_coords, (((0,), (0,)), ((), ())), preferred_element_type=jnp.float32
     )
-    half = kron_v.shape[0] // 2
+    half = rank // 2
     rows = jnp.concatenate([kron_v[pl.ds(i, half, stride=2), :] for i in range(2)], axis=1)
     for i in range(half):
         out[:, pl.ds(i * rows.shape[1], rows.shape[1])] = rows[i : i + 1].astype(out.dtype)
@@ -56,7 +60,9 @@
         in_specs=[pl.BlockSpec(memory_space=pl.ANY)] * 5,
         out_specs=pl.BlockSpec(memory_space=pltpu.VMEM),
         scratch_shapes=[
-            *(pltpu.VMEM((rows, model_width), jnp.bfloat16) for rows in (tokens, rank, tokens, rank)),
+            pltpu.VMEM((2 * tokens, model_width), jnp.bfloat16),
+            pltpu.VMEM((2 * rank, model_width), jnp.bfloat16),
+            pltpu.VMEM((model_width, 2 * rank), jnp.bfloat16),
             pltpu.VMEM((rank, rank), jnp.float32),
             pltpu.SMEM((1, 2), jnp.int32),
             pltpu.SemaphoreType.DMA((5,)),

time: 18.1 us -> 17.6 us (0.972)
  the two profiles are of different devices: /device:TPU:0 before, /device:TPU:11 now
where the time goes in v16:
time: 17.6 us; the launch traced here: 17.5 us
  starting transfers between devices  7.6 us (43%)
  waiting for transfers between devices  4.06 us (23%)
  Pallas kernels  2.92 us (17%)
  between operations  1.35 us (8%)
  matrix products  0.99 us (6%)
  other arithmetic  0.56 us (3%)
    ppermute x2, starting transfers between devices, fetch_pair(): return lax.ppermute(x, ('dp', 'layer'), moves + list(fill))  3.51 us
    ppermute x2, starting transfers between devices, to_owner(): return lax.ppermute(x, ('dp', 'layer'), moves)  3.34 us
    pallas_call x1, Pallas kernels, pair_gradient(): pl.pallas_call(functools.partial(pair_kernel, seq_len), out_shape=jax.Sha...  2.91 us
    ppermute x2, waiting for transfers between devices, to_owner(): return lax.ppermute(x, ('dp', 'layer'), moves)  2.86 us
    ppermute x2, waiting for transfers between devices, swap(): lax.ppermute(x, 'layer', [(i, i ^ 1) for i in range(lax.axis_size('layer'...  1.17 us
    dot_general x4, matrix products, score(): jnp.einsum('k,qk->q', jnp.where(is_own, mine, row), block, preferred_elem...  0.99 us
    ppermute x2, starting transfers between devices, swap(): lax.ppermute(x, 'layer', [(i, i ^ 1) for i in range(lax.axis_size('layer'...  0.75 us
    broadcast_in_dim x1, other arithmetic, shared_scores(): return ((first + second) * factor)[None]  0.51 us
  transfers between devices with their start and end apart: 6, of which 2 were waited for; matrix products, arithmetic and copies ran while one was open for 6% of the time, Pallas kernels for 17%

profile of v16, /device:TPU:11, one launch (start us, length us, event | category | flops | bytes accessed | tf_op | source)
XLA Modules:
  0.0 17.5 jit_solution(12104988477376950584)
XLA Ops:
  0.0 0.7 %collective-permute-start.2 = (bf16[64,4096]{1,0:T(8,128)(2,1)}, bf16[64,4096]{1,0:T(8,128)(2,1)S(1)}, u32[]{:S(2)}, u32[]{:S(2)}) collective-permute-start(bf16[64,4096]{1,0:T(8,128)(2,1)} %bitcast.45), channel_id=1, source_target_pairs={{0,1},{1,0},{2,3},{3,2},{4,5},{5,4},{6,7},{7,6},{8,9},{9,8},{10,11... | collective-permute-start | bytes 1572872 | tf_op jit(solution)/shard_map/ppermute | solution.py:91
  0.7 2.9 %shard_map.82 = bf16[1,4096]{1,0:T(2,128)(2,1)S(1)} custom-call(bf16[128,4096]{1,0:T(8,128)(2,1)} %bitcast.41, bf16[128,4096]{1,0:T(8,128)(2,1)} %bitcast.42, bf16[64,4096]{1,0:T(8,128)(2,1)} %bitcast.43, bf16[64,4096]{1,0:T(8,128)(2,1)} %bitcast.44, s32[1,2]{1,0:T(1,128)} %lengths.1), custom_call_target="tpu_custom_call" | custom-call | flops 134217728 | bytes 3145728 | tf_op jit(solution)/shard_map/pallas_call | solution.py:57
  3.6 0.0 copy-start
  3.6 0.1 collective-permute-start
  3.7 1.2 %collective-permute-done = bf16[1,4096]{1,0:T(2,128)(2,1)S(1)} collective-permute-done((bf16[1,4096]{1,0:T(2,128)(2,1)S(1)}, bf16[1,4096]{1,0:T(2,128)(2,1)S(1)}, u32[]{:S(2)}, u32[]{:S(2)}) %collective-permute-start) | collective-permute-done | bytes 8224 | tf_op jit(solution)/shard_map/ppermute | solution.py:91
  4.9 2.4 %collective-permute-start.4 = (bf16[2,4096]{1,0:T(2,128)(2,1)S(1)}, bf16[2,4096]{1,0:T(2,128)(2,1)S(1)}, u32[]{:S(2)}, u32[]{:S(2)}) collective-permute-start(bf16[2,4096]{1,0:T(2,128)(2,1)S(1)} %pad_maximum_fusion.rows), channel_id=1, source_target_pairs={{12,0},{5,1},{10,2},{9,5},{2,6},{15,7},{0,8},{13,9},{6,10},{8,12},... | collective-permute-start | bytes 49160 | tf_op jit(solution)/shard_map/ppermute | solution.py:105
  7.3 1.2 %collective-permute-start.1 = (bf16[2,4096]{1,0:T(2,128)(2,1)S(1)}, bf16[2,4096]{1,0:T(2,128)(2,1)S(1)}, u32[]{:S(2)}, u32[]{:S(2)}) collective-permute-start(bf16[2,4096]{1,0:T(2,128)(2,1)S(1)} %pad_maximum_fusion.rows), channel_id=1, source_target_pairs={{8,0},{6,2},{15,3},{0,4},{13,5},{10,6},{4,8},{14,10},{3,11},{5,13}... | collective-permute-start | bytes 49160 | tf_op jit(solution)/shard_map/ppermute | solution.py:105
  8.4 0.0 collective-permute-done.4
  8.4 0.0 collective-permute-done.2
  8.4 0.2 %convolution_bitcast_fusion = f32[64]{0:T(128)S(1)} fusion(bf16[64,4096]{1,0:T(8,128)(2,1)S(1)} %collective-permute-done.2, bf16[1,4096]{1,0:T(2,128)(2,1)S(1)} %collective-permute-done, pred[]{:T(512)S(6)} %or.23, bf16[2,4096]{1,0:T(2,128)(2,1)S(1)} %collective-permute-done.4), kind=kOutput, calls=%fused_computation | convolution fusion | flops 528384 | bytes 549121 | tf_op jit(solution)/shard_map/k,qk->q/dot_general | solution.py:136
  8.7 0.0 copy-done
  8.7 0.3 %fusion = f32[64]{0:T(128)S(1)} fusion(f32[64]{0:T(128)S(1)} %convolution_bitcast_fusion, bf16[1,4096]{1,0:T(2,128)(2,1)S(1)} %shard_map.82, pred[]{:T(512)S(6)} %or.23, bf16[2,4096]{1,0:T(2,128)(2,1)S(1)} %collective-permute-done.4, bf16[64,1,4096]{2,0,1:T(8,128)(2,1)S(1)} %copy-done), kind=kOutput, calls=%fused_computation.2 | convolution fusion | flops 528448 | bytes 549377 | tf_op jit(solution)/shard_map/k,qk->q/dot_general | solution.py:136
  8.9 3.3 %collective-permute-start.5 = (f32[64]{0:T(128)S(1)}, f32[64]{0:T(128)S(1)}, u32[]{:S(2)}, u32[]{:S(2)}) collective-permute-start(f32[64]{0:T(128)S(1)} %fusion), channel_id=1, source_target_pairs={{0,12},{1,4},{2,8},{3,0},{4,5},{5,9},{6,1},{7,13},{8,2},{9,14},{10... | collective-permute-start | bytes 776 | tf_op jit(solution)/shard_map/ppermute | solution.py:111
  12.3 0.0 collective-permute-done.1
  12.3 0.2 %convolution_bitcast_fusion.2 = f32[64]{0:T(128)S(1)} fusion(bf16[64,4096]{1,0:T(8,128)(2,1)S(1)} %collective-permute-done.2, bf16[1,4096]{1,0:T(2,128)(2,1)S(1)} %collective-permute-done, pred[]{:T(512)S(6)} %or.20, bf16[2,4096]{1,0:T(2,128)(2,1)S(1)} %collective-permute-done.1), kind=kOutput, calls=%fused_computation.3 | convolution fusion | flops 528384 | bytes 549121 | tf_op jit(solution)/shard_map/k,qk->q/dot_general | solution.py:136
  12.5 0.3 %fusion.1 = f32[64]{0:T(128)S(1)} fusion(f32[64]{0:T(128)S(1)} %convolution_bitcast_fusion.2, bf16[1,4096]{1,0:T(2,128)(2,1)S(1)} %shard_map.82, pred[]{:T(512)S(6)} %or.20, bf16[2,4096]{1,0:T(2,128)(2,1)S(1)} %collective-permute-done.1, bf16[64,1,4096]{2,0,1:T(8,128)(2,1)S(1)} %copy-done), kind=kOutput, calls=%fused_computation.5 | convolution fusion | flops 528448 | bytes 549377 | tf_op jit(solution)/shard_map/k,qk->q/dot_general | solution.py:136
  12.8 0.0 collective-permute-start.3
  14.1 0.0 collective-permute-done.5
  14.1 2.9 %collective-permute-done.3 = f32[64]{0:T(128)S(1)} collective-permute-done((f32[64]{0:T(128)S(1)}, f32[64]{0:T(128)S(1)}, u32[]{:S(2)}, u32[]{:S(2)}) %collective-permute-start.3) | collective-permute-done | bytes 288 | tf_op jit(solution)/shard_map/ppermute | solution.py:111
  17.0 0.5 %multiply_bitcast_fusion = f32[1,64]{1,0:T(1,128)} fusion(f32[64]{0:T(128)S(1)} %shard_map.83, f32[64]{0:T(128)S(1)} %collective-permute-done.3, f32[64]{0:T(128)S(1)} %collective-permute-done.5), kind=kLoop, calls=%fused_computation.19 | loop fusion | flops 128 | bytes 1024 | tf_op jit(solution)/shard_map/broadcast_in_dim | solution.py:141
  (2 shorter events, 0.1 us)
Async XLA Ops:
  0.0 8.4 %collective-permute-start.2 = (bf16[64,4096]{1,0:T(8,128)(2,1)}, bf16[64,4096]{1,0:T(8,128)(2,1)S(1)}, u32[]{:S(2)}, u32[]{:S(2)}) collective-permute-start(bf16[64,4096]{1,0:T(8,128)(2,1)} %bitcast.45), channel_id=1, source_target_pairs={{0,1},{1,0},{2,3},{3,2},{4,5},{5,4},{6,7},{7,6},{8,9},{9,8},{10,11... | collective-permute-start | bytes 1572872 | tf_op jit(solution)/shard_map/ppermute | solution.py:91
  3.6 5.1 %copy-start = (bf16[64,1,4096]{2,0,1:T(8,128)(2,1)S(1)}, bf16[64,1,4096]{2,0,1:T(8,128)(2,1)}, u32[]{:S(2)}) copy-start(bf16[64,1,4096]{2,0,1:T(8,128)(2,1)} %param.12) | copy-start | bytes 1572868
  3.6 1.2 %collective-permute-start = (bf16[1,4096]{1,0:T(2,128)(2,1)S(1)}, bf16[1,4096]{1,0:T(2,128)(2,1)S(1)}, u32[]{:S(2)}, u32[]{:S(2)}) collective-permute-start(bf16[1,4096]{1,0:T(2,128)(2,1)S(1)} %shard_map.82), channel_id=1, source_target_pairs={{0,1},{1,0},{2,3},{3,2},{4,5},{5,4},{6,7},{7,6},{8,9},{9,8},{10,11... | collective-permute-start | bytes 24584 | tf_op jit(solution)/shard_map/ppermute | solution.py:91
  4.9 3.5 %collective-permute-start.4 = (bf16[2,4096]{1,0:T(2,128)(2,1)S(1)}, bf16[2,4096]{1,0:T(2,128)(2,1)S(1)}, u32[]{:S(2)}, u32[]{:S(2)}) collective-permute-start(bf16[2,4096]{1,0:T(2,128)(2,1)S(1)} %pad_maximum_fusion.rows), channel_id=1, source_target_pairs={{12,0},{5,1},{10,2},{9,5},{2,6},{15,7},{0,8},{13,9},{6,10},{8,12},... | collective-permute-start | bytes 49160 | tf_op jit(solution)/shard_map/ppermute | solution.py:105
  7.3 5.0 %collective-permute-start.1 = (bf16[2,4096]{1,0:T(2,128)(2,1)S(1)}, bf16[2,4096]{1,0:T(2,128)(2,1)S(1)}, u32[]{:S(2)}, u32[]{:S(2)}) collective-permute-start(bf16[2,4096]{1,0:T(2,128)(2,1)S(1)} %pad_maximum_fusion.rows), channel_id=1, source_target_pairs={{8,0},{6,2},{15,3},{0,4},{13,5},{10,6},{4,8},{14,10},{3,11},{5,13}... | collective-permute-start | bytes 49160 | tf_op jit(solution)/shard_map/ppermute | solution.py:105
  8.9 5.2 %collective-permute-start.5 = (f32[64]{0:T(128)S(1)}, f32[64]{0:T(128)S(1)}, u32[]{:S(2)}, u32[]{:S(2)}) collective-permute-start(f32[64]{0:T(128)S(1)} %fusion), channel_id=1, source_target_pairs={{0,12},{1,4},{2,8},{3,0},{4,5},{5,9},{6,1},{7,13},{8,2},{9,14},{10... | collective-permute-start | bytes 776 | tf_op jit(solution)/shard_map/ppermute | solution.py:111
  12.8 4.2 %collective-permute-start.3 = (f32[64]{0:T(128)S(1)}, f32[64]{0:T(128)S(1)}, u32[]{:S(2)}, u32[]{:S(2)}) collective-permute-start(f32[64]{0:T(128)S(1)} %fusion.1), channel_id=1, source_target_pairs={{0,8},{1,0},{2,4},{3,12},{4,1},{5,13},{6,9},{7,5},{8,6},{9,10},{10... | collective-permute-start | bytes 776 | tf_op jit(solution)/shard_map/ppermute | solution.py:111

commit v17 on v16

--- a/solution.py
+++ b/solution.py
@@ -10,35 +10,32 @@
 
 FIRST = ((2, 0, 1, 3), (0, 3, 2, 1), (1, 2, 3, 0), (3, 1, 0, 2))
 SECOND = ((3, 1, 2, 0), (1, 2, 0, 3), (0, 3, 1, 2), (2, 0, 3, 1))
-PARTS = 4
+PIECE = 32
 
 
 def pair_kernel(seq_len, acts, grads, proj_in, proj_out, lengths, out, *scratch):
-    tokens_v, proj_v, turned_v, kron_v, lengths_s, sems = scratch
+    tokens_v, proj_v, kron_v, lengths_s, sems, lengths_sem = scratch
     tokens = acts.shape[0]
-    rank, model_width = proj_in.shape
-    limits = pltpu.make_async_copy(lengths, lengths_s, sems.at[4])
-    loads = [
-        pltpu.make_async_copy(src, dst.at[pl.ds(half * src.shape[0], src.shape[0])], sems.at[2 * i + half])
-        for i, (pair, dst) in enumerate((((proj_in, proj_out), proj_v), ((acts, grads), tokens_v)))
-        for half, src in enumerate(pair)
-    ]
+    rank = proj_in.shape[0]
+    limits = pltpu.make_async_copy(lengths, lengths_s, lengths_sem)
     limits.start()
-    for i, copy in enumerate(loads):
-        copy.start(priority=i % 2)
+    loads = []
+    for pair, dst in (((proj_in, proj_out), proj_v), ((acts, grads), tokens_v)):
+        for half, src in enumerate(pair):
+            for row in range(0, src.shape[0], PIECE):
+                to = dst.at[pl.ds(half * src.shape[0] + row, PIECE)]
+                loads.append(pltpu.make_async_copy(src.at[pl.ds(row, PIECE)], to, sems.at[len(loads)]))
+                loads[-1].start(priority=half)
+    for copy in loads:
+        copy.wait()
+    coords = lax.dot_general(
+        tokens_v[...], proj_v[...], (((1,), (1,)), ((), ())), preferred_element_type=jnp.float32
+    )
     limits.wait()
     token = lax.broadcasted_iota(jnp.int32, (tokens, 1), 0)
     side = token // seq_len
     live = token - side * seq_len < jnp.where(side == 0, lengths_s[0, 0], lengths_s[0, 1])
     weight = jnp.where(live, jnp.where(side == 0, 1.0, -1.0), 0.0)
-    for copy in loads[:2]:
-        copy.wait()
-    width = model_width // PARTS
-    for c in range(PARTS):
-        turned_v[pl.ds(c * width, width), :] = proj_v[:, pl.ds(c * width, width)].T
-    for copy in loads[2:]:
-        copy.wait()
-    coords = jnp.dot(tokens_v[...], turned_v[...], preferred_element_type=jnp.float32)
     in_coords = (coords[:tokens, :rank] * weight).astype(jnp.bfloat16)
     out_coords = coords[tokens:, rank:].astype(jnp.bfloat16)
     kron_v[...] = lax.dot_general(
@@ -62,10 +59,10 @@
         scratch_shapes=[
             pltpu.VMEM((2 * tokens, model_width), jnp.bfloat16),
             pltpu.VMEM((2 * rank, model_width), jnp.bfloat16),
-            pltpu.VMEM((model_width, 2 * rank), jnp.bfloat16),
             pltpu.VMEM((rank, rank), jnp.float32),
             pltpu.SMEM((1, 2), jnp.int32),
-            pltpu.SemaphoreType.DMA((5,)),
+            pltpu.SemaphoreType.DMA((2 * (tokens + rank) // PIECE,)),
+            pltpu.SemaphoreType.DMA,
         ],
         compiler_params=pltpu.CompilerParams(vmem_limit_bytes=32 * 1024 * 1024),
         cost_estimate=pl.CostEstimate(

time: 17.6 us -> 17.7 us (level)
  the two profiles are of different devices: /device:TPU:11 before, /device:TPU:15 now
where the time goes in v17:
time: 17.7 us; the launch traced here: 17.6 us
  starting transfers between devices  7.6 us (43%)
  waiting for transfers between devices  4.06 us (23%)
  Pallas kernels  2.99 us (17%)
  between operations  1.35 us (8%)
  matrix products  0.99 us (6%)
  other arithmetic  0.56 us (3%)
    ppermute x2, starting transfers between devices, fetch_pair(): return lax.ppermute(x, ('dp', 'layer'), moves + list(fill))  3.51 us
    ppermute x2, starting transfers between devices, to_owner(): return lax.ppermute(x, ('dp', 'layer'), moves)  3.34 us
    pallas_call x1, Pallas kernels, pair_gradient(): pl.pallas_call(functools.partial(pair_kernel, seq_len), out_shape=jax.Sha...  2.98 us
    ppermute x2, waiting for transfers between devices, to_owner(): return lax.ppermute(x, ('dp', 'layer'), moves)  2.86 us
    ppermute x2, waiting for transfers between devices, swap(): lax.ppermute(x, 'layer', [(i, i ^ 1) for i in range(lax.axis_size('layer'...  1.17 us
    dot_general x4, matrix products, score(): jnp.einsum('k,qk->q', jnp.where(is_own, mine, row), block, preferred_elem...  0.99 us
    ppermute x2, starting transfers between devices, swap(): lax.ppermute(x, 'layer', [(i, i ^ 1) for i in range(lax.axis_size('layer'...  0.75 us
    broadcast_in_dim x1, other arithmetic, shared_scores(): return ((first + second) * factor)[None]  0.51 us
  transfers between devices with their start and end apart: 6, of which 2 were waited for; matrix products, arithmetic and copies ran while one was open for 6% of the time, Pallas kernels for 17%

profile of v17, /device:TPU:15, one launch (start us, length us, event | category | flops | bytes accessed | tf_op | source)
XLA Modules:
  0.0 17.6 jit_solution(8072162303926186110)
XLA Ops:
  0.0 0.7 %collective-permute-start.2 = (bf16[64,4096]{1,0:T(8,128)(2,1)}, bf16[64,4096]{1,0:T(8,128)(2,1)S(1)}, u32[]{:S(2)}, u32[]{:S(2)}) collective-permute-start(bf16[64,4096]{1,0:T(8,128)(2,1)} %bitcast.45), channel_id=1, source_target_pairs={{0,1},{1,0},{2,3},{3,2},{4,5},{5,4},{6,7},{7,6},{8,9},{9,8},{10,11... | collective-permute-start | bytes 1572872 | tf_op jit(solution)/shard_map/ppermute | solution.py:88
  0.7 3.0 %shard_map.82 = bf16[1,4096]{1,0:T(2,128)(2,1)S(1)} custom-call(bf16[128,4096]{1,0:T(8,128)(2,1)} %bitcast.41, bf16[128,4096]{1,0:T(8,128)(2,1)} %bitcast.42, bf16[64,4096]{1,0:T(8,128)(2,1)} %bitcast.43, bf16[64,4096]{1,0:T(8,128)(2,1)} %bitcast.44, s32[1,2]{1,0:T(1,128)} %lengths.1), custom_call_target="tpu_custom_call" | custom-call | flops 134217728 | bytes 3145728 | tf_op jit(solution)/shard_map/pallas_call | solution.py:54
  3.7 0.0 copy-start
  3.7 0.1 collective-permute-start
  3.8 1.2 %collective-permute-done = bf16[1,4096]{1,0:T(2,128)(2,1)S(1)} collective-permute-done((bf16[1,4096]{1,0:T(2,128)(2,1)S(1)}, bf16[1,4096]{1,0:T(2,128)(2,1)S(1)}, u32[]{:S(2)}, u32[]{:S(2)}) %collective-permute-start) | collective-permute-done | bytes 8224 | tf_op jit(solution)/shard_map/ppermute | solution.py:88
  5.0 2.4 %collective-permute-start.4 = (bf16[2,4096]{1,0:T(2,128)(2,1)S(1)}, bf16[2,4096]{1,0:T(2,128)(2,1)S(1)}, u32[]{:S(2)}, u32[]{:S(2)}) collective-permute-start(bf16[2,4096]{1,0:T(2,128)(2,1)S(1)} %pad_maximum_fusion.rows), channel_id=1, source_target_pairs={{12,0},{5,1},{10,2},{9,5},{2,6},{15,7},{0,8},{13,9},{6,10},{8,12},... | collective-permute-start | bytes 49160 | tf_op jit(solution)/shard_map/ppermute | solution.py:102
  7.3 1.2 %collective-permute-start.1 = (bf16[2,4096]{1,0:T(2,128)(2,1)S(1)}, bf16[2,4096]{1,0:T(2,128)(2,1)S(1)}, u32[]{:S(2)}, u32[]{:S(2)}) collective-permute-start(bf16[2,4096]{1,0:T(2,128)(2,1)S(1)} %pad_maximum_fusion.rows), channel_id=1, source_target_pairs={{8,0},{6,2},{15,3},{0,4},{13,5},{10,6},{4,8},{14,10},{3,11},{5,13}... | collective-permute-start | bytes 49160 | tf_op jit(solution)/shard_map/ppermute | solution.py:102
  8.5 0.0 collective-permute-done.4
  8.5 0.0 collective-permute-done.2
  8.5 0.2 %convolution_bitcast_fusion = f32[64]{0:T(128)S(1)} fusion(bf16[64,4096]{1,0:T(8,128)(2,1)S(1)} %collective-permute-done.2, bf16[1,4096]{1,0:T(2,128)(2,1)S(1)} %collective-permute-done, pred[]{:T(512)S(6)} %or.23, bf16[2,4096]{1,0:T(2,128)(2,1)S(1)} %collective-permute-done.4), kind=kOutput, calls=%fused_computation | convolution fusion | flops 528384 | bytes 549121 | tf_op jit(solution)/shard_map/k,qk->q/dot_general | solution.py:133
  8.8 0.0 copy-done
  8.8 0.3 %fusion = f32[64]{0:T(128)S(1)} fusion(f32[64]{0:T(128)S(1)} %convolution_bitcast_fusion, bf16[1,4096]{1,0:T(2,128)(2,1)S(1)} %shard_map.82, pred[]{:T(512)S(6)} %or.23, bf16[2,4096]{1,0:T(2,128)(2,1)S(1)} %collective-permute-done.4, bf16[64,1,4096]{2,0,1:T(8,128)(2,1)S(1)} %copy-done), kind=kOutput, calls=%fused_computation.2 | convolution fusion | flops 528448 | bytes 549377 | tf_op jit(solution)/shard_map/k,qk->q/dot_general | solution.py:133
  9.0 3.3 %collective-permute-start.5 = (f32[64]{0:T(128)S(1)}, f32[64]{0:T(128)S(1)}, u32[]{:S(2)}, u32[]{:S(2)}) collective-permute-start(f32[64]{0:T(128)S(1)} %fusion), channel_id=1, source_target_pairs={{0,12},{1,4},{2,8},{3,0},{4,5},{5,9},{6,1},{7,13},{8,2},{9,14},{10... | collective-permute-start | bytes 776 | tf_op jit(solution)/shard_map/ppermute | solution.py:108
  12.3 0.0 collective-permute-done.1
  12.3 0.2 %convolution_bitcast_fusion.2 = f32[64]{0:T(128)S(1)} fusion(bf16[64,4096]{1,0:T(8,128)(2,1)S(1)} %collective-permute-done.2, bf16[1,4096]{1,0:T(2,128)(2,1)S(1)} %collective-permute-done, pred[]{:T(512)S(6)} %or.20, bf16[2,4096]{1,0:T(2,128)(2,1)S(1)} %collective-permute-done.1), kind=kOutput, calls=%fused_computation.3 | convolution fusion | flops 528384 | bytes 549121 | tf_op jit(solution)/shard_map/k,qk->q/dot_general | solution.py:133
  12.6 0.3 %fusion.1 = f32[64]{0:T(128)S(1)} fusion(f32[64]{0:T(128)S(1)} %convolution_bitcast_fusion.2, bf16[1,4096]{1,0:T(2,128)(2,1)S(1)} %shard_map.82, pred[]{:T(512)S(6)} %or.20, bf16[2,4096]{1,0:T(2,128)(2,1)S(1)} %collective-permute-done.1, bf16[64,1,4096]{2,0,1:T(8,128)(2,1)S(1)} %copy-done), kind=kOutput, calls=%fused_computation.5 | convolution fusion | flops 528448 | bytes 549377 | tf_op jit(solution)/shard_map/k,qk->q/dot_general | solution.py:133
  12.8 0.0 collective-permute-start.3
  14.2 0.0 collective-permute-done.5
  14.2 2.9 %collective-permute-done.3 = f32[64]{0:T(128)S(1)} collective-permute-done((f32[64]{0:T(128)S(1)}, f32[64]{0:T(128)S(1)}, u32[]{:S(2)}, u32[]{:S(2)}) %collective-permute-start.3) | collective-permute-done | bytes 288 | tf_op jit(solution)/shard_map/ppermute | solution.py:108
  17.0 0.5 %multiply_bitcast_fusion = f32[1,64]{1,0:T(1,128)} fusion(f32[64]{0:T(128)S(1)} %shard_map.83, f32[64]{0:T(128)S(1)} %collective-permute-done.3, f32[64]{0:T(128)S(1)} %collective-permute-done.5), kind=kLoop, calls=%fused_computation.19 | loop fusion | flops 128 | bytes 1024 | tf_op jit(solution)/shard_map/broadcast_in_dim | solution.py:138
  (2 shorter events, 0.1 us)
Async XLA Ops:
  0.0 8.5 %collective-permute-start.2 = (bf16[64,4096]{1,0:T(8,128)(2,1)}, bf16[64,4096]{1,0:T(8,128)(2,1)S(1)}, u32[]{:S(2)}, u32[]{:S(2)}) collective-permute-start(bf16[64,4096]{1,0:T(8,128)(2,1)} %bitcast.45), channel_id=1, source_target_pairs={{0,1},{1,0},{2,3},{3,2},{4,5},{5,4},{6,7},{7,6},{8,9},{9,8},{10,11... | collective-permute-start | bytes 1572872 | tf_op jit(solution)/shard_map/ppermute | solution.py:88
  3.7 5.1 %copy-start = (bf16[64,1,4096]{2,0,1:T(8,128)(2,1)S(1)}, bf16[64,1,4096]{2,0,1:T(8,128)(2,1)}, u32[]{:S(2)}) copy-start(bf16[64,1,4096]{2,0,1:T(8,128)(2,1)} %param.12) | copy-start | bytes 1572868
  3.7 1.2 %collective-permute-start = (bf16[1,4096]{1,0:T(2,128)(2,1)S(1)}, bf16[1,4096]{1,0:T(2,128)(2,1)S(1)}, u32[]{:S(2)}, u32[]{:S(2)}) collective-permute-start(bf16[1,4096]{1,0:T(2,128)(2,1)S(1)} %shard_map.82), channel_id=1, source_target_pairs={{0,1},{1,0},{2,3},{3,2},{4,5},{5,4},{6,7},{7,6},{8,9},{9,8},{10,11... | collective-permute-start | bytes 24584 | tf_op jit(solution)/shard_map/ppermute | solution.py:88
  5.0 3.5 %collective-permute-start.4 = (bf16[2,4096]{1,0:T(2,128)(2,1)S(1)}, bf16[2,4096]{1,0:T(2,128)(2,1)S(1)}, u32[]{:S(2)}, u32[]{:S(2)}) collective-permute-start(bf16[2,4096]{1,0:T(2,128)(2,1)S(1)} %pad_maximum_fusion.rows), channel_id=1, source_target_pairs={{12,0},{5,1},{10,2},{9,5},{2,6},{15,7},{0,8},{13,9},{6,10},{8,12},... | collective-permute-start | bytes 49160 | tf_op jit(solution)/shard_map/ppermute | solution.py:102
  7.3 5.0 %collective-permute-start.1 = (bf16[2,4096]{1,0:T(2,128)(2,1)S(1)}, bf16[2,4096]{1,0:T(2,128)(2,1)S(1)}, u32[]{:S(2)}, u32[]{:S(2)}) collective-permute-start(bf16[2,4096]{1,0:T(2,128)(2,1)S(1)} %pad_maximum_fusion.rows), channel_id=1, source_target_pairs={{8,0},{6,2},{15,3},{0,4},{13,5},{10,6},{4,8},{14,10},{3,11},{5,13}... | collective-permute-start | bytes 49160 | tf_op jit(solution)/shard_map/ppermute | solution.py:102
  9.0 5.2 %collective-permute-start.5 = (f32[64]{0:T(128)S(1)}, f32[64]{0:T(128)S(1)}, u32[]{:S(2)}, u32[]{:S(2)}) collective-permute-start(f32[64]{0:T(128)S(1)} %fusion), channel_id=1, source_target_pairs={{0,12},{1,4},{2,8},{3,0},{4,5},{5,9},{6,1},{7,13},{8,2},{9,14},{10... | collective-permute-start | bytes 776 | tf_op jit(solution)/shard_map/ppermute | solution.py:108
  12.8 4.2 %collective-permute-start.3 = (f32[64]{0:T(128)S(1)}, f32[64]{0:T(128)S(1)}, u32[]{:S(2)}, u32[]{:S(2)}) collective-permute-start(f32[64]{0:T(128)S(1)} %fusion.1), channel_id=1, source_target_pairs={{0,8},{1,0},{2,4},{3,12},{4,1},{5,13},{6,9},{7,5},{8,6},{9,10},{10... | collective-permute-start | bytes 776 | tf_op jit(solution)/shard_map/ppermute | solution.py:108

commit v18 on v16

--- a/solution.py
+++ b/solution.py
@@ -45,18 +45,16 @@
         out_coords, in_coords, (((0,), (0,)), ((), ())), preferred_element_type=jnp.float32
     )
     half = rank // 2
-    rows = jnp.concatenate([kron_v[pl.ds(i, half, stride=2), :] for i in range(2)], axis=1)
-    for i in range(half):
-        out[:, pl.ds(i * rows.shape[1], rows.shape[1])] = rows[i : i + 1].astype(out.dtype)
+    out[...] = jnp.concatenate([kron_v[pl.ds(i, half, stride=2), :] for i in range(2)], axis=1)
 
 
 def pair_gradient(acts_in, grads_out, proj_in, proj_out, lengths):
     _, sides, seq_len, _, model_width = acts_in.shape
     rank = proj_in.shape[2]
     tokens = sides * seq_len
-    return pl.pallas_call(
+    rows = pl.pallas_call(
         functools.partial(pair_kernel, seq_len),
-        out_shape=jax.ShapeDtypeStruct((1, rank * rank), jnp.bfloat16),
+        out_shape=jax.ShapeDtypeStruct((rank // 2, 2 * rank), jnp.float32),
         in_specs=[pl.BlockSpec(memory_space=pl.ANY)] * 5,
         out_specs=pl.BlockSpec(memory_space=pltpu.VMEM),
         scratch_shapes=[
@@ -85,6 +83,7 @@
             )
         )
     )
+    return lax.optimization_barrier(rows.reshape(1, rank * rank))
 
 
 def swap(x):
@@ -118,7 +117,7 @@
 
 def shared_scores(own_row, own_block, margin, labels, scale):
     blocks = own_block, swap(own_block)
-    rows = jnp.concatenate([own_row, swap(own_row)], axis=0)
+    rows = jnp.concatenate([own_row, swap(own_row)], axis=0).astype(jnp.bfloat16)
     first, second = fetch_pair(rows, FIRST), fetch_pair(rows, SECOND)
     factor = pl.pallas_call(
         functools.partial(factor_kernel, scale),
@@ -166,7 +165,7 @@
     if one_each and dp_size == layer_size == len(FIRST):
         return shared_scores(grad_rows, block, margin, labels, scale)
     factor = jax.nn.sigmoid(-margin) * jnp.where(labels == 0, 1.0, -1.0) / scale
-    rows = lax.all_gather(grad_rows, "dp", axis=0, tiled=True)
+    rows = lax.all_gather(grad_rows.astype(jnp.bfloat16), "dp", axis=0, tiled=True)
     scores = jnp.einsum("pk,qk->pq", rows, block, preferred_element_type=jnp.float32)
     scores = lax.all_to_all(scores, "dp", split_axis=0, concat_axis=1, tiled=True)
     summed = lax.psum_scatter(scores, "layer", scatter_dimension=1, tiled=True)

time: 17.6 us -> 17.7 us (level)
  no operation moved by 1% of the time
where the time goes in v18:
time: 17.7 us; the launch traced here: 17.5 us
  starting transfers between devices  7.6 us (43%)
  waiting for transfers between devices  4.06 us (23%)
  Pallas kernels  2.91 us (16%)
  between operations  1.36 us (8%)
  matrix products  0.99 us (6%)
  other arithmetic  0.57 us (3%)
    ppermute x2, starting transfers between devices, fetch_pair(): return lax.ppermute(x, ('dp', 'layer'), moves + list(fill))  3.51 us
    ppermute x2, starting transfers between devices, to_owner(): return lax.ppermute(x, ('dp', 'layer'), moves)  3.34 us
    pallas_call x1, Pallas kernels, pair_gradient(): pl.pallas_call(functools.partial(pair_kernel, seq_len), out_shape=jax.Sha...  2.9 us
    ppermute x2, waiting for transfers between devices, to_owner(): return lax.ppermute(x, ('dp', 'layer'), moves)  2.86 us
    ppermute x2, waiting for transfers between devices, swap(): lax.ppermute(x, 'layer', [(i, i ^ 1) for i in range(lax.axis_size('layer'...  1.17 us
    dot_general x4, matrix products, score(): jnp.einsum('k,qk->q', jnp.where(is_own, mine, row), block, preferred_elem...  0.99 us
    ppermute x2, starting transfers between devices, swap(): lax.ppermute(x, 'layer', [(i, i ^ 1) for i in range(lax.axis_size('layer'...  0.75 us
    broadcast_in_dim x1, other arithmetic, shared_scores(): return ((first + second) * factor)[None]  0.51 us
  transfers between devices with their start and end apart: 6, of which 2 were waited for; matrix products, arithmetic and copies ran while one was open for 6% of the time, Pallas kernels for 17%

profile of v18, /device:TPU:11, one launch (start us, length us, event | category | flops | bytes accessed | tf_op | source)
XLA Modules:
  0.0 17.5 jit_solution(3428024849347929759)
XLA Ops:
  0.0 0.7 %collective-permute-start.2 = (bf16[64,4096]{1,0:T(8,128)(2,1)}, bf16[64,4096]{1,0:T(8,128)(2,1)S(1)}, u32[]{:S(2)}, u32[]{:S(2)}) collective-permute-start(bf16[64,4096]{1,0:T(8,128)(2,1)} %bitcast.49), channel_id=1, source_target_pairs={{0,1},{1,0},{2,3},{3,2},{4,5},{5,4},{6,7},{7,6},{8,9},{9,8},{10,11... | collective-permute-start | bytes 1572872 | tf_op jit(solution)/shard_map/ppermute | solution.py:90
  0.7 2.9 %shard_map.82 = f32[32,128]{1,0:T(8,128)S(1)} custom-call(bf16[128,4096]{1,0:T(8,128)(2,1)} %bitcast.45, bf16[128,4096]{1,0:T(8,128)(2,1)} %bitcast.46, bf16[64,4096]{1,0:T(8,128)(2,1)} %bitcast.47, bf16[64,4096]{1,0:T(8,128)(2,1)} %bitcast.48, s32[1,2]{1,0:T(1,128)} %lengths.1), custom_call_target="tpu_custom_call" | custom-call | flops 134217728 | bytes 3145728 | tf_op jit(solution)/shard_map/pallas_call | solution.py:55
  3.6 0.0 copy-start
  3.6 0.1 collective-permute-start
  3.7 1.2 %collective-permute-done = bf16[1,4096]{1,0:T(2,128)(2,1)S(1)} collective-permute-done((bf16[1,4096]{1,0:T(2,128)(2,1)S(1)}, bf16[1,4096]{1,0:T(2,128)(2,1)S(1)}, u32[]{:S(2)}, u32[]{:S(2)}) %collective-permute-start) | collective-permute-done | bytes 8224 | tf_op jit(solution)/shard_map/ppermute | solution.py:90
  4.9 2.4 %collective-permute-start.4 = (bf16[2,4096]{1,0:T(2,128)(2,1)S(1)}, bf16[2,4096]{1,0:T(2,128)(2,1)S(1)}, u32[]{:S(2)}, u32[]{:S(2)}) collective-permute-start(bf16[2,4096]{1,0:T(2,128)(2,1)S(1)} %pad_maximum_fusion.rows), channel_id=1, source_target_pairs={{12,0},{5,1},{10,2},{9,5},{2,6},{15,7},{0,8},{13,9},{6,10},{8,12},... | collective-permute-start | bytes 49160 | tf_op jit(solution)/shard_map/ppermute | solution.py:104
  7.3 1.2 %collective-permute-start.1 = (bf16[2,4096]{1,0:T(2,128)(2,1)S(1)}, bf16[2,4096]{1,0:T(2,128)(2,1)S(1)}, u32[]{:S(2)}, u32[]{:S(2)}) collective-permute-start(bf16[2,4096]{1,0:T(2,128)(2,1)S(1)} %pad_maximum_fusion.rows), channel_id=1, source_target_pairs={{8,0},{6,2},{15,3},{0,4},{13,5},{10,6},{4,8},{14,10},{3,11},{5,13}... | collective-permute-start | bytes 49160 | tf_op jit(solution)/shard_map/ppermute | solution.py:104
  8.4 0.0 collective-permute-done.4
  8.5 0.0 collective-permute-done.2
  8.5 0.2 %convolution_bitcast_fusion = f32[64]{0:T(128)S(1)} fusion(bf16[64,4096]{1,0:T(8,128)(2,1)S(1)} %collective-permute-done.2, pred[]{:T(512)S(6)} %or.23, bf16[2,4096]{1,0:T(2,128)(2,1)S(1)} %collective-permute-done.4, bf16[1,4096]{1,0:T(2,128)(2,1)S(1)} %collective-permute-done), kind=kOutput, calls=%fused_computation | convolution fusion | flops 528384 | bytes 549121 | tf_op jit(solution)/shard_map/k,qk->q/dot_general | solution.py:135
  8.7 0.0 copy-done
  8.7 0.3 %fusion = f32[64]{0:T(128)S(1)} fusion(f32[64]{0:T(128)S(1)} %convolution_bitcast_fusion, pred[]{:T(512)S(6)} %or.23, bf16[2,4096]{1,0:T(2,128)(2,1)S(1)} %collective-permute-done.4, bf16[64,1,4096]{2,0,1:T(8,128)(2,1)S(1)} %copy-done, f32[1,4096]{1,0:T(1,128)S(1)} %bitcast.43), kind=kOutput, calls=%fused_computation.2 | convolution fusion | flops 532544 | bytes 557569 | tf_op jit(solution)/shard_map/k,qk->q/dot_general | solution.py:135
  9.0 3.3 %collective-permute-start.5 = (f32[64]{0:T(128)S(1)}, f32[64]{0:T(128)S(1)}, u32[]{:S(2)}, u32[]{:S(2)}) collective-permute-start(f32[64]{0:T(128)S(1)} %fusion), channel_id=1, source_target_pairs={{0,12},{1,4},{2,8},{3,0},{4,5},{5,9},{6,1},{7,13},{8,2},{9,14},{10... | collective-permute-start | bytes 776 | tf_op jit(solution)/shard_map/ppermute | solution.py:110
  12.3 0.0 collective-permute-done.1
  12.3 0.2 %convolution_bitcast_fusion.2 = f32[64]{0:T(128)S(1)} fusion(bf16[64,4096]{1,0:T(8,128)(2,1)S(1)} %collective-permute-done.2, pred[]{:T(512)S(6)} %or.20, bf16[2,4096]{1,0:T(2,128)(2,1)S(1)} %collective-permute-done.1, bf16[1,4096]{1,0:T(2,128)(2,1)S(1)} %collective-permute-done), kind=kOutput, calls=%fused_computation.3 | convolution fusion | flops 528384 | bytes 549121 | tf_op jit(solution)/shard_map/k,qk->q/dot_general | solution.py:135
  12.5 0.3 %fusion.1 = f32[64]{0:T(128)S(1)} fusion(f32[64]{0:T(128)S(1)} %convolution_bitcast_fusion.2, pred[]{:T(512)S(6)} %or.20, bf16[2,4096]{1,0:T(2,128)(2,1)S(1)} %collective-permute-done.1, bf16[64,1,4096]{2,0,1:T(8,128)(2,1)S(1)} %copy-done, f32[1,4096]{1,0:T(1,128)S(1)} %bitcast.44), kind=kOutput, calls=%fused_computation.5 | convolution fusion | flops 532544 | bytes 557569 | tf_op jit(solution)/shard_map/k,qk->q/dot_general | solution.py:135
  12.8 0.0 collective-permute-start.3
  14.1 0.0 collective-permute-done.5
  14.1 2.9 %collective-permute-done.3 = f32[64]{0:T(128)S(1)} collective-permute-done((f32[64]{0:T(128)S(1)}, f32[64]{0:T(128)S(1)}, u32[]{:S(2)}, u32[]{:S(2)}) %collective-permute-start.3) | collective-permute-done | bytes 288 | tf_op jit(solution)/shard_map/ppermute | solution.py:110
  17.0 0.5 %multiply_bitcast_fusion = f32[1,64]{1,0:T(1,128)} fusion(f32[64]{0:T(128)S(1)} %shard_map.83, f32[64]{0:T(128)S(1)} %collective-permute-done.3, f32[64]{0:T(128)S(1)} %collective-permute-done.5), kind=kLoop, calls=%fused_computation.19 | loop fusion | flops 128 | bytes 1024 | tf_op jit(solution)/shard_map/broadcast_in_dim | solution.py:140
  (3 shorter events, 0.1 us)
Async XLA Ops:
  0.0 8.5 %collective-permute-start.2 = (bf16[64,4096]{1,0:T(8,128)(2,1)}, bf16[64,4096]{1,0:T(8,128)(2,1)S(1)}, u32[]{:S(2)}, u32[]{:S(2)}) collective-permute-start(bf16[64,4096]{1,0:T(8,128)(2,1)} %bitcast.49), channel_id=1, source_target_pairs={{0,1},{1,0},{2,3},{3,2},{4,5},{5,4},{6,7},{7,6},{8,9},{9,8},{10,11... | collective-permute-start | bytes 1572872 | tf_op jit(solution)/shard_map/ppermute | solution.py:90
  3.6 5.1 %copy-start = (bf16[64,1,4096]{2,0,1:T(8,128)(2,1)S(1)}, bf16[64,1,4096]{2,0,1:T(8,128)(2,1)}, u32[]{:S(2)}) copy-start(bf16[64,1,4096]{2,0,1:T(8,128)(2,1)} %param.12) | copy-start | bytes 1572868
  3.6 1.2 %collective-permute-start = (bf16[1,4096]{1,0:T(2,128)(2,1)S(1)}, bf16[1,4096]{1,0:T(2,128)(2,1)S(1)}, u32[]{:S(2)}, u32[]{:S(2)}) collective-permute-start(bf16[1,4096]{1,0:T(2,128)(2,1)S(1)} %unstack.71), channel_id=1, source_target_pairs={{0,1},{1,0},{2,3},{3,2},{4,5},{5,4},{6,7},{7,6},{8,9},{9,8},{10,11... | collective-permute-start | bytes 24584 | tf_op jit(solution)/shard_map/ppermute | solution.py:90
  4.9 3.5 %collective-permute-start.4 = (bf16[2,4096]{1,0:T(2,128)(2,1)S(1)}, bf16[2,4096]{1,0:T(2,128)(2,1)S(1)}, u32[]{:S(2)}, u32[]{:S(2)}) collective-permute-start(bf16[2,4096]{1,0:T(2,128)(2,1)S(1)} %pad_maximum_fusion.rows), channel_id=1, source_target_pairs={{12,0},{5,1},{10,2},{9,5},{2,6},{15,7},{0,8},{13,9},{6,10},{8,12},... | collective-permute-start | bytes 49160 | tf_op jit(solution)/shard_map/ppermute | solution.py:104
  7.3 5.0 %collective-permute-start.1 = (bf16[2,4096]{1,0:T(2,128)(2,1)S(1)}, bf16[2,4096]{1,0:T(2,128)(2,1)S(1)}, u32[]{:S(2)}, u32[]{:S(2)}) collective-permute-start(bf16[2,4096]{1,0:T(2,128)(2,1)S(1)} %pad_maximum_fusion.rows), channel_id=1, source_target_pairs={{8,0},{6,2},{15,3},{0,4},{13,5},{10,6},{4,8},{14,10},{3,11},{5,13}... | collective-permute-start | bytes 49160 | tf_op jit(solution)/shard_map/ppermute | solution.py:104
  9.0 5.2 %collective-permute-start.5 = (f32[64]{0:T(128)S(1)}, f32[64]{0:T(128)S(1)}, u32[]{:S(2)}, u32[]{:S(2)}) collective-permute-start(f32[64]{0:T(128)S(1)} %fusion), channel_id=1, source_target_pairs={{0,12},{1,4},{2,8},{3,0},{4,5},{5,9},{6,1},{7,13},{8,2},{9,14},{10... | collective-permute-start | bytes 776 | tf_op jit(solution)/shard_map/ppermute | solution.py:110
  12.8 4.2 %collective-permute-start.3 = (f32[64]{0:T(128)S(1)}, f32[64]{0:T(128)S(1)}, u32[]{:S(2)}, u32[]{:S(2)}) collective-permute-start(f32[64]{0:T(128)S(1)} %fusion.1), channel_id=1, source_target_pairs={{0,8},{1,0},{2,4},{3,12},{4,1},{5,13},{6,9},{7,5},{8,6},{9,10},{10... | collective-permute-start | bytes 776 | tf_op jit(solution)/shard_map/ppermute | solution.py:110

commit v19 on v18

--- a/solution.py
+++ b/solution.py
@@ -8,8 +8,12 @@
 from jax.experimental.pallas import tpu as pltpu
 from jax.sharding import PartitionSpec as P
 
-FIRST = ((2, 0, 1, 3), (0, 3, 2, 1), (1, 2, 3, 0), (3, 1, 0, 2))
-SECOND = ((3, 1, 2, 0), (1, 2, 0, 3), (0, 3, 1, 2), (2, 0, 3, 1))
+FIRST = ((1, 0, 2, 3), (0, 3, 2, 1), (3, 2, 0, 1), (2, 1, 3, 0))
+FIRST_FROM = ((0, 0, 3, 2), (1, 1, 2, 2), (0, 0, 2, 3), (1, 1, 3, 3))
+SECOND = ((2, 3, 0, 1), (1, 2, 3, 0), (0, 1, 3, 2), (3, 0, 1, 2))
+SECOND_FROM = ((0, 0, 3, 2), (1, 1, 3, 2), (0, 0, 2, 2), (1, 1, 3, 3))
+
+
 PARTS = 4
 
 
@@ -90,18 +94,11 @@
     return lax.ppermute(x, "layer", [(i, i ^ 1) for i in range(lax.axis_size("layer"))])
 
 
-def own_places(slot):
-    return [(d, i) for d, row in enumerate(slot) for i, pair in enumerate(row) if pair == d]
-
-
-def fetch_pair(x, slot):
-    count = len(slot)
-    moves = [
-        (slot[d][i] * count + i, d * count + i) for d in range(count) for i in range(count) if slot[d][i] != d
-    ]
-    own = [d * count + i for d, i in own_places(slot)]
-    fill = zip(own, own[1::-1] + own[:1:-1])
-    return lax.ppermute(x, ("dp", "layer"), moves + list(fill))
+def fetch_pair(x, pairs, senders):
+    count = len(pairs)
+    places = [(d, i) for d in range(count) for i in range(count)]
+    moves = [(pairs[d][i] * count + senders[d][i], d * count + i) for d, i in places]
+    return lax.ppermute(x, ("dp", "layer"), moves)
 
 
 def to_owner(x, slot):
@@ -118,7 +115,7 @@
 def shared_scores(own_row, own_block, margin, labels, scale):
     blocks = own_block, swap(own_block)
     rows = jnp.concatenate([own_row, swap(own_row)], axis=0).astype(jnp.bfloat16)
-    first, second = fetch_pair(rows, FIRST), fetch_pair(rows, SECOND)
+    first, second = fetch_pair(rows, FIRST, FIRST_FROM), fetch_pair(rows, SECOND, SECOND_FROM)
     factor = pl.pallas_call(
         functools.partial(factor_kernel, scale),
         out_shape=jax.ShapeDtypeStruct(own_block.shape[:1], jnp.float32),
@@ -129,15 +126,16 @@
     )(margin, labels, rows)
     here = lax.axis_index("dp") * len(FIRST) + lax.axis_index("layer")
 
-    def score(got, slot):
-        is_own = functools.reduce(jnp.logical_or, [here == d * len(slot) + i for d, i in own_places(slot)])
+    def score(got, senders):
+        crossed = [d * len(row) + i for d, row in enumerate(senders) for i, sender in enumerate(row) if sender != i]
+        is_crossed = functools.reduce(jnp.logical_or, [here == i for i in crossed])
         return sum(
-            jnp.einsum("k,qk->q", jnp.where(is_own, mine, row), block, preferred_element_type=jnp.float32)
-            for mine, row, block in zip(rows, got, blocks)
+            jnp.einsum("k,qk->q", jnp.where(is_crossed, got[1 - i], got[i]), block, preferred_element_type=jnp.float32)
+            for i, block in enumerate(blocks)
         )
 
-    first, second = to_owner(score(first, FIRST), FIRST), to_owner(score(second, SECOND), SECOND)
-    return ((first + second) * factor)[None]
+    first, second = score(first, FIRST_FROM), score(second, SECOND_FROM)
+    return ((to_owner(first, FIRST) + to_owner(second, SECOND)) * factor)[None]
 
 
 def pair_gradients(acts_in, grads_out, proj_in, proj_out, lengths):

time: 17.7 us -> 16.3 us (0.921)
  the two profiles are of different devices: /device:TPU:11 before, /device:TPU:0 now
where the time goes in v19:
time: 16.3 us; the launch traced here: 16.1 us
  starting transfers between devices  8.43 us (52%)
  Pallas kernels  2.91 us (18%)
  waiting for transfers between devices  1.78 us (11%)
  between operations  1.36 us (8%)
  matrix products  0.99 us (6%)
  other arithmetic  0.57 us (3%)
    ppermute x2, starting transfers between devices, fetch_pair(): return lax.ppermute(x, ('dp', 'layer'), moves)  4.88 us
    ppermute x2, starting transfers between devices, to_owner(): return lax.ppermute(x, ('dp', 'layer'), moves)  2.98 us
    pallas_call x1, Pallas kernels, pair_gradient(): pl.pallas_call(functools.partial(pair_kernel, seq_len), out_shape=jax.Sha...  2.9 us
    ppermute x2, waiting for transfers between devices, swap(): lax.ppermute(x, 'layer', [(i, i ^ 1) for i in range(lax.axis_size('layer'...  1.13 us
    dot_general x4, matrix products, score(): jnp.einsum('k,qk->q', jnp.where(is_crossed, got[1 - i], got[i]), block, p...  0.99 us
    ppermute x2, waiting for transfers between devices, fetch_pair(): return lax.ppermute(x, ('dp', 'layer'), moves)  0.65 us
    ppermute x2, starting transfers between devices, swap(): lax.ppermute(x, 'layer', [(i, i ^ 1) for i in range(lax.axis_size('layer'...  0.57 us
    broadcast_in_dim x1, other arithmetic, shared_scores(): return ((to_owner(first, FIRST) + to_owner(second, SECOND)) * factor)[None]  0.52 us
  transfers between devices with their start and end apart: 6, of which 2 were waited for; matrix products, arithmetic and copies ran while one was open for 7% of the time, Pallas kernels for 18%

profile of v19, /device:TPU:0, one launch (start us, length us, event | category | flops | bytes accessed | tf_op | source)
XLA Modules:
  0.0 16.1 jit_solution(7473760986239220270)
XLA Ops:
  0.0 0.5 %collective-permute-start.2 = (bf16[64,4096]{1,0:T(8,128)(2,1)}, bf16[64,4096]{1,0:T(8,128)(2,1)S(1)}, u32[]{:S(2)}, u32[]{:S(2)}) collective-permute-start(bf16[64,4096]{1,0:T(8,128)(2,1)} %bitcast.47), channel_id=1, source_target_pairs={{0,1},{1,0},{2,3},{3,2},{4,5},{5,4},{6,7},{7,6},{8,9},{9,8},{10,11... | collective-permute-start | bytes 1572872 | tf_op jit(solution)/shard_map/ppermute | solution.py:94
  0.5 2.9 %shard_map.82 = f32[32,128]{1,0:T(8,128)S(1)} custom-call(bf16[128,4096]{1,0:T(8,128)(2,1)} %bitcast.43, bf16[128,4096]{1,0:T(8,128)(2,1)} %bitcast.44, bf16[64,4096]{1,0:T(8,128)(2,1)} %bitcast.45, bf16[64,4096]{1,0:T(8,128)(2,1)} %bitcast.46, s32[1,2]{1,0:T(1,128)} %lengths.1), custom_call_target="tpu_custom_call" | custom-call | flops 134217728 | bytes 3145728 | tf_op jit(solution)/shard_map/pallas_call | solution.py:59
  3.4 0.0 copy-start
  3.4 0.1 collective-permute-start
  3.5 1.1 %collective-permute-done = bf16[1,4096]{1,0:T(2,128)(2,1)S(1)} collective-permute-done((bf16[1,4096]{1,0:T(2,128)(2,1)S(1)}, bf16[1,4096]{1,0:T(2,128)(2,1)S(1)}, u32[]{:S(2)}, u32[]{:S(2)}) %collective-permute-start) | collective-permute-done | bytes 8224 | tf_op jit(solution)/shard_map/ppermute | solution.py:94
  4.7 3.8 %collective-permute-start.4 = (bf16[2,4096]{1,0:T(2,128)(2,1)S(1)}, bf16[2,4096]{1,0:T(2,128)(2,1)S(1)}, u32[]{:S(2)}, u32[]{:S(2)}) collective-permute-start(bf16[2,4096]{1,0:T(2,128)(2,1)S(1)} %pad_maximum_fusion.rows), channel_id=1, source_target_pairs={{8,0},{12,1},{3,2},{6,3},{5,4},{9,5},{15,6},{2,7},{0,8},{4,9},{14,... | collective-permute-start | bytes 49160 | tf_op jit(solution)/shard_map/ppermute | solution.py:101
  8.5 1.1 %collective-permute-start.1 = (bf16[2,4096]{1,0:T(2,128)(2,1)S(1)}, bf16[2,4096]{1,0:T(2,128)(2,1)S(1)}, u32[]{:S(2)}, u32[]{:S(2)}) collective-permute-start(bf16[2,4096]{1,0:T(2,128)(2,1)S(1)} %pad_maximum_fusion.rows), channel_id=1, source_target_pairs={{4,0},{0,1},{11,2},{14,3},{1,4},{13,5},{10,6},{6,7},{12,8},{8,9},{... | collective-permute-start | bytes 49160 | tf_op jit(solution)/shard_map/ppermute | solution.py:101
  9.6 0.6 %collective-permute-done.4 = bf16[2,4096]{1,0:T(2,128)(2,1)S(1)} collective-permute-done((bf16[2,4096]{1,0:T(2,128)(2,1)S(1)}, bf16[2,4096]{1,0:T(2,128)(2,1)S(1)}, u32[]{:S(2)}, u32[]{:S(2)}) %collective-permute-start.4) | collective-permute-done | bytes 16416 | tf_op jit(solution)/shard_map/ppermute | solution.py:101
  10.2 0.0 collective-permute-done.2
  10.2 0.2 %convolution_bitcast_fusion = f32[64]{0:T(128)S(1)} fusion(bf16[64,4096]{1,0:T(8,128)(2,1)S(1)} %collective-permute-done.2, pred[]{:T(512)S(6)} %or.54, bf16[2,4096]{1,0:T(2,128)(2,1)S(1)} %collective-permute-done.4), kind=kOutput, calls=%fused_computation | convolution fusion | flops 528384 | bytes 557313 | tf_op jit(solution)/shard_map/k,qk->q/dot_general | solution.py:133
  10.5 0.0 copy-done
  10.5 0.3 %fusion = f32[64]{0:T(128)S(1)} fusion(f32[64]{0:T(128)S(1)} %convolution_bitcast_fusion, pred[]{:T(512)S(6)} %or.54, bf16[2,4096]{1,0:T(2,128)(2,1)S(1)} %collective-permute-done.4, bf16[64,1,4096]{2,0,1:T(8,128)(2,1)S(1)} %copy-done), kind=kOutput, calls=%fused_computation.2 | convolution fusion | flops 528448 | bytes 557825 | tf_op jit(solution)/shard_map/k,qk->q/dot_general | solution.py:133
  10.7 2.9 %collective-permute-start.5 = (f32[64]{0:T(128)S(1)}, f32[64]{0:T(128)S(1)}, u32[]{:S(2)}, u32[]{:S(2)}) collective-permute-start(f32[64]{0:T(128)S(1)} %fusion), channel_id=1, source_target_pairs={{0,8},{1,12},{2,0},{3,4},{4,5},{5,9},{6,13},{7,1},{8,2},{9,6},{10,... | collective-permute-start | bytes 776 | tf_op jit(solution)/shard_map/ppermute | solution.py:107
  13.7 0.0 collective-permute-done.1
  13.7 0.2 %convolution_bitcast_fusion.2 = f32[64]{0:T(128)S(1)} fusion(bf16[64,4096]{1,0:T(8,128)(2,1)S(1)} %collective-permute-done.2, pred[]{:T(512)S(6)} %or.48, bf16[2,4096]{1,0:T(2,128)(2,1)S(1)} %collective-permute-done.1), kind=kOutput, calls=%fused_computation.3 | convolution fusion | flops 528384 | bytes 557313 | tf_op jit(solution)/shard_map/k,qk->q/dot_general | solution.py:133
  13.9 0.3 %fusion.1 = f32[64]{0:T(128)S(1)} fusion(f32[64]{0:T(128)S(1)} %convolution_bitcast_fusion.2, pred[]{:T(512)S(6)} %or.48, bf16[2,4096]{1,0:T(2,128)(2,1)S(1)} %collective-permute-done.1, bf16[64,1,4096]{2,0,1:T(8,128)(2,1)S(1)} %copy-done), kind=kOutput, calls=%fused_computation.5 | convolution fusion | flops 528448 | bytes 557825 | tf_op jit(solution)/shard_map/k,qk->q/dot_general | solution.py:133
  14.2 0.0 collective-permute-start.3
  15.5 0.0 collective-permute-done.5
  15.5 0.0 collective-permute-done.3
  15.5 0.5 %multiply_bitcast_fusion = f32[1,64]{1,0:T(1,128)} fusion(f32[64]{0:T(128)S(1)} %shard_map.83, f32[64]{0:T(128)S(1)} %collective-permute-done.3, f32[64]{0:T(128)S(1)} %collective-permute-done.5), kind=kLoop, calls=%fused_computation.23 | loop fusion | flops 128 | bytes 1024 | tf_op jit(solution)/shard_map/broadcast_in_dim | solution.py:138
  (3 shorter events, 0.1 us)
Async XLA Ops:
  0.0 10.2 %collective-permute-start.2 = (bf16[64,4096]{1,0:T(8,128)(2,1)}, bf16[64,4096]{1,0:T(8,128)(2,1)S(1)}, u32[]{:S(2)}, u32[]{:S(2)}) collective-permute-start(bf16[64,4096]{1,0:T(8,128)(2,1)} %bitcast.47), channel_id=1, source_target_pairs={{0,1},{1,0},{2,3},{3,2},{4,5},{5,4},{6,7},{7,6},{8,9},{9,8},{10,11... | collective-permute-start | bytes 1572872 | tf_op jit(solution)/shard_map/ppermute | solution.py:94
  3.4 7.1 %copy-start = (bf16[64,1,4096]{2,0,1:T(8,128)(2,1)S(1)}, bf16[64,1,4096]{2,0,1:T(8,128)(2,1)}, u32[]{:S(2)}) copy-start(bf16[64,1,4096]{2,0,1:T(8,128)(2,1)} %param.12) | copy-start | bytes 1572868
  3.4 1.2 %collective-permute-start = (bf16[1,4096]{1,0:T(2,128)(2,1)S(1)}, bf16[1,4096]{1,0:T(2,128)(2,1)S(1)}, u32[]{:S(2)}, u32[]{:S(2)}) collective-permute-start(bf16[1,4096]{1,0:T(2,128)(2,1)S(1)} %convert.11), channel_id=1, source_target_pairs={{0,1},{1,0},{2,3},{3,2},{4,5},{5,4},{6,7},{7,6},{8,9},{9,8},{10,11... | collective-permute-start | bytes 24584 | tf_op jit(solution)/shard_map/ppermute | solution.py:94
  4.7 5.5 %collective-permute-start.4 = (bf16[2,4096]{1,0:T(2,128)(2,1)S(1)}, bf16[2,4096]{1,0:T(2,128)(2,1)S(1)}, u32[]{:S(2)}, u32[]{:S(2)}) collective-permute-start(bf16[2,4096]{1,0:T(2,128)(2,1)S(1)} %pad_maximum_fusion.rows), channel_id=1, source_target_pairs={{8,0},{12,1},{3,2},{6,3},{5,4},{9,5},{15,6},{2,7},{0,8},{4,9},{14,... | collective-permute-start | bytes 49160 | tf_op jit(solution)/shard_map/ppermute | solution.py:101
  8.5 5.2 %collective-permute-start.1 = (bf16[2,4096]{1,0:T(2,128)(2,1)S(1)}, bf16[2,4096]{1,0:T(2,128)(2,1)S(1)}, u32[]{:S(2)}, u32[]{:S(2)}) collective-permute-start(bf16[2,4096]{1,0:T(2,128)(2,1)S(1)} %pad_maximum_fusion.rows), channel_id=1, source_target_pairs={{4,0},{0,1},{11,2},{14,3},{1,4},{13,5},{10,6},{6,7},{12,8},{8,9},{... | collective-permute-start | bytes 49160 | tf_op jit(solution)/shard_map/ppermute | solution.py:101
  10.7 4.8 %collective-permute-start.5 = (f32[64]{0:T(128)S(1)}, f32[64]{0:T(128)S(1)}, u32[]{:S(2)}, u32[]{:S(2)}) collective-permute-start(f32[64]{0:T(128)S(1)} %fusion), channel_id=1, source_target_pairs={{0,8},{1,12},{2,0},{3,4},{4,5},{5,9},{6,13},{7,1},{8,2},{9,6},{10,... | collective-permute-start | bytes 776 | tf_op jit(solution)/shard_map/ppermute | solution.py:107
  14.2 1.4 %collective-permute-start.3 = (f32[64]{0:T(128)S(1)}, f32[64]{0:T(128)S(1)}, u32[]{:S(2)}, u32[]{:S(2)}) collective-permute-start(f32[64]{0:T(128)S(1)} %fusion.1), channel_id=1, source_target_pairs={{0,4},{1,0},{2,8},{3,12},{4,1},{5,13},{6,9},{7,5},{8,14},{9,10},{1... | collective-permute-start | bytes 776 | tf_op jit(solution)/shard_map/ppermute | solution.py:107

commit v20 on v19

--- a/solution.py
+++ b/solution.py
@@ -8,10 +8,10 @@
 from jax.experimental.pallas import tpu as pltpu
 from jax.sharding import PartitionSpec as P
 
-FIRST = ((1, 0, 2, 3), (0, 3, 2, 1), (3, 2, 0, 1), (2, 1, 3, 0))
-FIRST_FROM = ((0, 0, 3, 2), (1, 1, 2, 2), (0, 0, 2, 3), (1, 1, 3, 3))
-SECOND = ((2, 3, 0, 1), (1, 2, 3, 0), (0, 1, 3, 2), (3, 0, 1, 2))
-SECOND_FROM = ((0, 0, 3, 2), (1, 1, 3, 2), (0, 0, 2, 2), (1, 1, 3, 3))
+FIRST = ((3, 0, 1, 2), (0, 2, 3, 1), (3, 1, 0, 2), (2, 1, 3, 0))
+FIRST_FROM = ((1, 0, 3, 3), (1, 0, 2, 2), (0, 0, 2, 2), (1, 1, 3, 3))
+SECOND = ((1, 2, 3, 0), (1, 3, 2, 0), (2, 0, 3, 1), (3, 0, 1, 2))
+SECOND_FROM = ((0, 0, 2, 2), (1, 0, 2, 3), (1, 0, 3, 2), (1, 1, 3, 3))
 
 
 PARTS = 4
@@ -40,11 +40,13 @@
     width = model_width // PARTS
     for c in range(PARTS):
         turned_v[pl.ds(c * width, width), :] = proj_v[:, pl.ds(c * width, width)].T
-    for copy in loads[2:]:
+    coords = []
+    for half, copy in enumerate(loads[2:]):
         copy.wait()
-    coords = jnp.dot(tokens_v[...], turned_v[...], preferred_element_type=jnp.float32)
-    in_coords = (coords[:tokens, :rank] * weight).astype(jnp.bfloat16)
-    out_coords = coords[tokens:, rank:].astype(jnp.bfloat16)
+        part = tokens_v[pl.ds(half * tokens, tokens), :]
+        coords.append(jnp.dot(part, turned_v[...], preferred_element_type=jnp.float32))
+    in_coords = (coords[0][:, :rank] * weight).astype(jnp.bfloat16)
+    out_coords = coords[1][:, rank:].astype(jnp.bfloat16)
     kron_v[...] = lax.dot_general(
         out_coords, in_coords, (((0,), (0,)), ((), ())), preferred_element_type=jnp.float32
     )
@@ -107,23 +109,23 @@
     return lax.ppermute(x, ("dp", "layer"), moves)
 
 
-def factor_kernel(scale, margin, label, rows, factor):
-    sign = jnp.where(label[0] == 0, 1.0, -1.0)
-    factor[...] = sign / ((1.0 + jnp.exp(jnp.full(factor.shape, margin[0], jnp.float32))) * scale)
+def sign_kernel(scale, label, rows, factor):
+    factor[...] = jnp.full(factor.shape, jnp.where(label[0] == 0, 1.0, -1.0) / scale, jnp.float32)
 
 
 def shared_scores(own_row, own_block, margin, labels, scale):
     blocks = own_block, swap(own_block)
-    rows = jnp.concatenate([own_row, swap(own_row)], axis=0).astype(jnp.bfloat16)
+    rows = jnp.concatenate([own_row, swap(own_row)], axis=0) * jax.nn.sigmoid(-margin)[:, None]
+    rows = rows.astype(jnp.bfloat16)
     first, second = fetch_pair(rows, FIRST, FIRST_FROM), fetch_pair(rows, SECOND, SECOND_FROM)
     factor = pl.pallas_call(
-        functools.partial(factor_kernel, scale),
+        functools.partial(sign_kernel, scale),
         out_shape=jax.ShapeDtypeStruct(own_block.shape[:1], jnp.float32),
-        in_specs=[pl.BlockSpec(memory_space=pltpu.SMEM)] * 2 + [pl.BlockSpec(memory_space=pl.ANY)],
+        in_specs=[pl.BlockSpec(memory_space=pltpu.SMEM), pl.BlockSpec(memory_space=pl.ANY)],
         out_specs=pl.BlockSpec(memory_space=pltpu.VMEM),
         compiler_params=pltpu.CompilerParams(vmem_limit_bytes=1024 * 1024),
         cost_estimate=pl.CostEstimate(flops=0, bytes_accessed=4 * own_block.shape[0], transcendentals=0),
-    )(margin, labels, rows)
+    )(labels, rows)
     here = lax.axis_index("dp") * len(FIRST) + lax.axis_index("layer")
 
     def score(got, senders):

time: 16.3 us -> 16.7 us (1.025)
  waiting for transfers between devices: 1.78 us -> 4.28 us
  starting transfers between devices: 8.43 us -> 6.18 us
    ppermute x2, waiting for transfers between devices: 0.65 us -> 3.29 us  [fetch_pair(): return lax.ppermute(x, ('dp', 'layer'), moves)]
    ppermute x2, starting transfers between devices: 2.98 us -> 0.72 us  [to_owner(): return lax.ppermute(x, ('dp', 'layer'), moves)]
    ppermute x2, waiting for transfers between devices: 1.13 us -> 0.36 us  [swap(): lax.ppermute(x, 'layer', [(i, i ^ 1) for i in range(lax.axis_size('layer'...]
    ppermute x2, waiting for transfers between devices: 0.01 us -> 0.62 us  [to_owner(): return lax.ppermute(x, ('dp', 'layer'), moves)]
  transfers between devices with their start and end apart: 6 -> 6, of which waited for: 2 -> 4; matrix products, arithmetic and copies ran while one was open for 7% -> 6% of each run, Pallas kernels for 18% -> 18%
where the time goes in v20:
time: 16.7 us; the launch traced here: 16.5 us
  starting transfers between devices  6.18 us (37%)
  waiting for transfers between devices  4.28 us (26%)
  Pallas kernels  3.04 us (18%)
  between operations  1.47 us (9%)
  matrix products  0.99 us (6%)
  other arithmetic  0.55 us (3%)
    ppermute x2, starting transfers between devices, fetch_pair(): return lax.ppermute(x, ('dp', 'layer'), moves)  4.89 us
    ppermute x2, waiting for transfers between devices, fetch_pair(): return lax.ppermute(x, ('dp', 'layer'), moves)  3.29 us
    pallas_call x1, Pallas kernels, pair_gradient(): pl.pallas_call(functools.partial(pair_kernel, seq_len), out_shape=jax.Sha...  3.04 us
    dot_general x4, matrix products, score(): jnp.einsum('k,qk->q', jnp.where(is_crossed, got[1 - i], got[i]), block, p...  0.99 us
    ppermute x2, starting transfers between devices, to_owner(): return lax.ppermute(x, ('dp', 'layer'), moves)  0.72 us
    ppermute x2, waiting for transfers between devices, to_owner(): return lax.ppermute(x, ('dp', 'layer'), moves)  0.62 us
    ppermute x2, starting transfers between devices, swap(): lax.ppermute(x, 'layer', [(i, i ^ 1) for i in range(lax.axis_size('layer'...  0.58 us
    broadcast_in_dim x1, other arithmetic, shared_scores(): return ((to_owner(first, FIRST) + to_owner(second, SECOND)) * factor)[None]  0.51 us
  transfers between devices with their start and end apart: 6, of which 4 were waited for; matrix products, arithmetic and copies ran while one was open for 6% of the time, Pallas kernels for 18%

profile of v20, /device:TPU:0, one launch (start us, length us, event | category | flops | bytes accessed | tf_op | source)
XLA Modules:
  0.0 16.5 jit_solution(14333974924757925130)
XLA Ops:
  0.0 0.5 %collective-permute-start.2 = (bf16[64,4096]{1,0:T(8,128)(2,1)}, bf16[64,4096]{1,0:T(8,128)(2,1)S(1)}, u32[]{:S(2)}, u32[]{:S(2)}) collective-permute-start(bf16[64,4096]{1,0:T(8,128)(2,1)} %bitcast.49), channel_id=1, source_target_pairs={{0,1},{1,0},{2,3},{3,2},{4,5},{5,4},{6,7},{7,6},{8,9},{9,8},{10,11... | collective-permute-start | bytes 1572872 | tf_op jit(solution)/shard_map/ppermute | solution.py:96
  0.5 3.0 %shard_map.82 = f32[32,128]{1,0:T(8,128)S(1)} custom-call(bf16[128,4096]{1,0:T(8,128)(2,1)} %bitcast.45, bf16[128,4096]{1,0:T(8,128)(2,1)} %bitcast.46, bf16[64,4096]{1,0:T(8,128)(2,1)} %bitcast.47, bf16[64,4096]{1,0:T(8,128)(2,1)} %bitcast.48, s32[1,2]{1,0:T(1,128)} %lengths.1), custom_call_target="tpu_custom_call" | custom-call | flops 134217728 | bytes 3145728 | tf_op jit(solution)/shard_map/pallas_call | solution.py:61
  3.5 0.0 copy-start
  3.5 0.1 collective-permute-start
  4.4 0.4 %collective-permute-done = f32[1,4096]{1,0:T(1,128)S(1)} collective-permute-done((f32[1,4096]{1,0:T(1,128)S(1)}, f32[1,4096]{1,0:T(1,128)S(1)}, u32[]{:S(2)}, u32[]{:S(2)}) %collective-permute-start) | collective-permute-done | bytes 16416 | tf_op jit(solution)/shard_map/ppermute | solution.py:96
  4.8 3.8 %collective-permute-start.4 = (bf16[2,4096]{1,0:T(2,128)(2,1)S(1)}, bf16[2,4096]{1,0:T(2,128)(2,1)S(1)}, u32[]{:S(2)}, u32[]{:S(2)}) collective-permute-start(bf16[2,4096]{1,0:T(2,128)(2,1)S(1)} %fusion.2.rows), channel_id=1, source_target_pairs={{4,0},{8,1},{14,2},{2,3},{5,4},{12,5},{10,6},{3,7},{9,8},{0,9},{15... | collective-permute-start | bytes 49160 | tf_op jit(solution)/shard_map/ppermute | solution.py:103
  8.6 1.1 %collective-permute-start.1 = (bf16[2,4096]{1,0:T(2,128)(2,1)S(1)}, bf16[2,4096]{1,0:T(2,128)(2,1)S(1)}, u32[]{:S(2)}, u32[]{:S(2)}) collective-permute-start(bf16[2,4096]{1,0:T(2,128)(2,1)S(1)} %fusion.2.rows), channel_id=1, source_target_pairs={{13,0},{0,1},{7,2},{11,3},{1,4},{8,5},{14,6},{6,7},{12,8},{4,9},{2... | collective-permute-start | bytes 49160 | tf_op jit(solution)/shard_map/ppermute | solution.py:103
  9.7 0.3 %collective-permute-done.4 = bf16[2,4096]{1,0:T(2,128)(2,1)S(1)} collective-permute-done((bf16[2,4096]{1,0:T(2,128)(2,1)S(1)}, bf16[2,4096]{1,0:T(2,128)(2,1)S(1)}, u32[]{:S(2)}, u32[]{:S(2)}) %collective-permute-start.4) | collective-permute-done | bytes 16416 | tf_op jit(solution)/shard_map/ppermute | solution.py:103
  10.0 0.0 collective-permute-done.2
  10.0 0.2 %convolution_bitcast_fusion = f32[64]{0:T(128)S(1)} fusion(bf16[64,4096]{1,0:T(8,128)(2,1)S(1)} %collective-permute-done.2, pred[]{:T(512)S(6)} %or.71, bf16[2,4096]{1,0:T(2,128)(2,1)S(1)} %collective-permute-done.4), kind=kOutput, calls=%fused_computation | convolution fusion | flops 528384 | bytes 557313 | tf_op jit(solution)/shard_map/k,qk->q/dot_general | solution.py:135
  10.2 0.0 copy-done
  10.2 0.3 %fusion = f32[64]{0:T(128)S(1)} fusion(f32[64]{0:T(128)S(1)} %convolution_bitcast_fusion, pred[]{:T(512)S(6)} %or.71, bf16[2,4096]{1,0:T(2,128)(2,1)S(1)} %collective-permute-done.4, bf16[64,1,4096]{2,0,1:T(8,128)(2,1)S(1)} %copy-done), kind=kOutput, calls=%fused_computation.2 | convolution fusion | flops 528448 | bytes 557825 | tf_op jit(solution)/shard_map/k,qk->q/dot_general | solution.py:135
  10.5 0.0 collective-permute-start.5
  10.5 3.0 %collective-permute-done.1 = bf16[2,4096]{1,0:T(2,128)(2,1)S(1)} collective-permute-done((bf16[2,4096]{1,0:T(2,128)(2,1)S(1)}, bf16[2,4096]{1,0:T(2,128)(2,1)S(1)}, u32[]{:S(2)}, u32[]{:S(2)}) %collective-permute-start.1) | collective-permute-done | bytes 16416 | tf_op jit(solution)/shard_map/ppermute | solution.py:103
  13.5 0.2 %convolution_bitcast_fusion.2 = f32[64]{0:T(128)S(1)} fusion(bf16[64,4096]{1,0:T(8,128)(2,1)S(1)} %collective-permute-done.2, pred[]{:T(512)S(6)} %or.62, bf16[2,4096]{1,0:T(2,128)(2,1)S(1)} %collective-permute-done.1), kind=kOutput, calls=%fused_computation.3 | convolution fusion | flops 528384 | bytes 557313 | tf_op jit(solution)/shard_map/k,qk->q/dot_general | solution.py:135
  13.8 0.3 %fusion.1 = f32[64]{0:T(128)S(1)} fusion(f32[64]{0:T(128)S(1)} %convolution_bitcast_fusion.2, pred[]{:T(512)S(6)} %or.62, bf16[2,4096]{1,0:T(2,128)(2,1)S(1)} %collective-permute-done.1, bf16[64,1,4096]{2,0,1:T(8,128)(2,1)S(1)} %copy-done), kind=kOutput, calls=%fused_computation.5 | convolution fusion | flops 528448 | bytes 557825 | tf_op jit(solution)/shard_map/k,qk->q/dot_general | solution.py:135
  14.0 0.7 %collective-permute-start.3 = (f32[64]{0:T(128)S(1)}, f32[64]{0:T(128)S(1)}, u32[]{:S(2)}, u32[]{:S(2)}) collective-permute-start(f32[64]{0:T(128)S(1)} %fusion.1), channel_id=1, source_target_pairs={{0,12},{1,0},{2,4},{3,8},{4,1},{5,9},{6,13},{7,5},{8,14},{9,6},{10... | collective-permute-start | bytes 776 | tf_op jit(solution)/shard_map/ppermute | solution.py:109
  15.4 0.0 collective-permute-done.5
  15.4 0.6 %collective-permute-done.3 = f32[64]{0:T(128)S(1)} collective-permute-done((f32[64]{0:T(128)S(1)}, f32[64]{0:T(128)S(1)}, u32[]{:S(2)}, u32[]{:S(2)}) %collective-permute-start.3) | collective-permute-done | bytes 288 | tf_op jit(solution)/shard_map/ppermute | solution.py:109
  16.0 0.5 %multiply_bitcast_fusion = f32[1,64]{1,0:T(1,128)} fusion(f32[64]{0:T(128)S(1)} %shard_map.83, f32[64]{0:T(128)S(1)} %collective-permute-done.3, f32[64]{0:T(128)S(1)} %collective-permute-done.5), kind=kLoop, calls=%fused_computation.24 | loop fusion | flops 128 | bytes 1024 | tf_op jit(solution)/shard_map/broadcast_in_dim | solution.py:140
  (2 shorter events, 0.0 us)
Async XLA Ops:
  0.0 10.0 %collective-permute-start.2 = (bf16[64,4096]{1,0:T(8,128)(2,1)}, bf16[64,4096]{1,0:T(8,128)(2,1)S(1)}, u32[]{:S(2)}, u32[]{:S(2)}) collective-permute-start(bf16[64,4096]{1,0:T(8,128)(2,1)} %bitcast.49), channel_id=1, source_target_pairs={{0,1},{1,0},{2,3},{3,2},{4,5},{5,4},{6,7},{7,6},{8,9},{9,8},{10,11... | collective-permute-start | bytes 1572872 | tf_op jit(solution)/shard_map/ppermute | solution.py:96
  3.5 6.7 %copy-start = (bf16[64,1,4096]{2,0,1:T(8,128)(2,1)S(1)}, bf16[64,1,4096]{2,0,1:T(8,128)(2,1)}, u32[]{:S(2)}) copy-start(bf16[64,1,4096]{2,0,1:T(8,128)(2,1)} %param.12) | copy-start | bytes 1572868
  3.5 1.2 %collective-permute-start = (f32[1,4096]{1,0:T(1,128)S(1)}, f32[1,4096]{1,0:T(1,128)S(1)}, u32[]{:S(2)}, u32[]{:S(2)}) collective-permute-start(f32[1,4096]{1,0:T(1,128)S(1)} %bitcast.43), channel_id=1, source_target_pairs={{0,1},{1,0},{2,3},{3,2},{4,5},{5,4},{6,7},{7,6},{8,9},{9,8},{10,11... | collective-permute-start | bytes 49160 | tf_op jit(solution)/shard_map/ppermute | solution.py:96
  4.8 5.2 %collective-permute-start.4 = (bf16[2,4096]{1,0:T(2,128)(2,1)S(1)}, bf16[2,4096]{1,0:T(2,128)(2,1)S(1)}, u32[]{:S(2)}, u32[]{:S(2)}) collective-permute-start(bf16[2,4096]{1,0:T(2,128)(2,1)S(1)} %fusion.2.rows), channel_id=1, source_target_pairs={{4,0},{8,1},{14,2},{2,3},{5,4},{12,5},{10,6},{3,7},{9,8},{0,9},{15... | collective-permute-start | bytes 49160 | tf_op jit(solution)/shard_map/ppermute | solution.py:103
  8.6 5.0 %collective-permute-start.1 = (bf16[2,4096]{1,0:T(2,128)(2,1)S(1)}, bf16[2,4096]{1,0:T(2,128)(2,1)S(1)}, u32[]{:S(2)}, u32[]{:S(2)}) collective-permute-start(bf16[2,4096]{1,0:T(2,128)(2,1)S(1)} %fusion.2.rows), channel_id=1, source_target_pairs={{13,0},{0,1},{7,2},{11,3},{1,4},{8,5},{14,6},{6,7},{12,8},{4,9},{2... | collective-permute-start | bytes 49160 | tf_op jit(solution)/shard_map/ppermute | solution.py:103
  10.5 4.9 %collective-permute-start.5 = (f32[64]{0:T(128)S(1)}, f32[64]{0:T(128)S(1)}, u32[]{:S(2)}, u32[]{:S(2)}) collective-permute-start(f32[64]{0:T(128)S(1)} %fusion), channel_id=1, source_target_pairs={{0,4},{1,8},{2,12},{3,0},{4,5},{5,13},{6,9},{7,1},{8,10},{9,2},{10... | collective-permute-start | bytes 776 | tf_op jit(solution)/shard_map/ppermute | solution.py:109
  14.0 2.0 %collective-permute-start.3 = (f32[64]{0:T(128)S(1)}, f32[64]{0:T(128)S(1)}, u32[]{:S(2)}, u32[]{:S(2)}) collective-permute-start(f32[64]{0:T(128)S(1)} %fusion.1), channel_id=1, source_target_pairs={{0,12},{1,0},{2,4},{3,8},{4,1},{5,9},{6,13},{7,5},{8,14},{9,6},{10... | collective-permute-start | bytes 776 | tf_op jit(solution)/shard_map/ppermute | solution.py:109

commit v21 on v19

--- a/solution.py
+++ b/solution.py
@@ -8,10 +8,10 @@
 from jax.experimental.pallas import tpu as pltpu
 from jax.sharding import PartitionSpec as P
 
-FIRST = ((1, 0, 2, 3), (0, 3, 2, 1), (3, 2, 0, 1), (2, 1, 3, 0))
-FIRST_FROM = ((0, 0, 3, 2), (1, 1, 2, 2), (0, 0, 2, 3), (1, 1, 3, 3))
-SECOND = ((2, 3, 0, 1), (1, 2, 3, 0), (0, 1, 3, 2), (3, 0, 1, 2))
-SECOND_FROM = ((0, 0, 3, 2), (1, 1, 3, 2), (0, 0, 2, 2), (1, 1, 3, 3))
+FIRST = ((2, 3, 0, 1), (1, 2, 3, 0), (0, 1, 3, 2), (3, 0, 1, 2))
+FIRST_FROM = ((0, 0, 3, 2), (1, 1, 3, 2), (0, 0, 2, 2), (1, 1, 3, 3))
+SECOND = ((1, 0, 2, 3), (0, 3, 2, 1), (3, 2, 0, 1), (2, 1, 3, 0))
+SECOND_FROM = ((0, 0, 3, 2), (1, 1, 2, 2), (0, 0, 2, 3), (1, 1, 3, 3))
 
 
 PARTS = 4
@@ -107,6 +107,17 @@
     return lax.ppermute(x, ("dp", "layer"), moves)
 
 
+def slot_kernel(senders, rows, own_block, other_block, out):
+    here = lax.axis_index("dp") * len(senders) + lax.axis_index("layer")
+    crossed = [d * len(row) + i for d, row in enumerate(senders) for i, sender in enumerate(row) if sender != i]
+    is_crossed = functools.reduce(jnp.logical_or, [here == i for i in crossed])
+    one, two = (
+        lax.dot_general(rows[...], block[...], (((1,), (1,)), ((), ())), preferred_element_type=jnp.float32)
+        for block in (own_block, other_block)
+    )
+    out[...] = jnp.where(is_crossed, one[1:] + two[:1], one[:1] + two[1:])
+
+
 def factor_kernel(scale, margin, label, rows, factor):
     sign = jnp.where(label[0] == 0, 1.0, -1.0)
     factor[...] = sign / ((1.0 + jnp.exp(jnp.full(factor.shape, margin[0], jnp.float32))) * scale)
@@ -124,18 +135,19 @@
         compiler_params=pltpu.CompilerParams(vmem_limit_bytes=1024 * 1024),
         cost_estimate=pl.CostEstimate(flops=0, bytes_accessed=4 * own_block.shape[0], transcendentals=0),
     )(margin, labels, rows)
-    here = lax.axis_index("dp") * len(FIRST) + lax.axis_index("layer")
 
     def score(got, senders):
-        crossed = [d * len(row) + i for d, row in enumerate(senders) for i, sender in enumerate(row) if sender != i]
-        is_crossed = functools.reduce(jnp.logical_or, [here == i for i in crossed])
-        return sum(
-            jnp.einsum("k,qk->q", jnp.where(is_crossed, got[1 - i], got[i]), block, preferred_element_type=jnp.float32)
-            for i, block in enumerate(blocks)
-        )
+        return pl.pallas_call(
+            functools.partial(slot_kernel, senders),
+            out_shape=jax.ShapeDtypeStruct((1, own_block.shape[0]), jnp.float32),
+            in_specs=[pl.BlockSpec(memory_space=pltpu.VMEM)] * 3,
+            out_specs=pl.BlockSpec(memory_space=pltpu.VMEM),
+            compiler_params=pltpu.CompilerParams(vmem_limit_bytes=1024 * 1024),
+            cost_estimate=pl.CostEstimate(flops=8 * own_block.size, bytes_accessed=4 * own_block.size, transcendentals=0),
+        )(*(pltpu.with_memory_space_constraint(x, pltpu.VMEM) for x in (got, *blocks)))
 
     first, second = score(first, FIRST_FROM), score(second, SECOND_FROM)
-    return ((to_owner(first, FIRST) + to_owner(second, SECOND)) * factor)[None]
+    return (to_owner(first, FIRST) + to_owner(second, SECOND)) * factor[None]
 
 
 def pair_gradients(acts_in, grads_out, proj_in, proj_out, lengths):

time: 16.3 us -> 16.1 us (0.988)
  matrix products: 0.99 us -> 0 us
  Pallas kernels: 2.91 us -> 3.72 us
    dot_general x4 -> x0, matrix products: 0.99 us -> none  [score(): jnp.einsum('k,qk->q', jnp.where(is_crossed, got[1 - i], got[i]), block, p...]
    pallas_call x0 -> x2, Pallas kernels: none -> 0.75 us  [score(): pl.pallas_call(functools.partial(slot_kernel, senders), out_shape=jax.Sha...]
    broadcast_in_dim x1 -> x0, other arithmetic: 0.52 us -> none  [shared_scores(): return ((to_owner(first, FIRST) + to_owner(second, SECOND)) * factor)[None]]
    mul x0 -> x1, other arithmetic: none -> 0.52 us  [shared_scores(): return (to_owner(first, FIRST) + to_owner(second, SECOND)) * factor[None]]
  transfers between devices with their start and end apart: 6 -> 6, of which waited for: 2 -> 2; matrix products, arithmetic and copies ran while one was open for 7% -> 0% of each run, Pallas kernels for 18% -> 24%
where the time goes in v21:
time: 16.1 us; the launch traced here: 15.8 us
  starting transfers between devices  8.4 us (52%)
  Pallas kernels  3.72 us (23%)
  waiting for transfers between devices  1.78 us (11%)
  between operations  1.37 us (9%)
  other arithmetic  0.57 us (4%)
    ppermute x2, starting transfers between devices, fetch_pair(): return lax.ppermute(x, ('dp', 'layer'), moves)  4.89 us
    pallas_call x1, Pallas kernels, pair_gradient(): pl.pallas_call(functools.partial(pair_kernel, seq_len), out_shape=jax.Sha...  2.96 us
    ppermute x2, starting transfers between devices, to_owner(): return lax.ppermute(x, ('dp', 'layer'), moves)  2.94 us
    ppermute x2, waiting for transfers between devices, swap(): lax.ppermute(x, 'layer', [(i, i ^ 1) for i in range(lax.axis_size('layer'...  1.13 us
    pallas_call x2, Pallas kernels, score(): pl.pallas_call(functools.partial(slot_kernel, senders), out_shape=jax.Sha...  0.75 us
    ppermute x2, waiting for transfers between devices, fetch_pair(): return lax.ppermute(x, ('dp', 'layer'), moves)  0.64 us
    ppermute x2, starting transfers between devices, swap(): lax.ppermute(x, 'layer', [(i, i ^ 1) for i in range(lax.axis_size('layer'...  0.57 us
    mul x1, other arithmetic, shared_scores(): return (to_owner(first, FIRST) + to_owner(second, SECOND)) * factor[None]  0.52 us
  transfers between devices with their start and end apart: 6, of which 2 were waited for; matrix products, arithmetic and copies ran while one was open for 0% of the time, Pallas kernels for 24%

profile of v21, /device:TPU:0, one launch (start us, length us, event | category | flops | bytes accessed | tf_op | source)
XLA Modules:
  0.0 15.8 jit_solution(5365034915353783391)
XLA Ops:
  0.0 0.5 %collective-permute-start.2 = (bf16[64,4096]{1,0:T(8,128)(2,1)}, bf16[64,4096]{1,0:T(8,128)(2,1)S(1)}, u32[]{:S(2)}, u32[]{:S(2)}) collective-permute-start(bf16[64,4096]{1,0:T(8,128)(2,1)} %bitcast.12), channel_id=1, source_target_pairs={{0,1},{1,0},{2,3},{3,2},{4,5},{5,4},{6,7},{7,6},{8,9},{9,8},{10,11... | collective-permute-start | bytes 1572872 | tf_op jit(solution)/shard_map/ppermute | solution.py:94
  0.5 0.0 copy-start
  0.5 3.0 %shard_map.82 = f32[32,128]{1,0:T(8,128)S(1)} custom-call(bf16[128,4096]{1,0:T(8,128)(2,1)} %bitcast.16, bf16[128,4096]{1,0:T(8,128)(2,1)} %bitcast.17, bf16[64,4096]{1,0:T(8,128)(2,1)} %bitcast.18, bf16[64,4096]{1,0:T(8,128)(2,1)} %bitcast.19, s32[1,2]{1,0:T(1,128)} %lengths.1), custom_call_target="tpu_custom_call" | custom-call | flops 134217728 | bytes 3145728 | tf_op jit(solution)/shard_map/pallas_call | solution.py:59
  3.4 0.1 collective-permute-start
  3.6 1.1 %collective-permute-done = bf16[1,4096]{1,0:T(2,128)(2,1)S(1)} collective-permute-done((bf16[1,4096]{1,0:T(2,128)(2,1)S(1)}, bf16[1,4096]{1,0:T(2,128)(2,1)S(1)}, u32[]{:S(2)}, u32[]{:S(2)}) %collective-permute-start) | collective-permute-done | bytes 8224 | tf_op jit(solution)/shard_map/ppermute | solution.py:94
  4.7 3.8 %collective-permute-start.1 = (bf16[2,4096]{1,0:T(2,128)(2,1)S(1)}, bf16[2,4096]{1,0:T(2,128)(2,1)S(1)}, u32[]{:S(2)}, u32[]{:S(2)}) collective-permute-start(bf16[2,4096]{1,0:T(2,128)(2,1)S(1)} %pad_maximum_fusion.rows), channel_id=1, source_target_pairs={{8,0},{12,1},{3,2},{6,3},{5,4},{9,5},{15,6},{2,7},{0,8},{4,9},{14,... | collective-permute-start | bytes 49160 | tf_op jit(solution)/shard_map/ppermute | solution.py:101
  8.5 1.1 %collective-permute-start.4 = (bf16[2,4096]{1,0:T(2,128)(2,1)S(1)}, bf16[2,4096]{1,0:T(2,128)(2,1)S(1)}, u32[]{:S(2)}, u32[]{:S(2)}) collective-permute-start(bf16[2,4096]{1,0:T(2,128)(2,1)S(1)} %pad_maximum_fusion.rows), channel_id=1, source_target_pairs={{4,0},{0,1},{11,2},{14,3},{1,4},{13,5},{10,6},{6,7},{12,8},{8,9},{... | collective-permute-start | bytes 49160 | tf_op jit(solution)/shard_map/ppermute | solution.py:101
  9.6 0.6 %collective-permute-done.1.rows = bf16[2,4096]{1,0:T(2,128)(2,1)S(1)} collective-permute-done((bf16[2,4096]{1,0:T(2,128)(2,1)S(1)}, bf16[2,4096]{1,0:T(2,128)(2,1)S(1)}, u32[]{:S(2)}, u32[]{:S(2)}) %collective-permute-start.1) | collective-permute-done | bytes 16416 | tf_op jit(solution)/shard_map/ppermute | solution.py:101
  10.3 0.0 collective-permute-done.2.other_block
  10.3 0.0 copy-done
  10.3 0.4 %shard_map.83 = f32[1,64]{1,0:T(1,128)S(1)} custom-call(bf16[2,4096]{1,0:T(2,128)(2,1)S(1)} %collective-permute-done.1.rows, bf16[64,4096]{1,0:T(8,128)(2,1)S(1)} %bitcast.13, bf16[64,4096]{1,0:T(8,128)(2,1)S(1)} %collective-permute-done.2.other_block), custom_call_target="tpu_custom_call" | custom-call | flops 2097152 | bytes 1048576 | tf_op jit(solution)/shard_map/pallas_call | solution.py:140
  10.6 2.9 %collective-permute-start.3 = (f32[1,64]{1,0:T(1,128)S(1)}, f32[1,64]{1,0:T(1,128)S(1)}, u32[]{:S(2)}, u32[]{:S(2)}) collective-permute-start(f32[1,64]{1,0:T(1,128)S(1)} %shard_map.83), channel_id=1, source_target_pairs={{0,8},{1,12},{2,0},{3,4},{4,5},{5,9},{6,13},{7,1},{8,2},{9,6},{10,... | collective-permute-start | bytes 776 | tf_op jit(solution)/shard_map/ppermute | solution.py:107
  13.6 0.0 collective-permute-done.4.rows
  13.6 0.4 %shard_map.84 = f32[1,64]{1,0:T(1,128)S(1)} custom-call(bf16[2,4096]{1,0:T(2,128)(2,1)S(1)} %collective-permute-done.4.rows, bf16[64,4096]{1,0:T(8,128)(2,1)S(1)} %bitcast.14, bf16[64,4096]{1,0:T(8,128)(2,1)S(1)} %collective-permute-done.2.other_block), custom_call_target="tpu_custom_call" | custom-call | flops 2097152 | bytes 1048576 | tf_op jit(solution)/shard_map/pallas_call | solution.py:140
  14.0 0.0 collective-permute-start.5
  15.3 0.0 collective-permute-done.3
  15.3 0.0 collective-permute-done.5
  15.3 0.5 %bitcast_multiply_fusion = f32[1,64]{1,0:T(1,128)} fusion(f32[64]{0:T(128)S(1)} %shard_map.85, f32[1,64]{1,0:T(1,128)S(1)} %collective-permute-done.3, f32[1,64]{1,0:T(1,128)S(1)} %collective-permute-done.5), kind=kLoop, calls=%fused_computation.1 | loop fusion | flops 128 | bytes 1024 | tf_op jit(solution)/shard_map/mul | solution.py:150
  (3 shorter events, 0.1 us)
Async XLA Ops:
  0.0 10.3 %collective-permute-start.2 = (bf16[64,4096]{1,0:T(8,128)(2,1)}, bf16[64,4096]{1,0:T(8,128)(2,1)S(1)}, u32[]{:S(2)}, u32[]{:S(2)}) collective-permute-start(bf16[64,4096]{1,0:T(8,128)(2,1)} %bitcast.12), channel_id=1, source_target_pairs={{0,1},{1,0},{2,3},{3,2},{4,5},{5,4},{6,7},{7,6},{8,9},{9,8},{10,11... | collective-permute-start | bytes 1572872 | tf_op jit(solution)/shard_map/ppermute | solution.py:94
  0.5 9.8 %copy-start = (bf16[64,1,4096]{2,0,1:T(8,128)(2,1)S(1)}, bf16[64,1,4096]{2,0,1:T(8,128)(2,1)}, u32[]{:S(2)}) copy-start(bf16[64,1,4096]{2,0,1:T(8,128)(2,1)} %param.12) | copy-start | bytes 1572868
  3.4 1.2 %collective-permute-start = (bf16[1,4096]{1,0:T(2,128)(2,1)S(1)}, bf16[1,4096]{1,0:T(2,128)(2,1)S(1)}, u32[]{:S(2)}, u32[]{:S(2)}) collective-permute-start(bf16[1,4096]{1,0:T(2,128)(2,1)S(1)} %convert.11), channel_id=1, source_target_pairs={{0,1},{1,0},{2,3},{3,2},{4,5},{5,4},{6,7},{7,6},{8,9},{9,8},{10,11... | collective-permute-start | bytes 24584 | tf_op jit(solution)/shard_map/ppermute | solution.py:94
  4.7 5.5 %collective-permute-start.1 = (bf16[2,4096]{1,0:T(2,128)(2,1)S(1)}, bf16[2,4096]{1,0:T(2,128)(2,1)S(1)}, u32[]{:S(2)}, u32[]{:S(2)}) collective-permute-start(bf16[2,4096]{1,0:T(2,128)(2,1)S(1)} %pad_maximum_fusion.rows), channel_id=1, source_target_pairs={{8,0},{12,1},{3,2},{6,3},{5,4},{9,5},{15,6},{2,7},{0,8},{4,9},{14,... | collective-permute-start | bytes 49160 | tf_op jit(solution)/shard_map/ppermute | solution.py:101
  8.5 5.0 %collective-permute-start.4 = (bf16[2,4096]{1,0:T(2,128)(2,1)S(1)}, bf16[2,4096]{1,0:T(2,128)(2,1)S(1)}, u32[]{:S(2)}, u32[]{:S(2)}) collective-permute-start(bf16[2,4096]{1,0:T(2,128)(2,1)S(1)} %pad_maximum_fusion.rows), channel_id=1, source_target_pairs={{4,0},{0,1},{11,2},{14,3},{1,4},{13,5},{10,6},{6,7},{12,8},{8,9},{... | collective-permute-start | bytes 49160 | tf_op jit(solution)/shard_map/ppermute | solution.py:101
  10.6 4.7 %collective-permute-start.3 = (f32[1,64]{1,0:T(1,128)S(1)}, f32[1,64]{1,0:T(1,128)S(1)}, u32[]{:S(2)}, u32[]{:S(2)}) collective-permute-start(f32[1,64]{1,0:T(1,128)S(1)} %shard_map.83), channel_id=1, source_target_pairs={{0,8},{1,12},{2,0},{3,4},{4,5},{5,9},{6,13},{7,1},{8,2},{9,6},{10,... | collective-permute-start | bytes 776 | tf_op jit(solution)/shard_map/ppermute | solution.py:107
  14.0 1.4 %collective-permute-start.5 = (f32[1,64]{1,0:T(1,128)S(1)}, f32[1,64]{1,0:T(1,128)S(1)}, u32[]{:S(2)}, u32[]{:S(2)}) collective-permute-start(f32[1,64]{1,0:T(1,128)S(1)} %shard_map.84), channel_id=1, source_target_pairs={{0,4},{1,0},{2,8},{3,12},{4,1},{5,13},{6,9},{7,5},{8,14},{9,10},{1... | collective-permute-start | bytes 776 | tf_op jit(solution)/shard_map/ppermute | solution.py:107

commit v22 on v21

--- a/solution.py
+++ b/solution.py
@@ -18,7 +18,7 @@
 
 
 def pair_kernel(seq_len, acts, grads, proj_in, proj_out, lengths, out, *scratch):
-    tokens_v, proj_v, turned_v, kron_v, lengths_s, sems = scratch
+    tokens_v, proj_v, turned_v, square_v, lengths_s, sems = scratch
     tokens = acts.shape[0]
     rank, model_width = proj_in.shape
     limits = pltpu.make_async_copy(lengths, lengths_s, sems.at[4])
@@ -43,13 +43,14 @@
     for copy in loads[2:]:
         copy.wait()
     coords = jnp.dot(tokens_v[...], turned_v[...], preferred_element_type=jnp.float32)
-    in_coords = (coords[:tokens, :rank] * weight).astype(jnp.bfloat16)
-    out_coords = coords[tokens:, rank:].astype(jnp.bfloat16)
-    kron_v[...] = lax.dot_general(
-        out_coords, in_coords, (((0,), (0,)), ((), ())), preferred_element_type=jnp.float32
+    square_v[...] = lax.dot_general(
+        coords[tokens:].astype(jnp.bfloat16),
+        (coords[:tokens] * weight).astype(jnp.bfloat16),
+        (((0,), (0,)), ((), ())),
+        preferred_element_type=jnp.float32,
     )
-    half = rank // 2
-    out[...] = jnp.concatenate([kron_v[pl.ds(i, half, stride=2), :] for i in range(2)], axis=1)
+    rows = [square_v[pl.ds(rank + i, rank // 2, stride=2), :] for i in range(2)]
+    out[...] = jnp.concatenate([x[:, :rank] for x in rows], axis=1)
 
 
 def pair_gradient(acts_in, grads_out, proj_in, proj_out, lengths):
@@ -65,7 +66,7 @@
             pltpu.VMEM((2 * tokens, model_width), jnp.bfloat16),
             pltpu.VMEM((2 * rank, model_width), jnp.bfloat16),
             pltpu.VMEM((model_width, 2 * rank), jnp.bfloat16),
-            pltpu.VMEM((rank, rank), jnp.float32),
+            pltpu.VMEM((2 * rank, 2 * rank), jnp.float32),
             pltpu.SMEM((1, 2), jnp.int32),
             pltpu.SemaphoreType.DMA((5,)),
         ],

time: 16.1 us -> 16 us (level)
  transfers between devices with their start and end apart: 6 -> 6, of which waited for: 2 -> 2; matrix products, arithmetic and copies ran while one was open for 0% -> 0% of each run, Pallas kernels for 24% -> 23%
where the time goes in v22:
time: 16 us; the launch traced here: 15.8 us
  starting transfers between devices  8.4 us (52%)
  Pallas kernels  3.66 us (23%)
  waiting for transfers between devices  1.78 us (11%)
  between operations  1.37 us (9%)
  other arithmetic  0.57 us (4%)
    ppermute x2, starting transfers between devices, fetch_pair(): return lax.ppermute(x, ('dp', 'layer'), moves)  4.89 us
    ppermute x2, starting transfers between devices, to_owner(): return lax.ppermute(x, ('dp', 'layer'), moves)  2.94 us
    pallas_call x1, Pallas kernels, pair_gradient(): pl.pallas_call(functools.partial(pair_kernel, seq_len), out_shape=jax.Sha...  2.9 us
    ppermute x2, waiting for transfers between devices, swap(): lax.ppermute(x, 'layer', [(i, i ^ 1) for i in range(lax.axis_size('layer'...  1.13 us
    pallas_call x2, Pallas kernels, score(): pl.pallas_call(functools.partial(slot_kernel, senders), out_shape=jax.Sha...  0.75 us
    ppermute x2, waiting for transfers between devices, fetch_pair(): return lax.ppermute(x, ('dp', 'layer'), moves)  0.64 us
    ppermute x2, starting transfers between devices, swap(): lax.ppermute(x, 'layer', [(i, i ^ 1) for i in range(lax.axis_size('layer'...  0.57 us
    mul x1, other arithmetic, shared_scores(): return (to_owner(first, FIRST) + to_owner(second, SECOND)) * factor[None]  0.52 us
  transfers between devices with their start and end apart: 6, of which 2 were waited for; matrix products, arithmetic and copies ran while one was open for 0% of the time, Pallas kernels for 23%

profile of v22, /device:TPU:0, one launch (start us, length us, event | category | flops | bytes accessed | tf_op | source)
XLA Modules:
  0.0 15.8 jit_solution(5477673773519903919)
XLA Ops:
  0.0 0.5 %collective-permute-start.2 = (bf16[64,4096]{1,0:T(8,128)(2,1)}, bf16[64,4096]{1,0:T(8,128)(2,1)S(1)}, u32[]{:S(2)}, u32[]{:S(2)}) collective-permute-start(bf16[64,4096]{1,0:T(8,128)(2,1)} %bitcast.12), channel_id=1, source_target_pairs={{0,1},{1,0},{2,3},{3,2},{4,5},{5,4},{6,7},{7,6},{8,9},{9,8},{10,11... | collective-permute-start | bytes 1572872 | tf_op jit(solution)/shard_map/ppermute | solution.py:95
  0.5 0.0 copy-start
  0.5 2.9 %shard_map.82 = f32[32,128]{1,0:T(8,128)S(1)} custom-call(bf16[128,4096]{1,0:T(8,128)(2,1)} %bitcast.16, bf16[128,4096]{1,0:T(8,128)(2,1)} %bitcast.17, bf16[64,4096]{1,0:T(8,128)(2,1)} %bitcast.18, bf16[64,4096]{1,0:T(8,128)(2,1)} %bitcast.19, s32[1,2]{1,0:T(1,128)} %lengths.1), custom_call_target="tpu_custom_call" | custom-call | flops 134217728 | bytes 3145728 | tf_op jit(solution)/shard_map/pallas_call | solution.py:60
  3.4 0.1 collective-permute-start
  3.5 1.1 %collective-permute-done = bf16[1,4096]{1,0:T(2,128)(2,1)S(1)} collective-permute-done((bf16[1,4096]{1,0:T(2,128)(2,1)S(1)}, bf16[1,4096]{1,0:T(2,128)(2,1)S(1)}, u32[]{:S(2)}, u32[]{:S(2)}) %collective-permute-start) | collective-permute-done | bytes 8224 | tf_op jit(solution)/shard_map/ppermute | solution.py:95
  4.7 3.8 %collective-permute-start.1 = (bf16[2,4096]{1,0:T(2,128)(2,1)S(1)}, bf16[2,4096]{1,0:T(2,128)(2,1)S(1)}, u32[]{:S(2)}, u32[]{:S(2)}) collective-permute-start(bf16[2,4096]{1,0:T(2,128)(2,1)S(1)} %pad_maximum_fusion.rows), channel_id=1, source_target_pairs={{8,0},{12,1},{3,2},{6,3},{5,4},{9,5},{15,6},{2,7},{0,8},{4,9},{14,... | collective-permute-start | bytes 49160 | tf_op jit(solution)/shard_map/ppermute | solution.py:102
  8.5 1.1 %collective-permute-start.4 = (bf16[2,4096]{1,0:T(2,128)(2,1)S(1)}, bf16[2,4096]{1,0:T(2,128)(2,1)S(1)}, u32[]{:S(2)}, u32[]{:S(2)}) collective-permute-start(bf16[2,4096]{1,0:T(2,128)(2,1)S(1)} %pad_maximum_fusion.rows), channel_id=1, source_target_pairs={{4,0},{0,1},{11,2},{14,3},{1,4},{13,5},{10,6},{6,7},{12,8},{8,9},{... | collective-permute-start | bytes 49160 | tf_op jit(solution)/shard_map/ppermute | solution.py:102
  9.6 0.6 %collective-permute-done.1.rows = bf16[2,4096]{1,0:T(2,128)(2,1)S(1)} collective-permute-done((bf16[2,4096]{1,0:T(2,128)(2,1)S(1)}, bf16[2,4096]{1,0:T(2,128)(2,1)S(1)}, u32[]{:S(2)}, u32[]{:S(2)}) %collective-permute-start.1) | collective-permute-done | bytes 16416 | tf_op jit(solution)/shard_map/ppermute | solution.py:102
  10.2 0.0 collective-permute-done.2.other_block
  10.2 0.0 copy-done
  10.2 0.4 %shard_map.83 = f32[1,64]{1,0:T(1,128)S(1)} custom-call(bf16[2,4096]{1,0:T(2,128)(2,1)S(1)} %collective-permute-done.1.rows, bf16[64,4096]{1,0:T(8,128)(2,1)S(1)} %bitcast.13, bf16[64,4096]{1,0:T(8,128)(2,1)S(1)} %collective-permute-done.2.other_block), custom_call_target="tpu_custom_call" | custom-call | flops 2097152 | bytes 1048576 | tf_op jit(solution)/shard_map/pallas_call | solution.py:141
  10.6 2.9 %collective-permute-start.3 = (f32[1,64]{1,0:T(1,128)S(1)}, f32[1,64]{1,0:T(1,128)S(1)}, u32[]{:S(2)}, u32[]{:S(2)}) collective-permute-start(f32[1,64]{1,0:T(1,128)S(1)} %shard_map.83), channel_id=1, source_target_pairs={{0,8},{1,12},{2,0},{3,4},{4,5},{5,9},{6,13},{7,1},{8,2},{9,6},{10,... | collective-permute-start | bytes 776 | tf_op jit(solution)/shard_map/ppermute | solution.py:108
  13.5 0.0 collective-permute-done.4.rows
  13.5 0.4 %shard_map.84 = f32[1,64]{1,0:T(1,128)S(1)} custom-call(bf16[2,4096]{1,0:T(2,128)(2,1)S(1)} %collective-permute-done.4.rows, bf16[64,4096]{1,0:T(8,128)(2,1)S(1)} %bitcast.14, bf16[64,4096]{1,0:T(8,128)(2,1)S(1)} %collective-permute-done.2.other_block), custom_call_target="tpu_custom_call" | custom-call | flops 2097152 | bytes 1048576 | tf_op jit(solution)/shard_map/pallas_call | solution.py:141
  13.9 0.0 collective-permute-start.5
  15.2 0.0 collective-permute-done.3
  15.3 0.0 collective-permute-done.5
  15.3 0.5 %bitcast_multiply_fusion = f32[1,64]{1,0:T(1,128)} fusion(f32[64]{0:T(128)S(1)} %shard_map.85, f32[1,64]{1,0:T(1,128)S(1)} %collective-permute-done.3, f32[1,64]{1,0:T(1,128)S(1)} %collective-permute-done.5), kind=kLoop, calls=%fused_computation.1 | loop fusion | flops 128 | bytes 1024 | tf_op jit(solution)/shard_map/mul | solution.py:151
  (3 shorter events, 0.1 us)
Async XLA Ops:
  0.0 10.2 %collective-permute-start.2 = (bf16[64,4096]{1,0:T(8,128)(2,1)}, bf16[64,4096]{1,0:T(8,128)(2,1)S(1)}, u32[]{:S(2)}, u32[]{:S(2)}) collective-permute-start(bf16[64,4096]{1,0:T(8,128)(2,1)} %bitcast.12), channel_id=1, source_target_pairs={{0,1},{1,0},{2,3},{3,2},{4,5},{5,4},{6,7},{7,6},{8,9},{9,8},{10,11... | collective-permute-start | bytes 1572872 | tf_op jit(solution)/shard_map/ppermute | solution.py:95
  0.5 9.8 %copy-start = (bf16[64,1,4096]{2,0,1:T(8,128)(2,1)S(1)}, bf16[64,1,4096]{2,0,1:T(8,128)(2,1)}, u32[]{:S(2)}) copy-start(bf16[64,1,4096]{2,0,1:T(8,128)(2,1)} %param.12) | copy-start | bytes 1572868
  3.4 1.2 %collective-permute-start = (bf16[1,4096]{1,0:T(2,128)(2,1)S(1)}, bf16[1,4096]{1,0:T(2,128)(2,1)S(1)}, u32[]{:S(2)}, u32[]{:S(2)}) collective-permute-start(bf16[1,4096]{1,0:T(2,128)(2,1)S(1)} %convert.11), channel_id=1, source_target_pairs={{0,1},{1,0},{2,3},{3,2},{4,5},{5,4},{6,7},{7,6},{8,9},{9,8},{10,11... | collective-permute-start | bytes 24584 | tf_op jit(solution)/shard_map/ppermute | solution.py:95
  4.7 5.5 %collective-permute-start.1 = (bf16[2,4096]{1,0:T(2,128)(2,1)S(1)}, bf16[2,4096]{1,0:T(2,128)(2,1)S(1)}, u32[]{:S(2)}, u32[]{:S(2)}) collective-permute-start(bf16[2,4096]{1,0:T(2,128)(2,1)S(1)} %pad_maximum_fusion.rows), channel_id=1, source_target_pairs={{8,0},{12,1},{3,2},{6,3},{5,4},{9,5},{15,6},{2,7},{0,8},{4,9},{14,... | collective-permute-start | bytes 49160 | tf_op jit(solution)/shard_map/ppermute | solution.py:102
  8.5 5.0 %collective-permute-start.4 = (bf16[2,4096]{1,0:T(2,128)(2,1)S(1)}, bf16[2,4096]{1,0:T(2,128)(2,1)S(1)}, u32[]{:S(2)}, u32[]{:S(2)}) collective-permute-start(bf16[2,4096]{1,0:T(2,128)(2,1)S(1)} %pad_maximum_fusion.rows), channel_id=1, source_target_pairs={{4,0},{0,1},{11,2},{14,3},{1,4},{13,5},{10,6},{6,7},{12,8},{8,9},{... | collective-permute-start | bytes 49160 | tf_op jit(solution)/shard_map/ppermute | solution.py:102
  10.6 4.7 %collective-permute-start.3 = (f32[1,64]{1,0:T(1,128)S(1)}, f32[1,64]{1,0:T(1,128)S(1)}, u32[]{:S(2)}, u32[]{:S(2)}) collective-permute-start(f32[1,64]{1,0:T(1,128)S(1)} %shard_map.83), channel_id=1, source_target_pairs={{0,8},{1,12},{2,0},{3,4},{4,5},{5,9},{6,13},{7,1},{8,2},{9,6},{10,... | collective-permute-start | bytes 776 | tf_op jit(solution)/shard_map/ppermute | solution.py:108
  13.9 1.4 %collective-permute-start.5 = (f32[1,64]{1,0:T(1,128)S(1)}, f32[1,64]{1,0:T(1,128)S(1)}, u32[]{:S(2)}, u32[]{:S(2)}) collective-permute-start(f32[1,64]{1,0:T(1,128)S(1)} %shard_map.84), channel_id=1, source_target_pairs={{0,4},{1,0},{2,8},{3,12},{4,1},{5,13},{6,9},{7,5},{8,14},{9,10},{1... | collective-permute-start | bytes 776 | tf_op jit(solution)/shard_map/ppermute | solution.py:108

commit v23 on v22

--- a/solution.py
+++ b/solution.py
@@ -17,7 +17,7 @@
 PARTS = 4
 
 
-def pair_kernel(seq_len, acts, grads, proj_in, proj_out, lengths, out, *scratch):
+def pair_kernel(seq_len, acts, grads, proj_in, proj_out, queries, lengths, out, queries_out, *scratch):
     tokens_v, proj_v, turned_v, square_v, lengths_s, sems = scratch
     tokens = acts.shape[0]
     rank, model_width = proj_in.shape
@@ -30,6 +30,8 @@
     limits.start()
     for i, copy in enumerate(loads):
         copy.start(priority=i % 2)
+    load_queries = pltpu.make_async_copy(queries, queries_out, sems.at[5])
+    load_queries.start(priority=1)
     limits.wait()
     token = lax.broadcasted_iota(jnp.int32, (tokens, 1), 0)
     side = token // seq_len
@@ -51,24 +53,28 @@
     )
     rows = [square_v[pl.ds(rank + i, rank // 2, stride=2), :] for i in range(2)]
     out[...] = jnp.concatenate([x[:, :rank] for x in rows], axis=1)
-
-
-def pair_gradient(acts_in, grads_out, proj_in, proj_out, lengths):
+    load_queries.wait()
+
+
+def pair_gradient(acts_in, grads_out, proj_in, proj_out, block, lengths):
     _, sides, seq_len, _, model_width = acts_in.shape
     rank = proj_in.shape[2]
     tokens = sides * seq_len
-    rows = pl.pallas_call(
+    rows, block = pl.pallas_call(
         functools.partial(pair_kernel, seq_len),
-        out_shape=jax.ShapeDtypeStruct((rank // 2, 2 * rank), jnp.float32),
-        in_specs=[pl.BlockSpec(memory_space=pl.ANY)] * 5,
-        out_specs=pl.BlockSpec(memory_space=pltpu.VMEM),
+        out_shape=(
+            jax.ShapeDtypeStruct((rank // 2, 2 * rank), jnp.float32),
+            jax.ShapeDtypeStruct(block.shape, block.dtype),
+        ),
+        in_specs=[pl.BlockSpec(memory_space=pl.ANY)] * 6,
+        out_specs=(pl.BlockSpec(memory_space=pltpu.VMEM),) * 2,
         scratch_shapes=[
             pltpu.VMEM((2 * tokens, model_width), jnp.bfloat16),
             pltpu.VMEM((2 * rank, model_width), jnp.bfloat16),
             pltpu.VMEM((model_width, 2 * rank), jnp.bfloat16),
             pltpu.VMEM((2 * rank, 2 * rank), jnp.float32),
             pltpu.SMEM((1, 2), jnp.int32),
-            pltpu.SemaphoreType.DMA((5,)),
+            pltpu.SemaphoreType.DMA((6,)),
         ],
         compiler_params=pltpu.CompilerParams(vmem_limit_bytes=32 * 1024 * 1024),
         cost_estimate=pl.CostEstimate(
@@ -84,11 +90,12 @@
                 grads_out.reshape(tokens, model_width),
                 jnp.swapaxes(proj_in, 1, 2).reshape(rank, model_width),
                 jnp.swapaxes(proj_out, 1, 2).reshape(rank, model_width),
+                block,
                 lengths,
             )
         )
     )
-    return lax.optimization_barrier(rows.reshape(1, rank * rank))
+    return lax.optimization_barrier(rows.reshape(1, rank * rank)), block
 
 
 def swap(x):
@@ -137,6 +144,7 @@
         cost_estimate=pl.CostEstimate(flops=0, bytes_accessed=4 * own_block.shape[0], transcendentals=0),
     )(margin, labels, rows)
 
+
     def score(got, senders):
         return pl.pallas_call(
             functools.partial(slot_kernel, senders),
@@ -170,8 +178,10 @@
     dp_size, layer_size = lax.axis_size("dp"), lax.axis_size("layer")
     block = query_grads.reshape(query_grads.shape[0], -1)
     one_each = pair_count == layer_count == 1 and side_count == 2
-    form = pair_gradient if one_each else pair_gradients
-    grad_rows = form(acts_in, grads_out, proj_in, proj_out, lengths)
+    if one_each:
+        grad_rows, block = pair_gradient(acts_in, grads_out, proj_in, proj_out, block, lengths)
+    else:
+        grad_rows = pair_gradients(acts_in, grads_out, proj_in, proj_out, lengths)
     scale = rank * math.sqrt(layer_count * layer_size) * math.sqrt(acts_in.shape[2])
     if one_each and dp_size == layer_size == len(FIRST):
         return shared_scores(grad_rows, block, margin, labels, scale)

time: 16 us -> 16.5 us (1.031)
  waiting for transfers between devices: 1.78 us -> 2.28 us
    ppermute x2, waiting for transfers between devices: 1.13 us -> 1.42 us  [swap(): lax.ppermute(x, 'layer', [(i, i ^ 1) for i in range(lax.axis_size('layer'...]
    ppermute x2, waiting for transfers between devices: 0.64 us -> 0.85 us  [fetch_pair(): return lax.ppermute(x, ('dp', 'layer'), moves)]
  transfers between devices with their start and end apart: 6 -> 6, of which waited for: 2 -> 2; matrix products, arithmetic and copies ran while one was open for 0% -> 0% of each run, Pallas kernels for 23% -> 5%
where the time goes in v23:
time: 16.5 us; the launch traced here: 16.3 us
  starting transfers between devices  8.47 us (51%)
  Pallas kernels  3.62 us (22%)
  waiting for transfers between devices  2.28 us (14%)
  between operations  1.36 us (8%)
  other arithmetic  0.57 us (3%)
    ppermute x2, starting transfers between devices, fetch_pair(): return lax.ppermute(x, ('dp', 'layer'), moves)  4.89 us
    ppermute x2, starting transfers between devices, to_owner(): return lax.ppermute(x, ('dp', 'layer'), moves)  2.94 us
    pallas_call x1, Pallas kernels, pair_gradient(): pl.pallas_call(functools.partial(pair_kernel, seq_len), out_shape=(jax.Sh...  2.85 us
    ppermute x2, waiting for transfers between devices, swap(): lax.ppermute(x, 'layer', [(i, i ^ 1) for i in range(lax.axis_size('layer'...  1.42 us
    ppermute x2, waiting for transfers between devices, fetch_pair(): return lax.ppermute(x, ('dp', 'layer'), moves)  0.85 us
    pallas_call x2, Pallas kernels, score(): pl.pallas_call(functools.partial(slot_kernel, senders), out_shape=jax.Sha...  0.76 us
    ppermute x2, starting transfers between devices, swap(): lax.ppermute(x, 'layer', [(i, i ^ 1) for i in range(lax.axis_size('layer'...  0.64 us
    mul x1, other arithmetic, shared_scores(): return (to_owner(first, FIRST) + to_owner(second, SECOND)) * factor[None]  0.52 us
  transfers between devices with their start and end apart: 6, of which 2 were waited for; matrix products, arithmetic and copies ran while one was open for 0% of the time, Pallas kernels for 5%

profile of v23, /device:TPU:0, one launch (start us, length us, event | category | flops | bytes accessed | tf_op | source)
XLA Modules:
  0.0 16.3 jit_solution(9700399109062423930)
XLA Ops:
  0.0 2.9 %shard_map.82 = (f32[32,128]{1,0:T(8,128)S(1)}, bf16[64,4096]{1,0:T(8,128)(2,1)S(1)}) custom-call(bf16[128,4096]{1,0:T(8,128)(2,1)} %bitcast.13, bf16[128,4096]{1,0:T(8,128)(2,1)} %bitcast.14, bf16[64,4096]{1,0:T(8,128)(2,1)} %bitcast.15, bf16[64,4096]{1,0:T(8,128)(2,1)} %bitcast.16, bf16[64,4096]{1,0:T(8,128)(2,1)} %bitcast.17, s32[1,2]{1,0:T(1,128)} %lengths.1), custom_call_target="tpu_custom_call" | custom-call | flops 134217728 | bytes 3145728 | tf_op jit(solution)/shard_map/pallas_call | solution.py:63
  2.9 0.5 %collective-permute-start.2 = (bf16[64,4096]{1,0:T(8,128)(2,1)S(1)}, bf16[64,4096]{1,0:T(8,128)(2,1)S(1)}, u32[]{:S(2)}, u32[]{:S(2)}) collective-permute-start(bf16[64,4096]{1,0:T(8,128)(2,1)S(1)} %get-tuple-element.8.own_block), channel_id=1, source_target_pairs={{0,1},{1,0},{2,3},{3,2},{4,5},{5,4},{6,7},{7,6},{8,9},{9,8},{10,11... | collective-permute-start | bytes 1572872 | tf_op jit(solution)/shard_map/ppermute | solution.py:102
  3.4 0.1 collective-permute-start
  3.5 1.4 %collective-permute-done = bf16[1,4096]{1,0:T(2,128)(2,1)S(1)} collective-permute-done((bf16[1,4096]{1,0:T(2,128)(2,1)S(1)}, bf16[1,4096]{1,0:T(2,128)(2,1)S(1)}, u32[]{:S(2)}, u32[]{:S(2)}) %collective-permute-start) | collective-permute-done | bytes 8224 | tf_op jit(solution)/shard_map/ppermute | solution.py:102
  5.0 4.0 %collective-permute-start.1 = (bf16[2,4096]{1,0:T(2,128)(2,1)S(1)}, bf16[2,4096]{1,0:T(2,128)(2,1)S(1)}, u32[]{:S(2)}, u32[]{:S(2)}) collective-permute-start(bf16[2,4096]{1,0:T(2,128)(2,1)S(1)} %pad_maximum_fusion.rows), channel_id=1, source_target_pairs={{8,0},{12,1},{3,2},{6,3},{5,4},{9,5},{15,6},{2,7},{0,8},{4,9},{14,... | collective-permute-start | bytes 49160 | tf_op jit(solution)/shard_map/ppermute | solution.py:109
  9.0 0.9 %collective-permute-start.4 = (bf16[2,4096]{1,0:T(2,128)(2,1)S(1)}, bf16[2,4096]{1,0:T(2,128)(2,1)S(1)}, u32[]{:S(2)}, u32[]{:S(2)}) collective-permute-start(bf16[2,4096]{1,0:T(2,128)(2,1)S(1)} %pad_maximum_fusion.rows), channel_id=1, source_target_pairs={{4,0},{0,1},{11,2},{14,3},{1,4},{13,5},{10,6},{6,7},{12,8},{8,9},{... | collective-permute-start | bytes 49160 | tf_op jit(solution)/shard_map/ppermute | solution.py:109
  9.9 0.8 %collective-permute-done.1.rows = bf16[2,4096]{1,0:T(2,128)(2,1)S(1)} collective-permute-done((bf16[2,4096]{1,0:T(2,128)(2,1)S(1)}, bf16[2,4096]{1,0:T(2,128)(2,1)S(1)}, u32[]{:S(2)}, u32[]{:S(2)}) %collective-permute-start.1) | collective-permute-done | bytes 16416 | tf_op jit(solution)/shard_map/ppermute | solution.py:109
  10.7 0.0 collective-permute-done.2.other_block
  10.7 0.4 %shard_map.83 = f32[1,64]{1,0:T(1,128)S(1)} custom-call(bf16[2,4096]{1,0:T(2,128)(2,1)S(1)} %collective-permute-done.1.rows, bf16[64,4096]{1,0:T(8,128)(2,1)S(1)} %get-tuple-element.8.own_block, bf16[64,4096]{1,0:T(8,128)(2,1)S(1)} %collective-permute-done.2.other_block), custom_call_target="tpu_custom_call" | custom-call | flops 2097152 | bytes 1048576 | tf_op jit(solution)/shard_map/pallas_call | solution.py:149
  11.1 2.9 %collective-permute-start.3 = (f32[1,64]{1,0:T(1,128)S(1)}, f32[1,64]{1,0:T(1,128)S(1)}, u32[]{:S(2)}, u32[]{:S(2)}) collective-permute-start(f32[1,64]{1,0:T(1,128)S(1)} %shard_map.83), channel_id=1, source_target_pairs={{0,8},{1,12},{2,0},{3,4},{4,5},{5,9},{6,13},{7,1},{8,2},{9,6},{10,... | collective-permute-start | bytes 776 | tf_op jit(solution)/shard_map/ppermute | solution.py:115
  14.0 0.0 collective-permute-done.4.rows
  14.0 0.4 %shard_map.84 = f32[1,64]{1,0:T(1,128)S(1)} custom-call(bf16[2,4096]{1,0:T(2,128)(2,1)S(1)} %collective-permute-done.4.rows, bf16[64,4096]{1,0:T(8,128)(2,1)S(1)} %get-tuple-element.8.own_block, bf16[64,4096]{1,0:T(8,128)(2,1)S(1)} %collective-permute-done.2.other_block), custom_call_target="tpu_custom_call" | custom-call | flops 2097152 | bytes 1048576 | tf_op jit(solution)/shard_map/pallas_call | solution.py:149
  14.4 0.0 collective-permute-start.5
  15.8 0.0 collective-permute-done.3
  15.8 0.0 collective-permute-done.5
  15.8 0.5 %bitcast_multiply_fusion = f32[1,64]{1,0:T(1,128)} fusion(f32[64]{0:T(128)S(1)} %shard_map.85, f32[1,64]{1,0:T(1,128)S(1)} %collective-permute-done.3, f32[1,64]{1,0:T(1,128)S(1)} %collective-permute-done.5), kind=kLoop, calls=%fused_computation.1 | loop fusion | flops 128 | bytes 1024 | tf_op jit(solution)/shard_map/mul | solution.py:159
  (3 shorter events, 0.1 us)
Async XLA Ops:
  2.9 7.9 %collective-permute-start.2 = (bf16[64,4096]{1,0:T(8,128)(2,1)S(1)}, bf16[64,4096]{1,0:T(8,128)(2,1)S(1)}, u32[]{:S(2)}, u32[]{:S(2)}) collective-permute-start(bf16[64,4096]{1,0:T(8,128)(2,1)S(1)} %get-tuple-element.8.own_block), channel_id=1, source_target_pairs={{0,1},{1,0},{2,3},{3,2},{4,5},{5,4},{6,7},{7,6},{8,9},{9,8},{10,11... | collective-permute-start | bytes 1572872 | tf_op jit(solution)/shard_map/ppermute | solution.py:102
  3.4 1.5 %collective-permute-start = (bf16[1,4096]{1,0:T(2,128)(2,1)S(1)}, bf16[1,4096]{1,0:T(2,128)(2,1)S(1)}, u32[]{:S(2)}, u32[]{:S(2)}) collective-permute-start(bf16[1,4096]{1,0:T(2,128)(2,1)S(1)} %convert.11), channel_id=1, source_target_pairs={{0,1},{1,0},{2,3},{3,2},{4,5},{5,4},{6,7},{7,6},{8,9},{9,8},{10,11... | collective-permute-start | bytes 24584 | tf_op jit(solution)/shard_map/ppermute | solution.py:102
  5.0 5.7 %collective-permute-start.1 = (bf16[2,4096]{1,0:T(2,128)(2,1)S(1)}, bf16[2,4096]{1,0:T(2,128)(2,1)S(1)}, u32[]{:S(2)}, u32[]{:S(2)}) collective-permute-start(bf16[2,4096]{1,0:T(2,128)(2,1)S(1)} %pad_maximum_fusion.rows), channel_id=1, source_target_pairs={{8,0},{12,1},{3,2},{6,3},{5,4},{9,5},{15,6},{2,7},{0,8},{4,9},{14,... | collective-permute-start | bytes 49160 | tf_op jit(solution)/shard_map/ppermute | solution.py:109
  9.0 5.0 %collective-permute-start.4 = (bf16[2,4096]{1,0:T(2,128)(2,1)S(1)}, bf16[2,4096]{1,0:T(2,128)(2,1)S(1)}, u32[]{:S(2)}, u32[]{:S(2)}) collective-permute-start(bf16[2,4096]{1,0:T(2,128)(2,1)S(1)} %pad_maximum_fusion.rows), channel_id=1, source_target_pairs={{4,0},{0,1},{11,2},{14,3},{1,4},{13,5},{10,6},{6,7},{12,8},{8,9},{... | collective-permute-start | bytes 49160 | tf_op jit(solution)/shard_map/ppermute | solution.py:109
  11.1 4.7 %collective-permute-start.3 = (f32[1,64]{1,0:T(1,128)S(1)}, f32[1,64]{1,0:T(1,128)S(1)}, u32[]{:S(2)}, u32[]{:S(2)}) collective-permute-start(f32[1,64]{1,0:T(1,128)S(1)} %shard_map.83), channel_id=1, source_target_pairs={{0,8},{1,12},{2,0},{3,4},{4,5},{5,9},{6,13},{7,1},{8,2},{9,6},{10,... | collective-permute-start | bytes 776 | tf_op jit(solution)/shard_map/ppermute | solution.py:115
  14.4 1.4 %collective-permute-start.5 = (f32[1,64]{1,0:T(1,128)S(1)}, f32[1,64]{1,0:T(1,128)S(1)}, u32[]{:S(2)}, u32[]{:S(2)}) collective-permute-start(f32[1,64]{1,0:T(1,128)S(1)} %shard_map.84), channel_id=1, source_target_pairs={{0,4},{1,0},{2,8},{3,12},{4,1},{5,13},{6,9},{7,5},{8,14},{9,10},{1... | collective-permute-start | bytes 776 | tf_op jit(solution)/shard_map/ppermute | solution.py:115

commit v24 on v21

--- a/solution.py
+++ b/solution.py
@@ -14,42 +14,36 @@
 SECOND_FROM = ((0, 0, 3, 2), (1, 1, 2, 2), (0, 0, 2, 3), (1, 1, 3, 3))
 
 
-PARTS = 4
+def pair_kernel(seq_len, acts, grads, proj_in, proj_out, lengths, out, *scratch):
+    *held, square_v, lengths_s, sems = scratch
+    limits = pltpu.make_async_copy(lengths, lengths_s, sems.at[len(held)])
+    limits.start()
+    loads = []
+    for src, dst, queue in zip((acts, proj_in, grads, proj_out), held, (0, 1, 1, 0)):
+        loads.append(pltpu.make_async_copy(src, dst, sems.at[len(loads)]))
+        loads[-1].start(priority=queue)
 
+    def project(first):
+        for copy in loads[first : first + 2]:
+            copy.wait()
+        tokens, proj = held[first : first + 2]
+        return lax.dot_general(
+            tokens[...], proj[...], (((1,), (1,)), ((), ())), preferred_element_type=jnp.float32
+        )
 
-def pair_kernel(seq_len, acts, grads, proj_in, proj_out, lengths, out, *scratch):
-    tokens_v, proj_v, turned_v, kron_v, lengths_s, sems = scratch
-    tokens = acts.shape[0]
-    rank, model_width = proj_in.shape
-    limits = pltpu.make_async_copy(lengths, lengths_s, sems.at[4])
-    loads = [
-        pltpu.make_async_copy(src, dst.at[pl.ds(half * src.shape[0], src.shape[0])], sems.at[2 * i + half])
-        for i, (pair, dst) in enumerate((((proj_in, proj_out), proj_v), ((acts, grads), tokens_v)))
-        for half, src in enumerate(pair)
-    ]
-    limits.start()
-    for i, copy in enumerate(loads):
-        copy.start(priority=i % 2)
+    coords = project(0)
     limits.wait()
-    token = lax.broadcasted_iota(jnp.int32, (tokens, 1), 0)
+    token = lax.broadcasted_iota(jnp.int32, (coords.shape[0], 1), 0)
     side = token // seq_len
     live = token - side * seq_len < jnp.where(side == 0, lengths_s[0, 0], lengths_s[0, 1])
     weight = jnp.where(live, jnp.where(side == 0, 1.0, -1.0), 0.0)
-    for copy in loads[:2]:
-        copy.wait()
-    width = model_width // PARTS
-    for c in range(PARTS):
-        turned_v[pl.ds(c * width, width), :] = proj_v[:, pl.ds(c * width, width)].T
-    for copy in loads[2:]:
-        copy.wait()
-    coords = jnp.dot(tokens_v[...], turned_v[...], preferred_element_type=jnp.float32)
-    in_coords = (coords[:tokens, :rank] * weight).astype(jnp.bfloat16)
-    out_coords = coords[tokens:, rank:].astype(jnp.bfloat16)
-    kron_v[...] = lax.dot_general(
+    in_coords = (coords * weight).astype(jnp.bfloat16)
+    out_coords = project(2).astype(jnp.bfloat16)
+    square_v[...] = lax.dot_general(
         out_coords, in_coords, (((0,), (0,)), ((), ())), preferred_element_type=jnp.float32
     )
-    half = rank // 2
-    out[...] = jnp.concatenate([kron_v[pl.ds(i, half, stride=2), :] for i in range(2)], axis=1)
+    half = square_v.shape[0] // 2
+    out[...] = jnp.concatenate([square_v[pl.ds(i, half, stride=2), :] for i in range(2)], axis=1)
 
 
 def pair_gradient(acts_in, grads_out, proj_in, proj_out, lengths):
@@ -62,9 +56,7 @@
         in_specs=[pl.BlockSpec(memory_space=pl.ANY)] * 5,
         out_specs=pl.BlockSpec(memory_space=pltpu.VMEM),
         scratch_shapes=[
-            pltpu.VMEM((2 * tokens, model_width), jnp.bfloat16),
-            pltpu.VMEM((2 * rank, model_width), jnp.bfloat16),
-            pltpu.VMEM((model_width, 2 * rank), jnp.bfloat16),
+            *(pltpu.VMEM((rows, model_width), jnp.bfloat16) for rows in (tokens, rank, tokens, rank)),
             pltpu.VMEM((rank, rank), jnp.float32),
             pltpu.SMEM((1, 2), jnp.int32),
             pltpu.SemaphoreType.DMA((5,)),

time: 16.1 us -> 16.3 us (1.012)
  Pallas kernels: 3.72 us -> 3.98 us
    pallas_call x1, Pallas kernels: 2.96 us -> 3.23 us  [pair_gradient(): pl.pallas_call(functools.partial(pair_kernel, seq_len), out_shape=jax.Sha...]
  transfers between devices with their start and end apart: 6 -> 6, of which waited for: 2 -> 2; matrix products, arithmetic and copies ran while one was open for 0% -> 0% of each run, Pallas kernels for 24% -> 25%
where the time goes in v24:
time: 16.3 us; the launch traced here: 16.1 us
  starting transfers between devices  8.4 us (52%)
  Pallas kernels  3.98 us (24%)
  waiting for transfers between devices  1.78 us (11%)
  between operations  1.37 us (8%)
  other arithmetic  0.57 us (3%)
    ppermute x2, starting transfers between devices, fetch_pair(): return lax.ppermute(x, ('dp', 'layer'), moves)  4.88 us
    pallas_call x1, Pallas kernels, pair_gradient(): pl.pallas_call(functools.partial(pair_kernel, seq_len), out_shape=jax.Sha...  3.23 us
    ppermute x2, starting transfers between devices, to_owner(): return lax.ppermute(x, ('dp', 'layer'), moves)  2.94 us
    ppermute x2, waiting for transfers between devices, swap(): lax.ppermute(x, 'layer', [(i, i ^ 1) for i in range(lax.axis_size('layer'...  1.13 us
    pallas_call x2, Pallas kernels, score(): pl.pallas_call(functools.partial(slot_kernel, senders), out_shape=jax.Sha...  0.75 us
    ppermute x2, waiting for transfers between devices, fetch_pair(): return lax.ppermute(x, ('dp', 'layer'), moves)  0.65 us
    ppermute x2, starting transfers between devices, swap(): lax.ppermute(x, 'layer', [(i, i ^ 1) for i in range(lax.axis_size('layer'...  0.57 us
    mul x1, other arithmetic, shared_scores(): return (to_owner(first, FIRST) + to_owner(second, SECOND)) * factor[None]  0.52 us
  transfers between devices with their start and end apart: 6, of which 2 were waited for; matrix products, arithmetic and copies ran while one was open for 0% of the time, Pallas kernels for 25%

profile of v24, /device:TPU:0, one launch (start us, length us, event | category | flops | bytes accessed | tf_op | source)
XLA Modules:
  0.0 16.1 jit_solution(172089468332560002)
XLA Ops:
  0.0 0.5 %collective-permute-start.2 = (bf16[64,4096]{1,0:T(8,128)(2,1)}, bf16[64,4096]{1,0:T(8,128)(2,1)S(1)}, u32[]{:S(2)}, u32[]{:S(2)}) collective-permute-start(bf16[64,4096]{1,0:T(8,128)(2,1)} %bitcast.12), channel_id=1, source_target_pairs={{0,1},{1,0},{2,3},{3,2},{4,5},{5,4},{6,7},{7,6},{8,9},{9,8},{10,11... | collective-permute-start | bytes 1572872 | tf_op jit(solution)/shard_map/ppermute | solution.py:86
  0.5 0.0 copy-start
  0.5 3.2 %shard_map.82 = f32[32,128]{1,0:T(8,128)S(1)} custom-call(bf16[128,4096]{1,0:T(8,128)(2,1)} %bitcast.16, bf16[128,4096]{1,0:T(8,128)(2,1)} %bitcast.17, bf16[64,4096]{1,0:T(8,128)(2,1)} %bitcast.18, bf16[64,4096]{1,0:T(8,128)(2,1)} %bitcast.19, s32[1,2]{1,0:T(1,128)} %lengths.1), custom_call_target="tpu_custom_call" | custom-call | flops 134217728 | bytes 3145728 | tf_op jit(solution)/shard_map/pallas_call | solution.py:53
  3.7 0.1 collective-permute-start
  3.8 1.1 %collective-permute-done = bf16[1,4096]{1,0:T(2,128)(2,1)S(1)} collective-permute-done((bf16[1,4096]{1,0:T(2,128)(2,1)S(1)}, bf16[1,4096]{1,0:T(2,128)(2,1)S(1)}, u32[]{:S(2)}, u32[]{:S(2)}) %collective-permute-start) | collective-permute-done | bytes 8224 | tf_op jit(solution)/shard_map/ppermute | solution.py:86
  5.0 3.8 %collective-permute-start.1 = (bf16[2,4096]{1,0:T(2,128)(2,1)S(1)}, bf16[2,4096]{1,0:T(2,128)(2,1)S(1)}, u32[]{:S(2)}, u32[]{:S(2)}) collective-permute-start(bf16[2,4096]{1,0:T(2,128)(2,1)S(1)} %pad_maximum_fusion.rows), channel_id=1, source_target_pairs={{8,0},{12,1},{3,2},{6,3},{5,4},{9,5},{15,6},{2,7},{0,8},{4,9},{14,... | collective-permute-start | bytes 49160 | tf_op jit(solution)/shard_map/ppermute | solution.py:93
  8.8 1.1 %collective-permute-start.4 = (bf16[2,4096]{1,0:T(2,128)(2,1)S(1)}, bf16[2,4096]{1,0:T(2,128)(2,1)S(1)}, u32[]{:S(2)}, u32[]{:S(2)}) collective-permute-start(bf16[2,4096]{1,0:T(2,128)(2,1)S(1)} %pad_maximum_fusion.rows), channel_id=1, source_target_pairs={{4,0},{0,1},{11,2},{14,3},{1,4},{13,5},{10,6},{6,7},{12,8},{8,9},{... | collective-permute-start | bytes 49160 | tf_op jit(solution)/shard_map/ppermute | solution.py:93
  9.9 0.6 %collective-permute-done.1.rows = bf16[2,4096]{1,0:T(2,128)(2,1)S(1)} collective-permute-done((bf16[2,4096]{1,0:T(2,128)(2,1)S(1)}, bf16[2,4096]{1,0:T(2,128)(2,1)S(1)}, u32[]{:S(2)}, u32[]{:S(2)}) %collective-permute-start.1) | collective-permute-done | bytes 16416 | tf_op jit(solution)/shard_map/ppermute | solution.py:93
  10.5 0.0 collective-permute-done.2.other_block
  10.5 0.0 copy-done
  10.5 0.4 %shard_map.83 = f32[1,64]{1,0:T(1,128)S(1)} custom-call(bf16[2,4096]{1,0:T(2,128)(2,1)S(1)} %collective-permute-done.1.rows, bf16[64,4096]{1,0:T(8,128)(2,1)S(1)} %bitcast.13, bf16[64,4096]{1,0:T(8,128)(2,1)S(1)} %collective-permute-done.2.other_block), custom_call_target="tpu_custom_call" | custom-call | flops 2097152 | bytes 1048576 | tf_op jit(solution)/shard_map/pallas_call | solution.py:132
  10.9 2.9 %collective-permute-start.3 = (f32[1,64]{1,0:T(1,128)S(1)}, f32[1,64]{1,0:T(1,128)S(1)}, u32[]{:S(2)}, u32[]{:S(2)}) collective-permute-start(f32[1,64]{1,0:T(1,128)S(1)} %shard_map.83), channel_id=1, source_target_pairs={{0,8},{1,12},{2,0},{3,4},{4,5},{5,9},{6,13},{7,1},{8,2},{9,6},{10,... | collective-permute-start | bytes 776 | tf_op jit(solution)/shard_map/ppermute | solution.py:99
  13.9 0.0 collective-permute-done.4.rows
  13.9 0.4 %shard_map.84 = f32[1,64]{1,0:T(1,128)S(1)} custom-call(bf16[2,4096]{1,0:T(2,128)(2,1)S(1)} %collective-permute-done.4.rows, bf16[64,4096]{1,0:T(8,128)(2,1)S(1)} %bitcast.14, bf16[64,4096]{1,0:T(8,128)(2,1)S(1)} %collective-permute-done.2.other_block), custom_call_target="tpu_custom_call" | custom-call | flops 2097152 | bytes 1048576 | tf_op jit(solution)/shard_map/pallas_call | solution.py:132
  14.2 0.0 collective-permute-start.5
  15.6 0.0 collective-permute-done.3
  15.6 0.0 collective-permute-done.5
  15.6 0.5 %bitcast_multiply_fusion = f32[1,64]{1,0:T(1,128)} fusion(f32[64]{0:T(128)S(1)} %shard_map.85, f32[1,64]{1,0:T(1,128)S(1)} %collective-permute-done.3, f32[1,64]{1,0:T(1,128)S(1)} %collective-permute-done.5), kind=kLoop, calls=%fused_computation.1 | loop fusion | flops 128 | bytes 1024 | tf_op jit(solution)/shard_map/mul | solution.py:142
  (3 shorter events, 0.1 us)
Async XLA Ops:
  0.0 10.5 %collective-permute-start.2 = (bf16[64,4096]{1,0:T(8,128)(2,1)}, bf16[64,4096]{1,0:T(8,128)(2,1)S(1)}, u32[]{:S(2)}, u32[]{:S(2)}) collective-permute-start(bf16[64,4096]{1,0:T(8,128)(2,1)} %bitcast.12), channel_id=1, source_target_pairs={{0,1},{1,0},{2,3},{3,2},{4,5},{5,4},{6,7},{7,6},{8,9},{9,8},{10,11... | collective-permute-start | bytes 1572872 | tf_op jit(solution)/shard_map/ppermute | solution.py:86
  0.5 10.1 %copy-start = (bf16[64,1,4096]{2,0,1:T(8,128)(2,1)S(1)}, bf16[64,1,4096]{2,0,1:T(8,128)(2,1)}, u32[]{:S(2)}) copy-start(bf16[64,1,4096]{2,0,1:T(8,128)(2,1)} %param.12) | copy-start | bytes 1572868
  3.7 1.2 %collective-permute-start = (bf16[1,4096]{1,0:T(2,128)(2,1)S(1)}, bf16[1,4096]{1,0:T(2,128)(2,1)S(1)}, u32[]{:S(2)}, u32[]{:S(2)}) collective-permute-start(bf16[1,4096]{1,0:T(2,128)(2,1)S(1)} %convert.11), channel_id=1, source_target_pairs={{0,1},{1,0},{2,3},{3,2},{4,5},{5,4},{6,7},{7,6},{8,9},{9,8},{10,11... | collective-permute-start | bytes 24584 | tf_op jit(solution)/shard_map/ppermute | solution.py:86
  5.0 5.5 %collective-permute-start.1 = (bf16[2,4096]{1,0:T(2,128)(2,1)S(1)}, bf16[2,4096]{1,0:T(2,128)(2,1)S(1)}, u32[]{:S(2)}, u32[]{:S(2)}) collective-permute-start(bf16[2,4096]{1,0:T(2,128)(2,1)S(1)} %pad_maximum_fusion.rows), channel_id=1, source_target_pairs={{8,0},{12,1},{3,2},{6,3},{5,4},{9,5},{15,6},{2,7},{0,8},{4,9},{14,... | collective-permute-start | bytes 49160 | tf_op jit(solution)/shard_map/ppermute | solution.py:93
  8.8 5.0 %collective-permute-start.4 = (bf16[2,4096]{1,0:T(2,128)(2,1)S(1)}, bf16[2,4096]{1,0:T(2,128)(2,1)S(1)}, u32[]{:S(2)}, u32[]{:S(2)}) collective-permute-start(bf16[2,4096]{1,0:T(2,128)(2,1)S(1)} %pad_maximum_fusion.rows), channel_id=1, source_target_pairs={{4,0},{0,1},{11,2},{14,3},{1,4},{13,5},{10,6},{6,7},{12,8},{8,9},{... | collective-permute-start | bytes 49160 | tf_op jit(solution)/shard_map/ppermute | solution.py:93
  10.9 4.7 %collective-permute-start.3 = (f32[1,64]{1,0:T(1,128)S(1)}, f32[1,64]{1,0:T(1,128)S(1)}, u32[]{:S(2)}, u32[]{:S(2)}) collective-permute-start(f32[1,64]{1,0:T(1,128)S(1)} %shard_map.83), channel_id=1, source_target_pairs={{0,8},{1,12},{2,0},{3,4},{4,5},{5,9},{6,13},{7,1},{8,2},{9,6},{10,... | collective-permute-start | bytes 776 | tf_op jit(solution)/shard_map/ppermute | solution.py:99
  14.2 1.4 %collective-permute-start.5 = (f32[1,64]{1,0:T(1,128)S(1)}, f32[1,64]{1,0:T(1,128)S(1)}, u32[]{:S(2)}, u32[]{:S(2)}) collective-permute-start(f32[1,64]{1,0:T(1,128)S(1)} %shard_map.84), channel_id=1, source_target_pairs={{0,4},{1,0},{2,8},{3,12},{4,1},{5,13},{6,9},{7,5},{8,14},{9,10},{1... | collective-permute-start | bytes 776 | tf_op jit(solution)/shard_map/ppermute | solution.py:99

commit v25 on v22

--- a/solution.py
+++ b/solution.py
@@ -14,35 +14,39 @@
 SECOND_FROM = ((0, 0, 3, 2), (1, 1, 2, 2), (0, 0, 2, 3), (1, 1, 3, 3))
 
 
-PARTS = 4
+CHUNKS = 2
 
 
 def pair_kernel(seq_len, acts, grads, proj_in, proj_out, lengths, out, *scratch):
-    tokens_v, proj_v, turned_v, square_v, lengths_s, sems = scratch
+    tokens_v, proj_v, square_v, lengths_s, sems, lengths_sem = scratch
     tokens = acts.shape[0]
     rank, model_width = proj_in.shape
-    limits = pltpu.make_async_copy(lengths, lengths_s, sems.at[4])
-    loads = [
-        pltpu.make_async_copy(src, dst.at[pl.ds(half * src.shape[0], src.shape[0])], sems.at[2 * i + half])
-        for i, (pair, dst) in enumerate((((proj_in, proj_out), proj_v), ((acts, grads), tokens_v)))
-        for half, src in enumerate(pair)
-    ]
+    width = model_width // CHUNKS
+    limits = pltpu.make_async_copy(lengths, lengths_s, lengths_sem)
     limits.start()
-    for i, copy in enumerate(loads):
-        copy.start(priority=i % 2)
+    loads = []
+    for c in range(CHUNKS):
+        part = pl.ds(c * width, width)
+        loads.append([])
+        for pair, dst in (((proj_in, proj_out), proj_v), ((acts, grads), tokens_v)):
+            for half, src in enumerate(pair):
+                to = dst.at[pl.ds(half * src.shape[0], src.shape[0]), part]
+                loads[c].append(pltpu.make_async_copy(src.at[:, part], to, sems.at[c, len(loads[c])]))
+                loads[c][-1].start(priority=CHUNKS - 1 - c)
     limits.wait()
     token = lax.broadcasted_iota(jnp.int32, (tokens, 1), 0)
     side = token // seq_len
     live = token - side * seq_len < jnp.where(side == 0, lengths_s[0, 0], lengths_s[0, 1])
     weight = jnp.where(live, jnp.where(side == 0, 1.0, -1.0), 0.0)
-    for copy in loads[:2]:
-        copy.wait()
-    width = model_width // PARTS
-    for c in range(PARTS):
-        turned_v[pl.ds(c * width, width), :] = proj_v[:, pl.ds(c * width, width)].T
-    for copy in loads[2:]:
-        copy.wait()
-    coords = jnp.dot(tokens_v[...], turned_v[...], preferred_element_type=jnp.float32)
+    coords = None
+    for c, copies in enumerate(loads):
+        for copy in copies:
+            copy.wait()
+        part = pl.ds(c * width, width)
+        term = lax.dot_general(
+            tokens_v[:, part], proj_v[:, part], (((1,), (1,)), ((), ())), preferred_element_type=jnp.float32
+        )
+        coords = term if coords is None else coords + term
     square_v[...] = lax.dot_general(
         coords[tokens:].astype(jnp.bfloat16),
         (coords[:tokens] * weight).astype(jnp.bfloat16),
@@ -65,10 +69,10 @@
         scratch_shapes=[
             pltpu.VMEM((2 * tokens, model_width), jnp.bfloat16),
             pltpu.VMEM((2 * rank, model_width), jnp.bfloat16),
-            pltpu.VMEM((model_width, 2 * rank), jnp.bfloat16),
             pltpu.VMEM((2 * rank, 2 * rank), jnp.float32),
             pltpu.SMEM((1, 2), jnp.int32),
-            pltpu.SemaphoreType.DMA((5,)),
+            pltpu.SemaphoreType.DMA((CHUNKS, 4)),
+            pltpu.SemaphoreType.DMA,
         ],
         compiler_params=pltpu.CompilerParams(vmem_limit_bytes=32 * 1024 * 1024),
         cost_estimate=pl.CostEstimate(

time: 16 us -> 16.1 us (level)
  transfers between devices with their start and end apart: 6 -> 6, of which waited for: 2 -> 2; matrix products, arithmetic and copies ran while one was open for 0% -> 0% of each run, Pallas kernels for 23% -> 24%
where the time goes in v25:
time: 16.1 us; the launch traced here: 15.9 us
  starting transfers between devices  8.41 us (52%)
  Pallas kernels  3.78 us (23%)
  waiting for transfers between devices  1.77 us (11%)
  between operations  1.37 us (9%)
  other arithmetic  0.57 us (4%)
    ppermute x2, starting transfers between devices, fetch_pair(): return lax.ppermute(x, ('dp', 'layer'), moves)  4.89 us
    pallas_call x1, Pallas kernels, pair_gradient(): pl.pallas_call(functools.partial(pair_kernel, seq_len), out_shape=jax.Sha...  3.02 us
    ppermute x2, starting transfers between devices, to_owner(): return lax.ppermute(x, ('dp', 'layer'), moves)  2.94 us
    ppermute x2, waiting for transfers between devices, swap(): lax.ppermute(x, 'layer', [(i, i ^ 1) for i in range(lax.axis_size('layer'...  1.13 us
    pallas_call x2, Pallas kernels, score(): pl.pallas_call(functools.partial(slot_kernel, senders), out_shape=jax.Sha...  0.75 us
    ppermute x2, waiting for transfers between devices, fetch_pair(): return lax.ppermute(x, ('dp', 'layer'), moves)  0.64 us
    ppermute x2, starting transfers between devices, swap(): lax.ppermute(x, 'layer', [(i, i ^ 1) for i in range(lax.axis_size('layer'...  0.58 us
    mul x1, other arithmetic, shared_scores(): return (to_owner(first, FIRST) + to_owner(second, SECOND)) * factor[None]  0.52 us
  transfers between devices with their start and end apart: 6, of which 2 were waited for; matrix products, arithmetic and copies ran while one was open for 0% of the time, Pallas kernels for 24%

profile of v25, /device:TPU:0, one launch (start us, length us, event | category | flops | bytes accessed | tf_op | source)
XLA Modules:
  0.0 15.9 jit_solution(14072341613354985822)
XLA Ops:
  0.0 0.5 %collective-permute-start.2 = (bf16[64,4096]{1,0:T(8,128)(2,1)}, bf16[64,4096]{1,0:T(8,128)(2,1)S(1)}, u32[]{:S(2)}, u32[]{:S(2)}) collective-permute-start(bf16[64,4096]{1,0:T(8,128)(2,1)} %bitcast.12), channel_id=1, source_target_pairs={{0,1},{1,0},{2,3},{3,2},{4,5},{5,4},{6,7},{7,6},{8,9},{9,8},{10,11... | collective-permute-start | bytes 1572872 | tf_op jit(solution)/shard_map/ppermute | solution.py:99
  0.5 0.0 copy-start
  0.5 3.0 %shard_map.82 = f32[32,128]{1,0:T(8,128)S(1)} custom-call(bf16[128,4096]{1,0:T(8,128)(2,1)} %bitcast.16, bf16[128,4096]{1,0:T(8,128)(2,1)} %bitcast.17, bf16[64,4096]{1,0:T(8,128)(2,1)} %bitcast.18, bf16[64,4096]{1,0:T(8,128)(2,1)} %bitcast.19, s32[1,2]{1,0:T(1,128)} %lengths.1), custom_call_target="tpu_custom_call" | custom-call | flops 134217728 | bytes 3145728 | tf_op jit(solution)/shard_map/pallas_call | solution.py:64
  3.5 0.1 collective-permute-start
  3.6 1.1 %collective-permute-done = bf16[1,4096]{1,0:T(2,128)(2,1)S(1)} collective-permute-done((bf16[1,4096]{1,0:T(2,128)(2,1)S(1)}, bf16[1,4096]{1,0:T(2,128)(2,1)S(1)}, u32[]{:S(2)}, u32[]{:S(2)}) %collective-permute-start) | collective-permute-done | bytes 8224 | tf_op jit(solution)/shard_map/ppermute | solution.py:99
  4.8 3.8 %collective-permute-start.1 = (bf16[2,4096]{1,0:T(2,128)(2,1)S(1)}, bf16[2,4096]{1,0:T(2,128)(2,1)S(1)}, u32[]{:S(2)}, u32[]{:S(2)}) collective-permute-start(bf16[2,4096]{1,0:T(2,128)(2,1)S(1)} %pad_maximum_fusion.rows), channel_id=1, source_target_pairs={{8,0},{12,1},{3,2},{6,3},{5,4},{9,5},{15,6},{2,7},{0,8},{4,9},{14,... | collective-permute-start | bytes 49160 | tf_op jit(solution)/shard_map/ppermute | solution.py:106
  8.6 1.1 %collective-permute-start.4 = (bf16[2,4096]{1,0:T(2,128)(2,1)S(1)}, bf16[2,4096]{1,0:T(2,128)(2,1)S(1)}, u32[]{:S(2)}, u32[]{:S(2)}) collective-permute-start(bf16[2,4096]{1,0:T(2,128)(2,1)S(1)} %pad_maximum_fusion.rows), channel_id=1, source_target_pairs={{4,0},{0,1},{11,2},{14,3},{1,4},{13,5},{10,6},{6,7},{12,8},{8,9},{... | collective-permute-start | bytes 49160 | tf_op jit(solution)/shard_map/ppermute | solution.py:106
  9.7 0.6 %collective-permute-done.1.rows = bf16[2,4096]{1,0:T(2,128)(2,1)S(1)} collective-permute-done((bf16[2,4096]{1,0:T(2,128)(2,1)S(1)}, bf16[2,4096]{1,0:T(2,128)(2,1)S(1)}, u32[]{:S(2)}, u32[]{:S(2)}) %collective-permute-start.1) | collective-permute-done | bytes 16416 | tf_op jit(solution)/shard_map/ppermute | solution.py:106
  10.3 0.0 collective-permute-done.2.other_block
  10.3 0.0 copy-done
  10.3 0.4 %shard_map.83 = f32[1,64]{1,0:T(1,128)S(1)} custom-call(bf16[2,4096]{1,0:T(2,128)(2,1)S(1)} %collective-permute-done.1.rows, bf16[64,4096]{1,0:T(8,128)(2,1)S(1)} %bitcast.13, bf16[64,4096]{1,0:T(8,128)(2,1)S(1)} %collective-permute-done.2.other_block), custom_call_target="tpu_custom_call" | custom-call | flops 2097152 | bytes 1048576 | tf_op jit(solution)/shard_map/pallas_call | solution.py:145
  10.7 2.9 %collective-permute-start.3 = (f32[1,64]{1,0:T(1,128)S(1)}, f32[1,64]{1,0:T(1,128)S(1)}, u32[]{:S(2)}, u32[]{:S(2)}) collective-permute-start(f32[1,64]{1,0:T(1,128)S(1)} %shard_map.83), channel_id=1, source_target_pairs={{0,8},{1,12},{2,0},{3,4},{4,5},{5,9},{6,13},{7,1},{8,2},{9,6},{10,... | collective-permute-start | bytes 776 | tf_op jit(solution)/shard_map/ppermute | solution.py:112
  13.6 0.0 collective-permute-done.4.rows
  13.7 0.4 %shard_map.84 = f32[1,64]{1,0:T(1,128)S(1)} custom-call(bf16[2,4096]{1,0:T(2,128)(2,1)S(1)} %collective-permute-done.4.rows, bf16[64,4096]{1,0:T(8,128)(2,1)S(1)} %bitcast.14, bf16[64,4096]{1,0:T(8,128)(2,1)S(1)} %collective-permute-done.2.other_block), custom_call_target="tpu_custom_call" | custom-call | flops 2097152 | bytes 1048576 | tf_op jit(solution)/shard_map/pallas_call | solution.py:145
  14.0 0.0 collective-permute-start.5
  15.4 0.0 collective-permute-done.3
  15.4 0.0 collective-permute-done.5
  15.4 0.5 %bitcast_multiply_fusion = f32[1,64]{1,0:T(1,128)} fusion(f32[64]{0:T(128)S(1)} %shard_map.85, f32[1,64]{1,0:T(1,128)S(1)} %collective-permute-done.3, f32[1,64]{1,0:T(1,128)S(1)} %collective-permute-done.5), kind=kLoop, calls=%fused_computation.1 | loop fusion | flops 128 | bytes 1024 | tf_op jit(solution)/shard_map/mul | solution.py:155
  (3 shorter events, 0.1 us)
Async XLA Ops:
  0.0 10.3 %collective-permute-start.2 = (bf16[64,4096]{1,0:T(8,128)(2,1)}, bf16[64,4096]{1,0:T(8,128)(2,1)S(1)}, u32[]{:S(2)}, u32[]{:S(2)}) collective-permute-start(bf16[64,4096]{1,0:T(8,128)(2,1)} %bitcast.12), channel_id=1, source_target_pairs={{0,1},{1,0},{2,3},{3,2},{4,5},{5,4},{6,7},{7,6},{8,9},{9,8},{10,11... | collective-permute-start | bytes 1572872 | tf_op jit(solution)/shard_map/ppermute | solution.py:99
  0.5 9.9 %copy-start = (bf16[64,1,4096]{2,0,1:T(8,128)(2,1)S(1)}, bf16[64,1,4096]{2,0,1:T(8,128)(2,1)}, u32[]{:S(2)}) copy-start(bf16[64,1,4096]{2,0,1:T(8,128)(2,1)} %param.12) | copy-start | bytes 1572868
  3.5 1.2 %collective-permute-start = (bf16[1,4096]{1,0:T(2,128)(2,1)S(1)}, bf16[1,4096]{1,0:T(2,128)(2,1)S(1)}, u32[]{:S(2)}, u32[]{:S(2)}) collective-permute-start(bf16[1,4096]{1,0:T(2,128)(2,1)S(1)} %convert.11), channel_id=1, source_target_pairs={{0,1},{1,0},{2,3},{3,2},{4,5},{5,4},{6,7},{7,6},{8,9},{9,8},{10,11... | collective-permute-start | bytes 24584 | tf_op jit(solution)/shard_map/ppermute | solution.py:99
  4.8 5.5 %collective-permute-start.1 = (bf16[2,4096]{1,0:T(2,128)(2,1)S(1)}, bf16[2,4096]{1,0:T(2,128)(2,1)S(1)}, u32[]{:S(2)}, u32[]{:S(2)}) collective-permute-start(bf16[2,4096]{1,0:T(2,128)(2,1)S(1)} %pad_maximum_fusion.rows), channel_id=1, source_target_pairs={{8,0},{12,1},{3,2},{6,3},{5,4},{9,5},{15,6},{2,7},{0,8},{4,9},{14,... | collective-permute-start | bytes 49160 | tf_op jit(solution)/shard_map/ppermute | solution.py:106
  8.6 5.0 %collective-permute-start.4 = (bf16[2,4096]{1,0:T(2,128)(2,1)S(1)}, bf16[2,4096]{1,0:T(2,128)(2,1)S(1)}, u32[]{:S(2)}, u32[]{:S(2)}) collective-permute-start(bf16[2,4096]{1,0:T(2,128)(2,1)S(1)} %pad_maximum_fusion.rows), channel_id=1, source_target_pairs={{4,0},{0,1},{11,2},{14,3},{1,4},{13,5},{10,6},{6,7},{12,8},{8,9},{... | collective-permute-start | bytes 49160 | tf_op jit(solution)/shard_map/ppermute | solution.py:106
  10.7 4.7 %collective-permute-start.3 = (f32[1,64]{1,0:T(1,128)S(1)}, f32[1,64]{1,0:T(1,128)S(1)}, u32[]{:S(2)}, u32[]{:S(2)}) collective-permute-start(f32[1,64]{1,0:T(1,128)S(1)} %shard_map.83), channel_id=1, source_target_pairs={{0,8},{1,12},{2,0},{3,4},{4,5},{5,9},{6,13},{7,1},{8,2},{9,6},{10,... | collective-permute-start | bytes 776 | tf_op jit(solution)/shard_map/ppermute | solution.py:112
  14.0 1.4 %collective-permute-start.5 = (f32[1,64]{1,0:T(1,128)S(1)}, f32[1,64]{1,0:T(1,128)S(1)}, u32[]{:S(2)}, u32[]{:S(2)}) collective-permute-start(f32[1,64]{1,0:T(1,128)S(1)} %shard_map.84), channel_id=1, source_target_pairs={{0,4},{1,0},{2,8},{3,12},{4,1},{5,13},{6,9},{7,5},{8,14},{9,10},{1... | collective-permute-start | bytes 776 | tf_op jit(solution)/shard_map/ppermute | solution.py:112

commit v26 on v22

--- a/solution.py
+++ b/solution.py
@@ -14,13 +14,25 @@
 SECOND_FROM = ((0, 0, 3, 2), (1, 1, 2, 2), (0, 0, 2, 3), (1, 1, 3, 3))
 
 
-PARTS = 4
+PROJECT_STEP = 1024
+SCORE_STEP = 1024
+
+
+def stepped(left, right, step):
+    def add(i, total):
+        part = pl.ds(pl.multiple_of(i * step, step), step)
+        return total + lax.dot_general(
+            left[:, part], right[:, part], (((1,), (1,)), ((), ())), preferred_element_type=jnp.float32
+        )
+
+    zero = jnp.zeros((left.shape[0], right.shape[0]), jnp.float32)
+    return lax.fori_loop(0, left.shape[1] // step, add, zero)
 
 
 def pair_kernel(seq_len, acts, grads, proj_in, proj_out, lengths, out, *scratch):
-    tokens_v, proj_v, turned_v, square_v, lengths_s, sems = scratch
+    tokens_v, proj_v, square_v, lengths_s, sems = scratch
     tokens = acts.shape[0]
-    rank, model_width = proj_in.shape
+    rank = proj_in.shape[0]
     limits = pltpu.make_async_copy(lengths, lengths_s, sems.at[4])
     loads = [
         pltpu.make_async_copy(src, dst.at[pl.ds(half * src.shape[0], src.shape[0])], sems.at[2 * i + half])
@@ -35,14 +47,9 @@
     side = token // seq_len
     live = token - side * seq_len < jnp.where(side == 0, lengths_s[0, 0], lengths_s[0, 1])
     weight = jnp.where(live, jnp.where(side == 0, 1.0, -1.0), 0.0)
-    for copy in loads[:2]:
+    for copy in loads:
         copy.wait()
-    width = model_width // PARTS
-    for c in range(PARTS):
-        turned_v[pl.ds(c * width, width), :] = proj_v[:, pl.ds(c * width, width)].T
-    for copy in loads[2:]:
-        copy.wait()
-    coords = jnp.dot(tokens_v[...], turned_v[...], preferred_element_type=jnp.float32)
+    coords = stepped(tokens_v, proj_v, PROJECT_STEP)
     square_v[...] = lax.dot_general(
         coords[tokens:].astype(jnp.bfloat16),
         (coords[:tokens] * weight).astype(jnp.bfloat16),
@@ -65,7 +72,6 @@
         scratch_shapes=[
             pltpu.VMEM((2 * tokens, model_width), jnp.bfloat16),
             pltpu.VMEM((2 * rank, model_width), jnp.bfloat16),
-            pltpu.VMEM((model_width, 2 * rank), jnp.bfloat16),
             pltpu.VMEM((2 * rank, 2 * rank), jnp.float32),
             pltpu.SMEM((1, 2), jnp.int32),
             pltpu.SemaphoreType.DMA((5,)),
@@ -112,10 +118,7 @@
     here = lax.axis_index("dp") * len(senders) + lax.axis_index("layer")
     crossed = [d * len(row) + i for d, row in enumerate(senders) for i, sender in enumerate(row) if sender != i]
     is_crossed = functools.reduce(jnp.logical_or, [here == i for i in crossed])
-    one, two = (
-        lax.dot_general(rows[...], block[...], (((1,), (1,)), ((), ())), preferred_element_type=jnp.float32)
-        for block in (own_block, other_block)
-    )
+    one, two = (stepped(rows, block, SCORE_STEP) for block in (own_block, other_block))
     out[...] = jnp.where(is_crossed, one[1:] + two[:1], one[:1] + two[1:])
 
 

time: 16 us -> 18.2 us (1.14)
  Pallas kernels: 3.66 us -> 5.86 us
    pallas_call x2, Pallas kernels: 0.75 us -> 2.43 us  [score(): pl.pallas_call(functools.partial(slot_kernel, senders), out_shape=jax.Sha...]
    pallas_call x1, Pallas kernels: 2.9 us -> 3.43 us  [pair_gradient(): pl.pallas_call(functools.partial(pair_kernel, seq_len), out_shape=jax.Sha...]
  transfers between devices with their start and end apart: 6 -> 6, of which waited for: 2 -> 2; matrix products, arithmetic and copies ran while one was open for 0% -> 0% of each run, Pallas kernels for 23% -> 33%
where the time goes in v26:
time: 18.2 us; the launch traced here: 18 us
  starting transfers between devices  8.43 us (46%)
  Pallas kernels  5.86 us (32%)
  waiting for transfers between devices  1.77 us (10%)
  between operations  1.37 us (8%)
  other arithmetic  0.57 us (3%)
    ppermute x2, starting transfers between devices, fetch_pair(): return lax.ppermute(x, ('dp', 'layer'), moves)  4.89 us
    pallas_call x1, Pallas kernels, pair_gradient(): pl.pallas_call(functools.partial(pair_kernel, seq_len), out_shape=jax.Sha...  3.43 us
    ppermute x2, starting transfers between devices, to_owner(): return lax.ppermute(x, ('dp', 'layer'), moves)  2.96 us
    pallas_call x2, Pallas kernels, score(): pl.pallas_call(functools.partial(slot_kernel, senders), out_shape=jax.Sha...  2.43 us
    ppermute x2, waiting for transfers between devices, swap(): lax.ppermute(x, 'layer', [(i, i ^ 1) for i in range(lax.axis_size('layer'...  1.12 us
    ppermute x2, waiting for transfers between devices, fetch_pair(): return lax.ppermute(x, ('dp', 'layer'), moves)  0.64 us
    ppermute x2, starting transfers between devices, swap(): lax.ppermute(x, 'layer', [(i, i ^ 1) for i in range(lax.axis_size('layer'...  0.58 us
    mul x1, other arithmetic, shared_scores(): return (to_owner(first, FIRST) + to_owner(second, SECOND)) * factor[None]  0.52 us
  transfers between devices with their start and end apart: 6, of which 2 were waited for; matrix products, arithmetic and copies ran while one was open for 0% of the time, Pallas kernels for 33%

profile of v26, /device:TPU:0, one launch (start us, length us, event | category | flops | bytes accessed | tf_op | source)
XLA Modules:
  0.0 18.0 jit_solution(2901782125993458373)
XLA Ops:
  0.0 0.5 %collective-permute-start.2 = (bf16[64,4096]{1,0:T(8,128)(2,1)}, bf16[64,4096]{1,0:T(8,128)(2,1)S(1)}, u32[]{:S(2)}, u32[]{:S(2)}) collective-permute-start(bf16[64,4096]{1,0:T(8,128)(2,1)} %bitcast.12), channel_id=1, source_target_pairs={{0,1},{1,0},{2,3},{3,2},{4,5},{5,4},{6,7},{7,6},{8,9},{9,8},{10,11... | collective-permute-start | bytes 1572872 | tf_op jit(solution)/shard_map/ppermute | solution.py:101
  0.5 0.0 copy-start
  0.5 3.4 %shard_map.82 = f32[32,128]{1,0:T(8,128)S(1)} custom-call(bf16[128,4096]{1,0:T(8,128)(2,1)} %bitcast.16, bf16[128,4096]{1,0:T(8,128)(2,1)} %bitcast.17, bf16[64,4096]{1,0:T(8,128)(2,1)} %bitcast.18, bf16[64,4096]{1,0:T(8,128)(2,1)} %bitcast.19, s32[1,2]{1,0:T(1,128)} %lengths.1), custom_call_target="tpu_custom_call" | custom-call | flops 134217728 | bytes 3145728 | tf_op jit(solution)/shard_map/pallas_call | solution.py:67
  3.9 0.1 collective-permute-start
  4.0 1.1 %collective-permute-done = bf16[1,4096]{1,0:T(2,128)(2,1)S(1)} collective-permute-done((bf16[1,4096]{1,0:T(2,128)(2,1)S(1)}, bf16[1,4096]{1,0:T(2,128)(2,1)S(1)}, u32[]{:S(2)}, u32[]{:S(2)}) %collective-permute-start) | collective-permute-done | bytes 8224 | tf_op jit(solution)/shard_map/ppermute | solution.py:101
  5.2 3.8 %collective-permute-start.1 = (bf16[2,4096]{1,0:T(2,128)(2,1)S(1)}, bf16[2,4096]{1,0:T(2,128)(2,1)S(1)}, u32[]{:S(2)}, u32[]{:S(2)}) collective-permute-start(bf16[2,4096]{1,0:T(2,128)(2,1)S(1)} %pad_maximum_fusion.rows), channel_id=1, source_target_pairs={{8,0},{12,1},{3,2},{6,3},{5,4},{9,5},{15,6},{2,7},{0,8},{4,9},{14,... | collective-permute-start | bytes 49160 | tf_op jit(solution)/shard_map/ppermute | solution.py:108
  9.0 1.1 %collective-permute-start.4 = (bf16[2,4096]{1,0:T(2,128)(2,1)S(1)}, bf16[2,4096]{1,0:T(2,128)(2,1)S(1)}, u32[]{:S(2)}, u32[]{:S(2)}) collective-permute-start(bf16[2,4096]{1,0:T(2,128)(2,1)S(1)} %pad_maximum_fusion.rows), channel_id=1, source_target_pairs={{4,0},{0,1},{11,2},{14,3},{1,4},{13,5},{10,6},{6,7},{12,8},{8,9},{... | collective-permute-start | bytes 49160 | tf_op jit(solution)/shard_map/ppermute | solution.py:108
  10.1 0.6 %collective-permute-done.1.rows = bf16[2,4096]{1,0:T(2,128)(2,1)S(1)} collective-permute-done((bf16[2,4096]{1,0:T(2,128)(2,1)S(1)}, bf16[2,4096]{1,0:T(2,128)(2,1)S(1)}, u32[]{:S(2)}, u32[]{:S(2)}) %collective-permute-start.1) | collective-permute-done | bytes 16416 | tf_op jit(solution)/shard_map/ppermute | solution.py:108
  10.7 0.0 collective-permute-done.2.other_block
  10.7 0.0 copy-done
  10.7 1.2 %shard_map.83 = f32[1,64]{1,0:T(1,128)S(1)} custom-call(bf16[2,4096]{1,0:T(2,128)(2,1)S(1)} %collective-permute-done.1.rows, bf16[64,4096]{1,0:T(8,128)(2,1)S(1)} %bitcast.13, bf16[64,4096]{1,0:T(8,128)(2,1)S(1)} %collective-permute-done.2.other_block), custom_call_target="tpu_custom_call" | custom-call | flops 2097152 | bytes 1048576 | tf_op jit(solution)/shard_map/pallas_call | solution.py:144
  12.0 2.9 %collective-permute-start.3 = (f32[1,64]{1,0:T(1,128)S(1)}, f32[1,64]{1,0:T(1,128)S(1)}, u32[]{:S(2)}, u32[]{:S(2)}) collective-permute-start(f32[1,64]{1,0:T(1,128)S(1)} %shard_map.83), channel_id=1, source_target_pairs={{0,8},{1,12},{2,0},{3,4},{4,5},{5,9},{6,13},{7,1},{8,2},{9,6},{10,... | collective-permute-start | bytes 776 | tf_op jit(solution)/shard_map/ppermute | solution.py:114
  14.9 0.0 collective-permute-done.4.rows
  14.9 1.2 %shard_map.84 = f32[1,64]{1,0:T(1,128)S(1)} custom-call(bf16[2,4096]{1,0:T(2,128)(2,1)S(1)} %collective-permute-done.4.rows, bf16[64,4096]{1,0:T(8,128)(2,1)S(1)} %bitcast.14, bf16[64,4096]{1,0:T(8,128)(2,1)S(1)} %collective-permute-done.2.other_block), custom_call_target="tpu_custom_call" | custom-call | flops 2097152 | bytes 1048576 | tf_op jit(solution)/shard_map/pallas_call | solution.py:144
  16.1 0.0 collective-permute-start.5
  17.5 0.0 collective-permute-done.3
  17.5 0.0 collective-permute-done.5
  17.5 0.5 %bitcast_multiply_fusion = f32[1,64]{1,0:T(1,128)} fusion(f32[64]{0:T(128)S(1)} %shard_map.85, f32[1,64]{1,0:T(1,128)S(1)} %collective-permute-done.3, f32[1,64]{1,0:T(1,128)S(1)} %collective-permute-done.5), kind=kLoop, calls=%fused_computation.1 | loop fusion | flops 128 | bytes 1024 | tf_op jit(solution)/shard_map/mul | solution.py:154
  (3 shorter events, 0.1 us)
Async XLA Ops:
  0.0 10.7 %collective-permute-start.2 = (bf16[64,4096]{1,0:T(8,128)(2,1)}, bf16[64,4096]{1,0:T(8,128)(2,1)S(1)}, u32[]{:S(2)}, u32[]{:S(2)}) collective-permute-start(bf16[64,4096]{1,0:T(8,128)(2,1)} %bitcast.12), channel_id=1, source_target_pairs={{0,1},{1,0},{2,3},{3,2},{4,5},{5,4},{6,7},{7,6},{8,9},{9,8},{10,11... | collective-permute-start | bytes 1572872 | tf_op jit(solution)/shard_map/ppermute | solution.py:101
  0.5 10.3 %copy-start = (bf16[64,1,4096]{2,0,1:T(8,128)(2,1)S(1)}, bf16[64,1,4096]{2,0,1:T(8,128)(2,1)}, u32[]{:S(2)}) copy-start(bf16[64,1,4096]{2,0,1:T(8,128)(2,1)} %param.12) | copy-start | bytes 1572868
  3.9 1.2 %collective-permute-start = (bf16[1,4096]{1,0:T(2,128)(2,1)S(1)}, bf16[1,4096]{1,0:T(2,128)(2,1)S(1)}, u32[]{:S(2)}, u32[]{:S(2)}) collective-permute-start(bf16[1,4096]{1,0:T(2,128)(2,1)S(1)} %convert.11), channel_id=1, source_target_pairs={{0,1},{1,0},{2,3},{3,2},{4,5},{5,4},{6,7},{7,6},{8,9},{9,8},{10,11... | collective-permute-start | bytes 24584 | tf_op jit(solution)/shard_map/ppermute | solution.py:101
  5.2 5.5 %collective-permute-start.1 = (bf16[2,4096]{1,0:T(2,128)(2,1)S(1)}, bf16[2,4096]{1,0:T(2,128)(2,1)S(1)}, u32[]{:S(2)}, u32[]{:S(2)}) collective-permute-start(bf16[2,4096]{1,0:T(2,128)(2,1)S(1)} %pad_maximum_fusion.rows), channel_id=1, source_target_pairs={{8,0},{12,1},{3,2},{6,3},{5,4},{9,5},{15,6},{2,7},{0,8},{4,9},{14,... | collective-permute-start | bytes 49160 | tf_op jit(solution)/shard_map/ppermute | solution.py:108
  9.0 5.9 %collective-permute-start.4 = (bf16[2,4096]{1,0:T(2,128)(2,1)S(1)}, bf16[2,4096]{1,0:T(2,128)(2,1)S(1)}, u32[]{:S(2)}, u32[]{:S(2)}) collective-permute-start(bf16[2,4096]{1,0:T(2,128)(2,1)S(1)} %pad_maximum_fusion.rows), channel_id=1, source_target_pairs={{4,0},{0,1},{11,2},{14,3},{1,4},{13,5},{10,6},{6,7},{12,8},{8,9},{... | collective-permute-start | bytes 49160 | tf_op jit(solution)/shard_map/ppermute | solution.py:108
  12.0 5.5 %collective-permute-start.3 = (f32[1,64]{1,0:T(1,128)S(1)}, f32[1,64]{1,0:T(1,128)S(1)}, u32[]{:S(2)}, u32[]{:S(2)}) collective-permute-start(f32[1,64]{1,0:T(1,128)S(1)} %shard_map.83), channel_id=1, source_target_pairs={{0,8},{1,12},{2,0},{3,4},{4,5},{5,9},{6,13},{7,1},{8,2},{9,6},{10,... | collective-permute-start | bytes 776 | tf_op jit(solution)/shard_map/ppermute | solution.py:114
  16.1 1.4 %collective-permute-start.5 = (f32[1,64]{1,0:T(1,128)S(1)}, f32[1,64]{1,0:T(1,128)S(1)}, u32[]{:S(2)}, u32[]{:S(2)}) collective-permute-start(f32[1,64]{1,0:T(1,128)S(1)} %shard_map.84), channel_id=1, source_target_pairs={{0,4},{1,0},{2,8},{3,12},{4,1},{5,13},{6,9},{7,5},{8,14},{9,10},{1... | collective-permute-start | bytes 776 | tf_op jit(solution)/shard_map/ppermute | solution.py:114

commit v27 on v22

--- a/solution.py
+++ b/solution.py
@@ -112,11 +112,13 @@
     here = lax.axis_index("dp") * len(senders) + lax.axis_index("layer")
     crossed = [d * len(row) + i for d, row in enumerate(senders) for i, sender in enumerate(row) if sender != i]
     is_crossed = functools.reduce(jnp.logical_or, [here == i for i in crossed])
-    one, two = (
-        lax.dot_general(rows[...], block[...], (((1,), (1,)), ((), ())), preferred_element_type=jnp.float32)
-        for block in (own_block, other_block)
-    )
-    out[...] = jnp.where(is_crossed, one[1:] + two[:1], one[:1] + two[1:])
+    both = rows[...].astype(jnp.float32)
+    lanes = 128
+    total = jnp.zeros((own_block.shape[0], lanes), jnp.float32)
+    for block, row in ((own_block, jnp.where(is_crossed, both[1:], both[:1])), (other_block, jnp.where(is_crossed, both[:1], both[1:]))):
+        for at in range(0, block.shape[1], lanes):
+            total += block[:, pl.ds(at, lanes)].astype(jnp.float32) * row[:, at : at + lanes]
+    out[...] = jnp.sum(total.T, axis=0, keepdims=True)
 
 
 def factor_kernel(scale, margin, label, rows, factor):

time: 16 us -> 16 us (level)
  no operation moved by 1% of the time
where the time goes in v27:
time: 16 us; the launch traced here: 15.8 us
  starting transfers between devices  8.51 us (53%)
  Pallas kernels  3.62 us (23%)
  waiting for transfers between devices  1.78 us (11%)
  between operations  1.35 us (8%)
  other arithmetic  0.57 us (4%)
    ppermute x2, starting transfers between devices, fetch_pair(): return lax.ppermute(x, ('dp', 'layer'), moves)  4.89 us
    ppermute x2, starting transfers between devices, to_owner(): return lax.ppermute(x, ('dp', 'layer'), moves)  3.04 us
    pallas_call x1, Pallas kernels, pair_gradient(): pl.pallas_call(functools.partial(pair_kernel, seq_len), out_shape=jax.Sha...  2.9 us
    ppermute x2, waiting for transfers between devices, swap(): lax.ppermute(x, 'layer', [(i, i ^ 1) for i in range(lax.axis_size('layer'...  1.13 us
    pallas_call x2, Pallas kernels, score(): pl.pallas_call(functools.partial(slot_kernel, senders), out_shape=jax.Sha...  0.71 us
    ppermute x2, waiting for transfers between devices, fetch_pair(): return lax.ppermute(x, ('dp', 'layer'), moves)  0.64 us
    ppermute x2, starting transfers between devices, swap(): lax.ppermute(x, 'layer', [(i, i ^ 1) for i in range(lax.axis_size('layer'...  0.57 us
    mul x1, other arithmetic, shared_scores(): return (to_owner(first, FIRST) + to_owner(second, SECOND)) * factor[None]  0.52 us
  transfers between devices with their start and end apart: 6, of which 2 were waited for; matrix products, arithmetic and copies ran while one was open for 0% of the time, Pallas kernels for 23%

profile of v27, /device:TPU:0, one launch (start us, length us, event | category | flops | bytes accessed | tf_op | source)
XLA Modules:
  0.0 15.8 jit_solution(1584081102035921933)
XLA Ops:
  0.0 0.5 %collective-permute-start.2 = (bf16[64,4096]{1,0:T(8,128)(2,1)}, bf16[64,4096]{1,0:T(8,128)(2,1)S(1)}, u32[]{:S(2)}, u32[]{:S(2)}) collective-permute-start(bf16[64,4096]{1,0:T(8,128)(2,1)} %bitcast.12), channel_id=1, source_target_pairs={{0,1},{1,0},{2,3},{3,2},{4,5},{5,4},{6,7},{7,6},{8,9},{9,8},{10,11... | collective-permute-start | bytes 1572872 | tf_op jit(solution)/shard_map/ppermute | solution.py:95
  0.5 0.0 copy-start
  0.5 2.9 %shard_map.82 = f32[32,128]{1,0:T(8,128)S(1)} custom-call(bf16[128,4096]{1,0:T(8,128)(2,1)} %bitcast.16, bf16[128,4096]{1,0:T(8,128)(2,1)} %bitcast.17, bf16[64,4096]{1,0:T(8,128)(2,1)} %bitcast.18, bf16[64,4096]{1,0:T(8,128)(2,1)} %bitcast.19, s32[1,2]{1,0:T(1,128)} %lengths.1), custom_call_target="tpu_custom_call" | custom-call | flops 134217728 | bytes 3145728 | tf_op jit(solution)/shard_map/pallas_call | solution.py:60
  3.4 0.1 collective-permute-start
  3.5 1.1 %collective-permute-done = bf16[1,4096]{1,0:T(2,128)(2,1)S(1)} collective-permute-done((bf16[1,4096]{1,0:T(2,128)(2,1)S(1)}, bf16[1,4096]{1,0:T(2,128)(2,1)S(1)}, u32[]{:S(2)}, u32[]{:S(2)}) %collective-permute-start) | collective-permute-done | bytes 8224 | tf_op jit(solution)/shard_map/ppermute | solution.py:95
  4.7 3.8 %collective-permute-start.1 = (bf16[2,4096]{1,0:T(2,128)(2,1)S(1)}, bf16[2,4096]{1,0:T(2,128)(2,1)S(1)}, u32[]{:S(2)}, u32[]{:S(2)}) collective-permute-start(bf16[2,4096]{1,0:T(2,128)(2,1)S(1)} %pad_maximum_fusion.rows), channel_id=1, source_target_pairs={{8,0},{12,1},{3,2},{6,3},{5,4},{9,5},{15,6},{2,7},{0,8},{4,9},{14,... | collective-permute-start | bytes 49160 | tf_op jit(solution)/shard_map/ppermute | solution.py:102
  8.5 1.1 %collective-permute-start.4 = (bf16[2,4096]{1,0:T(2,128)(2,1)S(1)}, bf16[2,4096]{1,0:T(2,128)(2,1)S(1)}, u32[]{:S(2)}, u32[]{:S(2)}) collective-permute-start(bf16[2,4096]{1,0:T(2,128)(2,1)S(1)} %pad_maximum_fusion.rows), channel_id=1, source_target_pairs={{4,0},{0,1},{11,2},{14,3},{1,4},{13,5},{10,6},{6,7},{12,8},{8,9},{... | collective-permute-start | bytes 49160 | tf_op jit(solution)/shard_map/ppermute | solution.py:102
  9.6 0.6 %collective-permute-done.1.rows = bf16[2,4096]{1,0:T(2,128)(2,1)S(1)} collective-permute-done((bf16[2,4096]{1,0:T(2,128)(2,1)S(1)}, bf16[2,4096]{1,0:T(2,128)(2,1)S(1)}, u32[]{:S(2)}, u32[]{:S(2)}) %collective-permute-start.1) | collective-permute-done | bytes 16416 | tf_op jit(solution)/shard_map/ppermute | solution.py:102
  10.2 0.0 collective-permute-done.2.other_block
  10.2 0.0 copy-done
  10.2 0.4 %shard_map.83 = f32[1,64]{1,0:T(1,128)S(1)} custom-call(bf16[2,4096]{1,0:T(2,128)(2,1)S(1)} %collective-permute-done.1.rows, bf16[64,4096]{1,0:T(8,128)(2,1)S(1)} %bitcast.13, bf16[64,4096]{1,0:T(8,128)(2,1)S(1)} %collective-permute-done.2.other_block), custom_call_target="tpu_custom_call" | custom-call | flops 2097152 | bytes 1048576 | tf_op jit(solution)/shard_map/pallas_call | solution.py:143
  10.6 3.0 %collective-permute-start.3 = (f32[1,64]{1,0:T(1,128)S(1)}, f32[1,64]{1,0:T(1,128)S(1)}, u32[]{:S(2)}, u32[]{:S(2)}) collective-permute-start(f32[1,64]{1,0:T(1,128)S(1)} %shard_map.83), channel_id=1, source_target_pairs={{0,8},{1,12},{2,0},{3,4},{4,5},{5,9},{6,13},{7,1},{8,2},{9,6},{10,... | collective-permute-start | bytes 776 | tf_op jit(solution)/shard_map/ppermute | solution.py:108
  13.6 0.0 collective-permute-done.4.rows
  13.6 0.4 %shard_map.84 = f32[1,64]{1,0:T(1,128)S(1)} custom-call(bf16[2,4096]{1,0:T(2,128)(2,1)S(1)} %collective-permute-done.4.rows, bf16[64,4096]{1,0:T(8,128)(2,1)S(1)} %bitcast.14, bf16[64,4096]{1,0:T(8,128)(2,1)S(1)} %collective-permute-done.2.other_block), custom_call_target="tpu_custom_call" | custom-call | flops 2097152 | bytes 1048576 | tf_op jit(solution)/shard_map/pallas_call | solution.py:143
  13.9 0.1 collective-permute-start.5
  15.3 0.0 collective-permute-done.3
  15.3 0.0 collective-permute-done.5
  15.3 0.5 %bitcast_multiply_fusion = f32[1,64]{1,0:T(1,128)} fusion(f32[64]{0:T(128)S(1)} %shard_map.85, f32[1,64]{1,0:T(1,128)S(1)} %collective-permute-done.3, f32[1,64]{1,0:T(1,128)S(1)} %collective-permute-done.5), kind=kLoop, calls=%fused_computation.1 | loop fusion | flops 128 | bytes 1024 | tf_op jit(solution)/shard_map/mul | solution.py:153
  (3 shorter events, 0.1 us)
Async XLA Ops:
  0.0 10.2 %collective-permute-start.2 = (bf16[64,4096]{1,0:T(8,128)(2,1)}, bf16[64,4096]{1,0:T(8,128)(2,1)S(1)}, u32[]{:S(2)}, u32[]{:S(2)}) collective-permute-start(bf16[64,4096]{1,0:T(8,128)(2,1)} %bitcast.12), channel_id=1, source_target_pairs={{0,1},{1,0},{2,3},{3,2},{4,5},{5,4},{6,7},{7,6},{8,9},{9,8},{10,11... | collective-permute-start | bytes 1572872 | tf_op jit(solution)/shard_map/ppermute | solution.py:95
  0.5 9.8 %copy-start = (bf16[64,1,4096]{2,0,1:T(8,128)(2,1)S(1)}, bf16[64,1,4096]{2,0,1:T(8,128)(2,1)}, u32[]{:S(2)}) copy-start(bf16[64,1,4096]{2,0,1:T(8,128)(2,1)} %param.12) | copy-start | bytes 1572868
  3.4 1.2 %collective-permute-start = (bf16[1,4096]{1,0:T(2,128)(2,1)S(1)}, bf16[1,4096]{1,0:T(2,128)(2,1)S(1)}, u32[]{:S(2)}, u32[]{:S(2)}) collective-permute-start(bf16[1,4096]{1,0:T(2,128)(2,1)S(1)} %convert.11), channel_id=1, source_target_pairs={{0,1},{1,0},{2,3},{3,2},{4,5},{5,4},{6,7},{7,6},{8,9},{9,8},{10,11... | collective-permute-start | bytes 24584 | tf_op jit(solution)/shard_map/ppermute | solution.py:95
  4.7 5.5 %collective-permute-start.1 = (bf16[2,4096]{1,0:T(2,128)(2,1)S(1)}, bf16[2,4096]{1,0:T(2,128)(2,1)S(1)}, u32[]{:S(2)}, u32[]{:S(2)}) collective-permute-start(bf16[2,4096]{1,0:T(2,128)(2,1)S(1)} %pad_maximum_fusion.rows), channel_id=1, source_target_pairs={{8,0},{12,1},{3,2},{6,3},{5,4},{9,5},{15,6},{2,7},{0,8},{4,9},{14,... | collective-permute-start | bytes 49160 | tf_op jit(solution)/shard_map/ppermute | solution.py:102
  8.5 5.1 %collective-permute-start.4 = (bf16[2,4096]{1,0:T(2,128)(2,1)S(1)}, bf16[2,4096]{1,0:T(2,128)(2,1)S(1)}, u32[]{:S(2)}, u32[]{:S(2)}) collective-permute-start(bf16[2,4096]{1,0:T(2,128)(2,1)S(1)} %pad_maximum_fusion.rows), channel_id=1, source_target_pairs={{4,0},{0,1},{11,2},{14,3},{1,4},{13,5},{10,6},{6,7},{12,8},{8,9},{... | collective-permute-start | bytes 49160 | tf_op jit(solution)/shard_map/ppermute | solution.py:102
  10.6 4.7 %collective-permute-start.3 = (f32[1,64]{1,0:T(1,128)S(1)}, f32[1,64]{1,0:T(1,128)S(1)}, u32[]{:S(2)}, u32[]{:S(2)}) collective-permute-start(f32[1,64]{1,0:T(1,128)S(1)} %shard_map.83), channel_id=1, source_target_pairs={{0,8},{1,12},{2,0},{3,4},{4,5},{5,9},{6,13},{7,1},{8,2},{9,6},{10,... | collective-permute-start | bytes 776 | tf_op jit(solution)/shard_map/ppermute | solution.py:108
  13.9 1.4 %collective-permute-start.5 = (f32[1,64]{1,0:T(1,128)S(1)}, f32[1,64]{1,0:T(1,128)S(1)}, u32[]{:S(2)}, u32[]{:S(2)}) collective-permute-start(f32[1,64]{1,0:T(1,128)S(1)} %shard_map.84), channel_id=1, source_target_pairs={{0,4},{1,0},{2,8},{3,12},{4,1},{5,13},{6,9},{7,5},{8,14},{9,10},{1... | collective-permute-start | bytes 776 | tf_op jit(solution)/shard_map/ppermute | solution.py:108

commit v28 on v27

--- a/solution.py
+++ b/solution.py
@@ -112,13 +112,16 @@
     here = lax.axis_index("dp") * len(senders) + lax.axis_index("layer")
     crossed = [d * len(row) + i for d, row in enumerate(senders) for i, sender in enumerate(row) if sender != i]
     is_crossed = functools.reduce(jnp.logical_or, [here == i for i in crossed])
+    two = lax.dot_general(
+        rows[...], other_block[...], (((1,), (1,)), ((), ())), preferred_element_type=jnp.float32
+    )
     both = rows[...].astype(jnp.float32)
+    row = jnp.where(is_crossed, both[1:], both[:1])
     lanes = 128
-    total = jnp.zeros((own_block.shape[0], lanes), jnp.float32)
-    for block, row in ((own_block, jnp.where(is_crossed, both[1:], both[:1])), (other_block, jnp.where(is_crossed, both[:1], both[1:]))):
-        for at in range(0, block.shape[1], lanes):
-            total += block[:, pl.ds(at, lanes)].astype(jnp.float32) * row[:, at : at + lanes]
-    out[...] = jnp.sum(total.T, axis=0, keepdims=True)
+    one = jnp.zeros((own_block.shape[0], lanes), jnp.float32)
+    for at in range(0, own_block.shape[1], lanes):
+        one += own_block[:, pl.ds(at, lanes)].astype(jnp.float32) * row[:, at : at + lanes]
+    out[...] = jnp.sum(one.T, axis=0, keepdims=True) + jnp.where(is_crossed, two[:1], two[1:])
 
 
 def factor_kernel(scale, margin, label, rows, factor):

time: 16 us -> 15.9 us (level)
  Pallas kernels: 3.62 us -> 3.45 us
    pallas_call x2, Pallas kernels: 0.71 us -> 0.54 us  [score(): pl.pallas_call(functools.partial(slot_kernel, senders), out_shape=jax.Sha...]
  transfers between devices with their start and end apart: 6 -> 6, of which waited for: 2 -> 2; matrix products, arithmetic and copies ran while one was open for 0% -> 0% of each run, Pallas kernels for 23% -> 22%
where the time goes in v28:
time: 15.9 us; the launch traced here: 15.7 us
  starting transfers between devices  8.5 us (53%)
  Pallas kernels  3.45 us (22%)
  waiting for transfers between devices  1.78 us (11%)
  between operations  1.35 us (8%)
  other arithmetic  0.57 us (4%)
    ppermute x2, starting transfers between devices, fetch_pair(): return lax.ppermute(x, ('dp', 'layer'), moves)  4.89 us
    ppermute x2, starting transfers between devices, to_owner(): return lax.ppermute(x, ('dp', 'layer'), moves)  3.04 us
    pallas_call x1, Pallas kernels, pair_gradient(): pl.pallas_call(functools.partial(pair_kernel, seq_len), out_shape=jax.Sha...  2.9 us
    ppermute x2, waiting for transfers between devices, swap(): lax.ppermute(x, 'layer', [(i, i ^ 1) for i in range(lax.axis_size('layer'...  1.13 us
    ppermute x2, waiting for transfers between devices, fetch_pair(): return lax.ppermute(x, ('dp', 'layer'), moves)  0.64 us
    ppermute x2, starting transfers between devices, swap(): lax.ppermute(x, 'layer', [(i, i ^ 1) for i in range(lax.axis_size('layer'...  0.57 us
    pallas_call x2, Pallas kernels, score(): pl.pallas_call(functools.partial(slot_kernel, senders), out_shape=jax.Sha...  0.54 us
    mul x1, other arithmetic, shared_scores(): return (to_owner(first, FIRST) + to_owner(second, SECOND)) * factor[None]  0.52 us
  transfers between devices with their start and end apart: 6, of which 2 were waited for; matrix products, arithmetic and copies ran while one was open for 0% of the time, Pallas kernels for 22%

profile of v28, /device:TPU:0, one launch (start us, length us, event | category | flops | bytes accessed | tf_op | source)
XLA Modules:
  0.0 15.7 jit_solution(12792505724613674147)
XLA Ops:
  0.0 0.5 %collective-permute-start.2 = (bf16[64,4096]{1,0:T(8,128)(2,1)}, bf16[64,4096]{1,0:T(8,128)(2,1)S(1)}, u32[]{:S(2)}, u32[]{:S(2)}) collective-permute-start(bf16[64,4096]{1,0:T(8,128)(2,1)} %bitcast.12), channel_id=1, source_target_pairs={{0,1},{1,0},{2,3},{3,2},{4,5},{5,4},{6,7},{7,6},{8,9},{9,8},{10,11... | collective-permute-start | bytes 1572872 | tf_op jit(solution)/shard_map/ppermute | solution.py:95
  0.5 0.0 copy-start
  0.5 2.9 %shard_map.82 = f32[32,128]{1,0:T(8,128)S(1)} custom-call(bf16[128,4096]{1,0:T(8,128)(2,1)} %bitcast.16, bf16[128,4096]{1,0:T(8,128)(2,1)} %bitcast.17, bf16[64,4096]{1,0:T(8,128)(2,1)} %bitcast.18, bf16[64,4096]{1,0:T(8,128)(2,1)} %bitcast.19, s32[1,2]{1,0:T(1,128)} %lengths.1), custom_call_target="tpu_custom_call" | custom-call | flops 134217728 | bytes 3145728 | tf_op jit(solution)/shard_map/pallas_call | solution.py:60
  3.4 0.1 collective-permute-start
  3.5 1.1 %collective-permute-done = bf16[1,4096]{1,0:T(2,128)(2,1)S(1)} collective-permute-done((bf16[1,4096]{1,0:T(2,128)(2,1)S(1)}, bf16[1,4096]{1,0:T(2,128)(2,1)S(1)}, u32[]{:S(2)}, u32[]{:S(2)}) %collective-permute-start) | collective-permute-done | bytes 8224 | tf_op jit(solution)/shard_map/ppermute | solution.py:95
  4.7 3.8 %collective-permute-start.1 = (bf16[2,4096]{1,0:T(2,128)(2,1)S(1)}, bf16[2,4096]{1,0:T(2,128)(2,1)S(1)}, u32[]{:S(2)}, u32[]{:S(2)}) collective-permute-start(bf16[2,4096]{1,0:T(2,128)(2,1)S(1)} %pad_maximum_fusion.rows), channel_id=1, source_target_pairs={{8,0},{12,1},{3,2},{6,3},{5,4},{9,5},{15,6},{2,7},{0,8},{4,9},{14,... | collective-permute-start | bytes 49160 | tf_op jit(solution)/shard_map/ppermute | solution.py:102
  8.5 1.1 %collective-permute-start.4 = (bf16[2,4096]{1,0:T(2,128)(2,1)S(1)}, bf16[2,4096]{1,0:T(2,128)(2,1)S(1)}, u32[]{:S(2)}, u32[]{:S(2)}) collective-permute-start(bf16[2,4096]{1,0:T(2,128)(2,1)S(1)} %pad_maximum_fusion.rows), channel_id=1, source_target_pairs={{4,0},{0,1},{11,2},{14,3},{1,4},{13,5},{10,6},{6,7},{12,8},{8,9},{... | collective-permute-start | bytes 49160 | tf_op jit(solution)/shard_map/ppermute | solution.py:102
  9.6 0.6 %collective-permute-done.1.rows = bf16[2,4096]{1,0:T(2,128)(2,1)S(1)} collective-permute-done((bf16[2,4096]{1,0:T(2,128)(2,1)S(1)}, bf16[2,4096]{1,0:T(2,128)(2,1)S(1)}, u32[]{:S(2)}, u32[]{:S(2)}) %collective-permute-start.1) | collective-permute-done | bytes 16416 | tf_op jit(solution)/shard_map/ppermute | solution.py:102
  10.2 0.0 collective-permute-done.2.other_block
  10.2 0.0 copy-done
  10.2 0.3 %shard_map.83 = f32[1,64]{1,0:T(1,128)S(1)} custom-call(bf16[2,4096]{1,0:T(2,128)(2,1)S(1)} %collective-permute-done.1.rows, bf16[64,4096]{1,0:T(8,128)(2,1)S(1)} %bitcast.13, bf16[64,4096]{1,0:T(8,128)(2,1)S(1)} %collective-permute-done.2.other_block), custom_call_target="tpu_custom_call" | custom-call | flops 2097152 | bytes 1048576 | tf_op jit(solution)/shard_map/pallas_call | solution.py:146
  10.5 3.0 %collective-permute-start.3 = (f32[1,64]{1,0:T(1,128)S(1)}, f32[1,64]{1,0:T(1,128)S(1)}, u32[]{:S(2)}, u32[]{:S(2)}) collective-permute-start(f32[1,64]{1,0:T(1,128)S(1)} %shard_map.83), channel_id=1, source_target_pairs={{0,8},{1,12},{2,0},{3,4},{4,5},{5,9},{6,13},{7,1},{8,2},{9,6},{10,... | collective-permute-start | bytes 776 | tf_op jit(solution)/shard_map/ppermute | solution.py:108
  13.5 0.0 collective-permute-done.4.rows
  13.5 0.3 %shard_map.84 = f32[1,64]{1,0:T(1,128)S(1)} custom-call(bf16[2,4096]{1,0:T(2,128)(2,1)S(1)} %collective-permute-done.4.rows, bf16[64,4096]{1,0:T(8,128)(2,1)S(1)} %bitcast.14, bf16[64,4096]{1,0:T(8,128)(2,1)S(1)} %collective-permute-done.2.other_block), custom_call_target="tpu_custom_call" | custom-call | flops 2097152 | bytes 1048576 | tf_op jit(solution)/shard_map/pallas_call | solution.py:146
  13.7 0.1 collective-permute-start.5
  15.1 0.0 collective-permute-done.3
  15.1 0.0 collective-permute-done.5
  15.1 0.5 %bitcast_multiply_fusion = f32[1,64]{1,0:T(1,128)} fusion(f32[64]{0:T(128)S(1)} %shard_map.85, f32[1,64]{1,0:T(1,128)S(1)} %collective-permute-done.3, f32[1,64]{1,0:T(1,128)S(1)} %collective-permute-done.5), kind=kLoop, calls=%fused_computation.1 | loop fusion | flops 128 | bytes 1024 | tf_op jit(solution)/shard_map/mul | solution.py:156
  (3 shorter events, 0.1 us)
Async XLA Ops:
  0.0 10.2 %collective-permute-start.2 = (bf16[64,4096]{1,0:T(8,128)(2,1)}, bf16[64,4096]{1,0:T(8,128)(2,1)S(1)}, u32[]{:S(2)}, u32[]{:S(2)}) collective-permute-start(bf16[64,4096]{1,0:T(8,128)(2,1)} %bitcast.12), channel_id=1, source_target_pairs={{0,1},{1,0},{2,3},{3,2},{4,5},{5,4},{6,7},{7,6},{8,9},{9,8},{10,11... | collective-permute-start | bytes 1572872 | tf_op jit(solution)/shard_map/ppermute | solution.py:95
  0.5 9.8 %copy-start = (bf16[64,1,4096]{2,0,1:T(8,128)(2,1)S(1)}, bf16[64,1,4096]{2,0,1:T(8,128)(2,1)}, u32[]{:S(2)}) copy-start(bf16[64,1,4096]{2,0,1:T(8,128)(2,1)} %param.12) | copy-start | bytes 1572868
  3.4 1.2 %collective-permute-start = (bf16[1,4096]{1,0:T(2,128)(2,1)S(1)}, bf16[1,4096]{1,0:T(2,128)(2,1)S(1)}, u32[]{:S(2)}, u32[]{:S(2)}) collective-permute-start(bf16[1,4096]{1,0:T(2,128)(2,1)S(1)} %convert.11), channel_id=1, source_target_pairs={{0,1},{1,0},{2,3},{3,2},{4,5},{5,4},{6,7},{7,6},{8,9},{9,8},{10,11... | collective-permute-start | bytes 24584 | tf_op jit(solution)/shard_map/ppermute | solution.py:95
  4.7 5.5 %collective-permute-start.1 = (bf16[2,4096]{1,0:T(2,128)(2,1)S(1)}, bf16[2,4096]{1,0:T(2,128)(2,1)S(1)}, u32[]{:S(2)}, u32[]{:S(2)}) collective-permute-start(bf16[2,4096]{1,0:T(2,128)(2,1)S(1)} %pad_maximum_fusion.rows), channel_id=1, source_target_pairs={{8,0},{12,1},{3,2},{6,3},{5,4},{9,5},{15,6},{2,7},{0,8},{4,9},{14,... | collective-permute-start | bytes 49160 | tf_op jit(solution)/shard_map/ppermute | solution.py:102
  8.5 5.0 %collective-permute-start.4 = (bf16[2,4096]{1,0:T(2,128)(2,1)S(1)}, bf16[2,4096]{1,0:T(2,128)(2,1)S(1)}, u32[]{:S(2)}, u32[]{:S(2)}) collective-permute-start(bf16[2,4096]{1,0:T(2,128)(2,1)S(1)} %pad_maximum_fusion.rows), channel_id=1, source_target_pairs={{4,0},{0,1},{11,2},{14,3},{1,4},{13,5},{10,6},{6,7},{12,8},{8,9},{... | collective-permute-start | bytes 49160 | tf_op jit(solution)/shard_map/ppermute | solution.py:102
  10.5 4.6 %collective-permute-start.3 = (f32[1,64]{1,0:T(1,128)S(1)}, f32[1,64]{1,0:T(1,128)S(1)}, u32[]{:S(2)}, u32[]{:S(2)}) collective-permute-start(f32[1,64]{1,0:T(1,128)S(1)} %shard_map.83), channel_id=1, source_target_pairs={{0,8},{1,12},{2,0},{3,4},{4,5},{5,9},{6,13},{7,1},{8,2},{9,6},{10,... | collective-permute-start | bytes 776 | tf_op jit(solution)/shard_map/ppermute | solution.py:108
  13.7 1.4 %collective-permute-start.5 = (f32[1,64]{1,0:T(1,128)S(1)}, f32[1,64]{1,0:T(1,128)S(1)}, u32[]{:S(2)}, u32[]{:S(2)}) collective-permute-start(f32[1,64]{1,0:T(1,128)S(1)} %shard_map.84), channel_id=1, source_target_pairs={{0,4},{1,0},{2,8},{3,12},{4,1},{5,13},{6,9},{7,5},{8,14},{9,10},{1... | collective-permute-start | bytes 776 | tf_op jit(solution)/shard_map/ppermute | solution.py:108

commit v29 on v28

--- a/solution.py
+++ b/solution.py
@@ -42,7 +42,9 @@
         turned_v[pl.ds(c * width, width), :] = proj_v[:, pl.ds(c * width, width)].T
     for copy in loads[2:]:
         copy.wait()
-    coords = jnp.dot(tokens_v[...], turned_v[...], preferred_element_type=jnp.float32)
+    halves = [pl.ds(at, model_width // 2) for at in (0, model_width // 2)]
+    low, high = (jnp.dot(tokens_v[:, part], turned_v[part, :], preferred_element_type=jnp.float32) for part in halves)
+    coords = low + high
     square_v[...] = lax.dot_general(
         coords[tokens:].astype(jnp.bfloat16),
         (coords[:tokens] * weight).astype(jnp.bfloat16),

time: 15.9 us -> 15.9 us (level)
  no operation moved by 1% of the time
where the time goes in v29:
time: 15.9 us; the launch traced here: 15.7 us
  starting transfers between devices  8.5 us (53%)
  Pallas kernels  3.45 us (22%)
  waiting for transfers between devices  1.78 us (11%)
  between operations  1.35 us (8%)
  other arithmetic  0.57 us (4%)
    ppermute x2, starting transfers between devices, fetch_pair(): return lax.ppermute(x, ('dp', 'layer'), moves)  4.89 us
    ppermute x2, starting transfers between devices, to_owner(): return lax.ppermute(x, ('dp', 'layer'), moves)  3.04 us
    pallas_call x1, Pallas kernels, pair_gradient(): pl.pallas_call(functools.partial(pair_kernel, seq_len), out_shape=jax.Sha...  2.9 us
    ppermute x2, waiting for transfers between devices, swap(): lax.ppermute(x, 'layer', [(i, i ^ 1) for i in range(lax.axis_size('layer'...  1.13 us
    ppermute x2, waiting for transfers between devices, fetch_pair(): return lax.ppermute(x, ('dp', 'layer'), moves)  0.64 us
    ppermute x2, starting transfers between devices, swap(): lax.ppermute(x, 'layer', [(i, i ^ 1) for i in range(lax.axis_size('layer'...  0.57 us
    pallas_call x2, Pallas kernels, score(): pl.pallas_call(functools.partial(slot_kernel, senders), out_shape=jax.Sha...  0.54 us
    mul x1, other arithmetic, shared_scores(): return (to_owner(first, FIRST) + to_owner(second, SECOND)) * factor[None]  0.52 us
  transfers between devices with their start and end apart: 6, of which 2 were waited for; matrix products, arithmetic and copies ran while one was open for 0% of the time, Pallas kernels for 22%

profile of v29, /device:TPU:0, one launch (start us, length us, event | category | flops | bytes accessed | tf_op | source)
XLA Modules:
  0.0 15.7 jit_solution(4470982980817871312)
XLA Ops:
  0.0 0.5 %collective-permute-start.2 = (bf16[64,4096]{1,0:T(8,128)(2,1)}, bf16[64,4096]{1,0:T(8,128)(2,1)S(1)}, u32[]{:S(2)}, u32[]{:S(2)}) collective-permute-start(bf16[64,4096]{1,0:T(8,128)(2,1)} %bitcast.12), channel_id=1, source_target_pairs={{0,1},{1,0},{2,3},{3,2},{4,5},{5,4},{6,7},{7,6},{8,9},{9,8},{10,11... | collective-permute-start | bytes 1572872 | tf_op jit(solution)/shard_map/ppermute | solution.py:97
  0.5 0.0 copy-start
  0.5 2.9 %shard_map.82 = f32[32,128]{1,0:T(8,128)S(1)} custom-call(bf16[128,4096]{1,0:T(8,128)(2,1)} %bitcast.16, bf16[128,4096]{1,0:T(8,128)(2,1)} %bitcast.17, bf16[64,4096]{1,0:T(8,128)(2,1)} %bitcast.18, bf16[64,4096]{1,0:T(8,128)(2,1)} %bitcast.19, s32[1,2]{1,0:T(1,128)} %lengths.1), custom_call_target="tpu_custom_call" | custom-call | flops 134217728 | bytes 3145728 | tf_op jit(solution)/shard_map/pallas_call | solution.py:62
  3.4 0.1 collective-permute-start
  3.5 1.1 %collective-permute-done = bf16[1,4096]{1,0:T(2,128)(2,1)S(1)} collective-permute-done((bf16[1,4096]{1,0:T(2,128)(2,1)S(1)}, bf16[1,4096]{1,0:T(2,128)(2,1)S(1)}, u32[]{:S(2)}, u32[]{:S(2)}) %collective-permute-start) | collective-permute-done | bytes 8224 | tf_op jit(solution)/shard_map/ppermute | solution.py:97
  4.7 3.8 %collective-permute-start.1 = (bf16[2,4096]{1,0:T(2,128)(2,1)S(1)}, bf16[2,4096]{1,0:T(2,128)(2,1)S(1)}, u32[]{:S(2)}, u32[]{:S(2)}) collective-permute-start(bf16[2,4096]{1,0:T(2,128)(2,1)S(1)} %pad_maximum_fusion.rows), channel_id=1, source_target_pairs={{8,0},{12,1},{3,2},{6,3},{5,4},{9,5},{15,6},{2,7},{0,8},{4,9},{14,... | collective-permute-start | bytes 49160 | tf_op jit(solution)/shard_map/ppermute | solution.py:104
  8.5 1.1 %collective-permute-start.4 = (bf16[2,4096]{1,0:T(2,128)(2,1)S(1)}, bf16[2,4096]{1,0:T(2,128)(2,1)S(1)}, u32[]{:S(2)}, u32[]{:S(2)}) collective-permute-start(bf16[2,4096]{1,0:T(2,128)(2,1)S(1)} %pad_maximum_fusion.rows), channel_id=1, source_target_pairs={{4,0},{0,1},{11,2},{14,3},{1,4},{13,5},{10,6},{6,7},{12,8},{8,9},{... | collective-permute-start | bytes 49160 | tf_op jit(solution)/shard_map/ppermute | solution.py:104
  9.6 0.6 %collective-permute-done.1.rows = bf16[2,4096]{1,0:T(2,128)(2,1)S(1)} collective-permute-done((bf16[2,4096]{1,0:T(2,128)(2,1)S(1)}, bf16[2,4096]{1,0:T(2,128)(2,1)S(1)}, u32[]{:S(2)}, u32[]{:S(2)}) %collective-permute-start.1) | collective-permute-done | bytes 16416 | tf_op jit(solution)/shard_map/ppermute | solution.py:104
  10.2 0.0 collective-permute-done.2.other_block
  10.2 0.0 copy-done
  10.2 0.3 %shard_map.83 = f32[1,64]{1,0:T(1,128)S(1)} custom-call(bf16[2,4096]{1,0:T(2,128)(2,1)S(1)} %collective-permute-done.1.rows, bf16[64,4096]{1,0:T(8,128)(2,1)S(1)} %bitcast.13, bf16[64,4096]{1,0:T(8,128)(2,1)S(1)} %collective-permute-done.2.other_block), custom_call_target="tpu_custom_call" | custom-call | flops 2097152 | bytes 1048576 | tf_op jit(solution)/shard_map/pallas_call | solution.py:148
  10.5 3.0 %collective-permute-start.3 = (f32[1,64]{1,0:T(1,128)S(1)}, f32[1,64]{1,0:T(1,128)S(1)}, u32[]{:S(2)}, u32[]{:S(2)}) collective-permute-start(f32[1,64]{1,0:T(1,128)S(1)} %shard_map.83), channel_id=1, source_target_pairs={{0,8},{1,12},{2,0},{3,4},{4,5},{5,9},{6,13},{7,1},{8,2},{9,6},{10,... | collective-permute-start | bytes 776 | tf_op jit(solution)/shard_map/ppermute | solution.py:110
  13.5 0.0 collective-permute-done.4.rows
  13.5 0.3 %shard_map.84 = f32[1,64]{1,0:T(1,128)S(1)} custom-call(bf16[2,4096]{1,0:T(2,128)(2,1)S(1)} %collective-permute-done.4.rows, bf16[64,4096]{1,0:T(8,128)(2,1)S(1)} %bitcast.14, bf16[64,4096]{1,0:T(8,128)(2,1)S(1)} %collective-permute-done.2.other_block), custom_call_target="tpu_custom_call" | custom-call | flops 2097152 | bytes 1048576 | tf_op jit(solution)/shard_map/pallas_call | solution.py:148
  13.7 0.1 collective-permute-start.5
  15.1 0.0 collective-permute-done.3
  15.1 0.0 collective-permute-done.5
  15.1 0.5 %bitcast_multiply_fusion = f32[1,64]{1,0:T(1,128)} fusion(f32[64]{0:T(128)S(1)} %shard_map.85, f32[1,64]{1,0:T(1,128)S(1)} %collective-permute-done.3, f32[1,64]{1,0:T(1,128)S(1)} %collective-permute-done.5), kind=kLoop, calls=%fused_computation.1 | loop fusion | flops 128 | bytes 1024 | tf_op jit(solution)/shard_map/mul | solution.py:158
  (3 shorter events, 0.1 us)
Async XLA Ops:
  0.0 10.2 %collective-permute-start.2 = (bf16[64,4096]{1,0:T(8,128)(2,1)}, bf16[64,4096]{1,0:T(8,128)(2,1)S(1)}, u32[]{:S(2)}, u32[]{:S(2)}) collective-permute-start(bf16[64,4096]{1,0:T(8,128)(2,1)} %bitcast.12), channel_id=1, source_target_pairs={{0,1},{1,0},{2,3},{3,2},{4,5},{5,4},{6,7},{7,6},{8,9},{9,8},{10,11... | collective-permute-start | bytes 1572872 | tf_op jit(solution)/shard_map/ppermute | solution.py:97
  0.5 9.8 %copy-start = (bf16[64,1,4096]{2,0,1:T(8,128)(2,1)S(1)}, bf16[64,1,4096]{2,0,1:T(8,128)(2,1)}, u32[]{:S(2)}) copy-start(bf16[64,1,4096]{2,0,1:T(8,128)(2,1)} %param.12) | copy-start | bytes 1572868
  3.4 1.2 %collective-permute-start = (bf16[1,4096]{1,0:T(2,128)(2,1)S(1)}, bf16[1,4096]{1,0:T(2,128)(2,1)S(1)}, u32[]{:S(2)}, u32[]{:S(2)}) collective-permute-start(bf16[1,4096]{1,0:T(2,128)(2,1)S(1)} %convert.11), channel_id=1, source_target_pairs={{0,1},{1,0},{2,3},{3,2},{4,5},{5,4},{6,7},{7,6},{8,9},{9,8},{10,11... | collective-permute-start | bytes 24584 | tf_op jit(solution)/shard_map/ppermute | solution.py:97
  4.7 5.5 %collective-permute-start.1 = (bf16[2,4096]{1,0:T(2,128)(2,1)S(1)}, bf16[2,4096]{1,0:T(2,128)(2,1)S(1)}, u32[]{:S(2)}, u32[]{:S(2)}) collective-permute-start(bf16[2,4096]{1,0:T(2,128)(2,1)S(1)} %pad_maximum_fusion.rows), channel_id=1, source_target_pairs={{8,0},{12,1},{3,2},{6,3},{5,4},{9,5},{15,6},{2,7},{0,8},{4,9},{14,... | collective-permute-start | bytes 49160 | tf_op jit(solution)/shard_map/ppermute | solution.py:104
  8.5 5.0 %collective-permute-start.4 = (bf16[2,4096]{1,0:T(2,128)(2,1)S(1)}, bf16[2,4096]{1,0:T(2,128)(2,1)S(1)}, u32[]{:S(2)}, u32[]{:S(2)}) collective-permute-start(bf16[2,4096]{1,0:T(2,128)(2,1)S(1)} %pad_maximum_fusion.rows), channel_id=1, source_target_pairs={{4,0},{0,1},{11,2},{14,3},{1,4},{13,5},{10,6},{6,7},{12,8},{8,9},{... | collective-permute-start | bytes 49160 | tf_op jit(solution)/shard_map/ppermute | solution.py:104
  10.5 4.6 %collective-permute-start.3 = (f32[1,64]{1,0:T(1,128)S(1)}, f32[1,64]{1,0:T(1,128)S(1)}, u32[]{:S(2)}, u32[]{:S(2)}) collective-permute-start(f32[1,64]{1,0:T(1,128)S(1)} %shard_map.83), channel_id=1, source_target_pairs={{0,8},{1,12},{2,0},{3,4},{4,5},{5,9},{6,13},{7,1},{8,2},{9,6},{10,... | collective-permute-start | bytes 776 | tf_op jit(solution)/shard_map/ppermute | solution.py:110
  13.7 1.4 %collective-permute-start.5 = (f32[1,64]{1,0:T(1,128)S(1)}, f32[1,64]{1,0:T(1,128)S(1)}, u32[]{:S(2)}, u32[]{:S(2)}) collective-permute-start(f32[1,64]{1,0:T(1,128)S(1)} %shard_map.84), channel_id=1, source_target_pairs={{0,4},{1,0},{2,8},{3,12},{4,1},{5,13},{6,9},{7,5},{8,14},{9,10},{1... | collective-permute-start | bytes 776 | tf_op jit(solution)/shard_map/ppermute | solution.py:110

commit v30 on v28

--- a/solution.py
+++ b/solution.py
@@ -112,15 +112,19 @@
     here = lax.axis_index("dp") * len(senders) + lax.axis_index("layer")
     crossed = [d * len(row) + i for d, row in enumerate(senders) for i, sender in enumerate(row) if sender != i]
     is_crossed = functools.reduce(jnp.logical_or, [here == i for i in crossed])
+    width = own_block.shape[1]
+    quarter = width // 4
+    rest = pl.ds(quarter, width - quarter)
     two = lax.dot_general(
-        rows[...], other_block[...], (((1,), (1,)), ((), ())), preferred_element_type=jnp.float32
+        rows[:, rest], other_block[:, rest], (((1,), (1,)), ((), ())), preferred_element_type=jnp.float32
     )
     both = rows[...].astype(jnp.float32)
-    row = jnp.where(is_crossed, both[1:], both[:1])
+    own_row, other_row = jnp.where(is_crossed, both[1:], both[:1]), jnp.where(is_crossed, both[:1], both[1:])
     lanes = 128
     one = jnp.zeros((own_block.shape[0], lanes), jnp.float32)
-    for at in range(0, own_block.shape[1], lanes):
-        one += own_block[:, pl.ds(at, lanes)].astype(jnp.float32) * row[:, at : at + lanes]
+    for block, row, end in ((own_block, own_row, width), (other_block, other_row, quarter)):
+        for at in range(0, end, lanes):
+            one += block[:, pl.ds(at, lanes)].astype(jnp.float32) * row[:, at : at + lanes]
     out[...] = jnp.sum(one.T, axis=0, keepdims=True) + jnp.where(is_crossed, two[:1], two[1:])
 
 

time: 15.9 us -> 15.9 us (level)
  no operation moved by 1% of the time
where the time goes in v30:
time: 15.9 us; the launch traced here: 15.7 us
  starting transfers between devices  8.51 us (54%)
  Pallas kernels  3.48 us (22%)
  waiting for transfers between devices  1.78 us (11%)
  between operations  1.35 us (8%)
  other arithmetic  0.57 us (4%)
    ppermute x2, starting transfers between devices, fetch_pair(): return lax.ppermute(x, ('dp', 'layer'), moves)  4.89 us
    ppermute x2, starting transfers between devices, to_owner(): return lax.ppermute(x, ('dp', 'layer'), moves)  3.04 us
    pallas_call x1, Pallas kernels, pair_gradient(): pl.pallas_call(functools.partial(pair_kernel, seq_len), out_shape=jax.Sha...  2.9 us
    ppermute x2, waiting for transfers between devices, swap(): lax.ppermute(x, 'layer', [(i, i ^ 1) for i in range(lax.axis_size('layer'...  1.13 us
    ppermute x2, waiting for transfers between devices, fetch_pair(): return lax.ppermute(x, ('dp', 'layer'), moves)  0.64 us
    ppermute x2, starting transfers between devices, swap(): lax.ppermute(x, 'layer', [(i, i ^ 1) for i in range(lax.axis_size('layer'...  0.57 us
    pallas_call x2, Pallas kernels, score(): pl.pallas_call(functools.partial(slot_kernel, senders), out_shape=jax.Sha...  0.57 us
    mul x1, other arithmetic, shared_scores(): return (to_owner(first, FIRST) + to_owner(second, SECOND)) * factor[None]  0.52 us
  transfers between devices with their start and end apart: 6, of which 2 were waited for; matrix products, arithmetic and copies ran while one was open for 0% of the time, Pallas kernels for 22%

profile of v30, /device:TPU:0, one launch (start us, length us, event | category | flops | bytes accessed | tf_op | source)
XLA Modules:
  0.0 15.7 jit_solution(1247708573068155215)
XLA Ops:
  0.0 0.5 %collective-permute-start.2 = (bf16[64,4096]{1,0:T(8,128)(2,1)}, bf16[64,4096]{1,0:T(8,128)(2,1)S(1)}, u32[]{:S(2)}, u32[]{:S(2)}) collective-permute-start(bf16[64,4096]{1,0:T(8,128)(2,1)} %bitcast.12), channel_id=1, source_target_pairs={{0,1},{1,0},{2,3},{3,2},{4,5},{5,4},{6,7},{7,6},{8,9},{9,8},{10,11... | collective-permute-start | bytes 1572872 | tf_op jit(solution)/shard_map/ppermute | solution.py:95
  0.5 0.0 copy-start
  0.5 2.9 %shard_map.82 = f32[32,128]{1,0:T(8,128)S(1)} custom-call(bf16[128,4096]{1,0:T(8,128)(2,1)} %bitcast.16, bf16[128,4096]{1,0:T(8,128)(2,1)} %bitcast.17, bf16[64,4096]{1,0:T(8,128)(2,1)} %bitcast.18, bf16[64,4096]{1,0:T(8,128)(2,1)} %bitcast.19, s32[1,2]{1,0:T(1,128)} %lengths.1), custom_call_target="tpu_custom_call" | custom-call | flops 134217728 | bytes 3145728 | tf_op jit(solution)/shard_map/pallas_call | solution.py:60
  3.4 0.1 collective-permute-start
  3.5 1.1 %collective-permute-done = bf16[1,4096]{1,0:T(2,128)(2,1)S(1)} collective-permute-done((bf16[1,4096]{1,0:T(2,128)(2,1)S(1)}, bf16[1,4096]{1,0:T(2,128)(2,1)S(1)}, u32[]{:S(2)}, u32[]{:S(2)}) %collective-permute-start) | collective-permute-done | bytes 8224 | tf_op jit(solution)/shard_map/ppermute | solution.py:95
  4.7 3.8 %collective-permute-start.1 = (bf16[2,4096]{1,0:T(2,128)(2,1)S(1)}, bf16[2,4096]{1,0:T(2,128)(2,1)S(1)}, u32[]{:S(2)}, u32[]{:S(2)}) collective-permute-start(bf16[2,4096]{1,0:T(2,128)(2,1)S(1)} %pad_maximum_fusion.rows), channel_id=1, source_target_pairs={{8,0},{12,1},{3,2},{6,3},{5,4},{9,5},{15,6},{2,7},{0,8},{4,9},{14,... | collective-permute-start | bytes 49160 | tf_op jit(solution)/shard_map/ppermute | solution.py:102
  8.5 1.1 %collective-permute-start.4 = (bf16[2,4096]{1,0:T(2,128)(2,1)S(1)}, bf16[2,4096]{1,0:T(2,128)(2,1)S(1)}, u32[]{:S(2)}, u32[]{:S(2)}) collective-permute-start(bf16[2,4096]{1,0:T(2,128)(2,1)S(1)} %pad_maximum_fusion.rows), channel_id=1, source_target_pairs={{4,0},{0,1},{11,2},{14,3},{1,4},{13,5},{10,6},{6,7},{12,8},{8,9},{... | collective-permute-start | bytes 49160 | tf_op jit(solution)/shard_map/ppermute | solution.py:102
  9.6 0.6 %collective-permute-done.1.rows = bf16[2,4096]{1,0:T(2,128)(2,1)S(1)} collective-permute-done((bf16[2,4096]{1,0:T(2,128)(2,1)S(1)}, bf16[2,4096]{1,0:T(2,128)(2,1)S(1)}, u32[]{:S(2)}, u32[]{:S(2)}) %collective-permute-start.1) | collective-permute-done | bytes 16416 | tf_op jit(solution)/shard_map/ppermute | solution.py:102
  10.2 0.0 collective-permute-done.2.other_block
  10.2 0.0 copy-done
  10.2 0.3 %shard_map.83 = f32[1,64]{1,0:T(1,128)S(1)} custom-call(bf16[2,4096]{1,0:T(2,128)(2,1)S(1)} %collective-permute-done.1.rows, bf16[64,4096]{1,0:T(8,128)(2,1)S(1)} %bitcast.13, bf16[64,4096]{1,0:T(8,128)(2,1)S(1)} %collective-permute-done.2.other_block), custom_call_target="tpu_custom_call" | custom-call | flops 2097152 | bytes 1048576 | tf_op jit(solution)/shard_map/pallas_call | solution.py:150
  10.5 3.0 %collective-permute-start.3 = (f32[1,64]{1,0:T(1,128)S(1)}, f32[1,64]{1,0:T(1,128)S(1)}, u32[]{:S(2)}, u32[]{:S(2)}) collective-permute-start(f32[1,64]{1,0:T(1,128)S(1)} %shard_map.83), channel_id=1, source_target_pairs={{0,8},{1,12},{2,0},{3,4},{4,5},{5,9},{6,13},{7,1},{8,2},{9,6},{10,... | collective-permute-start | bytes 776 | tf_op jit(solution)/shard_map/ppermute | solution.py:108
  13.5 0.0 collective-permute-done.4.rows
  13.5 0.3 %shard_map.84 = f32[1,64]{1,0:T(1,128)S(1)} custom-call(bf16[2,4096]{1,0:T(2,128)(2,1)S(1)} %collective-permute-done.4.rows, bf16[64,4096]{1,0:T(8,128)(2,1)S(1)} %bitcast.14, bf16[64,4096]{1,0:T(8,128)(2,1)S(1)} %collective-permute-done.2.other_block), custom_call_target="tpu_custom_call" | custom-call | flops 2097152 | bytes 1048576 | tf_op jit(solution)/shard_map/pallas_call | solution.py:150
  13.8 0.1 collective-permute-start.5
  15.2 0.0 collective-permute-done.3
  15.2 0.0 collective-permute-done.5
  15.2 0.5 %bitcast_multiply_fusion = f32[1,64]{1,0:T(1,128)} fusion(f32[64]{0:T(128)S(1)} %shard_map.85, f32[1,64]{1,0:T(1,128)S(1)} %collective-permute-done.3, f32[1,64]{1,0:T(1,128)S(1)} %collective-permute-done.5), kind=kLoop, calls=%fused_computation.1 | loop fusion | flops 128 | bytes 1024 | tf_op jit(solution)/shard_map/mul | solution.py:160
  (3 shorter events, 0.1 us)
Async XLA Ops:
  0.0 10.2 %collective-permute-start.2 = (bf16[64,4096]{1,0:T(8,128)(2,1)}, bf16[64,4096]{1,0:T(8,128)(2,1)S(1)}, u32[]{:S(2)}, u32[]{:S(2)}) collective-permute-start(bf16[64,4096]{1,0:T(8,128)(2,1)} %bitcast.12), channel_id=1, source_target_pairs={{0,1},{1,0},{2,3},{3,2},{4,5},{5,4},{6,7},{7,6},{8,9},{9,8},{10,11... | collective-permute-start | bytes 1572872 | tf_op jit(solution)/shard_map/ppermute | solution.py:95
  0.5 9.8 %copy-start = (bf16[64,1,4096]{2,0,1:T(8,128)(2,1)S(1)}, bf16[64,1,4096]{2,0,1:T(8,128)(2,1)}, u32[]{:S(2)}) copy-start(bf16[64,1,4096]{2,0,1:T(8,128)(2,1)} %param.12) | copy-start | bytes 1572868
  3.4 1.2 %collective-permute-start = (bf16[1,4096]{1,0:T(2,128)(2,1)S(1)}, bf16[1,4096]{1,0:T(2,128)(2,1)S(1)}, u32[]{:S(2)}, u32[]{:S(2)}) collective-permute-start(bf16[1,4096]{1,0:T(2,128)(2,1)S(1)} %convert.11), channel_id=1, source_target_pairs={{0,1},{1,0},{2,3},{3,2},{4,5},{5,4},{6,7},{7,6},{8,9},{9,8},{10,11... | collective-permute-start | bytes 24584 | tf_op jit(solution)/shard_map/ppermute | solution.py:95
  4.7 5.5 %collective-permute-start.1 = (bf16[2,4096]{1,0:T(2,128)(2,1)S(1)}, bf16[2,4096]{1,0:T(2,128)(2,1)S(1)}, u32[]{:S(2)}, u32[]{:S(2)}) collective-permute-start(bf16[2,4096]{1,0:T(2,128)(2,1)S(1)} %pad_maximum_fusion.rows), channel_id=1, source_target_pairs={{8,0},{12,1},{3,2},{6,3},{5,4},{9,5},{15,6},{2,7},{0,8},{4,9},{14,... | collective-permute-start | bytes 49160 | tf_op jit(solution)/shard_map/ppermute | solution.py:102
  8.5 5.0 %collective-permute-start.4 = (bf16[2,4096]{1,0:T(2,128)(2,1)S(1)}, bf16[2,4096]{1,0:T(2,128)(2,1)S(1)}, u32[]{:S(2)}, u32[]{:S(2)}) collective-permute-start(bf16[2,4096]{1,0:T(2,128)(2,1)S(1)} %pad_maximum_fusion.rows), channel_id=1, source_target_pairs={{4,0},{0,1},{11,2},{14,3},{1,4},{13,5},{10,6},{6,7},{12,8},{8,9},{... | collective-permute-start | bytes 49160 | tf_op jit(solution)/shard_map/ppermute | solution.py:102
  10.5 4.7 %collective-permute-start.3 = (f32[1,64]{1,0:T(1,128)S(1)}, f32[1,64]{1,0:T(1,128)S(1)}, u32[]{:S(2)}, u32[]{:S(2)}) collective-permute-start(f32[1,64]{1,0:T(1,128)S(1)} %shard_map.83), channel_id=1, source_target_pairs={{0,8},{1,12},{2,0},{3,4},{4,5},{5,9},{6,13},{7,1},{8,2},{9,6},{10,... | collective-permute-start | bytes 776 | tf_op jit(solution)/shard_map/ppermute | solution.py:108
  13.8 1.4 %collective-permute-start.5 = (f32[1,64]{1,0:T(1,128)S(1)}, f32[1,64]{1,0:T(1,128)S(1)}, u32[]{:S(2)}, u32[]{:S(2)}) collective-permute-start(f32[1,64]{1,0:T(1,128)S(1)} %shard_map.84), channel_id=1, source_target_pairs={{0,4},{1,0},{2,8},{3,12},{4,1},{5,13},{6,9},{7,5},{8,14},{9,10},{1... | collective-permute-start | bytes 776 | tf_op jit(solution)/shard_map/ppermute | solution.py:108

commit v31 on v28

--- a/solution.py
+++ b/solution.py
@@ -112,16 +112,21 @@
     here = lax.axis_index("dp") * len(senders) + lax.axis_index("layer")
     crossed = [d * len(row) + i for d, row in enumerate(senders) for i, sender in enumerate(row) if sender != i]
     is_crossed = functools.reduce(jnp.logical_or, [here == i for i in crossed])
-    two = lax.dot_general(
-        rows[...], other_block[...], (((1,), (1,)), ((), ())), preferred_element_type=jnp.float32
+    width = own_block.shape[1]
+    kept = width - width // 4
+    rest = pl.ds(kept, width - kept)
+    end, two = (
+        lax.dot_general(left, right, (((1,), (1,)), ((), ())), preferred_element_type=jnp.float32)
+        for left, right in ((rows[:, rest], own_block[:, rest]), (rows[...], other_block[...]))
     )
     both = rows[...].astype(jnp.float32)
     row = jnp.where(is_crossed, both[1:], both[:1])
     lanes = 128
     one = jnp.zeros((own_block.shape[0], lanes), jnp.float32)
-    for at in range(0, own_block.shape[1], lanes):
+    for at in range(0, kept, lanes):
         one += own_block[:, pl.ds(at, lanes)].astype(jnp.float32) * row[:, at : at + lanes]
-    out[...] = jnp.sum(one.T, axis=0, keepdims=True) + jnp.where(is_crossed, two[:1], two[1:])
+    dots = jnp.where(is_crossed, end[1:] + two[:1], end[:1] + two[1:])
+    out[...] = jnp.sum(one.T, axis=0, keepdims=True) + dots
 
 
 def factor_kernel(scale, margin, label, rows, factor):

time: 15.9 us -> 15.9 us (level)
  no operation moved by 1% of the time
where the time goes in v31:
time: 15.9 us; the launch traced here: 15.7 us
  starting transfers between devices  8.46 us (53%)
  Pallas kernels  3.49 us (22%)
  waiting for transfers between devices  1.78 us (11%)
  between operations  1.35 us (8%)
  other arithmetic  0.57 us (4%)
    ppermute x2, starting transfers between devices, fetch_pair(): return lax.ppermute(x, ('dp', 'layer'), moves)  4.89 us
    ppermute x2, starting transfers between devices, to_owner(): return lax.ppermute(x, ('dp', 'layer'), moves)  3 us
    pallas_call x1, Pallas kernels, pair_gradient(): pl.pallas_call(functools.partial(pair_kernel, seq_len), out_shape=jax.Sha...  2.9 us
    ppermute x2, waiting for transfers between devices, swap(): lax.ppermute(x, 'layer', [(i, i ^ 1) for i in range(lax.axis_size('layer'...  1.13 us
    ppermute x2, waiting for transfers between devices, fetch_pair(): return lax.ppermute(x, ('dp', 'layer'), moves)  0.64 us
    pallas_call x2, Pallas kernels, score(): pl.pallas_call(functools.partial(slot_kernel, senders), out_shape=jax.Sha...  0.58 us
    ppermute x2, starting transfers between devices, swap(): lax.ppermute(x, 'layer', [(i, i ^ 1) for i in range(lax.axis_size('layer'...  0.57 us
    mul x1, other arithmetic, shared_scores(): return (to_owner(first, FIRST) + to_owner(second, SECOND)) * factor[None]  0.52 us
  transfers between devices with their start and end apart: 6, of which 2 were waited for; matrix products, arithmetic and copies ran while one was open for 0% of the time, Pallas kernels for 22%

profile of v31, /device:TPU:0, one launch (start us, length us, event | category | flops | bytes accessed | tf_op | source)
XLA Modules:
  0.0 15.7 jit_solution(11024916743830951169)
XLA Ops:
  0.0 0.5 %collective-permute-start.2 = (bf16[64,4096]{1,0:T(8,128)(2,1)}, bf16[64,4096]{1,0:T(8,128)(2,1)S(1)}, u32[]{:S(2)}, u32[]{:S(2)}) collective-permute-start(bf16[64,4096]{1,0:T(8,128)(2,1)} %bitcast.12), channel_id=1, source_target_pairs={{0,1},{1,0},{2,3},{3,2},{4,5},{5,4},{6,7},{7,6},{8,9},{9,8},{10,11... | collective-permute-start | bytes 1572872 | tf_op jit(solution)/shard_map/ppermute | solution.py:95
  0.5 0.0 copy-start
  0.5 2.9 %shard_map.82 = f32[32,128]{1,0:T(8,128)S(1)} custom-call(bf16[128,4096]{1,0:T(8,128)(2,1)} %bitcast.16, bf16[128,4096]{1,0:T(8,128)(2,1)} %bitcast.17, bf16[64,4096]{1,0:T(8,128)(2,1)} %bitcast.18, bf16[64,4096]{1,0:T(8,128)(2,1)} %bitcast.19, s32[1,2]{1,0:T(1,128)} %lengths.1), custom_call_target="tpu_custom_call" | custom-call | flops 134217728 | bytes 3145728 | tf_op jit(solution)/shard_map/pallas_call | solution.py:60
  3.4 0.1 collective-permute-start
  3.5 1.1 %collective-permute-done = bf16[1,4096]{1,0:T(2,128)(2,1)S(1)} collective-permute-done((bf16[1,4096]{1,0:T(2,128)(2,1)S(1)}, bf16[1,4096]{1,0:T(2,128)(2,1)S(1)}, u32[]{:S(2)}, u32[]{:S(2)}) %collective-permute-start) | collective-permute-done | bytes 8224 | tf_op jit(solution)/shard_map/ppermute | solution.py:95
  4.7 3.8 %collective-permute-start.1 = (bf16[2,4096]{1,0:T(2,128)(2,1)S(1)}, bf16[2,4096]{1,0:T(2,128)(2,1)S(1)}, u32[]{:S(2)}, u32[]{:S(2)}) collective-permute-start(bf16[2,4096]{1,0:T(2,128)(2,1)S(1)} %pad_maximum_fusion.rows), channel_id=1, source_target_pairs={{8,0},{12,1},{3,2},{6,3},{5,4},{9,5},{15,6},{2,7},{0,8},{4,9},{14,... | collective-permute-start | bytes 49160 | tf_op jit(solution)/shard_map/ppermute | solution.py:102
  8.5 1.1 %collective-permute-start.4 = (bf16[2,4096]{1,0:T(2,128)(2,1)S(1)}, bf16[2,4096]{1,0:T(2,128)(2,1)S(1)}, u32[]{:S(2)}, u32[]{:S(2)}) collective-permute-start(bf16[2,4096]{1,0:T(2,128)(2,1)S(1)} %pad_maximum_fusion.rows), channel_id=1, source_target_pairs={{4,0},{0,1},{11,2},{14,3},{1,4},{13,5},{10,6},{6,7},{12,8},{8,9},{... | collective-permute-start | bytes 49160 | tf_op jit(solution)/shard_map/ppermute | solution.py:102
  9.6 0.6 %collective-permute-done.1.rows = bf16[2,4096]{1,0:T(2,128)(2,1)S(1)} collective-permute-done((bf16[2,4096]{1,0:T(2,128)(2,1)S(1)}, bf16[2,4096]{1,0:T(2,128)(2,1)S(1)}, u32[]{:S(2)}, u32[]{:S(2)}) %collective-permute-start.1) | collective-permute-done | bytes 16416 | tf_op jit(solution)/shard_map/ppermute | solution.py:102
  10.2 0.0 collective-permute-done.2.other_block
  10.2 0.0 copy-done
  10.2 0.3 %shard_map.83 = f32[1,64]{1,0:T(1,128)S(1)} custom-call(bf16[2,4096]{1,0:T(2,128)(2,1)S(1)} %collective-permute-done.1.rows, bf16[64,4096]{1,0:T(8,128)(2,1)S(1)} %bitcast.13, bf16[64,4096]{1,0:T(8,128)(2,1)S(1)} %collective-permute-done.2.other_block), custom_call_target="tpu_custom_call" | custom-call | flops 2097152 | bytes 1048576 | tf_op jit(solution)/shard_map/pallas_call | solution.py:151
  10.5 3.0 %collective-permute-start.3 = (f32[1,64]{1,0:T(1,128)S(1)}, f32[1,64]{1,0:T(1,128)S(1)}, u32[]{:S(2)}, u32[]{:S(2)}) collective-permute-start(f32[1,64]{1,0:T(1,128)S(1)} %shard_map.83), channel_id=1, source_target_pairs={{0,8},{1,12},{2,0},{3,4},{4,5},{5,9},{6,13},{7,1},{8,2},{9,6},{10,... | collective-permute-start | bytes 776 | tf_op jit(solution)/shard_map/ppermute | solution.py:108
  13.5 0.0 collective-permute-done.4.rows
  13.5 0.3 %shard_map.84 = f32[1,64]{1,0:T(1,128)S(1)} custom-call(bf16[2,4096]{1,0:T(2,128)(2,1)S(1)} %collective-permute-done.4.rows, bf16[64,4096]{1,0:T(8,128)(2,1)S(1)} %bitcast.14, bf16[64,4096]{1,0:T(8,128)(2,1)S(1)} %collective-permute-done.2.other_block), custom_call_target="tpu_custom_call" | custom-call | flops 2097152 | bytes 1048576 | tf_op jit(solution)/shard_map/pallas_call | solution.py:151
  13.8 0.0 collective-permute-start.5
  15.1 0.0 collective-permute-done.3
  15.1 0.0 collective-permute-done.5
  15.1 0.5 %bitcast_multiply_fusion = f32[1,64]{1,0:T(1,128)} fusion(f32[64]{0:T(128)S(1)} %shard_map.85, f32[1,64]{1,0:T(1,128)S(1)} %collective-permute-done.3, f32[1,64]{1,0:T(1,128)S(1)} %collective-permute-done.5), kind=kLoop, calls=%fused_computation.1 | loop fusion | flops 128 | bytes 1024 | tf_op jit(solution)/shard_map/mul | solution.py:161
  (3 shorter events, 0.1 us)
Async XLA Ops:
  0.0 10.2 %collective-permute-start.2 = (bf16[64,4096]{1,0:T(8,128)(2,1)}, bf16[64,4096]{1,0:T(8,128)(2,1)S(1)}, u32[]{:S(2)}, u32[]{:S(2)}) collective-permute-start(bf16[64,4096]{1,0:T(8,128)(2,1)} %bitcast.12), channel_id=1, source_target_pairs={{0,1},{1,0},{2,3},{3,2},{4,5},{5,4},{6,7},{7,6},{8,9},{9,8},{10,11... | collective-permute-start | bytes 1572872 | tf_op jit(solution)/shard_map/ppermute | solution.py:95
  0.5 9.8 %copy-start = (bf16[64,1,4096]{2,0,1:T(8,128)(2,1)S(1)}, bf16[64,1,4096]{2,0,1:T(8,128)(2,1)}, u32[]{:S(2)}) copy-start(bf16[64,1,4096]{2,0,1:T(8,128)(2,1)} %param.12) | copy-start | bytes 1572868
  3.4 1.2 %collective-permute-start = (bf16[1,4096]{1,0:T(2,128)(2,1)S(1)}, bf16[1,4096]{1,0:T(2,128)(2,1)S(1)}, u32[]{:S(2)}, u32[]{:S(2)}) collective-permute-start(bf16[1,4096]{1,0:T(2,128)(2,1)S(1)} %convert.11), channel_id=1, source_target_pairs={{0,1},{1,0},{2,3},{3,2},{4,5},{5,4},{6,7},{7,6},{8,9},{9,8},{10,11... | collective-permute-start | bytes 24584 | tf_op jit(solution)/shard_map/ppermute | solution.py:95
  4.7 5.5 %collective-permute-start.1 = (bf16[2,4096]{1,0:T(2,128)(2,1)S(1)}, bf16[2,4096]{1,0:T(2,128)(2,1)S(1)}, u32[]{:S(2)}, u32[]{:S(2)}) collective-permute-start(bf16[2,4096]{1,0:T(2,128)(2,1)S(1)} %pad_maximum_fusion.rows), channel_id=1, source_target_pairs={{8,0},{12,1},{3,2},{6,3},{5,4},{9,5},{15,6},{2,7},{0,8},{4,9},{14,... | collective-permute-start | bytes 49160 | tf_op jit(solution)/shard_map/ppermute | solution.py:102
  8.5 5.0 %collective-permute-start.4 = (bf16[2,4096]{1,0:T(2,128)(2,1)S(1)}, bf16[2,4096]{1,0:T(2,128)(2,1)S(1)}, u32[]{:S(2)}, u32[]{:S(2)}) collective-permute-start(bf16[2,4096]{1,0:T(2,128)(2,1)S(1)} %pad_maximum_fusion.rows), channel_id=1, source_target_pairs={{4,0},{0,1},{11,2},{14,3},{1,4},{13,5},{10,6},{6,7},{12,8},{8,9},{... | collective-permute-start | bytes 49160 | tf_op jit(solution)/shard_map/ppermute | solution.py:102
  10.5 4.6 %collective-permute-start.3 = (f32[1,64]{1,0:T(1,128)S(1)}, f32[1,64]{1,0:T(1,128)S(1)}, u32[]{:S(2)}, u32[]{:S(2)}) collective-permute-start(f32[1,64]{1,0:T(1,128)S(1)} %shard_map.83), channel_id=1, source_target_pairs={{0,8},{1,12},{2,0},{3,4},{4,5},{5,9},{6,13},{7,1},{8,2},{9,6},{10,... | collective-permute-start | bytes 776 | tf_op jit(solution)/shard_map/ppermute | solution.py:108
  13.8 1.4 %collective-permute-start.5 = (f32[1,64]{1,0:T(1,128)S(1)}, f32[1,64]{1,0:T(1,128)S(1)}, u32[]{:S(2)}, u32[]{:S(2)}) collective-permute-start(f32[1,64]{1,0:T(1,128)S(1)} %shard_map.84), channel_id=1, source_target_pairs={{0,4},{1,0},{2,8},{3,12},{4,1},{5,13},{6,9},{7,5},{8,14},{9,10},{1... | collective-permute-start | bytes 776 | tf_op jit(solution)/shard_map/ppermute | solution.py:108
